TPU v7x, 32 devices: a whole 2x2x4 slice. The times are simulated.
32 devices in a mesh: grp: 8 (over y, x, core), rep: 4 (over z).
Axes of the slice: x: 2, y: 2, z: 4, core: 2. Of those that a mesh axis runs over, the one named last changes fastest.
Arguments:
- tokens: bfloat16 [16384, 1536], P(('grp', 'rep')), may hold values from -6 to 6
- condition: bfloat16 [64, 1536], P(('grp', 'rep')), may hold values from -6 to 6
- caption: bfloat16 [64, 128, 4096], P(('grp', 'rep')), may hold values from -6 to 6
- caption_len: int32 [64], P(('grp', 'rep')), may hold values from 16 to 128, as said below
- item_kind: int32 [64], P(('grp', 'rep')), may hold values 0 or 1
- out_cotangent: bfloat16 [16384, 1536], P(('grp', 'rep')), may hold values from -6 to 6
- norm_gains: bfloat16 [6, 1536], P(None, ('grp', 'rep')), may hold values from 0.099609375 to 1.8984375
- ada_weight: bfloat16 [1536, 6144], P(('grp', 'rep')), may hold values from -0.15625 to 0.15625
- qkv_weight: bfloat16 [1536, 4608], P(('grp', 'rep')), may hold values from -0.15625 to 0.15625
- out_weight: bfloat16 [1536, 1536], P(('grp', 'rep')), may hold values from -1.25 to 1.25
- text_weight: bfloat16 [4096, 3072], P(('grp', 'rep')), may hold values from -0.09375 to 0.09375
- gate_up_weight: bfloat16 [1536, 8192], P(('grp', 'rep')), may hold values from -0.15625 to 0.15625
- down_weight: bfloat16 [4096, 1536], P(('grp', 'rep')), may hold values from -0.1875 to 0.1875
Outputs:
- layer_out: bfloat16 [16384, 1536], P(('grp', 'rep'))
- tokens_grad: float32 [16384, 1536], P(('grp', 'rep'))
- norm_gains_grad: float32 [6, 1536], P(None, ('grp', 'rep'))
- ada_weight_grad: float32 [1536, 6144], P(('grp', 'rep'))
- qkv_weight_grad: float32 [1536, 4608], P(('grp', 'rep'))
- out_weight_grad: float32 [1536, 1536], P(('grp', 'rep'))
- text_weight_grad: float32 [4096, 3072], P(('grp', 'rep'))
- gate_up_weight_grad: float32 [1536, 8192], P(('grp', 'rep'))
- down_weight_grad: float32 [4096, 1536], P(('grp', 'rep'))
Inputs may be any that keep to these rules, and one draw needn't show every extreme that they name: Slots below caption_len of an item hold its caption, the rest of its 128 slots are padding; some item uses all 128. `item_kind`: 1 marks a clip of four frames of (8) x (8) patches, 0 an image of 16 x 16 patches.
All inputs are finite; a program needn't handle non-finite values. No bound on the sum of `item_kind` on one device may be relied on, other than what follows from the above.
Results may differ from a plain program's by a relative error of at most 0.02.
Values may be sent and summed in bfloat16 or wider, within the bound.
No kernel may reach another device: no remote copies, remote signals or barrier semaphores. Data moves between devices by JAX's collectives and lax.ppermute only.
A program may use at most 384 MiB of HBM per device.

v0:
```python
import math

import jax
import jax.numpy as jnp
from jax import lax
from jax.sharding import PartitionSpec as P

D = 1536
HEADS = 24
HEAD_DIM = 64
TEXT_DIM = 4096
SIDE = 16


EPSILON = 1e-06


def norm_rows(values, gain_row):
    return (
        values * lax.rsqrt(jnp.mean(values * values, axis=-1, keepdims=True) + EPSILON) * gain_row
    )


def turn_half(values):
    first_q, second, third_q, fourth = jnp.split(values, 4, axis=-1)
    return jnp.concatenate([-second, first_q, -fourth, third_q], axis=-1)


def rope_tables(item_kind, item_len):
    position = jnp.arange(item_len, dtype=jnp.int32)[None, :]
    half_side = SIDE // 2
    frame_index = position // (half_side * half_side)
    within = position % (half_side * half_side)
    is_clip = item_kind[:, None] == 1
    row_index = jnp.where(is_clip, frame_index * half_side + within // half_side, position // SIDE)
    columns = jnp.where(is_clip, within % half_side, position % SIDE)
    lane_index = jnp.arange(HEAD_DIM, dtype=jnp.int32)
    quarter = HEAD_DIM // 4
    frequency = jnp.exp(-(lane_index % quarter).astype(jnp.float32) * (math.log(10000.0) / quarter))
    coordinate = jnp.where(
        lane_index[None, None, :] < 2 * quarter, row_index[:, :, None], columns[:, :, None]
    ).astype(jnp.float32)
    angles = coordinate * frequency
    return (jnp.cos(angles), jnp.sin(angles))


def modulate(values, gain_row, scaling):
    return norm_rows(values, gain_row) * (1.0 + scaling[:, None, :])


def rotated_norm(values, gain_row, cosine, sine_table):
    normal_rows = norm_rows(values, gain_row)
    return normal_rows * cosine[:, :, None, :] + turn_half(normal_rows) * sine_table[:, :, None, :]


def silu_product(gate_half, up_half):
    return jax.nn.silu(gate_half) * up_half


def score_rows(queries, key_rows, text_valid, scaling):
    scores = (
        jnp.einsum("ishd,ithd->ihst", queries, key_rows, preferred_element_type=jnp.float32)
        * scaling
    )
    if text_valid is not None:
        scores = jnp.where(text_valid, scores, -1e30)
    return scores


def attend(queries, key_rows, values, text_valid, scaling):
    scores = score_rows(queries, key_rows, text_valid, scaling)
    row_max = jnp.max(scores, axis=-1, keepdims=True)
    shifted = jnp.exp(scores - row_max)
    row_sum = jnp.sum(shifted, axis=-1, keepdims=True)
    attn_probs = (shifted / row_sum).astype(jnp.bfloat16)
    attended = jnp.einsum("ihst,ithd->ishd", attn_probs, values, preferred_element_type=jnp.float32)
    return (attended, row_max + jnp.log(row_sum))


def attend_back(queries, key_rows, values, text_valid, scaling, log_sum, grad_attended):
    scores = score_rows(queries, key_rows, text_valid, scaling)
    attn_probs = jnp.exp(scores - log_sum)
    grad_values = jnp.einsum(
        "ihst,ishd->ithd",
        attn_probs.astype(jnp.bfloat16),
        grad_attended,
        preferred_element_type=jnp.float32,
    )
    grad_probs = jnp.einsum(
        "ishd,ithd->ihst", grad_attended, values, preferred_element_type=jnp.float32
    )
    inner_sum = jnp.sum(attn_probs * grad_probs, axis=-1, keepdims=True)
    grad_scores = (attn_probs * (grad_probs - inner_sum)).astype(jnp.bfloat16)
    grad_queries = (
        jnp.einsum("ihst,ithd->ishd", grad_scores, key_rows, preferred_element_type=jnp.float32)
        * scaling
    )
    grad_keys = (
        jnp.einsum("ihst,ishd->ithd", grad_scores, queries, preferred_element_type=jnp.float32)
        * scaling
    )
    return (grad_queries, grad_keys, grad_values)


def gather_text_ada(norm_gains, ada_weight, text_weight):
    return (
        lax.all_gather(norm_gains, ("grp", "rep"), axis=1, tiled=True),
        lax.all_gather(ada_weight, ("grp", "rep"), axis=0, tiled=True),
        lax.all_gather(text_weight, ("grp", "rep"), axis=0, tiled=True),
    )


def gather_attention(qkv_weight, out_weight):
    return (
        lax.all_gather(qkv_weight, ("grp", "rep"), axis=0, tiled=True),
        lax.all_gather(out_weight, ("grp", "rep"), axis=0, tiled=True),
    )


def gather_mlp(gate_up_weight, down_weight):
    return (
        lax.all_gather(gate_up_weight, ("grp", "rep"), axis=0, tiled=True),
        lax.all_gather(down_weight, ("grp", "rep"), axis=0, tiled=True),
    )


def reduce_mlp(grad_terms):
    grouped = (
        lax.psum_scatter(
            grad_terms[0].astype(jnp.bfloat16), "grp", scatter_dimension=0, tiled=True
        ).astype(jnp.float32),
        lax.psum_scatter(
            grad_terms[1].astype(jnp.bfloat16), "grp", scatter_dimension=0, tiled=True
        ).astype(jnp.float32),
    )
    summed = (
        lax.psum_scatter(
            grouped[0].astype(jnp.bfloat16), "rep", scatter_dimension=0, tiled=True
        ).astype(jnp.float32),
        lax.psum_scatter(
            grouped[1].astype(jnp.bfloat16), "rep", scatter_dimension=0, tiled=True
        ).astype(jnp.float32),
    )
    return summed


def reduce_attention(grad_terms):
    grouped = (
        lax.psum_scatter(
            grad_terms[0].astype(jnp.bfloat16), "grp", scatter_dimension=0, tiled=True
        ).astype(jnp.float32),
        lax.psum_scatter(
            grad_terms[1].astype(jnp.bfloat16), "grp", scatter_dimension=0, tiled=True
        ).astype(jnp.float32),
    )
    summed = (
        lax.psum_scatter(
            grouped[0].astype(jnp.bfloat16), "rep", scatter_dimension=0, tiled=True
        ).astype(jnp.float32),
        lax.psum_scatter(
            grouped[1].astype(jnp.bfloat16), "rep", scatter_dimension=0, tiled=True
        ).astype(jnp.float32),
    )
    return summed


def reduce_text_ada(grad_terms):
    grouped = (
        lax.psum_scatter(
            grad_terms[0].astype(jnp.bfloat16), "grp", scatter_dimension=1, tiled=True
        ).astype(jnp.float32),
        lax.psum_scatter(
            grad_terms[1].astype(jnp.bfloat16), "grp", scatter_dimension=0, tiled=True
        ).astype(jnp.float32),
        lax.psum_scatter(
            grad_terms[2].astype(jnp.bfloat16), "grp", scatter_dimension=0, tiled=True
        ).astype(jnp.float32),
    )
    summed = (
        lax.psum_scatter(
            grouped[0].astype(jnp.bfloat16), "rep", scatter_dimension=1, tiled=True
        ).astype(jnp.float32),
        lax.psum_scatter(
            grouped[1].astype(jnp.bfloat16), "rep", scatter_dimension=0, tiled=True
        ).astype(jnp.float32),
        lax.psum_scatter(
            grouped[2].astype(jnp.bfloat16), "rep", scatter_dimension=0, tiled=True
        ).astype(jnp.float32),
    )
    return summed


def local(
    tokens,
    condition,
    caption,
    caption_len,
    item_kind,
    out_cotangent,
    norm_gains,
    ada_weight,
    qkv_weight,
    out_weight,
    text_weight,
    gate_up_weight,
    down_weight,
):
    item_count = condition.shape[0]
    item_len = tokens.shape[0] // item_count
    text_len = caption.shape[1]
    row_count = item_count * item_len
    text_count = item_count * text_len
    scaling = HEAD_DIM ** (-0.5)
    head_shape = (HEADS, HEAD_DIM)
    full_shape = (item_count, item_len, HEADS, HEAD_DIM)
    text_shape = (item_count, text_len, HEADS, HEAD_DIM)
    gains_full, ada_full, text_full = gather_text_ada(norm_gains, ada_weight, text_weight)
    qkv_full, out_full = gather_attention(qkv_weight, out_weight)
    gate_up_full, down_full = gather_mlp(gate_up_weight, down_weight)
    gain_rows = gains_full.astype(jnp.float32)
    activated = jax.nn.silu(condition.astype(jnp.float32)).astype(jnp.bfloat16)
    modulation = jnp.dot(activated, ada_full, preferred_element_type=jnp.float32)
    scale_attn, gate_attn, scale_mlp, gate_mlp = jnp.split(modulation, 4, axis=1)
    cosine, sine_table = rope_tables(item_kind, item_len)

    def rotate_rows(values, gain_row):
        return rotated_norm(values, gain_row, cosine, sine_table)

    token_rows = tokens.astype(jnp.float32).reshape(item_count, item_len, D)
    normed = (
        modulate(token_rows, gain_rows[0], scale_attn).astype(jnp.bfloat16).reshape(row_count, D)
    )
    qkv_rows = jnp.dot(normed, qkv_full, preferred_element_type=jnp.float32)
    query_raw, key_raw, value_raw = [
        section.reshape(full_shape) for section in jnp.split(qkv_rows, 3, axis=1)
    ]
    query_gain = gain_rows[1].reshape(head_shape)
    key_gain = gain_rows[2].reshape(head_shape)
    text_gain = gain_rows[3].reshape(head_shape)
    queries = rotate_rows(query_raw, query_gain).astype(jnp.bfloat16)
    key_rows = rotate_rows(key_raw, key_gain).astype(jnp.bfloat16)
    values = value_raw.astype(jnp.bfloat16)
    caption_rows = caption.reshape(text_count, TEXT_DIM)
    text_proj = jnp.dot(caption_rows, text_full, preferred_element_type=jnp.float32)
    text_key_raw, text_value_raw = [
        section.reshape(text_shape) for section in jnp.split(text_proj, 2, axis=1)
    ]
    text_keys = norm_rows(text_key_raw, text_gain).astype(jnp.bfloat16)
    text_values = text_value_raw.astype(jnp.bfloat16)
    text_valid = (jnp.arange(text_len, dtype=jnp.int32)[None, :] < caption_len[:, None])[
        :, None, None, :
    ]
    own_out, own_logsum = attend(queries, key_rows, values, None, scaling)
    text_out, text_logsum = attend(queries, text_keys, text_values, text_valid, scaling)
    cross_gate = jnp.tanh(gain_rows[5])
    text_flat = text_out.reshape(item_count, item_len, D)
    mixed_heads = (
        (own_out.reshape(item_count, item_len, D) + cross_gate * text_flat)
        .astype(jnp.bfloat16)
        .reshape(row_count, D)
    )
    branch = jnp.dot(mixed_heads, out_full, preferred_element_type=jnp.float32).reshape(
        item_count, item_len, D
    )
    attn_gate = jnp.tanh(gate_attn)[:, None, :]
    middle = token_rows + attn_gate * branch
    mlp_input = modulate(middle, gain_rows[4], scale_mlp).astype(jnp.bfloat16).reshape(row_count, D)
    gate_up = jnp.dot(mlp_input, gate_up_full, preferred_element_type=jnp.float32)
    gate_half, up_half = jnp.split(gate_up, 2, axis=1)
    hidden = silu_product(gate_half, up_half).astype(jnp.bfloat16)
    result = jnp.dot(hidden, down_full, preferred_element_type=jnp.float32).reshape(
        item_count, item_len, D
    )
    mlp_gate = jnp.tanh(gate_mlp)[:, None, :]
    layer_out = (middle + mlp_gate * result).astype(jnp.bfloat16).reshape(row_count, D)
    qkv_back, out_back = gather_attention(qkv_weight, out_weight)
    gate_up_back, down_back = gather_mlp(gate_up_weight, down_weight)
    grad_top = out_cotangent.astype(jnp.float32).reshape(item_count, item_len, D)
    grad_mlp_gate = jnp.sum(grad_top * result, axis=1) * (1.0 - jnp.tanh(gate_mlp) ** 2)
    grad_result = (mlp_gate * grad_top).astype(jnp.bfloat16).reshape(row_count, D)
    down_grad = jnp.einsum("nf,nd->fd", hidden, grad_result, preferred_element_type=jnp.float32)
    grad_hidden = jnp.einsum(
        "nd,fd->nf", grad_result, down_back, preferred_element_type=jnp.float32
    )
    unused, pull_silu = jax.vjp(silu_product, gate_half, up_half)
    grad_gate, grad_up = pull_silu(grad_hidden)
    grad_gate_rows = jnp.concatenate([grad_gate, grad_up], axis=1).astype(jnp.bfloat16)
    gate_up_grad = jnp.einsum(
        "nd,nf->df", mlp_input, grad_gate_rows, preferred_element_type=jnp.float32
    )
    grad_mlp_input = jnp.einsum(
        "nf,df->nd", grad_gate_rows, gate_up_back, preferred_element_type=jnp.float32
    )
    unused, pull_mlp_norm = jax.vjp(modulate, middle, gain_rows[4], scale_mlp)
    grad_middle_norm, grad_mlp_gain, grad_scale_mlp = pull_mlp_norm(
        grad_mlp_input.reshape(item_count, item_len, D)
    )
    grad_middle = grad_top + grad_middle_norm
    gate_up_weight_grad, down_weight_grad = reduce_mlp((gate_up_grad, down_grad))
    grad_attn_gate = jnp.sum(grad_middle * branch, axis=1) * (1.0 - jnp.tanh(gate_attn) ** 2)
    grad_branch = (attn_gate * grad_middle).astype(jnp.bfloat16).reshape(row_count, D)
    out_grad = jnp.einsum("nd,ne->de", mixed_heads, grad_branch, preferred_element_type=jnp.float32)
    grad_mixed = jnp.einsum(
        "ne,de->nd", grad_branch, out_back, preferred_element_type=jnp.float32
    ).reshape(item_count, item_len, D)
    grad_cross_gate = jnp.sum(grad_mixed * text_flat, axis=(0, 1)) * (1.0 - cross_gate**2)
    grad_own = grad_mixed.astype(jnp.bfloat16).reshape(full_shape)
    grad_read = (cross_gate * grad_mixed).astype(jnp.bfloat16).reshape(full_shape)
    own_queries, own_keys, own_values = attend_back(
        queries, key_rows, values, None, scaling, own_logsum, grad_own
    )
    read_queries, read_keys, read_values = attend_back(
        queries, text_keys, text_values, text_valid, scaling, text_logsum, grad_read
    )
    unused, pull_query = jax.vjp(rotate_rows, query_raw, query_gain)
    grad_query_raw, grad_query_gain = pull_query(own_queries + read_queries)
    unused, pull_key = jax.vjp(rotate_rows, key_raw, key_gain)
    grad_key_raw, grad_key_gain = pull_key(own_keys)
    grad_qkv_rows = jnp.concatenate(
        [
            grad_query_raw.reshape(row_count, D),
            grad_key_raw.reshape(row_count, D),
            own_values.reshape(row_count, D),
        ],
        axis=1,
    ).astype(jnp.bfloat16)
    qkv_grad = jnp.einsum("nd,ne->de", normed, grad_qkv_rows, preferred_element_type=jnp.float32)
    grad_normed = jnp.einsum(
        "ne,de->nd", grad_qkv_rows, qkv_back, preferred_element_type=jnp.float32
    )
    qkv_weight_grad, out_weight_grad = reduce_attention((qkv_grad, out_grad))
    unused, pull_text = jax.vjp(norm_rows, text_key_raw, text_gain)
    grad_text_key, grad_text_gain = pull_text(read_keys)
    grad_text_rows = jnp.concatenate(
        [grad_text_key.reshape(text_count, D), read_values.reshape(text_count, D)], axis=1
    ).astype(jnp.bfloat16)
    text_grad = jnp.einsum(
        "nk,ne->ke", caption_rows, grad_text_rows, preferred_element_type=jnp.float32
    )
    unused, pull_attn_norm = jax.vjp(modulate, token_rows, gain_rows[0], scale_attn)
    grad_token_norm, grad_attn_gain, grad_scale_attn = pull_attn_norm(
        grad_normed.reshape(item_count, item_len, D)
    )
    tokens_grad = (grad_middle + grad_token_norm).reshape(row_count, D)
    grad_modulation = jnp.concatenate(
        [grad_scale_attn, grad_attn_gate, grad_scale_mlp, grad_mlp_gate], axis=1
    ).astype(jnp.bfloat16)
    gains_grad = jnp.stack(
        [
            grad_attn_gain,
            grad_query_gain.reshape(D),
            grad_key_gain.reshape(D),
            grad_text_gain.reshape(D),
            grad_mlp_gain,
            grad_cross_gate,
        ],
        axis=0,
    )
    ada_grad = jnp.einsum(
        "id,ie->de", activated, grad_modulation, preferred_element_type=jnp.float32
    )
    norm_gains_grad, ada_weight_grad, text_weight_grad = reduce_text_ada(
        (gains_grad, ada_grad, text_grad)
    )
    return (
        layer_out,
        tokens_grad,
        norm_gains_grad,
        ada_weight_grad,
        qkv_weight_grad,
        out_weight_grad,
        text_weight_grad,
        gate_up_weight_grad,
        down_weight_grad,
    )


def solution(mesh):
    placed = (
        P(("grp", "rep"), None),
        P(("grp", "rep"), None),
        P(("grp", "rep"), None, None),
        P(("grp", "rep")),
        P(("grp", "rep")),
        P(("grp", "rep"), None),
        P(None, ("grp", "rep")),
        P(("grp", "rep"), None),
        P(("grp", "rep"), None),
        P(("grp", "rep"), None),
        P(("grp", "rep"), None),
        P(("grp", "rep"), None),
        P(("grp", "rep"), None),
    )
    return jax.shard_map(
        local,
        mesh=mesh,
        in_specs=placed,
        out_specs=(
            P(("grp", "rep"), None),
            P(("grp", "rep"), None),
            P(None, ("grp", "rep")),
            P(("grp", "rep"), None),
            P(("grp", "rep"), None),
            P(("grp", "rep"), None),
            P(("grp", "rep"), None),
            P(("grp", "rep"), None),
            P(("grp", "rep"), None),
        ),
        check_vma=False,
    )
```

profile of v0, /device:TPU:8, one launch (start us, length us, event | category | flops | bytes accessed | tf_op | source)
XLA Modules:
  0.0 1923.2 jit_solution(12411006885375722546)
XLA Ops:
  11.2 65.5 %all-gather = bf16[32,48,6]{1,2,0:T(8,128)(2,1)S(1)} all-gather(bf16[1,48,6]{1,2,0:T(8,128)(2,1)S(1)} %bitcast.199), channel_id=1, replica_groups=mesh['grp'=8,'rep'=4] {'grp','rep'}, dimensions={0}, use_global_device_ids=true | all-gather | bytes 19008 | tf_op jit(solution)/shard_map/all_gather | solution.py:107
  81.8 54.0 %all-gather.8.cloned.1.call-done = bf16[1536,6144]{1,0:T(8,128)(2,1)} async-done(((bf16[48,6144]{1,0:T(8,128)(2,1)}), bf16[1536,6144]{1,0:T(8,128)(2,1)}) %all-gather.8.cloned.1.call-update) | async-done | bytes 18874384 | tf_op jit(solution)/shard_map/all_gather | solution.py:108
  146.6 93.9 %all-gather.10.cloned.1.call-done = bf16[1536,4608]{1,0:T(8,128)(2,1)} async-done(((bf16[48,4608]{1,0:T(8,128)(2,1)}), bf16[1536,4608]{1,0:T(8,128)(2,1)}) %all-gather.10.cloned.1.call-update) | async-done | bytes 14155792 | tf_op jit(solution)/shard_map/all_gather | solution.py:115
  310.9 84.3 %all-gather.12.cloned.1.call-done = bf16[4096,3072]{1,0:T(8,128)(2,1)} async-done(((bf16[128,3072]{1,0:T(8,128)(2,1)}), bf16[4096,3072]{1,0:T(8,128)(2,1)}) %all-gather.12.cloned.1.call-update) | async-done | bytes 25165840 | tf_op jit(solution)/shard_map/all_gather | solution.py:109
  437.5 24.3 %all-gather.14.cloned.1.call-done = bf16[1536,1536]{1,0:T(8,128)(2,1)} async-done(((bf16[48,1536]{1,0:T(8,128)(2,1)}), bf16[1536,1536]{1,0:T(8,128)(2,1)}) %all-gather.14.cloned.1.call-update) | async-done | bytes 4718608 | tf_op jit(solution)/shard_map/all_gather | solution.py:116
  473.8 142.0 %all-gather.16.cloned.1.call-done = bf16[1536,8192]{1,0:T(8,128)(2,1)} async-done(((bf16[48,8192]{1,0:T(8,128)(2,1)}), bf16[1536,8192]{1,0:T(8,128)(2,1)}) %all-gather.16.cloned.1.call-update) | async-done | bytes 25165840 | tf_op jit(solution)/shard_map/all_gather | solution.py:122
  615.8 21.9 %fusion.98 = f32[512,8192]{1,0:T(8,128)} fusion(bf16[512,1536]{1,0:T(8,128)(2,1)} %bitcast.193, bf16[1536,8192]{1,0:T(8,128)(2,1)} %all-gather.16.cloned.1.call-done), kind=kOutput, calls=%fused_computation.224 | convolution fusion | flops 12884901888 | bytes 43515904 | tf_op jit(solution)/shard_map/dot_general | solution.py:268
  637.7 76.3 %all-gather.18.cloned.1.call-done = bf16[4096,1536]{1,0:T(8,128)(2,1)} async-done(((bf16[128,1536]{1,0:T(8,128)(2,1)}), bf16[4096,1536]{1,0:T(8,128)(2,1)}) %all-gather.18.cloned.1.call-update) | async-done | bytes 12582928 | tf_op jit(solution)/shard_map/all_gather | solution.py:123
  714.0 19.1 fusion.3
  733.1 20.5 %fusion.12 = f32[512,1536]{1,0:T(8,128)} fusion(bf16[1536,8192]{1,0:T(8,128)(2,1)} %all-gather.16.cloned.1.call-done, bf16[512,4096]{1,0:T(8,128)(2,1)} %get-tuple-element.90, bf16[512,4096]{1,0:T(8,128)(2,1)} %get-tuple-element.89), kind=kOutput, calls=%fused_computation.34 | convolution fusion | flops 12901679104 | bytes 36700160 | tf_op jit(solution)/shard_map/nf,df->nd/dot_general | solution.py:291
  862.5 14.3 multiply_reduce_fusion.11
  951.0 20.7 %convolution_convert_fusion = bf16[1536,8192]{1,0:T(8,128)(2,1)} fusion(bf16[512,1536]{1,0:T(8,128)(2,1)} %bitcast.194, bf16[512,4096]{1,0:T(8,128)(2,1)} %get-tuple-element.90, bf16[512,4096]{1,0:T(8,128)(2,1)} %get-tuple-element.89), kind=kOutput, calls=%fused_computation | convolution fusion | flops 12914262016 | bytes 35127296 | tf_op jit(solution)/shard_map/nd,nf->df/dot_general | solution.py:288
  973.0 91.4 %reduce-scatter.39.cloned.1.call-done = bf16[512,1536]{1,0:T(8,128)(2,1)} async-done(((bf16[4096,1536]{1,0:T(8,128)(2,1)}), bf16[512,1536]{1,0:T(8,128)(2,1)}) %reduce-scatter.39.cloned.1.call-update) | async-done | bytes 1572880 | tf_op jit(solution)/shard_map/reduce_scatter | solution.py:132
  1064.5 104.5 %reduce-scatter.25.cloned.1.call-done = bf16[192,4608]{1,0:T(8,128)(2,1)} async-done(((bf16[1536,4608]{1,0:T(8,128)(2,1)}), bf16[192,4608]{1,0:T(8,128)(2,1)}) %reduce-scatter.25.cloned.1.call-update) | async-done | bytes 1769488 | tf_op jit(solution)/shard_map/reduce_scatter | solution.py:149
  1169.1 130.2 %reduce-scatter.21.cloned.1.call-done = bf16[192,6144]{1,0:T(8,128)(2,1)} async-done(((bf16[1536,6144]{1,0:T(8,128)(2,1)}), bf16[192,6144]{1,0:T(8,128)(2,1)}) %reduce-scatter.21.cloned.1.call-update) | async-done | bytes 2359312 | tf_op jit(solution)/shard_map/reduce_scatter | solution.py:172
  1299.3 160.7 %reduce-scatter.33.cloned.1.call-done = bf16[512,3072]{0,1:T(8,128)(2,1)} async-done(((bf16[4096,3072]{0,1:T(8,128)(2,1)}), bf16[512,3072]{0,1:T(8,128)(2,1)}) %reduce-scatter.33.cloned.1.call-update) | async-done | bytes 3145744 | tf_op jit(solution)/shard_map/reduce_scatter | solution.py:175
  1464.8 156.3 %reduce-scatter.35.cloned.1.call-done = bf16[192,8192]{1,0:T(8,128)(2,1)} async-done(((bf16[1536,8192]{1,0:T(8,128)(2,1)}), bf16[192,8192]{1,0:T(8,128)(2,1)}) %reduce-scatter.35.cloned.1.call-update) | async-done | bytes 3145744 | tf_op jit(solution)/shard_map/reduce_scatter | solution.py:129
  1621.1 18.4 reduce-scatter.45.cloned.1.call-done
  1640.9 21.0 %reduce-scatter.31.cloned.1.call-done = bf16[48,1536]{1,0:T(8,128)(2,1)} async-done(((bf16[192,1536]{1,0:T(8,128)(2,1)}), bf16[48,1536]{1,0:T(8,128)(2,1)}) %reduce-scatter.31.cloned.1.call-update) | async-done | bytes 147472 | tf_op jit(solution)/shard_map/reduce_scatter | solution.py:160
  1663.5 35.8 %reduce-scatter.41.cloned.1.call-done = bf16[128,1536]{1,0:T(8,128)(2,1)} async-done(((bf16[512,1536]{1,0:T(8,128)(2,1)}), bf16[128,1536]{1,0:T(8,128)(2,1)}) %reduce-scatter.41.cloned.1.call-update) | async-done | bytes 393232 | tf_op jit(solution)/shard_map/reduce_scatter | solution.py:140
  1701.3 37.8 %reduce-scatter.27.cloned.1.call-done = bf16[48,4608]{1,0:T(8,128)(2,1)} async-done(((bf16[192,4608]{1,0:T(8,128)(2,1)}), bf16[48,4608]{1,0:T(8,128)(2,1)}) %reduce-scatter.27.cloned.1.call-update) | async-done | bytes 442384 | tf_op jit(solution)/shard_map/reduce_scatter | solution.py:157
  1741.0 47.3 %reduce-scatter.23.cloned.1.call-done = bf16[48,6144]{1,0:T(8,128)(2,1)} async-done(((bf16[192,6144]{1,0:T(8,128)(2,1)}), bf16[48,6144]{1,0:T(8,128)(2,1)}) %reduce-scatter.23.cloned.1.call-update) | async-done | bytes 589840 | tf_op jit(solution)/shard_map/reduce_scatter | solution.py:183
  1790.5 60.6 %reduce-scatter.47.cloned.1.call-done = bf16[128,3072]{1,0:T(8,128)(2,1)} async-done(((bf16[512,3072]{1,0:T(8,128)(2,1)}), bf16[128,3072]{1,0:T(8,128)(2,1)}) %reduce-scatter.47.cloned.1.call-update) | async-done | bytes 786448
  1854.0 59.6 %reduce-scatter.37.cloned.1.call-done = bf16[48,8192]{1,0:T(8,128)(2,1)} async-done(((bf16[192,8192]{1,0:T(8,128)(2,1)}), bf16[48,8192]{1,0:T(8,128)(2,1)}) %reduce-scatter.37.cloned.1.call-update) | async-done | bytes 786448 | tf_op jit(solution)/shard_map/reduce_scatter | solution.py:137
  (315 shorter events, 347.1 us)
Async XLA Ops:
  7.2 388.0 %copy-start = (bf16[2,128,4096]{2,1,0:T(8,128)(2,1)S(1)}, bf16[2,128,4096]{2,1,0:T(8,128)(2,1)}, u32[]{:S(2)}) copy-start(bf16[2,128,4096]{2,1,0:T(8,128)(2,1)} %param.15) | copy-start | bytes 6291460
  7.2 128.5 %all-gather.8.cloned.1.call-start = ((), (), s32[]{:S(2)}) async-start(), calls=%async_computation.14 | async-start | bytes 19464192 | tf_op jit(solution)/shard_map/all_gather | solution.py:108
  8.0 232.5 %all-gather.10.cloned.1.call-start = ((), (), s32[]{:S(2)}) async-start(), calls=%async_computation.15 | async-start | bytes 14598144 | tf_op jit(solution)/shard_map/all_gather | solution.py:115
  8.7 386.5 %all-gather.12.cloned.1.call-start = ((), (), s32[]{:S(2)}) async-start(), calls=%async_computation.16 | async-start | bytes 25952256 | tf_op jit(solution)/shard_map/all_gather | solution.py:109
  9.5 452.4 %all-gather.14.cloned.1.call-start = ((), (), s32[]{:S(2)}) async-start(), calls=%async_computation.17 | async-start | bytes 4866048 | tf_op jit(solution)/shard_map/all_gather | solution.py:116
  10.0 605.8 %all-gather.16.cloned.1.call-start = ((), (), s32[]{:S(2)}) async-start(), calls=%async_computation.18 | async-start | bytes 25952256 | tf_op jit(solution)/shard_map/all_gather | solution.py:122
  10.6 703.4 %all-gather.18.cloned.1.call-start = ((), (), s32[]{:S(2)}) async-start(), calls=%async_computation.19 | async-start | bytes 12976128 | tf_op jit(solution)/shard_map/all_gather | solution.py:123
  11.2 960.7 %reduce-scatter.43.cloned.1.call-start = ((), (), s32[]{:S(2)}) async-start(), calls=%async_computation.31 | async-start | bytes 442368
  77.0 343.1 %copy-start.45 = (f32[24,64]{1,0:T(8,128)}, f32[24,64]{1,0:T(8,128)S(1)}, u32[]{:S(2)}) copy-start(f32[24,64]{1,0:T(8,128)S(1)} %mul.653) | copy-start | bytes 18436
  77.1 213.1 %copy-start.52 = (f32[24,64]{1,0:T(8,128)}, f32[24,64]{1,0:T(8,128)S(1)}, u32[]{:S(2)}) copy-start(f32[24,64]{1,0:T(8,128)S(1)} %mul.643) | copy-start | bytes 18436
  77.2 213.0 %copy-start.54 = (f32[24,64]{1,0:T(8,128)}, f32[24,64]{1,0:T(8,128)S(1)}, u32[]{:S(2)}) copy-start(f32[24,64]{1,0:T(8,128)S(1)} %mul.627) | copy-start | bytes 18436
  877.9 94.6 %reduce-scatter.29.cloned.1.call-start = ((), (), s32[]{:S(2)}) async-start(), calls=%async_computation.24 | async-start | bytes 5308416 | tf_op jit(solution)/shard_map/reduce_scatter | solution.py:152
  885.3 179.1 %reduce-scatter.39.cloned.1.call-start = ((), (), s32[]{:S(2)}) async-start(), calls=%async_computation.29 | async-start | bytes 14155776 | tf_op jit(solution)/shard_map/reduce_scatter | solution.py:132
  897.0 272.0 %reduce-scatter.25.cloned.1.call-start = ((), (), s32[]{:S(2)}) async-start(), calls=%async_computation.22 | async-start | bytes 15925248 | tf_op jit(solution)/shard_map/reduce_scatter | solution.py:149
  909.9 389.3 %reduce-scatter.21.cloned.1.call-start = ((), (), s32[]{:S(2)}) async-start(), calls=%async_computation.20 | async-start | bytes 21233664 | tf_op jit(solution)/shard_map/reduce_scatter | solution.py:172
  928.8 531.2 %reduce-scatter.33.cloned.1.call-start = ((), (), s32[]{:S(2)}) async-start(), calls=%async_computation.26 | async-start | bytes 28311552 | tf_op jit(solution)/shard_map/reduce_scatter | solution.py:175
  950.7 670.3 %reduce-scatter.35.cloned.1.call-start = ((), (), s32[]{:S(2)}) async-start(), calls=%async_computation.27 | async-start | bytes 28311552 | tf_op jit(solution)/shard_map/reduce_scatter | solution.py:129
  971.8 667.7 %reduce-scatter.45.cloned.1.call-start = ((), (), s32[]{:S(2)}) async-start(), calls=%async_computation.32 | async-start | bytes 61440
  972.4 689.5 %reduce-scatter.31.cloned.1.call-start = ((), (), s32[]{:S(2)}) async-start(), calls=%async_computation.25 | async-start | bytes 737280 | tf_op jit(solution)/shard_map/reduce_scatter | solution.py:160
  973.0 726.3 %reduce-scatter.41.cloned.1.call-start = ((), (), s32[]{:S(2)}) async-start(), calls=%async_computation.30 | async-start | bytes 1966080 | tf_op jit(solution)/shard_map/reduce_scatter | solution.py:140
  1064.5 674.6 %reduce-scatter.27.cloned.1.call-start = ((), (), s32[]{:S(2)}) async-start(), calls=%async_computation.23 | async-start | bytes 2211840 | tf_op jit(solution)/shard_map/reduce_scatter | solution.py:157
  1169.0 619.3 %reduce-scatter.23.cloned.1.call-start = ((), (), s32[]{:S(2)}) async-start(), calls=%async_computation.21 | async-start | bytes 2949120 | tf_op jit(solution)/shard_map/reduce_scatter | solution.py:183
  1299.3 551.8 %reduce-scatter.47.cloned.1.call-start = ((), (), s32[]{:S(2)}) async-start(), calls=%async_computation.33 | async-start | bytes 3932160
  1464.7 448.9 %reduce-scatter.37.cloned.1.call-start = ((), (), s32[]{:S(2)}) async-start(), calls=%async_computation.28 | async-start | bytes 3932160 | tf_op jit(solution)/shard_map/reduce_scatter | solution.py:137
  (68 other events, 869.8 us)
Sparse Core Ops, SparseCore 0:
  10.9 124.8 all-gather.7
  138.6 101.8 all-gather.9
  243.3 151.8 all-gather.11
  397.8 63.9 all-gather.13
  464.5 151.1 all-gather.15
  618.5 95.4 all-gather.17
  878.0 32.6 reduce-scatter.42
  914.2 53.8 reduce-scatter.28
  972.0 92.3 reduce-scatter.38
  1068.3 100.6 reduce-scatter.24
  1173.1 126.1 reduce-scatter.20
  1303.2 156.8 reduce-scatter.32
  1464.1 156.8 reduce-scatter.34
  1623.2 16.2 reduce-scatter.44
  1641.6 20.2 reduce-scatter.30
  1664.0 35.2 reduce-scatter.40
  1701.5 37.5 reduce-scatter.26
  1741.3 46.9 reduce-scatter.22
  1790.7 60.3 reduce-scatter.46
  1853.4 60.2 reduce-scatter.36
where the time goes:
time: 1930 us; the launch traced here: 1920 us
  waiting for transfers between devices  1400 us (73%)
  matrix products  259 us (13%)
  local copies, waits for them, and re-layouts  93.9 us (5%)
  other arithmetic  84 us (4%)
  blocking collectives  65.5 us (3%)
    reduce_scatter x1, waiting for transfers between devices, reduce_text_ada(): lax.psum_scatter(grad_terms[2].astype(jnp.bfloat16), 'grp', scatter_dimen...  161 us
    reduce_scatter x1, waiting for transfers between devices, reduce_mlp(): lax.psum_scatter(grad_terms[0].astype(jnp.bfloat16), 'grp', scatter_dimen...  156 us
    all_gather x1, waiting for transfers between devices, gather_mlp(): lax.all_gather(gate_up_weight, ('grp', 'rep'), axis=0, tiled=True)  142 us
    reduce_scatter x1, waiting for transfers between devices, reduce_text_ada(): lax.psum_scatter(grad_terms[1].astype(jnp.bfloat16), 'grp', scatter_dimen...  130 us
    reduce_scatter x1, waiting for transfers between devices, reduce_attention(): lax.psum_scatter(grad_terms[0].astype(jnp.bfloat16), 'grp', scatter_dimen...  105 us
    all_gather x1, waiting for transfers between devices, gather_attention(): lax.all_gather(qkv_weight, ('grp', 'rep'), axis=0, tiled=True)  93.9 us
    reduce_scatter x1, waiting for transfers between devices, reduce_mlp(): lax.psum_scatter(grad_terms[1].astype(jnp.bfloat16), 'grp', scatter_dimen...  91.4 us
    all_gather x1, waiting for transfers between devices, gather_text_ada(): lax.all_gather(text_weight, ('grp', 'rep'), axis=0, tiled=True)  84.3 us
  transfers between devices with their start and end apart: 20, of which 18 were waited for; matrix products, arithmetic and copies ran while one was open for 14% of the time, Pallas kernels for 0%

commit v1 on v0

v1 whole, which is shorter than its diff:
```python
import math

import jax
import jax.numpy as jnp
from jax import lax
from jax.sharding import Mesh
from jax.sharding import PartitionSpec as P

D = 1536
HEADS = 24
HEAD_DIM = 64
TEXT_DIM = 4096
FF = 4096
SIDE = 16
RANKS = 4
AXES = ("hi", "mid", "core", "rep")


EPSILON = 1e-06


def norm_rows(values, gain_row):
    return (
        values * lax.rsqrt(jnp.mean(values * values, axis=-1, keepdims=True) + EPSILON) * gain_row
    )


def turn_half(values):
    first_q, second, third_q, fourth = jnp.split(values, 4, axis=-1)
    return jnp.concatenate([-second, first_q, -fourth, third_q], axis=-1)


def rope_tables(item_kind, item_len):
    position = jnp.arange(item_len, dtype=jnp.int32)[None, :]
    half_side = SIDE // 2
    frame_index = position // (half_side * half_side)
    within = position % (half_side * half_side)
    is_clip = item_kind[:, None] == 1
    row_index = jnp.where(is_clip, frame_index * half_side + within // half_side, position // SIDE)
    columns = jnp.where(is_clip, within % half_side, position % SIDE)
    lane_index = jnp.arange(HEAD_DIM, dtype=jnp.int32)
    quarter = HEAD_DIM // 4
    frequency = jnp.exp(-(lane_index % quarter).astype(jnp.float32) * (math.log(10000.0) / quarter))
    coordinate = jnp.where(
        lane_index[None, None, :] < 2 * quarter, row_index[:, :, None], columns[:, :, None]
    ).astype(jnp.float32)
    angles = coordinate * frequency
    return (jnp.cos(angles), jnp.sin(angles))


def modulate(values, gain_row, scaling):
    return norm_rows(values, gain_row) * (1.0 + scaling[:, None, :])


def rotated_norm(values, gain_row, cosine, sine_table):
    normal_rows = norm_rows(values, gain_row)
    return normal_rows * cosine[:, :, None, :] + turn_half(normal_rows) * sine_table[:, :, None, :]


def silu_product(gate_half, up_half):
    return jax.nn.silu(gate_half) * up_half


def score_rows(queries, key_rows, text_valid, scaling):
    scores = (
        jnp.einsum("ishd,ithd->ihst", queries, key_rows, preferred_element_type=jnp.float32)
        * scaling
    )
    if text_valid is not None:
        scores = jnp.where(text_valid, scores, -1e30)
    return scores


def attend(queries, key_rows, values, text_valid, scaling):
    scores = score_rows(queries, key_rows, text_valid, scaling)
    row_max = jnp.max(scores, axis=-1, keepdims=True)
    shifted = jnp.exp(scores - row_max)
    row_sum = jnp.sum(shifted, axis=-1, keepdims=True)
    attn_probs = (shifted / row_sum).astype(jnp.bfloat16)
    attended = jnp.einsum("ihst,ithd->ishd", attn_probs, values, preferred_element_type=jnp.float32)
    return (attended, row_max + jnp.log(row_sum))


def attend_back(queries, key_rows, values, text_valid, scaling, log_sum, grad_attended):
    scores = score_rows(queries, key_rows, text_valid, scaling)
    attn_probs = jnp.exp(scores - log_sum)
    grad_values = jnp.einsum(
        "ihst,ishd->ithd",
        attn_probs.astype(jnp.bfloat16),
        grad_attended,
        preferred_element_type=jnp.float32,
    )
    grad_probs = jnp.einsum(
        "ishd,ithd->ihst", grad_attended, values, preferred_element_type=jnp.float32
    )
    inner_sum = jnp.sum(attn_probs * grad_probs, axis=-1, keepdims=True)
    grad_scores = (attn_probs * (grad_probs - inner_sum)).astype(jnp.bfloat16)
    grad_queries = (
        jnp.einsum("ihst,ithd->ishd", grad_scores, key_rows, preferred_element_type=jnp.float32)
        * scaling
    )
    grad_keys = (
        jnp.einsum("ihst,ishd->ithd", grad_scores, queries, preferred_element_type=jnp.float32)
        * scaling
    )
    return (grad_queries, grad_keys, grad_values)


def dot(left, right):
    return jnp.dot(left, right, preferred_element_type=jnp.float32)


def dot_left(left, right):
    return lax.dot_general(left, right, (((0,), (0,)), ((), ())), preferred_element_type=jnp.float32)


def dot_right(left, right):
    return lax.dot_general(left, right, (((1,), (1,)), ((), ())), preferred_element_type=jnp.float32)


def swap(block, axis, count=2, step=1):
    return lax.ppermute(block, axis, [(at, at ^ step) for at in range(count)])


def spread(block, axis, count):
    if count & (count - 1):
        return lax.all_gather(block, axis)
    block, step = block[None], 1
    while step < count:
        other = swap(block, axis, count, step)
        low = (lax.axis_index(axis) & step) == 0
        block = jnp.where(
            low, jnp.concatenate([block, other]), jnp.concatenate([other, block])
        )
        step *= 2
    return block


def fold(block, axis, count):
    if count & (count - 1):
        return lax.psum_scatter(block, axis, scatter_dimension=0)
    step = count // 2
    while step:
        half = block.shape[0] // 2
        low = (lax.axis_index(axis) & step) == 0
        lower, upper = block[:half], block[half:]
        block = jnp.where(low, lower, upper) + swap(
            jnp.where(low, upper, lower), axis, count, step
        )
        step //= 2
    return block[0]


def trade(block, axis):
    low = lax.axis_index(axis) == 0
    kept = jnp.where(low, block[0], block[1])
    got = swap(jnp.where(low, block[1], block[0]), axis)
    return jnp.where(low, jnp.stack([kept, got]), jnp.stack([got, kept]))


def trade_ranks(block):
    block = trade(block, "mid")
    return jnp.swapaxes(trade(jnp.swapaxes(block, 0, 1), "core"), 0, 1)


def pick(stack, index):
    return lax.dynamic_index_in_dim(stack, index, 0, keepdims=False)


def share(rows):
    far = swap(rows, "mid")
    return (
        jnp.concatenate([rows, swap(rows, "core")]),
        jnp.concatenate([far, swap(far, "core")]),
    )


def settle(near, far):
    half = near.shape[0] // 2
    across = far[:half] + swap(far[half:].astype(jnp.bfloat16), "core").astype(jnp.float32)
    moved = swap(across.astype(jnp.bfloat16), "mid").astype(jnp.float32)
    return near[:half] + swap(near[half:].astype(jnp.bfloat16), "core").astype(jnp.float32) + moved


class Layout:
    def __init__(self, hi, rep, out_rows):
        self.hi, self.rep = hi, rep
        self.aligned = (rep * out_rows) % HEAD_DIM == 0
        self.head_groups = hi if self.aligned else 1
        self.rank = lax.axis_index("mid") * 2 + lax.axis_index("core")

    def by_rank(self, weight, sections, groups):
        rows, columns = weight.shape
        width = columns // (sections * groups * RANKS)
        view = weight.reshape(rows, sections * groups, RANKS, width)
        view = jnp.transpose(view, (2, 0, 1, 3))
        return view.reshape(2, 2, rows, sections * groups * width)

    def from_ranks(self, blocks, sections, groups):
        _, _, rows, per_rank = blocks.shape
        width = per_rank // (sections * groups)
        view = blocks.reshape(RANKS, rows, sections * groups, width)
        return jnp.transpose(view, (1, 2, 0, 3)).reshape(rows, RANKS * per_rank)

    def gather_columns(self, blocks):
        stacked = spread(lax.all_gather(blocks, "rep"), "hi", self.hi)
        natural = jnp.transpose(stacked, (0, 2, 3, 1, 4, 5))
        return natural.reshape(-1, blocks.shape[-1])

    def reduce_columns(self, grad, rows):
        view = grad.astype(jnp.bfloat16).reshape(self.hi, 2, 2, self.rep, rows, -1)
        view = jnp.transpose(view, (0, 3, 1, 2, 4, 5))
        summed = fold(view, "hi", self.hi)
        return lax.psum_scatter(summed, "rep", scatter_dimension=0)

    def gather_rows(self, block):
        stacked = spread(lax.all_gather(block, "rep", tiled=True), "hi", self.hi)
        return stacked.reshape(-1, block.shape[-1])

    def reduce_rows(self, grad):
        summed = fold(grad.astype(jnp.bfloat16).reshape(self.hi, -1, grad.shape[-1]), "hi", self.hi)
        return lax.psum_scatter(summed, "rep", scatter_dimension=0, tiled=True)

    def rank_lanes(self, rows, groups):
        view = rows.reshape(rows.shape[0], groups, RANKS, -1)
        return lax.dynamic_index_in_dim(view, self.rank, 2, keepdims=False).reshape(rows.shape[0], -1)

    def place_lanes(self, row):
        view = row.reshape(self.head_groups, 1, -1)
        at = (jnp.arange(RANKS) == self.rank).astype(row.dtype)[None, :, None]
        return (view * at).reshape(-1)


def local(
    hi_count,
    rep_count,
    tokens,
    condition,
    caption,
    caption_len,
    item_kind,
    out_cotangent,
    norm_gains,
    ada_weight,
    qkv_weight,
    out_weight,
    text_weight,
    gate_up_weight,
    down_weight,
):
    bf16, f32 = jnp.bfloat16, jnp.float32
    item_count = condition.shape[0]
    item_len = tokens.shape[0] // item_count
    text_len = caption.shape[1]
    row_count = item_count * item_len
    rows = qkv_weight.shape[0]
    scaling = HEAD_DIM ** (-0.5)
    plan = Layout(hi_count, rep_count, out_weight.shape[0])
    rank_heads = HEADS // RANKS
    rank_width = rank_heads * HEAD_DIM
    head_shape = (rank_heads, HEAD_DIM)
    hi_at, mid_at, core_at, rep_at = [lax.axis_index(name) for name in AXES]
    device_shape = (hi_count, 2, 2, rep_count)

    qkv_mine = trade_ranks(plan.by_rank(qkv_weight, 3, plan.head_groups))
    text_mine = trade_ranks(plan.by_rank(text_weight, 2, plan.head_groups))
    gate_up_mine = trade_ranks(plan.by_rank(gate_up_weight, 2, hi_count))
    qkv_rank = plan.gather_columns(qkv_mine)
    if plan.aligned:
        out_rank = plan.gather_rows(out_weight)
    else:
        out_whole = lax.all_gather(out_weight, AXES, axis=0, tiled=True)
        out_rank = pick(out_whole.reshape(RANKS, rank_width, D), plan.rank)
    text_rank = plan.gather_columns(text_mine)
    gate_up_rank = plan.gather_columns(gate_up_mine)
    down_rank = plan.gather_rows(down_weight)

    small = jnp.concatenate(
        [
            condition.reshape(-1),
            norm_gains.reshape(-1),
            caption_len.astype(bf16),
            item_kind.astype(bf16),
        ]
    )
    for axis, count in (("rep", rep_count), ("core", 2), ("mid", 2), ("hi", hi_count)):
        small = spread(small, axis, count)
    cut = [condition.size, condition.size + norm_gains.size]
    cut.append(cut[1] + item_count)
    conditions, gains, lengths, kinds = jnp.split(small, cut, axis=-1)
    activated = jax.nn.silu(conditions.astype(f32)).astype(bf16).reshape(-1, D)
    gain_rows = jnp.moveaxis(
        gains.astype(f32).reshape(device_shape + (6, norm_gains.shape[1])), 4, 0
    ).reshape(6, D)
    block_at = ((hi_at * 2 + mid_at) * 2 + core_at) * rep_count + rep_at
    activated_mine = lax.dynamic_slice_in_dim(activated, block_at * rows, rows, axis=1)

    def group_items(values):
        view = lax.dynamic_index_in_dim(pick(values, hi_at), rep_at, 2, keepdims=False)
        near, far = pick(view, mid_at), pick(view, 1 - mid_at)
        order = [core_at, 1 - core_at]
        return [
            jnp.concatenate([pick(side, at) for at in order]).astype(jnp.int32)
            for side in (near, far)
        ]

    near_len, far_len = group_items(lengths)
    near_kind, far_kind = group_items(kinds)

    partial = dot(activated_mine, ada_weight).reshape(device_shape + (item_count, 4 * D))
    partial = fold(jnp.moveaxis(partial, 2, 0), "core", 2)
    partial = fold(jnp.moveaxis(partial, 1, 0), "mid", 2)
    partial = fold(partial, "hi", hi_count)
    modulation = fold(partial, "rep", rep_count)
    scale_attn, gate_attn, scale_mlp, gate_mlp = jnp.split(modulation, 4, axis=1)

    token_rows = tokens.astype(f32).reshape(item_count, item_len, D)
    normed = (
        modulate(token_rows, gain_rows[0], scale_attn).astype(bf16).reshape(row_count, D)
    )
    mlp_gate = jnp.tanh(gate_mlp)[:, None, :]
    grad_top = out_cotangent.astype(f32).reshape(item_count, item_len, D)
    grad_result = (mlp_gate * grad_top).astype(bf16).reshape(row_count, D)
    head_gains = plan.rank_lanes(gain_rows, plan.head_groups)
    query_gain, key_gain, text_gain = [head_gains[at].reshape(head_shape) for at in (1, 2, 3)]
    cross_gate = jnp.tanh(head_gains[5])

    normed_sides = share(normed)
    caption_sides = share(caption.reshape(-1, TEXT_DIM))
    result_sides = share(grad_result)

    def attention(normed_side, caption_side, kind, length):
        count = kind.shape[0]
        full_shape = (count, item_len) + head_shape
        text_shape = (count, text_len) + head_shape
        cosine, sine_table = rope_tables(kind, item_len)
        qkv_rows = dot(normed_side, qkv_rank)
        query_raw, key_raw, value_raw = [
            section.reshape(full_shape) for section in jnp.split(qkv_rows, 3, axis=1)
        ]
        queries = rotated_norm(query_raw, query_gain, cosine, sine_table).astype(bf16)
        key_rows = rotated_norm(key_raw, key_gain, cosine, sine_table).astype(bf16)
        values = value_raw.astype(bf16)
        text_proj = dot(caption_side, text_rank)
        text_key_raw, text_value_raw = [
            section.reshape(text_shape) for section in jnp.split(text_proj, 2, axis=1)
        ]
        text_keys = norm_rows(text_key_raw, text_gain).astype(bf16)
        text_values = text_value_raw.astype(bf16)
        text_valid = (jnp.arange(text_len, dtype=jnp.int32)[None, :] < length[:, None])[
            :, None, None, :
        ]
        own_out, own_logsum = attend(queries, key_rows, values, None, scaling)
        text_out, text_logsum = attend(queries, text_keys, text_values, text_valid, scaling)
        text_flat = text_out.reshape(-1, rank_width)
        mixed = (own_out.reshape(-1, rank_width) + cross_gate * text_flat).astype(bf16)

        def back(grad_branch_side):
            grad_mixed = dot_right(grad_branch_side, out_rank)
            grad_cross_gate = jnp.sum(grad_mixed * text_flat, axis=0) * (1.0 - cross_gate**2)
            grad_own = grad_mixed.astype(bf16).reshape(full_shape)
            grad_read = (cross_gate * grad_mixed).astype(bf16).reshape(full_shape)
            own_queries, own_keys, own_values = attend_back(
                queries, key_rows, values, None, scaling, own_logsum, grad_own
            )
            read_queries, read_keys, read_values = attend_back(
                queries, text_keys, text_values, text_valid, scaling, text_logsum, grad_read
            )

            def rotate_rows(values, gain_row):
                return rotated_norm(values, gain_row, cosine, sine_table)

            _, pull_query = jax.vjp(rotate_rows, query_raw, query_gain)
            grad_query_raw, grad_query_gain = pull_query(own_queries + read_queries)
            _, pull_key = jax.vjp(rotate_rows, key_raw, key_gain)
            grad_key_raw, grad_key_gain = pull_key(own_keys)
            _, pull_text = jax.vjp(norm_rows, text_key_raw, text_gain)
            grad_text_key, grad_text_gain = pull_text(read_keys)
            grad_qkv_rows = jnp.concatenate(
                [part.reshape(-1, rank_width) for part in (grad_query_raw, grad_key_raw, own_values)],
                axis=1,
            ).astype(bf16)
            grad_text_rows = jnp.concatenate(
                [part.reshape(-1, rank_width) for part in (grad_text_key, read_values)], axis=1
            ).astype(bf16)
            gain_terms = jnp.stack(
                [
                    grad_query_gain.reshape(-1),
                    grad_key_gain.reshape(-1),
                    grad_text_gain.reshape(-1),
                    grad_cross_gate,
                ]
            )
            return grad_qkv_rows, grad_text_rows, gain_terms

        return mixed, back

    mixed_far, back_far = attention(normed_sides[1], caption_sides[1], far_kind, far_len)
    mixed_near, back_near = attention(normed_sides[0], caption_sides[0], near_kind, near_len)
    branch = settle(dot(mixed_near, out_rank), dot(mixed_far, out_rank)).reshape(
        item_count, item_len, D
    )
    attn_gate = jnp.tanh(gate_attn)[:, None, :]
    middle = token_rows + attn_gate * branch
    mlp_input = modulate(middle, gain_rows[4], scale_mlp).astype(bf16).reshape(row_count, D)
    input_sides = share(mlp_input)

    def feed(input_side, result_side):
        gate_half, up_half = jnp.split(dot(input_side, gate_up_rank), 2, axis=1)
        hidden = silu_product(gate_half, up_half).astype(bf16)
        grad_hidden = dot_right(result_side, down_rank)
        _, pull_silu = jax.vjp(silu_product, gate_half, up_half)
        grad_gate_rows = jnp.concatenate(pull_silu(grad_hidden), axis=1).astype(bf16)
        return hidden, grad_gate_rows, dot_right(grad_gate_rows, gate_up_rank)

    hidden_near, gate_rows_near, grad_input_near = feed(input_sides[0], result_sides[0])
    hidden_far, gate_rows_far, grad_input_far = feed(input_sides[1], result_sides[1])
    grad_mlp_input = settle(grad_input_near, grad_input_far)
    input_all = jnp.concatenate(input_sides)
    gate_up_grad = dot_left(input_all, jnp.concatenate([gate_rows_near, gate_rows_far]))
    gate_up_parts = plan.reduce_columns(gate_up_grad, rows)
    hidden_all = jnp.concatenate([hidden_near, hidden_far])
    down_grad = dot_left(hidden_all, jnp.concatenate(result_sides))
    down_weight_grad = plan.reduce_rows(down_grad).astype(f32)
    result = settle(dot(hidden_near, down_rank), dot(hidden_far, down_rank)).reshape(
        item_count, item_len, D
    )
    layer_out = (middle + mlp_gate * result).astype(bf16).reshape(row_count, D)
    grad_mlp_gate = jnp.sum(grad_top * result, axis=1) * (1.0 - jnp.tanh(gate_mlp) ** 2)
    _, pull_mlp_norm = jax.vjp(modulate, middle, gain_rows[4], scale_mlp)
    grad_middle_norm, grad_mlp_gain, grad_scale_mlp = pull_mlp_norm(
        grad_mlp_input.reshape(item_count, item_len, D)
    )
    grad_middle = grad_top + grad_middle_norm

    grad_attn_gate = jnp.sum(grad_middle * branch, axis=1) * (1.0 - jnp.tanh(gate_attn) ** 2)
    grad_branch = (attn_gate * grad_middle).astype(bf16).reshape(row_count, D)
    branch_sides = share(grad_branch)
    qkv_rows_near, text_rows_near, gain_terms_near = back_near(branch_sides[0])
    qkv_rows_far, text_rows_far, gain_terms_far = back_far(branch_sides[1])
    grad_normed = settle(dot_right(qkv_rows_near, qkv_rank), dot_right(qkv_rows_far, qkv_rank))
    out_grad = dot_left(jnp.concatenate([mixed_near, mixed_far]), jnp.concatenate(branch_sides))
    if plan.aligned:
        out_weight_grad = plan.reduce_rows(out_grad).astype(f32)
    else:
        at = (jnp.arange(RANKS) == plan.rank).astype(bf16)[:, None, None]
        placed = (out_grad.astype(bf16)[None] * at).reshape(D, D)
        out_weight_grad = lax.psum_scatter(placed, AXES, scatter_dimension=0, tiled=True).astype(f32)
    qkv_grad = dot_left(jnp.concatenate(normed_sides), jnp.concatenate([qkv_rows_near, qkv_rows_far]))
    qkv_parts = plan.reduce_columns(qkv_grad, rows)
    text_grad = dot_left(
        jnp.concatenate(caption_sides), jnp.concatenate([text_rows_near, text_rows_far])
    )
    text_parts = plan.reduce_columns(text_grad, text_weight.shape[0])

    _, pull_attn_norm = jax.vjp(modulate, token_rows, gain_rows[0], scale_attn)
    grad_token_norm, grad_attn_gain, grad_scale_attn = pull_attn_norm(
        grad_normed.reshape(item_count, item_len, D)
    )
    tokens_grad = (grad_middle + grad_token_norm).reshape(row_count, D)

    grad_modulation = jnp.concatenate(
        [grad_scale_attn, grad_attn_gate, grad_scale_mlp, grad_mlp_gate], axis=1
    ).astype(bf16)
    gain_terms = [plan.place_lanes(row) for row in gain_terms_near + gain_terms_far]
    gains_grad = jnp.stack(
        [grad_attn_gain, gain_terms[0], gain_terms[1], gain_terms[2], grad_mlp_gain, gain_terms[3]]
    ).astype(bf16)
    for axis, count in (("rep", rep_count), ("core", 2), ("mid", 2), ("hi", hi_count)):
        both = spread(
            jnp.concatenate([grad_modulation.reshape(-1), gains_grad.reshape(-1)]), axis, count
        )
        grad_modulation = both[:, : grad_modulation.size]
        gains_grad = jnp.sum(
            both[:, grad_modulation[0].size :].astype(f32), axis=0
        ).astype(bf16)
    ada_weight_grad = dot_left(activated_mine, grad_modulation.reshape(-1, 4 * D))
    norm_gains_grad = lax.dynamic_slice_in_dim(
        gains_grad.reshape(6, D), block_at * norm_gains.shape[1], norm_gains.shape[1], axis=1
    ).astype(f32)

    qkv_weight_grad = plan.from_ranks(trade_ranks(qkv_parts), 3, plan.head_groups).astype(f32)
    text_weight_grad = plan.from_ranks(trade_ranks(text_parts), 2, plan.head_groups).astype(f32)
    gate_up_weight_grad = plan.from_ranks(trade_ranks(gate_up_parts), 2, hi_count).astype(f32)
    return (
        layer_out,
        tokens_grad,
        norm_gains_grad,
        ada_weight_grad,
        qkv_weight_grad,
        out_weight_grad,
        text_weight_grad,
        gate_up_weight_grad,
        down_weight_grad,
    )


def solution(mesh):
    grp, rep = mesh.devices.shape
    hi = grp // RANKS
    inner = Mesh(mesh.devices.reshape(hi, 2, 2, rep), AXES)
    rows = P(AXES, None)

    def step(*arrays):
        return local(hi, rep, *arrays)

    return jax.shard_map(
        step,
        mesh=inner,
        in_specs=(
            rows,
            rows,
            P(AXES, None, None),
            P(AXES),
            P(AXES),
            rows,
            P(None, AXES),
            rows,
            rows,
            rows,
            rows,
            rows,
            rows,
        ),
        out_specs=(rows, rows, P(None, AXES), rows, rows, rows, rows, rows, rows),
        check_vma=False,
    )
```

time: 1930 us -> 1100 us (0.57)
  waiting for transfers between devices: 1400 us -> 376 us
  local copies, waits for them, and re-layouts: 93.9 us -> 217 us
  other arithmetic: 84 us -> 189 us
  starting transfers between devices: 1.43 us -> 55.7 us
  blocking collectives: 65.5 us -> 16.8 us
  matrix products: 259 us -> 215 us
    reduce_scatter x11 -> x5, waiting for transfers between devices: 845 us -> 28.1 us  [the longest x3 28.1 us: reduce_columns(): return lax.psum_scatter(summed, 'rep', scatter_dimension=0)]
    all_gather x6 -> x4, waiting for transfers between devices: 475 us -> 34.5 us  [the longest x1 20.7 us: gather_rows(): stacked = spread(lax.all_gather(block, 'rep', tiled=True), 'hi', self.hi)]
    ppermute x0 -> x64, waiting for transfers between devices: none -> 314 us  [swap(): return lax.ppermute(block, axis, [(at, at ^ step) for at in range(count)])]
    unnamed x23 -> x9, waiting for transfers between devices: 83.9 us -> 0.15 us
    ppermute x0 -> x64, starting transfers between devices: none -> 54.9 us  [swap(): return lax.ppermute(block, axis, [(at, at ^ step) for at in range(count)])]
    all_gather x1, blocking collectives: 65.5 us -> 16.8 us  [gather_rows(): stacked = spread(lax.all_gather(block, 'rep', tiled=True), 'hi', self.hi)]
    select_n x1 -> x39, other arithmetic: 0.07 us -> 46.8 us  [the longest x14 25.8 us: spread(): jnp.where(low, jnp.concatenate([block, other]), jnp.concatenate([other, b...]
    dot_general x16 -> x25, matrix products: 210 us -> 169 us  [the longest x6 59 us: dot_left(): lax.dot_general(left, right, (((0,), (0,)), ((), ())), preferred_element_...]
  transfers between devices with their start and end apart: 20 -> 73, of which waited for: 18 -> 24; matrix products, arithmetic and copies ran while one was open for 14% -> 51% of each run, Pallas kernels for 0% -> 0%
where the time goes in v1:
time: 1100 us; the launch traced here: 1090 us
  waiting for transfers between devices  376 us (34%)
  local copies, waits for them, and re-layouts  217 us (20%)
  matrix products  215 us (20%)
  other arithmetic  189 us (17%)
  starting transfers between devices  55.7 us (5%)
  between operations  17.8 us (2%)
  blocking collectives  16.8 us (2%)
    ppermute x64, waiting for transfers between devices, swap(): return lax.ppermute(block, axis, [(at, at ^ step) for at in range(count)])  314 us
    dot_general x6, matrix products, dot_left(): lax.dot_general(left, right, (((0,), (0,)), ((), ())), preferred_element_...  59 us
    dot_general x11, matrix products, dot(): return jnp.dot(left, right, preferred_element_type=jnp.float32)  56.1 us
    ppermute x64, starting transfers between devices, swap(): return lax.ppermute(block, axis, [(at, at ^ step) for at in range(count)])  54.9 us
    unnamed x437, local copies, waits for them, and re-layouts  54.7 us
    dot_general x8, matrix products, dot_right(): lax.dot_general(left, right, (((1,), (1,)), ((), ())), preferred_element_...  54.2 us
    reduce_scatter x3, waiting for transfers between devices, reduce_columns(): return lax.psum_scatter(summed, 'rep', scatter_dimension=0)  28.1 us
    select_n x14, other arithmetic, spread(): jnp.where(low, jnp.concatenate([block, other]), jnp.concatenate([other, b...  25.8 us
  transfers between devices with their start and end apart: 73, of which 24 were waited for; matrix products, arithmetic and copies ran while one was open for 51% of the time, Pallas kernels for 0%

profile of v1, /device:TPU:8, one launch (start us, length us, event | category | flops | bytes accessed | tf_op | source)
XLA Modules:
  0.0 1088.0 jit_solution(13980419229579853374)
XLA Ops:
  20.8 16.8 %all_gather.28 = bf16[192,1536]{1,0:T(8,128)(2,1)S(1)} all-gather(bf16[48,1536]{1,0:T(8,128)(2,1)} %param.22), channel_id=1, replica_groups=mesh['hi'=2,'mid'=2,'core'=2,'rep'=4] {'rep'}, dimensions={0}, use_global_device_ids=true | all-gather | bytes 737280 | tf_op jit(solution)/shard_map/all_gather | solution.py:217
  59.0 16.8 %collective-permute-done.3 = bf16[1,2,4,3364]{3,2,1,0:T(4,128)(2,1)S(1)} collective-permute-done((bf16[1,2,4,3364]{3,2,1,0:T(4,128)(2,1)S(1)}, bf16[1,2,4,3364]{3,2,1,0:T(4,128)(2,1)S(1)}, u32[]{:S(2)}, u32[]{:S(2)}) %collective-permute-start.3) | collective-permute-done | bytes 53856 | tf_op jit(solution)/shard_map/ppermute | solution.py:122
  103.3 9.8 collective-permute-done.6
  143.3 13.7 %all-gather.10.cloned.1.call-done = bf16[8,2,48,1152]{3,2,0,1:T(8,128)(2,1)} async-done(((bf16[2,2,48,1152]{3,2,0,1:T(8,128)(2,1)}), bf16[8,2,48,1152]{3,2,0,1:T(8,128)(2,1)}) %all-gather.10.cloned.1.call-update) | async-done | bytes 1769488 | tf_op jit(solution)/shard_map/all_gather | solution.py:206
  170.6 28.8 %collective-permute-done.20 = bf16[512,1536]{1,0:T(8,128)(2,1)} collective-permute-done((bf16[512,1536]{1,0:T(8,128)(2,1)}, bf16[512,1536]{1,0:T(8,128)(2,1)}, u32[]{:S(2)}, u32[]{:S(2)}) %collective-permute-start.20) | collective-permute-done | bytes 1572896 | tf_op jit(solution)/shard_map/ppermute | solution.py:122
  303.0 42.6 %collective-permute-done.17 = bf16[1,4,2,2,128,768]{5,4,1,3,2,0:T(8,128)(2,1)} collective-permute-done((bf16[1,4,2,2,128,768]{5,4,1,3,2,0:T(8,128)(2,1)}, bf16[1,4,2,2,128,768]{5,4,1,3,2,0:T(8,128)(2,1)}, u32[]{:S(2)}, u32[]{:S(2)}) %collective-permute-start.17) | collective-permute-done | bytes 3145760 | tf_op jit(solution)/shard_map/ppermute | solution.py:122
  409.0 20.7 %all-gather.8.cloned.1.call-done = bf16[512,1536]{1,0:T(8,128)(2,1)} async-done(((bf16[128,1536]{1,0:T(8,128)(2,1)}), bf16[512,1536]{1,0:T(8,128)(2,1)}) %all-gather.8.cloned.1.call-update) | async-done | bytes 1572880 | tf_op jit(solution)/shard_map/all_gather | solution.py:217
  434.9 30.6 %collective-permute-done.25 = bf16[512,1536]{1,0:T(8,128)(2,1)} collective-permute-done((bf16[512,1536]{1,0:T(8,128)(2,1)}, bf16[512,1536]{1,0:T(8,128)(2,1)}, u32[]{:S(2)}, u32[]{:S(2)}) %collective-permute-start.25) | collective-permute-done | bytes 1572896 | tf_op jit(solution)/shard_map/ppermute | solution.py:122
  470.9 29.3 %collective-permute-done.30 = bf16[1,512,1536]{2,1,0:T(8,128)(2,1)} collective-permute-done((bf16[1,512,1536]{2,1,0:T(8,128)(2,1)}, bf16[1,512,1536]{2,1,0:T(8,128)(2,1)}, u32[]{:S(2)}, u32[]{:S(2)}) %collective-permute-start.30) | collective-permute-done | bytes 1572896 | tf_op jit(solution)/shard_map/ppermute | solution.py:122
  538.8 9.9 fusion.128
  548.7 9.5 fusion.60
  566.9 9.2 fusion.63
  597.4 10.1 fusion.87
  609.0 23.4 %collective-permute-done.41 = bf16[512,1536]{1,0:T(8,128)(2,1)S(1)} collective-permute-done((bf16[512,1536]{1,0:T(8,128)(2,1)S(1)}, bf16[512,1536]{1,0:T(8,128)(2,1)S(1)}, u32[]{:S(2)}, u32[]{:S(2)}) %collective-permute-start.41) | collective-permute-done | bytes 1572896 | tf_op jit(solution)/shard_map/ppermute | solution.py:122
  637.7 19.8 %fusion.16 = bf16[1536,2048]{1,0:T(8,128)(2,1)} fusion(bf16[1024,1024]{1,0:T(8,128)(2,1)} %get-tuple-element.99, bf16[1024,1024]{1,0:T(8,128)(2,1)} %get-tuple-element.98, bf16[1024,1024]{1,0:T(8,128)(2,1)} %get-tuple-element.97, bf16[1024,1024]{1,0:T(8,128)(2,1)} %get-tuple-element.96, bf16[512,1536]{1,0:T(8,128)(2,1)} %copy-done.189, ...), kind=kOutput, calls=%fused_computation.16 | convolution fusion | flops 12946767872 | bytes 20971520 | tf_op jit(solution)/shard_map/dot_general | solution.py:114
  660.9 11.3 %collective-permute-done.44 = bf16[512,1536]{1,0:T(8,128)(2,1)} collective-permute-done((bf16[512,1536]{1,0:T(8,128)(2,1)}, bf16[512,1536]{1,0:T(8,128)(2,1)}, u32[]{:S(2)}, u32[]{:S(2)}) %collective-permute-start.44) | collective-permute-done | bytes 1572896 | tf_op jit(solution)/shard_map/ppermute | solution.py:122
  711.4 46.1 %collective-permute-done.56 = bf16[1,192,1536]{2,1,0:T(8,128)(2,1)S(1)} collective-permute-done((bf16[1,192,1536]{2,1,0:T(8,128)(2,1)S(1)}, bf16[1,192,1536]{2,1,0:T(8,128)(2,1)S(1)}, u32[]{:S(2)}, u32[]{:S(2)}) %collective-permute-start.56) | collective-permute-done | bytes 589856 | tf_op jit(solution)/shard_map/ppermute | solution.py:122
  808.5 11.4 %fusion.19 = bf16[4096,768]{1,0:T(8,128)(2,1)} fusion(bf16[256,4096]{1,0:T(8,128)(2,1)} %collective-permute-done.23, bf16[256,4096]{1,0:T(8,128)(2,1)} %collective-permute-done.22, bf16[256,4096]{1,0:T(8,128)(2,1)} %collective-permute-done.14, bf16[256,4096]{1,0:T(8,128)(2,1)} %bitcast.37, bf16[512,384]{0,1:T(8,128)(2,1)S(1)} %bitcast.600, ...), kind=kOutput, calls=%fused_computation.18 | convolution fusion | flops 6485442560 | bytes 16252928 | tf_op jit(solution)/shard_map/dot_general | solution.py:114
  898.0 10.5 convolution_convert_fusion
  916.1 17.3 %collective-permute-done.47 = bf16[512,1536]{1,0:T(8,128)(2,1)} collective-permute-done((bf16[512,1536]{1,0:T(8,128)(2,1)}, bf16[512,1536]{1,0:T(8,128)(2,1)}, u32[]{:S(2)}, u32[]{:S(2)}) %collective-permute-start.47) | collective-permute-done | bytes 1572896 | tf_op jit(solution)/shard_map/ppermute | solution.py:122
  933.5 10.3 fusion.105
  980.8 10.2 collective-permute-done.51
  1032.5 28.0 %reduce-scatter.10.cloned.1.call-done = bf16[1,2,2,128,768]{3,4,2,1,0:T(8,128)(2,1)} async-done(((bf16[4,2,2,128,768]{3,4,2,1,0:T(8,128)(2,1)}), bf16[1,2,2,128,768]{3,4,2,1,0:T(8,128)(2,1)}) %reduce-scatter.10.cloned.1.call-update) | async-done | bytes 786448 | tf_op jit(solution)/shard_map/reduce_scatter | solution.py:214
  1063.4 9.3 collective-permute-done.58
  (940 shorter events, 624.6 us)
Async XLA Ops:
  7.2 149.9 %all-gather.10.cloned.1.call-start = ((), (), s32[]{:S(2)}) async-start(), calls=%async_computation.11 | async-start | bytes 2211840 | tf_op jit(solution)/shard_map/all_gather | solution.py:206
  13.8 84.2 %collective-permute-start.11 = (bf16[2,48,1152]{2,1,0:T(8,128)(2,1)}, bf16[2,48,1152]{2,1,0:T(8,128)(2,1)}, u32[]{:S(2)}, u32[]{:S(2)}) collective-permute-start(bf16[2,48,1152]{2,1,0:T(8,128)(2,1)} %select_n.882), channel_id=1, source_target_pairs={{0,8},{8,0},{1,9},{9,1},{2,10},{10,2},{3,11},{11,3},{4,12},{12,4},... | collective-permute-start | bytes 663560 | tf_op jit(solution)/shard_map/ppermute | solution.py:122
  18.8 80.6 %collective-permute-start.15 = (bf16[2,128,768]{1,2,0:T(8,128)(2,1)}, bf16[2,128,768]{1,2,0:T(8,128)(2,1)}, u32[]{:S(2)}, u32[]{:S(2)}) collective-permute-start(bf16[2,128,768]{1,2,0:T(8,128)(2,1)} %bitcast.42), channel_id=1, source_target_pairs={{0,8},{8,0},{1,9},{9,1},{2,10},{10,2},{3,11},{11,3},{4,12},{12,4},... | collective-permute-start | bytes 1179656 | tf_op jit(solution)/shard_map/ppermute | solution.py:122
  18.9 151.2 %collective-permute-start.22 = (bf16[256,4096]{1,0:T(8,128)(2,1)}, bf16[256,4096]{1,0:T(8,128)(2,1)}, u32[]{:S(2)}, u32[]{:S(2)}) collective-permute-start(bf16[256,4096]{1,0:T(8,128)(2,1)} %bitcast.37), channel_id=1, source_target_pairs={{0,8},{8,0},{1,9},{9,1},{2,10},{10,2},{3,11},{11,3},{4,12},{12,4},... | collective-permute-start | bytes 6291464 | tf_op jit(solution)/shard_map/ppermute | solution.py:122
  37.6 128.3 %collective-permute-start.18 = (bf16[1,192,1536]{2,1,0:T(8,128)(2,1)S(1)}, bf16[1,192,1536]{2,1,0:T(8,128)(2,1)}, u32[]{:S(2)}, u32[]{:S(2)}) collective-permute-start(bf16[1,192,1536]{2,1,0:T(8,128)(2,1)S(1)} %bitcast.583), channel_id=1, source_target_pairs={{0,16},{16,0},{1,17},{17,1},{2,18},{18,2},{3,19},{19,3},{4,20},{20... | collective-permute-start | bytes 1769480 | tf_op jit(solution)/shard_map/ppermute | solution.py:122
  80.6 83.9 %collective-permute-start.27 = (bf16[2,48,2048]{2,1,0:T(8,128)(2,1)}, bf16[2,48,2048]{2,1,0:T(8,128)(2,1)}, u32[]{:S(2)}, u32[]{:S(2)}) collective-permute-start(bf16[2,48,2048]{2,1,0:T(8,128)(2,1)} %select_n.943), channel_id=1, source_target_pairs={{0,8},{8,0},{1,9},{9,1},{2,10},{10,2},{3,11},{11,3},{4,12},{12,4},... | collective-permute-start | bytes 1179656 | tf_op jit(solution)/shard_map/ppermute | solution.py:122
  116.0 155.3 %all-gather.12.cloned.1.call-start = ((), (), s32[]{:S(2)}) async-start(), calls=%async_computation.12 | async-start | bytes 3932160 | tf_op jit(solution)/shard_map/all_gather | solution.py:206
  127.0 269.0 %all-gather.14.cloned.1.call-start = ((), (), s32[]{:S(2)}) async-start(), calls=%async_computation.13 | async-start | bytes 3932160 | tf_op jit(solution)/shard_map/all_gather | solution.py:206
  168.9 186.1 %collective-permute-start.14 = (bf16[256,4096]{1,0:T(8,128)(2,1)}, bf16[256,4096]{1,0:T(8,128)(2,1)}, u32[]{:S(2)}, u32[]{:S(2)}) collective-permute-start(bf16[256,4096]{1,0:T(8,128)(2,1)} %bitcast.37), channel_id=1, source_target_pairs={{0,4},{4,0},{1,5},{5,1},{2,6},{6,2},{3,7},{7,3},{8,12},{12,8},{9,1... | collective-permute-start | bytes 6291464 | tf_op jit(solution)/shard_map/ppermute | solution.py:122
  170.0 259.7 %all-gather.8.cloned.1.call-start = ((), (), s32[]{:S(2)}) async-start(), calls=%async_computation.5 | async-start | bytes 1966080 | tf_op jit(solution)/shard_map/all_gather | solution.py:217
  170.1 179.7 %collective-permute-start.23 = (bf16[256,4096]{1,0:T(8,128)(2,1)}, bf16[256,4096]{1,0:T(8,128)(2,1)}, u32[]{:S(2)}, u32[]{:S(2)}) collective-permute-start(bf16[256,4096]{1,0:T(8,128)(2,1)} %collective-permute-done.22), channel_id=1, source_target_pairs={{0,4},{4,0},{1,5},{5,1},{2,6},{6,2},{3,7},{7,3},{8,12},{12,8},{9,1... | collective-permute-start | bytes 6291464 | tf_op jit(solution)/shard_map/ppermute | solution.py:122
  391.8 378.5 %reduce-scatter.14.cloned.1.call-start = ((), (), s32[]{:S(2)}) async-start(), calls=%async_computation.10 | async-start | bytes 1966080 | tf_op jit(solution)/shard_map/reduce_scatter | solution.py:222
  396.0 118.1 %collective-permute-start.29 = (bf16[1,4,2,2,48,2048]{5,4,3,2,1,0:T(8,128)(2,1)}, bf16[1,4,2,2,48,2048]{5,4,3,2,1,0:T(8,128)(2,1)}, u32[]{:S(2)}, u32[]{:S(2)}) collective-permute-start(bf16[1,4,2,2,48,2048]{5,4,3,2,1,0:T(8,128)(2,1)} %bitcast.579), channel_id=1, source_target_pairs={{0,16},{16,0},{1,17},{17,1},{2,18},{18,2},{3,19},{19,3},{4,20},{20... | collective-permute-start | bytes 9437192 | tf_op jit(solution)/shard_map/ppermute | solution.py:122
  434.3 114.3 %collective-permute-start.36 = (bf16[512,1536]{1,0:T(8,128)(2,1)}, bf16[512,1536]{1,0:T(8,128)(2,1)}, u32[]{:S(2)}, u32[]{:S(2)}) collective-permute-start(bf16[512,1536]{1,0:T(8,128)(2,1)} %fusion.110), channel_id=1, source_target_pairs={{0,4},{4,0},{1,5},{5,1},{2,6},{6,2},{3,7},{7,3},{8,12},{12,8},{9,1... | collective-permute-start | bytes 4718600 | tf_op jit(solution)/shard_map/ppermute | solution.py:122
  434.4 132.5 %collective-permute-start.39 = (bf16[512,1536]{1,0:T(8,128)(2,1)}, bf16[512,1536]{1,0:T(8,128)(2,1)}, u32[]{:S(2)}, u32[]{:S(2)}) collective-permute-start(bf16[512,1536]{1,0:T(8,128)(2,1)} %collective-permute-done.38), channel_id=1, source_target_pairs={{0,4},{4,0},{1,5},{5,1},{2,6},{6,2},{3,7},{7,3},{8,12},{12,8},{9,1... | collective-permute-start | bytes 4718600 | tf_op jit(solution)/shard_map/ppermute | solution.py:122
  607.7 76.0 %collective-permute-start.63 = (bf16[1,512,1536]{2,1,0:T(8,128)(2,1)S(1)}, bf16[1,512,1536]{2,1,0:T(8,128)(2,1)}, u32[]{:S(2)}, u32[]{:S(2)}) collective-permute-start(bf16[1,512,1536]{2,1,0:T(8,128)(2,1)S(1)} %select_bitcast_fusion), channel_id=1, source_target_pairs={{0,16},{16,0},{1,17},{17,1},{2,18},{18,2},{3,19},{19,3},{4,20},{20... | collective-permute-start | bytes 4718600 | tf_op jit(solution)/shard_map/ppermute | solution.py:122
  674.1 89.7 %collective-permute-start.60 = (bf16[1,4,2,2,48,2048]{5,4,3,2,1,0:T(8,128)(2,1)}, bf16[1,4,2,2,48,2048]{5,4,3,2,1,0:T(8,128)(2,1)}, u32[]{:S(2)}, u32[]{:S(2)}) collective-permute-start(bf16[1,4,2,2,48,2048]{5,4,3,2,1,0:T(8,128)(2,1)} %broadcast_select_fusion), channel_id=1, source_target_pairs={{0,16},{16,0},{1,17},{17,1},{2,18},{18,2},{3,19},{19,3},{4,20},{20... | collective-permute-start | bytes 9437192 | tf_op jit(solution)/shard_map/ppermute | solution.py:122
  687.3 272.9 %reduce-scatter.8.cloned.1.call-start = ((), (), s32[]{:S(2)}) async-start(), calls=%async_computation.7 | async-start | bytes 737280 | tf_op jit(solution)/shard_map/reduce_scatter | solution.py:222
  711.2 204.3 %collective-permute-start.31 = (bf16[512,1536]{1,0:T(8,128)(2,1)}, bf16[512,1536]{1,0:T(8,128)(2,1)}, u32[]{:S(2)}, u32[]{:S(2)}) collective-permute-start(bf16[512,1536]{1,0:T(8,128)(2,1)} %slice.566), channel_id=1, source_target_pairs={{0,4},{4,0},{1,5},{5,1},{2,6},{6,2},{3,7},{7,3},{8,12},{12,8},{9,1... | collective-permute-start | bytes 4718600 | tf_op jit(solution)/shard_map/ppermute | solution.py:122
  758.5 206.8 %reduce-scatter.12.cloned.1.call-start = ((), (), s32[]{:S(2)}) async-start(), calls=%async_computation.9 | async-start | bytes 3932160 | tf_op jit(solution)/shard_map/reduce_scatter | solution.py:214
  762.5 153.6 %collective-permute-start.35 = (bf16[512,1536]{1,0:T(8,128)(2,1)}, bf16[512,1536]{1,0:T(8,128)(2,1)}, u32[]{:S(2)}, u32[]{:S(2)}) collective-permute-start(bf16[512,1536]{1,0:T(8,128)(2,1)} %fusion.116), channel_id=1, source_target_pairs={{0,8},{8,0},{1,9},{9,1},{2,10},{10,2},{3,11},{11,3},{4,12},{12,4},... | collective-permute-start | bytes 4718600 | tf_op jit(solution)/shard_map/ppermute | solution.py:122
  769.9 255.1 %reduce-scatter.6.cloned.1.call-start = ((), (), s32[]{:S(2)}) async-start(), calls=%async_computation.6 | async-start | bytes 2211840 | tf_op jit(solution)/shard_map/reduce_scatter | solution.py:214
  833.4 137.6 %collective-permute-start.57 = (bf16[1,4,2,2,128,768]{4,5,3,2,1,0:T(8,128)(2,1)}, bf16[1,4,2,2,128,768]{4,5,3,2,1,0:T(8,128)(2,1)}, u32[]{:S(2)}, u32[]{:S(2)}) collective-permute-start(bf16[1,4,2,2,128,768]{4,5,3,2,1,0:T(8,128)(2,1)} %broadcast_select_fusion.1), channel_id=1, source_target_pairs={{0,16},{16,0},{1,17},{17,1},{2,18},{18,2},{3,19},{19,3},{4,20},{20... | collective-permute-start | bytes 9437192 | tf_op jit(solution)/shard_map/ppermute | solution.py:122
  960.1 100.4 %reduce-scatter.10.cloned.1.call-start = ((), (), s32[]{:S(2)}) async-start(), calls=%async_computation.8 | async-start | bytes 3932160 | tf_op jit(solution)/shard_map/reduce_scatter | solution.py:214
  (253 other events, 4667.4 us)
Sparse Core Ops, SparseCore 0:
  116.1 40.8 all-gather.9
  159.2 62.8 all-gather.11
  223.6 62.1 all-gather.13
  391.9 37.8 all-gather.7
  687.4 35.9 reduce-scatter.13
  758.6 20.8 reduce-scatter.7
  781.7 60.8 reduce-scatter.11
  960.2 38.2 reduce-scatter.5
  1000.9 59.5 reduce-scatter.9

commit v2 on v1

v2 whole, which is shorter than its diff:
```python
import math

import jax
import jax.numpy as jnp
from jax import lax
from jax.experimental import pallas as pl
from jax.experimental.pallas import tpu as pltpu
from jax.sharding import Mesh
from jax.sharding import PartitionSpec as P

D = 1536
HEADS = 24
HEAD_DIM = 64
TEXT_DIM = 4096
FF = 4096
SIDE = 16
RANKS = 4
LANES = 128
MIB = 1 << 20
AXES = ("hi", "mid", "core", "rep")


EPSILON = 1e-06


def norm_rows(values, gain_row):
    return (
        values * lax.rsqrt(jnp.mean(values * values, axis=-1, keepdims=True) + EPSILON) * gain_row
    )


def rope_tables(item_kind, item_len):
    position = jnp.arange(item_len, dtype=jnp.int32)[None, :]
    half_side = SIDE // 2
    frame_index = position // (half_side * half_side)
    within = position % (half_side * half_side)
    is_clip = item_kind[:, None] == 1
    row_index = jnp.where(is_clip, frame_index * half_side + within // half_side, position // SIDE)
    columns = jnp.where(is_clip, within % half_side, position % SIDE)
    lane_index = jnp.arange(HEAD_DIM, dtype=jnp.int32)
    quarter = HEAD_DIM // 4
    frequency = jnp.exp(-(lane_index % quarter).astype(jnp.float32) * (math.log(10000.0) / quarter))
    coordinate = jnp.where(
        lane_index[None, None, :] < 2 * quarter, row_index[:, :, None], columns[:, :, None]
    ).astype(jnp.float32)
    angles = coordinate * frequency
    return (jnp.cos(angles), jnp.sin(angles))


def modulate(values, gain_row, scaling):
    return norm_rows(values, gain_row) * (1.0 + scaling[:, None, :])


def silu_product(gate_half, up_half):
    return jax.nn.silu(gate_half) * up_half


def dot(left, right):
    return jnp.dot(left, right, preferred_element_type=jnp.float32)


def dot_left(left, right):
    return lax.dot_general(left, right, (((0,), (0,)), ((), ())), preferred_element_type=jnp.float32)


def dot_right(left, right):
    return lax.dot_general(left, right, (((1,), (1,)), ((), ())), preferred_element_type=jnp.float32)


def lane_index(shape):
    return lax.broadcasted_iota(jnp.int32, shape, len(shape) - 1)

def head_sums(values):
    first = lane_index(values.shape) < HEAD_DIM
    low = jnp.sum(jnp.where(first, values, 0.0), axis=-1, keepdims=True)
    high = jnp.sum(jnp.where(first, 0.0, values), axis=-1, keepdims=True)
    return jnp.where(first, low, high)

def partner(values):
    quarter = HEAD_DIM // 4
    width = values.shape[-1]
    low = lane_index(values.shape) % (2 * quarter) < quarter
    return jnp.where(low, pltpu.roll(values, width - quarter, 1), pltpu.roll(values, quarter, 1))

def stack_heads(values):
    first = lane_index(values.shape) < HEAD_DIM
    zero = jnp.zeros_like(values)
    return jnp.concatenate([jnp.where(first, values, zero), jnp.where(first, zero, values)])

def join_heads(stacked):
    rows = stacked.shape[0] // 2
    first = lane_index((rows, stacked.shape[1])) < HEAD_DIM
    return jnp.where(first, stacked[:rows], stacked[rows:])

def inverse_rms(raw):
    return lax.rsqrt(head_sums(raw * raw) * (1.0 / HEAD_DIM) + EPSILON)

def attend_kernel(kind_ref, len_ref, qkv_ref, text_ref, text_value_ref, gain_ref, cos_ref, sin_ref, q_ref, k_ref, tk_ref, mixed_ref, read_ref):
    item = pl.program_id(0)
    kind, length = kind_ref[item], len_ref[item]
    width = q_ref.shape[1]
    cosine, sine = cos_ref[kind], sin_ref[kind]
    scaling = HEAD_DIM ** (-0.5)
    for at in range(0, width, LANES):
        lanes = slice(at, at + LANES)
        turned = []
        for part, out_ref in ((0, q_ref), (1, k_ref)):
            raw = qkv_ref[:, part * width + at : part * width + at + LANES]
            normal = raw * inverse_rms(raw) * gain_ref[part : part + 1, lanes]
            rows = (normal * cosine + partner(normal) * sine).astype(jnp.bfloat16)
            out_ref[:, lanes] = rows
            turned.append(rows)
        queries, keys = turned
        values = qkv_ref[:, 2 * width + at : 2 * width + at + LANES].astype(jnp.bfloat16)
        text_raw = text_ref[:, lanes]
        text_keys = (text_raw * inverse_rms(text_raw) * gain_ref[2:3, lanes]).astype(jnp.bfloat16)
        tk_ref[:, lanes] = text_keys
        text_values = text_value_ref[:, lanes].astype(jnp.bfloat16)
        stacked = stack_heads(queries)
        own = dot_right(stacked, keys) * scaling
        own = jnp.exp(own - jnp.max(own, axis=-1, keepdims=True))
        own_out = dot(own.astype(jnp.bfloat16), values) / jnp.sum(own, axis=-1, keepdims=True)
        text = dot_right(stacked, text_keys) * scaling
        text = jnp.where(lane_index(text.shape) < length, text, -1e30)
        text = jnp.exp(text - jnp.max(text, axis=-1, keepdims=True))
        text_out = dot(text.astype(jnp.bfloat16), text_values) / jnp.sum(text, axis=-1, keepdims=True)
        read = join_heads(text_out)
        read_ref[:, lanes] = read
        mixed_ref[:, lanes] = (join_heads(own_out) + gain_ref[3:4, lanes] * read).astype(jnp.bfloat16)

def head_norm_back(grad, raw, gain_row):
    inverse = inverse_rms(raw)
    scaled = grad * gain_row
    normal = raw * inverse
    inner = head_sums(scaled * normal) * (1.0 / HEAD_DIM)
    return inverse * (scaled - normal * inner), jnp.sum(grad * normal, axis=0, keepdims=True)

def attend_back_kernel(kind_ref, len_ref, qkv_ref, text_ref, text_value_ref, gain_ref, cos_ref, sin_ref, q_ref, k_ref, tk_ref, read_ref, grad_ref, gqkv_ref, gtext_ref, gains_ref):
    item = pl.program_id(0)
    kind, length = kind_ref[item], len_ref[item]
    width = q_ref.shape[1]
    cosine, sine = cos_ref[kind], sin_ref[kind]
    scaling = HEAD_DIM ** (-0.5)

    @pl.when(item == 0)
    def _():
        gains_ref[...] = jnp.zeros_like(gains_ref)

    def one(stacked, keys, values, stacked_grad, valid):
        scores = dot_right(keys, stacked) * scaling
        if valid is not None:
            scores = jnp.where(valid(scores.shape), scores, -1e30)
        probs = jnp.exp(scores - jnp.max(scores, axis=0, keepdims=True))
        probs = probs * (1.0 / jnp.sum(probs, axis=0, keepdims=True))
        grad_values = dot(probs.astype(jnp.bfloat16), stacked_grad)
        grad_probs = dot_right(values, stacked_grad)
        inner = jnp.sum(probs * grad_probs, axis=0, keepdims=True)
        grad_scores = (probs * (grad_probs - inner)).astype(jnp.bfloat16)
        grad_keys = dot(grad_scores, stacked) * scaling
        grad_queries = dot_left(keys, grad_scores)
        return grad_queries, grad_keys, grad_values

    for at in range(0, width, LANES):
        lanes = slice(at, at + LANES)
        grad = grad_ref[:, lanes]
        cross = gain_ref[3:4, lanes]
        values = qkv_ref[:, 2 * width + at : 2 * width + at + LANES].astype(jnp.bfloat16)
        text_values = text_value_ref[:, lanes].astype(jnp.bfloat16)
        stacked = stack_heads(q_ref[:, lanes])
        own_queries, own_keys, own_values = one(
            stacked, k_ref[:, lanes], values, stack_heads(grad.astype(jnp.bfloat16)), None
        )
        read_queries, read_keys, read_values = one(
            stacked, tk_ref[:, lanes], text_values, stack_heads((cross * grad).astype(jnp.bfloat16)),
            lambda shape: lax.broadcasted_iota(jnp.int32, shape, 0) < length,
        )
        grad_queries = join_heads((own_queries + read_queries).T) * scaling
        for part, turned in ((0, grad_queries), (1, own_keys)):
            raw = qkv_ref[:, part * width + at : part * width + at + LANES]
            back = turned * cosine + partner(turned * sine)
            grad_raw, gain = head_norm_back(back, raw, gain_ref[part : part + 1, lanes])
            gqkv_ref[:, part * width + at : part * width + at + LANES] = grad_raw.astype(jnp.bfloat16)
            gains_ref[part : part + 1, lanes] += gain
        gqkv_ref[:, 2 * width + at : 2 * width + at + LANES] = own_values.astype(jnp.bfloat16)
        grad_text, gain = head_norm_back(read_keys, text_ref[:, lanes], gain_ref[2:3, lanes])
        gtext_ref[:, lanes] = grad_text.astype(jnp.bfloat16)
        gains_ref[2:3, lanes] += gain
        gtext_ref[:, width + at : width + at + LANES] = read_values.astype(jnp.bfloat16)
        gains_ref[3:4, lanes] += jnp.sum(grad * read_ref[:, lanes], axis=0, keepdims=True)

def item_call(kernel, items, operands, outs, name):
    def rows(shape):
        return pl.BlockSpec((shape[0] // items, shape[1]), lambda i, *_: (i, 0))
    def full(shape):
        return pl.BlockSpec(shape, lambda i, *_: (0,) * len(shape))
    def call(scalars, *arrays):
        in_specs = [rows(a.shape) if i in operands else full(a.shape) for i, a in enumerate(arrays)]
        return pl.pallas_call(
            kernel,
            grid_spec=pltpu.PrefetchScalarGridSpec(
                num_scalar_prefetch=len(scalars), grid=(items,), in_specs=in_specs,
                out_specs=[rows(s.shape) if cut else full(s.shape) for s, cut in outs]),
            out_shape=[s for s, _ in outs],
            compiler_params=pltpu.CompilerParams(dimension_semantics=("arbitrary",), vmem_limit_bytes=48*MIB),
            name=name,
        )(*scalars, *arrays)
    return call

def attend(kind, length, qkv_raw, text_raw, text_value_raw, gains, cosine, sine):
    items=kind.shape[0]; n=qkv_raw.shape[0]; width=qkv_raw.shape[1]//3; t=text_raw.shape[0]
    S=jax.ShapeDtypeStruct
    outs=[(S((n,width),jnp.bfloat16),True),(S((n,width),jnp.bfloat16),True),(S((t,width),jnp.bfloat16),True),(S((n,width),jnp.bfloat16),True),(S((n,width),jnp.float32),True)]
    return item_call(attend_kernel, items, (0,1,2), outs, "attend")((kind,length), qkv_raw, text_raw, text_value_raw, gains, cosine, sine)

def attend_back(kind, length, qkv_raw, text_raw, text_value_raw, gains, cosine, sine, q, k, tk, read, grad):
    items=kind.shape[0]; n=qkv_raw.shape[0]; width=qkv_raw.shape[1]//3; t=text_raw.shape[0]
    S=jax.ShapeDtypeStruct
    outs=[(S((n,3*width),jnp.bfloat16),True),(S((t,2*width),jnp.bfloat16),True),(S((4,width),jnp.float32),False)]
    return item_call(attend_back_kernel, items, (0,1,2,6,7,8,9,10), outs, "attend_back")((kind,length), qkv_raw, text_raw, text_value_raw, gains, cosine, sine, q,k,tk,read,grad)


def feed_kernel(input_ref, result_ref, gate_ref, up_ref, down_ref, hidden_ref, grad_gate_ref, grad_up_ref, grad_ref):
    rows = input_ref[...]
    gate = dot(rows, gate_ref[...])
    up = dot(rows, up_ref[...])
    grad_hidden = dot_right(result_ref[...], down_ref[...])
    sigmoid = 1.0 / (1.0 + jnp.exp(-gate))
    silu = gate * sigmoid
    hidden_ref[...] = (silu * up).astype(jnp.bfloat16)
    grad_gate = (grad_hidden * up * (sigmoid + silu * (1.0 - sigmoid))).astype(jnp.bfloat16)
    grad_up = (grad_hidden * silu).astype(jnp.bfloat16)
    grad_gate_ref[...] = grad_gate
    grad_up_ref[...] = grad_up
    grad_ref[...] = dot_right(grad_gate, gate_ref[...]) + dot_right(grad_up, up_ref[...])


def feed(rows, grad_result, gate_rank, up_rank, down_rank):
    count, width = rows.shape[0], gate_rank.shape[1]
    block = 256

    def cut(columns):
        return pl.BlockSpec((block, columns), lambda i: (i, 0))

    def whole(array):
        return pl.BlockSpec(array.shape, lambda i: (0, 0), pipeline_mode=pl.Buffered(1))

    hidden = jax.ShapeDtypeStruct((count, width), jnp.bfloat16)
    return pl.pallas_call(
        feed_kernel,
        grid=(count // block,),
        in_specs=[cut(D), cut(D), whole(gate_rank), whole(up_rank), whole(down_rank)],
        out_specs=[cut(width), cut(width), cut(width), cut(D)],
        out_shape=[hidden, hidden, hidden, jax.ShapeDtypeStruct((count, D), jnp.float32)],
        compiler_params=pltpu.CompilerParams(
            dimension_semantics=("arbitrary",), vmem_limit_bytes=56 * MIB
        ),
        name="feed",
    )(rows, grad_result, gate_rank, up_rank, down_rank)


def swap(block, axis, count=2, step=1):
    return lax.ppermute(block, axis, [(at, at ^ step) for at in range(count)])


def spread(block, axis, count):
    if count & (count - 1):
        return lax.all_gather(block, axis)
    block, step = block[None], 1
    while step < count:
        other = swap(block, axis, count, step)
        low = (lax.axis_index(axis) & step) == 0
        block = jnp.where(
            low, jnp.concatenate([block, other]), jnp.concatenate([other, block])
        )
        step *= 2
    return block


def fold(block, axis, count):
    if count & (count - 1):
        return lax.psum_scatter(block, axis, scatter_dimension=0)
    step = count // 2
    while step:
        half = block.shape[0] // 2
        low = (lax.axis_index(axis) & step) == 0
        lower, upper = block[:half], block[half:]
        block = jnp.where(low, lower, upper) + swap(
            jnp.where(low, upper, lower), axis, count, step
        )
        step //= 2
    return block[0]


def trade_ranks(block):
    return lax.all_to_all(block, ("mid", "core"), 0, 0, tiled=True)


def pick(stack, index):
    return lax.dynamic_index_in_dim(stack, index, 0, keepdims=False)


def pair(rows):
    return jnp.concatenate([rows, swap(rows, "core")])


def settle_far(far):
    half = far.shape[0] // 2
    return far[:half] + swap(far[half:].astype(jnp.bfloat16), "core").astype(jnp.float32)


def settle_near(near):
    half = near.shape[0] // 2
    return near[:half] + swap(near[half:].astype(jnp.bfloat16), "core").astype(jnp.float32)


def settle_move(across):
    return swap(across.astype(jnp.bfloat16), "mid").astype(jnp.float32)


class Layout:
    def __init__(self, hi, rep, out_rows):
        self.hi, self.rep = hi, rep
        self.aligned = (rep * out_rows) % HEAD_DIM == 0
        self.head_groups = hi if self.aligned else 1
        self.rank = lax.axis_index("mid") * 2 + lax.axis_index("core")

    def by_rank(self, weight, sections, groups):
        rows, columns = weight.shape
        width = columns // (sections * groups * RANKS)
        view = weight.reshape(rows, sections * groups, RANKS, width)
        view = jnp.transpose(view, (2, 0, 1, 3))
        return view.reshape(RANKS, rows, sections * groups * width)

    def from_ranks(self, blocks, sections, groups):
        _, rows, per_rank = blocks.shape
        width = per_rank // (sections * groups)
        view = blocks.reshape(RANKS, rows, sections * groups, width)
        return jnp.transpose(view, (1, 2, 0, 3)).reshape(rows, RANKS * per_rank)

    def ordered(self, values):
        if self.hi != 2:
            return values
        half = values.shape[-1] // 2
        turned = jnp.concatenate([values[..., half:], values[..., :half]], axis=-1)
        return jnp.where(lax.axis_index("hi") == 0, values, turned)

    def across_hi(self, block):
        if self.hi == 2:
            return jnp.stack([block, swap(block, "hi")])
        return spread(block, "hi", self.hi)

    def natural_rows(self, stacked):
        view = stacked.reshape(self.hi, self.rep, RANKS, -1, stacked.shape[-1])
        return jnp.transpose(view, (0, 2, 1, 3, 4)).reshape(-1, stacked.shape[-1])

    def product(self, left_sides, right_sides, cut):
        near, far = [
            dot_left(cut(left), right) for left, right in zip(left_sides, right_sides, strict=True)
        ]
        return near + far

    def product_moved(self, left_sides, right_sides):
        half = left_sides[0].shape[1] // 2 if self.hi == 2 else 0
        return self.product(left_sides, right_sides, lambda left: left[:, half:]).astype(jnp.bfloat16)

    def move(self, moved):
        if self.hi == 2:
            return swap(moved, "hi")
        return fold(moved.reshape(self.hi, -1, moved.shape[1]), "hi", self.hi)

    def product_kept(self, left_sides, right_sides):
        if self.hi != 2:
            return None
        half = left_sides[0].shape[1] // 2
        return self.product(left_sides, right_sides, lambda left: left[:, :half])

    def total(self, kept, arrived):
        if kept is None:
            return arrived
        return (kept + arrived.astype(jnp.float32)).astype(jnp.bfloat16)

    def by_rep(self, summed):
        view = summed.reshape(RANKS, self.rep, -1, summed.shape[1])
        return jnp.transpose(view, (1, 0, 2, 3)).reshape(self.rep, -1, summed.shape[1])

    def reduce(self, blocks):
        flat = blocks.reshape(-1, blocks.shape[-1])
        return lax.psum_scatter(flat, "rep", scatter_dimension=0, tiled=True)

    def rank_lanes(self, rows, groups):
        view = rows.reshape(rows.shape[0], groups, RANKS, -1)
        return lax.dynamic_index_in_dim(view, self.rank, 2, keepdims=False).reshape(rows.shape[0], -1)

    def place_lanes(self, row):
        view = row.reshape(self.head_groups, 1, -1)
        at = (jnp.arange(RANKS) == self.rank).astype(row.dtype)[None, :, None]
        return (view * at).reshape(-1)


def fence(*values):
    return lax.optimization_barrier(values)


def local(
    hi_count,
    rep_count,
    tokens,
    condition,
    caption,
    caption_len,
    item_kind,
    out_cotangent,
    norm_gains,
    ada_weight,
    qkv_weight,
    out_weight,
    text_weight,
    gate_up_weight,
    down_weight,
):
    bf16, f32 = jnp.bfloat16, jnp.float32
    item_count = condition.shape[0]
    item_len = tokens.shape[0] // item_count
    row_count = item_count * item_len
    rows = qkv_weight.shape[0]
    plan = Layout(hi_count, rep_count, out_weight.shape[0])
    rank_width = HEADS // RANKS * HEAD_DIM
    hi_at, mid_at, core_at, rep_at = [lax.axis_index(name) for name in AXES]
    device_shape = (hi_count, 2, 2, rep_count)

    feed_width = FF // RANKS
    devices = hi_count * RANKS * rep_count
    block_at = (hi_at * RANKS + plan.rank) * rep_count + rep_at

    def z_gather(block):
        return lax.all_gather(block.reshape(-1, block.shape[-1]), "rep", tiled=True)

    down_z = z_gather(down_weight)
    qkv_mine = trade_ranks(plan.by_rank(qkv_weight, 3, plan.head_groups))
    qkv_mine = qkv_mine.reshape(RANKS * rows, 3 * rank_width)
    if plan.aligned:
        qkv_mine = jnp.concatenate([qkv_mine, out_weight.reshape(-1, 3 * rank_width)])
    else:
        out_whole = lax.all_gather(out_weight, AXES, axis=0, tiled=True)
        out_rank = pick(out_whole.reshape(RANKS, rank_width, D), plan.rank)

    head = condition.reshape(item_count, devices, rows)
    head = jnp.transpose(head, (1, 0, 2)).reshape(devices, -1)
    rest = jnp.concatenate(
        [norm_gains.reshape(-1), caption_len.astype(bf16), item_kind.astype(bf16)]
    )
    small = jnp.concatenate([head, jnp.broadcast_to(rest, (devices, rest.size))], axis=1)
    qkv_mine, small = fence(qkv_mine, small)
    qkv_z = z_gather(qkv_mine)
    small = lax.all_to_all(small, AXES, 0, 0, tiled=True)
    cut = [head.shape[1], head.shape[1] + norm_gains.size]
    cut.append(cut[1] + item_count)
    conditions, gains, lengths, kinds = jnp.split(small, cut, axis=-1)
    activated_mine = jax.nn.silu(conditions.astype(f32)).astype(bf16).reshape(-1, rows)
    gain_rows = jnp.moveaxis(gains.astype(f32).reshape(devices, 6, -1), 1, 0).reshape(6, D)
    lengths, kinds = [
        values.reshape(device_shape + (item_count,)) for values in (lengths, kinds)
    ]

    def group_items(values):
        view = lax.dynamic_index_in_dim(pick(values, hi_at), rep_at, 2, keepdims=False)
        near, far = pick(view, mid_at), pick(view, 1 - mid_at)
        order = [core_at, 1 - core_at]
        return [
            jnp.concatenate([pick(side, at) for at in order]).astype(jnp.int32)
            for side in (near, far)
        ]

    lengths_sides = group_items(lengths)
    kinds_sides = group_items(kinds)
    cosine, sine = rope_tables(jnp.arange(2), item_len)
    signs = jnp.where(jnp.arange(HEAD_DIM) % (HEAD_DIM // 2) < HEAD_DIM // 4, -1.0, 1.0)
    cosine, sine = jnp.tile(cosine, (1, 1, 2)), jnp.tile(sine * signs, (1, 1, 2))
    head_gains = plan.rank_lanes(gain_rows, plan.head_groups)
    cross_gate = jnp.tanh(head_gains[5])
    head_gains = jnp.concatenate([head_gains[1:4], cross_gate[None]])
    tables = (head_gains, cosine, sine)
    scalars = list(zip(kinds_sides, lengths_sides, strict=True))

    text_weight, conditions = fence(text_weight, activated_mine)
    text_mine = trade_ranks(plan.by_rank(text_weight, 2, plan.head_groups))
    partial = dot(conditions, ada_weight).astype(bf16).reshape(devices, item_count, 4 * D)
    text_mine, partial, down_z = fence(text_mine, partial, down_z)
    down_rank = plan.across_hi(down_z)
    modulation = jnp.sum(lax.all_to_all(partial, AXES, 0, 0, tiled=True).astype(f32), axis=0)
    qkv_z, down_rank, modulation, text_mine = fence(qkv_z, down_rank, modulation, text_mine)

    scale_attn, gate_attn, scale_mlp, gate_mlp = jnp.split(modulation, 4, axis=1)
    captions = plan.ordered(caption.reshape(-1, TEXT_DIM))
    text_key_z = z_gather(text_mine[..., :rank_width])
    captions_far = swap(captions, "mid")
    qkv_rank = plan.across_hi(qkv_z)
    gate_up_mine = trade_ranks(plan.by_rank(gate_up_weight, 2, hi_count))
    token_rows = tokens.astype(f32).reshape(item_count, item_len, D)
    normed = modulate(token_rows, gain_rows[0], scale_attn)
    normed = plan.ordered(normed.astype(bf16).reshape(row_count, D))
    mlp_gate = jnp.tanh(gate_mlp)[:, None, :]
    grad_top = out_cotangent.astype(f32).reshape(item_count, item_len, D)
    grad_result = (mlp_gate * grad_top).astype(bf16).reshape(row_count, D)
    text_key_z, captions_far, qkv_rank, gate_up_mine, normed, grad_result = fence(
        text_key_z, captions_far, qkv_rank, gate_up_mine, normed, grad_result
    )

    text_value_z = z_gather(text_mine[..., rank_width:])
    text_key_rank = plan.across_hi(text_key_z)
    normed_far = swap(normed, "mid")
    caption_sides = (pair(captions), pair(captions_far))
    normed_near = pair(normed)
    if plan.aligned:
        blocks = qkv_rank.reshape(hi_count, rep_count, -1, 3 * rank_width)
        out_rank = blocks[:, :, RANKS * rows :].reshape(hi_count, -1)
        if hi_count == 2:
            out_rank = jnp.where(hi_at == 0, out_rank, out_rank[::-1])
        out_rank = out_rank.reshape(rank_width, D)
        qkv_rank = blocks[:, :, : RANKS * rows]
    qkv_rank = plan.natural_rows(qkv_rank)
    text_value_z, text_key_rank, normed_far, caption_sides, normed_near, qkv_rank, out_rank = fence(
        text_value_z, text_key_rank, normed_far, caption_sides, normed_near, qkv_rank, out_rank
    )

    gate_z = z_gather(gate_up_mine[..., :feed_width])
    text_value_rank = plan.across_hi(text_value_z)
    result_far = swap(grad_result, "mid")
    normed_sides = (normed_near, pair(normed_far))
    text_key_rank = plan.natural_rows(text_key_rank)
    qkv_raw = [dot(side, qkv_rank) for side in normed_sides]
    text_key_raw = [dot(side, text_key_rank) for side in caption_sides]
    down_rank = down_rank.reshape(hi_count, -1)
    if hi_count == 2:
        down_rank = jnp.where(hi_at == 0, down_rank, down_rank[::-1])
    down_rank = down_rank.reshape(feed_width, D)
    gate_z, text_value_rank, result_far, normed_sides, qkv_raw, text_key_raw, down_rank = fence(
        gate_z, text_value_rank, result_far, normed_sides, qkv_raw, text_key_raw, down_rank
    )

    up_z = z_gather(gate_up_mine[..., feed_width:])
    gate_rank = plan.across_hi(gate_z)
    text_value_rank = plan.natural_rows(text_value_rank)
    text_value_raw = [dot(side, text_value_rank) for side in caption_sides]
    raw_near, raw_far = zip(qkv_raw, text_key_raw, text_value_raw, strict=True)
    kept_far = attend(*scalars[1], *raw_far, *tables)
    up_z, gate_rank, raw_near, raw_far, kept_far = fence(
        up_z, gate_rank, raw_near, raw_far, kept_far
    )

    across = settle_far(dot(kept_far[3], out_rank))
    across, raw_near, up_z = fence(across, raw_near, up_z)
    up_rank = plan.across_hi(up_z)
    arrived = settle_move(across)
    kept_near = attend(*scalars[0], *raw_near, *tables)
    up_rank, arrived, kept_near = fence(up_rank, arrived, kept_near)

    branch = settle_near(dot(kept_near[3], out_rank)) + arrived
    branch = branch.reshape(item_count, item_len, D)
    attn_gate = jnp.tanh(gate_attn)[:, None, :]
    middle = token_rows + attn_gate * branch
    mlp_input = modulate(middle, gain_rows[4], scale_mlp)
    mlp_input = plan.ordered(mlp_input.astype(bf16).reshape(row_count, D))
    feed_weights = (plan.natural_rows(gate_rank), plan.natural_rows(up_rank), down_rank)
    result_sides = (pair(grad_result), pair(result_far))
    input_near = pair(mlp_input)
    feed_weights, mlp_input, input_near, result_sides = fence(
        feed_weights, mlp_input, input_near, result_sides
    )

    input_far = swap(mlp_input, "mid")
    hidden_near, gate_near, up_near, partial_near = feed(input_near, result_sides[0], *feed_weights)
    input_far, hidden_near, gate_near, up_near, partial_near = fence(
        input_far, hidden_near, gate_near, up_near, partial_near
    )
    input_sides = (input_near, pair(input_far))
    hidden_far, gate_far, up_far, partial_far = feed(input_sides[1], result_sides[1], *feed_weights)
    across = settle_far(partial_far)
    across, gate_far, up_far, hidden_far = fence(across, gate_far, up_far, hidden_far)
    arrived = settle_move(across)
    gate_sides, up_sides, hidden_sides = (gate_near, gate_far), (up_near, up_far), (hidden_near, hidden_far)
    hidden_turned = [plan.ordered(side) for side in hidden_sides]
    gate_moved = plan.product_moved(input_sides, gate_sides)
    up_moved = plan.product_moved(input_sides, up_sides)
    near = settle_near(partial_near)
    arrived, gate_moved, up_moved, near = fence(arrived, gate_moved, up_moved, near)

    gate_moved = plan.move(gate_moved)
    grad_mlp_input = plan.ordered(near + arrived)
    _, pull_mlp_norm = jax.vjp(modulate, middle, gain_rows[4], scale_mlp)
    grad_middle_norm, grad_mlp_gain, grad_scale_mlp = pull_mlp_norm(
        grad_mlp_input.reshape(item_count, item_len, D)
    )
    grad_middle = grad_top + grad_middle_norm
    grad_attn_gate = jnp.sum(grad_middle * branch, axis=1) * (1.0 - jnp.tanh(gate_attn) ** 2)
    grad_branch = (attn_gate * grad_middle).astype(bf16).reshape(row_count, D)
    branch_near = pair(grad_branch)
    mixed_near = dot_right(branch_near, out_rank)
    gate_kept = plan.product_kept(input_sides, gate_sides)
    gate_moved, gate_kept, grad_branch, branch_near, mixed_near = fence(
        gate_moved, gate_kept, grad_branch, branch_near, mixed_near
    )

    def attention_back(at, kept, raw, grad_mixed):
        queries, key_rows, text_keys, _, read = kept
        return attend_back(
            *scalars[at], *raw, *tables, queries, key_rows, text_keys, read, grad_mixed
        )

    gate_grad = plan.by_rep(plan.total(gate_kept, gate_moved))
    gate_grad, up_moved, grad_branch, mixed_near = fence(
        gate_grad, up_moved, grad_branch, mixed_near
    )
    gate_parts = plan.reduce(gate_grad)
    branch_far = swap(grad_branch, "mid")
    up_moved = plan.move(up_moved)
    qkv_near, text_near, gain_near = attention_back(0, kept_near, raw_near, mixed_near)
    branch_far, up_moved, qkv_near, text_near, gain_near = fence(
        branch_far, up_moved, qkv_near, text_near, gain_near
    )

    branch_sides = (branch_near, pair(branch_far))
    up_grad = plan.by_rep(plan.total(plan.product_kept(input_sides, up_sides), up_moved))
    mixed_far = dot_right(branch_sides[1], out_rank)
    down_moved = plan.product_moved(hidden_turned, result_sides)
    up_grad, mixed_far, down_moved = fence(up_grad, mixed_far, down_moved)
    up_parts = plan.reduce(up_grad)
    down_moved = plan.move(down_moved)
    qkv_far, text_far, gain_far = attention_back(1, kept_far, raw_far, mixed_far)
    down_moved, qkv_far, text_far, gain_far = fence(down_moved, qkv_far, text_far, gain_far)

    text_sides, qkv_sides, mixed_sides = (text_near, text_far), (qkv_near, qkv_far), (kept_near[3], kept_far[3])
    mixed_sides = [plan.ordered(side) for side in mixed_sides]
    down_kept = plan.product_kept(hidden_turned, result_sides)
    down_grad = plan.total(down_kept, down_moved).reshape(rep_count, -1, D)
    across = settle_far(dot_right(qkv_far, qkv_rank))
    text_moved = plan.product_moved(caption_sides, text_sides)
    down_grad, across, text_moved, hidden_sides = fence(down_grad, across, text_moved, hidden_sides)
    down_weight_grad = plan.reduce(down_grad).astype(f32)
    arrived = settle_move(across)
    text_moved = plan.move(text_moved)
    text_kept = plan.product_kept(caption_sides, text_sides)
    qkv_moved = plan.product_moved(normed_sides, qkv_sides)
    grad_normed = settle_near(dot_right(qkv_near, qkv_rank))
    partial_result = [dot(side, down_rank) for side in hidden_sides]
    result_near, across = settle_near(partial_result[0]), settle_far(partial_result[1])
    if plan.aligned:
        out_moved = plan.product_moved(mixed_sides, branch_sides)
    if plan.aligned and hi_count == 2:
        qkv_moved = jnp.concatenate([qkv_moved.reshape(-1), out_moved.reshape(-1)])
        qkv_moved = qkv_moved.reshape(-1, 3 * rank_width)
    arrived, text_moved, text_kept, qkv_moved, grad_normed, result_near, across = fence(
        arrived, text_moved, text_kept, qkv_moved, grad_normed, result_near, across
    )

    text_grad = plan.by_rep(plan.total(text_kept, text_moved))
    text_grad, qkv_moved, grad_normed, across = fence(text_grad, qkv_moved, grad_normed, across)
    text_parts = plan.reduce(text_grad)
    qkv_moved = plan.move(qkv_moved)
    if plan.aligned and hi_count != 2:
        out_moved = plan.move(out_moved)
    result = (result_near + settle_move(across)).reshape(item_count, item_len, D)
    layer_out = (middle + mlp_gate * result).astype(bf16).reshape(row_count, D)
    grad_mlp_gate = jnp.sum(grad_top * result, axis=1) * (1.0 - jnp.tanh(gate_mlp) ** 2)
    grad_normed = plan.ordered(grad_normed + arrived)
    _, pull_attn_norm = jax.vjp(modulate, token_rows, gain_rows[0], scale_attn)
    grad_token_norm, grad_attn_gain, grad_scale_attn = pull_attn_norm(
        grad_normed.reshape(item_count, item_len, D)
    )
    tokens_grad = (grad_middle + grad_token_norm).reshape(row_count, D)
    qkv_kept = plan.product_kept(normed_sides, qkv_sides)
    if plan.aligned:
        out_kept = plan.product_kept(mixed_sides, branch_sides)
        if out_kept is not None:
            split = qkv_kept.shape[0]
            qkv_moved, out_moved = qkv_moved[:split], qkv_moved[split:].reshape(out_kept.shape)
        qkv_grad = plan.total(qkv_kept, qkv_moved)
        out_grad = plan.total(out_kept, out_moved)
        qkv_grad = jnp.concatenate(
            [plan.by_rep(qkv_grad), out_grad.reshape(rep_count, -1, 3 * rank_width)], axis=1
        )
    else:
        qkv_grad = plan.by_rep(plan.total(qkv_kept, qkv_moved))
        at = (jnp.arange(RANKS) == plan.rank).astype(bf16)[:, None, None]
        out_grad = plan.product(mixed_sides, branch_sides, lambda left: left)
        placed = (out_grad.astype(bf16)[None] * at).reshape(D, D)
        out_weight_grad = lax.psum_scatter(placed, AXES, scatter_dimension=0, tiled=True).astype(f32)
    qkv_parts = plan.reduce(qkv_grad)
    if plan.aligned:
        out_weight_grad = qkv_parts[RANKS * rows :].reshape(-1, D).astype(f32)
        qkv_parts = qkv_parts[: RANKS * rows]

    grad_modulation = jnp.concatenate(
        [grad_scale_attn, grad_attn_gate, grad_scale_mlp, grad_mlp_gate], axis=1
    ).astype(bf16)
    gain_terms = gain_near + gain_far
    gain_terms = gain_terms.at[3].multiply(1.0 - cross_gate**2)
    gain_terms = [plan.place_lanes(row) for row in gain_terms]
    gains_grad = jnp.stack(
        [grad_attn_gain, gain_terms[0], gain_terms[1], gain_terms[2], grad_mlp_gain, gain_terms[3]]
    ).astype(bf16)
    gain_blocks = jnp.moveaxis(gains_grad.reshape(6, devices, -1), 1, 0).reshape(devices, -1)
    modulations = jnp.broadcast_to(grad_modulation.reshape(-1), (devices, grad_modulation.size))
    both = lax.all_to_all(
        jnp.concatenate([modulations, gain_blocks], axis=1), AXES, 0, 0, tiled=True
    )
    ada_weight_grad = dot_left(activated_mine, both[:, : modulations.shape[1]].reshape(-1, 4 * D))
    norm_gains_grad = jnp.sum(both[:, modulations.shape[1] :].astype(f32), axis=0).reshape(6, -1)

    def whole(parts, weight, sections, groups):
        blocks = trade_ranks(parts.reshape(RANKS, weight.shape[0], -1))
        return plan.from_ranks(blocks, sections, groups).astype(f32)

    gate_up_weight_grad = whole(
        jnp.concatenate([gate_parts, up_parts], axis=-1), gate_up_weight, 2, hi_count
    )
    text_weight_grad = whole(text_parts, text_weight, 2, plan.head_groups)
    qkv_weight_grad = whole(qkv_parts, qkv_weight, 3, plan.head_groups)
    return (
        layer_out,
        tokens_grad,
        norm_gains_grad,
        ada_weight_grad,
        qkv_weight_grad,
        out_weight_grad,
        text_weight_grad,
        gate_up_weight_grad,
        down_weight_grad,
    )


def solution(mesh):
    grp, rep = mesh.devices.shape
    hi = grp // RANKS
    inner = Mesh(mesh.devices.reshape(hi, 2, 2, rep), AXES)
    rows = P(AXES, None)

    def step(*arrays):
        return local(hi, rep, *arrays)

    return jax.shard_map(
        step,
        mesh=inner,
        in_specs=(
            rows,
            rows,
            P(AXES, None, None),
            P(AXES),
            P(AXES),
            rows,
            P(None, AXES),
            rows,
            rows,
            rows,
            rows,
            rows,
            rows,
        ),
        out_specs=(rows, rows, P(None, AXES), rows, rows, rows, rows, rows, rows),
        check_vma=False,
    )
```

time: 1100 us -> 3420 us (3.11)
  local copies, waits for them, and re-layouts: 217 us -> 2610 us
  Pallas kernels: 0 us -> 119 us
  waiting for transfers between devices: 376 us -> 279 us
  matrix products: 215 us -> 134 us
  other arithmetic: 189 us -> 147 us
    rev x0 -> x2, local copies, waits for them, and re-layouts: none -> 2450 us  [the longest x1 2400 us: local(): down_rank = jnp.where(hi_at == 0, down_rank, down_rank[::-1])]
    ppermute x64 -> x38, waiting for transfers between devices: 314 us -> 190 us  [swap(): return lax.ppermute(block, axis, [(at, at ^ step) for at in range(count)])]
    pallas_call x0 -> x6, Pallas kernels: none -> 119 us  [the longest x4 72.2 us: call(): pl.pallas_call(kernel, grid_spec=pltpu.PrefetchScalarGridSpec(num_scalar_...]
    all_to_all x0 -> x8, waiting for transfers between devices: none -> 85.7 us  [the longest x1 33.4 us: local(): lax.all_to_all(jnp.concatenate([modulations, gain_blocks], axis=1), AXES,...]
    dot_general x24 -> x0, matrix products: 45.7 us -> none  [the longest x4 18.8 us: attend_back(): jnp.einsum('ishd,ithd->ihst', grad_attended, values, preferred_element_ty...]
    dot_general x8 -> x4, matrix products: 54.2 us -> 15.8 us  [dot_right(): lax.dot_general(left, right, (((1,), (1,)), ((), ())), preferred_element_...]
    all_to_all x0 -> x8, starting transfers between devices: none -> 34.7 us  [the longest x6 22.5 us: trade_ranks(): return lax.all_to_all(block, ('mid', 'core'), 0, 0, tiled=True)]
    dot_general x6 -> x25, matrix products: 59 us -> 78.8 us  [dot_left(): lax.dot_general(left, right, (((0,), (0,)), ((), ())), preferred_element_...]
  transfers between devices with their start and end apart: 73 -> 57, of which waited for: 24 -> 19; matrix products, arithmetic and copies ran while one was open for 51% -> 84% of each run, Pallas kernels for 0% -> 4%
where the time goes in v2:
time: 3420 us; the launch traced here: 3380 us
  local copies, waits for them, and re-layouts  2610 us (76%)
  waiting for transfers between devices  279 us (8%)
  other arithmetic  147 us (4%)
  matrix products  134 us (4%)
  Pallas kernels  119 us (3%)
  starting transfers between devices  65.4 us (2%)
    rev x1, local copies, waits for them, and re-layouts, local(): down_rank = jnp.where(hi_at == 0, down_rank, down_rank[::-1])  2400 us
    ppermute x38, waiting for transfers between devices, swap(): return lax.ppermute(block, axis, [(at, at ^ step) for at in range(count)])  190 us
    dot_general x25, matrix products, dot_left(): lax.dot_general(left, right, (((0,), (0,)), ((), ())), preferred_element_...  78.8 us
    pallas_call x4, Pallas kernels, call(): pl.pallas_call(kernel, grid_spec=pltpu.PrefetchScalarGridSpec(num_scalar_...  72.2 us
  transfers between devices with their start and end apart: 57, of which 19 were waited for; matrix products, arithmetic and copies ran while one was open for 84% of the time, Pallas kernels for 4%

profile of v2, /device:TPU:8, one launch (start us, length us, event | category | flops | bytes accessed | tf_op | source)
XLA Modules:
  0.0 3378.2 jit_solution(6688473550569404501)
XLA Ops:
  24.5 10.9 all_to_all.59
  45.2 7.5 all-to-all-done.2
  69.2 31.3 all-to-all-done.3
  134.8 2396.7 %rev.7 = bf16[2,786432]{1,0:T(2,128)(2,1)} reverse(bf16[2,786432]{1,0:T(2,128)(2,1)} %bitcast.242), dimensions={0} | reverse | bytes 6291456 | tf_op jit(solution)/shard_map/rev | solution.py:535
  2558.6 58.2 %rev.6 = bf16[2,294912]{1,0:T(2,128)(2,1)S(1)} reverse(bf16[2,294912]{1,0:T(2,128)(2,1)S(1)} %bitcast.258), dimensions={0} | reverse | bytes 2359296 | tf_op jit(solution)/shard_map/rev | solution.py:518
  2642.5 9.3 fusion.108.qkv_ref
  2668.3 9.3 collective-permute-done.8
  2687.2 15.5 attend.2
  2705.9 9.7 collective-permute-done.11
  2729.3 15.1 attend.3
  2744.4 18.3 collective-permute-done.13
  2799.9 23.2 feed.2
  2823.1 11.7 collective-permute-done.19
  2847.2 23.5 feed.3
  2895.4 24.7 collective-permute-done.22
  2943.7 23.9 collective-permute-done.24
  2985.2 21.4 attend_back.2
  3038.5 20.2 attend_back.3
  3132.2 18.2 collective-permute-done.31
  3160.5 23.8 collective-permute-done.32
  3211.6 14.9 collective-permute-done.36
  3234.2 26.9 collective-permute-done.37
  3281.6 7.6 all-to-all-start.5
  3298.9 33.4 all-to-all-done.5
  (639 shorter events, 506.8 us)
Async XLA Ops:
  14.5 98.3 %all-gather.7.cloned.1.call-start = ((), (), s32[]{:S(2)}) async-start(), calls=%async_computation.14 | async-start | bytes 2949120 | tf_op jit(solution)/shard_map/all_gather | solution.py:436
  52.8 53.6 %collective-permute-start = (bf16[512,1536]{1,0:T(8,128)(2,1)}, bf16[512,1536]{1,0:T(8,128)(2,1)}, u32[]{:S(2)}, u32[]{:S(2)}) collective-permute-start(bf16[512,1536]{1,0:T(8,128)(2,1)} %all-gather.9.cloned.1.call-done), channel_id=1, source_target_pairs={{0,16},{16,0},{1,17},{17,1},{2,18},{18,2},{3,19},{19,3},{4,20},{20... | collective-permute-start | bytes 4718600 | tf_op jit(solution)/shard_map/ppermute | solution.py:262
  63.6 2489.9 %collective-permute-start.1 = (bf16[256,4096]{1,0:T(8,128)(2,1)}, bf16[256,4096]{1,0:T(8,128)(2,1)}, u32[]{:S(2)}, u32[]{:S(2)}) collective-permute-start(bf16[256,4096]{1,0:T(8,128)(2,1)} %maximum_select_fusion.2), channel_id=1, source_target_pairs={{0,8},{8,0},{1,9},{9,1},{2,10},{10,2},{3,11},{11,3},{4,12},{12,4},... | collective-permute-start | bytes 6291464 | tf_op jit(solution)/shard_map/ppermute | solution.py:262
  65.1 55.6 %collective-permute-start.5 = (bf16[256,4096]{1,0:T(8,128)(2,1)}, bf16[256,4096]{1,0:T(8,128)(2,1)}, u32[]{:S(2)}, u32[]{:S(2)}) collective-permute-start(bf16[256,4096]{1,0:T(8,128)(2,1)} %maximum_select_fusion.2), channel_id=1, source_target_pairs={{0,4},{4,0},{1,5},{5,1},{2,6},{6,2},{3,7},{7,3},{8,12},{12,8},{9,1... | collective-permute-start | bytes 6291464 | tf_op jit(solution)/shard_map/ppermute | solution.py:262
  100.5 2453.1 %all-to-all-start.4 = ((bf16[4,48,2048]{2,1,0:T(8,128)(2,1)}), bf16[4,48,2048]{2,1,0:T(8,128)(2,1)S(1)}, u32[]{:S(2)}, u32[]{:S(2)}) async-start(bf16[4,48,2048]{2,1,0:T(8,128)(2,1)} %reshape.855), calls=%async_computation.4 | async-start | bytes 1572864 | tf_op jit(solution)/shard_map/all_to_all | solution.py:295
  104.0 2449.6 %all-gather.11.cloned.1.call-start = ((), (), s32[]{:S(2)}) async-start(), calls=%async_computation.16 | async-start | bytes 1966080 | tf_op jit(solution)/shard_map/all_gather | solution.py:436
  114.9 2526.0 %all-gather.17.cloned.1.call-start = ((), (), s32[]{:S(2)}) async-start(), calls=%async_computation.19 | async-start | bytes 1966080 | tf_op jit(solution)/shard_map/all_gather | solution.py:436
  125.4 2423.1 %collective-permute-start.2 = (bf16[1024,1152]{1,0:T(8,128)(2,1)}, bf16[1024,1152]{1,0:T(8,128)(2,1)}, u32[]{:S(2)}, u32[]{:S(2)}) collective-permute-start(bf16[1024,1152]{1,0:T(8,128)(2,1)} %all-gather.7.cloned.1.call-done), channel_id=1, source_target_pairs={{0,16},{16,0},{1,17},{17,1},{2,18},{18,2},{3,19},{19,3},{4,20},{20... | collective-permute-start | bytes 7077896 | tf_op jit(solution)/shard_map/ppermute | solution.py:262
  2531.5 148.1 %all-gather.15.cloned.1.call-start = ((), (), s32[]{:S(2)}) async-start(), calls=%async_computation.18 | async-start | bytes 1966080 | tf_op jit(solution)/shard_map/all_gather | solution.py:436
  2553.6 87.4 %collective-permute-start.4 = (bf16[512,1536]{1,0:T(8,128)(2,1)}, bf16[512,1536]{1,0:T(8,128)(2,1)}, u32[]{:S(2)}, u32[]{:S(2)}) collective-permute-start(bf16[512,1536]{1,0:T(8,128)(2,1)} %maximum_select_fusion.5), channel_id=1, source_target_pairs={{0,8},{8,0},{1,9},{9,1},{2,10},{10,2},{3,11},{11,3},{4,12},{12,4},... | collective-permute-start | bytes 4718600 | tf_op jit(solution)/shard_map/ppermute | solution.py:262
  2555.1 77.4 %collective-permute-start.7 = (bf16[512,1536]{1,0:T(8,128)(2,1)}, bf16[512,1536]{1,0:T(8,128)(2,1)}, u32[]{:S(2)}, u32[]{:S(2)}) collective-permute-start(bf16[512,1536]{1,0:T(8,128)(2,1)} %maximum_select_fusion.5), channel_id=1, source_target_pairs={{0,4},{4,0},{1,5},{5,1},{2,6},{6,2},{3,7},{7,3},{8,12},{12,8},{9,1... | collective-permute-start | bytes 4718600 | tf_op jit(solution)/shard_map/ppermute | solution.py:262
  2555.1 73.4 %collective-permute-start.3 = (bf16[2048,384]{1,0:T(8,128)(2,1)}, bf16[2048,384]{1,0:T(8,128)(2,1)}, u32[]{:S(2)}, u32[]{:S(2)}) collective-permute-start(bf16[2048,384]{1,0:T(8,128)(2,1)} %all-gather.11.cloned.1.call-done), channel_id=1, source_target_pairs={{0,16},{16,0},{1,17},{17,1},{2,18},{18,2},{3,19},{19,3},{4,20},{20... | collective-permute-start | bytes 4718600 | tf_op jit(solution)/shard_map/ppermute | solution.py:262
  2555.8 80.5 %collective-permute-start.6 = (bf16[256,4096]{1,0:T(8,128)(2,1)}, bf16[256,4096]{1,0:T(8,128)(2,1)}, u32[]{:S(2)}, u32[]{:S(2)}) collective-permute-start(bf16[256,4096]{1,0:T(8,128)(2,1)} %collective-permute-done.1), channel_id=1, source_target_pairs={{0,4},{4,0},{1,5},{5,1},{2,6},{6,2},{3,7},{7,3},{8,12},{12,8},{9,1... | collective-permute-start | bytes 6291464 | tf_op jit(solution)/shard_map/ppermute | solution.py:262
  2619.0 100.0 %all-gather.13.cloned.1.call-start = ((), (), s32[]{:S(2)}) async-start(), calls=%async_computation.17 | async-start | bytes 1966080 | tf_op jit(solution)/shard_map/all_gather | solution.py:436
  2627.8 51.8 %collective-permute-start.9 = (bf16[512,1536]{1,0:T(8,128)(2,1)S(1)}, bf16[512,1536]{1,0:T(8,128)(2,1)}, u32[]{:S(2)}, u32[]{:S(2)}) collective-permute-start(bf16[512,1536]{1,0:T(8,128)(2,1)S(1)} %copy-done.63), channel_id=1, source_target_pairs={{0,8},{8,0},{1,9},{9,1},{2,10},{10,2},{3,11},{11,3},{4,12},{12,4},... | collective-permute-start | bytes 4718600 | tf_op jit(solution)/shard_map/ppermute | solution.py:262
  2628.2 572.3 %reduce-scatter.10.cloned.1.call-start = ((), (), s32[]{:S(2)}) async-start(), calls=%async_computation.22 | async-start | bytes 1966080 | tf_op jit(solution)/shard_map/reduce_scatter | solution.py:388
  2980.8 219.7 %reduce-scatter.12.cloned.1.call-start = ((), (), s32[]{:S(2)}) async-start(), calls=%async_computation.23 | async-start | bytes 1966080 | tf_op jit(solution)/shard_map/reduce_scatter | solution.py:388
  3036.1 260.8 %reduce-scatter.14.cloned.1.call-start = ((), (), s32[]{:S(2)}) async-start(), calls=%async_computation.24 | async-start | bytes 1966080 | tf_op jit(solution)/shard_map/reduce_scatter | solution.py:388
  3114.2 70.1 %collective-permute-start.32 = (bf16[2048,768]{1,0:T(8,128)(2,1)}, bf16[2048,768]{1,0:T(8,128)(2,1)}, u32[]{:S(2)}, u32[]{:S(2)}) collective-permute-start(bf16[2048,768]{1,0:T(8,128)(2,1)} %add_convert_fusion.1), channel_id=1, source_target_pairs={{0,16},{16,0},{1,17},{17,1},{2,18},{18,2},{3,19},{19,3},{4,20},{20... | collective-permute-start | bytes 9437192 | tf_op jit(solution)/shard_map/ppermute | solution.py:262
  3126.2 206.1 %reduce-scatter.8.cloned.1.call-start = ((), (), s32[]{:S(2)}) async-start(), calls=%async_computation.21 | async-start | bytes 3932160 | tf_op jit(solution)/shard_map/reduce_scatter | solution.py:388
  3202.7 78.9 %all-to-all-start.8 = ((bf16[4,48,2048]{2,1,0:T(8,128)(2,1)}), bf16[4,48,2048]{2,1,0:T(8,128)(2,1)}, u32[]{:S(2)}, u32[]{:S(2)}) async-start(bf16[4,48,2048]{2,1,0:T(8,128)(2,1)} %bitcast.288), calls=%async_computation.12 | async-start | bytes 1572864 | tf_op jit(solution)/shard_map/all_to_all | solution.py:295
  3207.0 147.9 %reduce-scatter.6.cloned.1.call-start = ((), (), s32[]{:S(2)}) async-start(), calls=%async_computation.20 | async-start | bytes 2949120 | tf_op jit(solution)/shard_map/reduce_scatter | solution.py:388
  3207.2 54.0 %collective-permute-start.37 = (bf16[1024,1152]{1,0:T(8,128)(2,1)}, bf16[1024,1152]{1,0:T(8,128)(2,1)}, u32[]{:S(2)}, u32[]{:S(2)}) collective-permute-start(bf16[1024,1152]{1,0:T(8,128)(2,1)} %reshape.884), channel_id=1, source_target_pairs={{0,16},{16,0},{1,17},{17,1},{2,18},{18,2},{3,19},{19,3},{4,20},{20... | collective-permute-start | bytes 7077896 | tf_op jit(solution)/shard_map/ppermute | solution.py:262
  3281.6 50.8 %all-to-all-start.5 = ((bf16[32,2,6288]{2,1,0:T(2,128)(2,1)}), bf16[32,2,6288]{2,1,0:T(2,128)(2,1)}, u32[]{:S(2)}, u32[]{:S(2)}) async-start(bf16[32,2,6288]{2,1,0:T(2,128)(2,1)} %reshape.954), calls=%async_computation.5 | async-start | bytes 1638400 | tf_op jit(solution)/shard_map/all_to_all | solution.py:704
  (171 other events, 7308.4 us)
Sparse Core Ops, SparseCore 0:
  9.6 37.7 all-gather.8
  49.6 63.1 all-gather.6
  115.1 38.3 all-gather.10
  2531.7 37.3 all-gather.16
  2619.1 37.2 all-gather.14
  2657.8 35.9 all-gather.12
  2980.9 34.4 reduce-scatter.9
  3036.3 35.1 reduce-scatter.11
  3126.3 35.5 reduce-scatter.13
  3188.9 61.9 reduce-scatter.7
  3278.7 66.8 reduce-scatter.5

commit v3 on v2

--- a/solution.py
+++ b/solution.py
@@ -95,12 +95,36 @@
 def inverse_rms(raw):
     return lax.rsqrt(head_sums(raw * raw) * (1.0 / HEAD_DIM) + EPSILON)
 
-def attend_kernel(kind_ref, len_ref, qkv_ref, text_ref, text_value_ref, gain_ref, cos_ref, sin_ref, q_ref, k_ref, tk_ref, mixed_ref, read_ref):
+def attend_kernel(
+    kind_ref,
+    len_ref,
+    rows_ref,
+    caption_ref,
+    qkv_weight_ref,
+    key_weight_ref,
+    value_weight_ref,
+    out_weight_ref,
+    gain_ref,
+    cos_ref,
+    sin_ref,
+    qkv_ref,
+    text_ref,
+    text_value_ref,
+    q_ref,
+    k_ref,
+    tk_ref,
+    mixed_ref,
+    read_ref,
+    branch_ref,
+):
     item = pl.program_id(0)
     kind, length = kind_ref[item], len_ref[item]
     width = q_ref.shape[1]
     cosine, sine = cos_ref[kind], sin_ref[kind]
     scaling = HEAD_DIM ** (-0.5)
+    qkv_ref[...] = dot(rows_ref[...], qkv_weight_ref[...])
+    text_ref[...] = dot(caption_ref[...], key_weight_ref[...])
+    text_value_ref[...] = dot(caption_ref[...], value_weight_ref[...])
     for at in range(0, width, LANES):
         lanes = slice(at, at + LANES)
         turned = []
@@ -127,6 +151,8 @@
         read = join_heads(text_out)
         read_ref[:, lanes] = read
         mixed_ref[:, lanes] = (join_heads(own_out) + gain_ref[3:4, lanes] * read).astype(jnp.bfloat16)
+    branch_ref[...] = dot(mixed_ref[...], out_weight_ref[...])
+
 
 def head_norm_back(grad, raw, gain_row):
     inverse = inverse_rms(raw)
@@ -135,12 +161,33 @@
     inner = head_sums(scaled * normal) * (1.0 / HEAD_DIM)
     return inverse * (scaled - normal * inner), jnp.sum(grad * normal, axis=0, keepdims=True)
 
-def attend_back_kernel(kind_ref, len_ref, qkv_ref, text_ref, text_value_ref, gain_ref, cos_ref, sin_ref, q_ref, k_ref, tk_ref, read_ref, grad_ref, gqkv_ref, gtext_ref, gains_ref):
+def attend_back_kernel(
+    kind_ref,
+    len_ref,
+    branch_ref,
+    qkv_ref,
+    text_ref,
+    text_value_ref,
+    q_ref,
+    k_ref,
+    tk_ref,
+    read_ref,
+    qkv_weight_ref,
+    out_weight_ref,
+    gain_ref,
+    cos_ref,
+    sin_ref,
+    gqkv_ref,
+    gtext_ref,
+    grad_rows_ref,
+    gains_ref,
+):
     item = pl.program_id(0)
     kind, length = kind_ref[item], len_ref[item]
     width = q_ref.shape[1]
     cosine, sine = cos_ref[kind], sin_ref[kind]
     scaling = HEAD_DIM ** (-0.5)
+    grad_mixed = dot_right(branch_ref[...], out_weight_ref[...])
 
     @pl.when(item == 0)
     def _():
@@ -162,7 +209,7 @@
 
     for at in range(0, width, LANES):
         lanes = slice(at, at + LANES)
-        grad = grad_ref[:, lanes]
+        grad = grad_mixed[:, lanes]
         cross = gain_ref[3:4, lanes]
         values = qkv_ref[:, 2 * width + at : 2 * width + at + LANES].astype(jnp.bfloat16)
         text_values = text_value_ref[:, lanes].astype(jnp.bfloat16)
@@ -187,36 +234,96 @@
         gains_ref[2:3, lanes] += gain
         gtext_ref[:, width + at : width + at + LANES] = read_values.astype(jnp.bfloat16)
         gains_ref[3:4, lanes] += jnp.sum(grad * read_ref[:, lanes], axis=0, keepdims=True)
-
-def item_call(kernel, items, operands, outs, name):
-    def rows(shape):
-        return pl.BlockSpec((shape[0] // items, shape[1]), lambda i, *_: (i, 0))
-    def full(shape):
-        return pl.BlockSpec(shape, lambda i, *_: (0,) * len(shape))
-    def call(scalars, *arrays):
-        in_specs = [rows(a.shape) if i in operands else full(a.shape) for i, a in enumerate(arrays)]
-        return pl.pallas_call(
-            kernel,
-            grid_spec=pltpu.PrefetchScalarGridSpec(
-                num_scalar_prefetch=len(scalars), grid=(items,), in_specs=in_specs,
-                out_specs=[rows(s.shape) if cut else full(s.shape) for s, cut in outs]),
-            out_shape=[s for s, _ in outs],
-            compiler_params=pltpu.CompilerParams(dimension_semantics=("arbitrary",), vmem_limit_bytes=48*MIB),
-            name=name,
-        )(*scalars, *arrays)
-    return call
-
-def attend(kind, length, qkv_raw, text_raw, text_value_raw, gains, cosine, sine):
-    items=kind.shape[0]; n=qkv_raw.shape[0]; width=qkv_raw.shape[1]//3; t=text_raw.shape[0]
-    S=jax.ShapeDtypeStruct
-    outs=[(S((n,width),jnp.bfloat16),True),(S((n,width),jnp.bfloat16),True),(S((t,width),jnp.bfloat16),True),(S((n,width),jnp.bfloat16),True),(S((n,width),jnp.float32),True)]
-    return item_call(attend_kernel, items, (0,1,2), outs, "attend")((kind,length), qkv_raw, text_raw, text_value_raw, gains, cosine, sine)
-
-def attend_back(kind, length, qkv_raw, text_raw, text_value_raw, gains, cosine, sine, q, k, tk, read, grad):
-    items=kind.shape[0]; n=qkv_raw.shape[0]; width=qkv_raw.shape[1]//3; t=text_raw.shape[0]
-    S=jax.ShapeDtypeStruct
-    outs=[(S((n,3*width),jnp.bfloat16),True),(S((t,2*width),jnp.bfloat16),True),(S((4,width),jnp.float32),False)]
-    return item_call(attend_back_kernel, items, (0,1,2,6,7,8,9,10), outs, "attend_back")((kind,length), qkv_raw, text_raw, text_value_raw, gains, cosine, sine, q,k,tk,read,grad)
+    grad_rows_ref[...] = dot_right(gqkv_ref[...], qkv_weight_ref[...])
+
+def item_call(kernel, scalars, by_item, whole, outs, summed, name):
+    items = scalars[0].shape[0]
+
+    def cut(array):
+        return pl.BlockSpec((array.shape[0] // items, array.shape[1]), lambda i, *_: (i, 0))
+
+    def all_of(array):
+        zeros = (0,) * len(array.shape)
+        return pl.BlockSpec(array.shape, lambda i, *_: zeros, pipeline_mode=pl.Buffered(1))
+
+    return pl.pallas_call(
+        kernel,
+        grid_spec=pltpu.PrefetchScalarGridSpec(
+            num_scalar_prefetch=len(scalars),
+            grid=(items,),
+            in_specs=[cut(array) for array in by_item] + [all_of(array) for array in whole],
+            out_specs=[cut(array) for array in outs]
+            + [pl.BlockSpec(array.shape, lambda i, *_: (0, 0)) for array in summed],
+        ),
+        out_shape=outs + summed,
+        compiler_params=pltpu.CompilerParams(
+            dimension_semantics=("arbitrary",), vmem_limit_bytes=56 * MIB
+        ),
+        name=name,
+    )(*scalars, *by_item, *whole)
+
+
+def attend(scalars, rows, captions, qkv_rank, key_rank, value_rank, out_rank, tables):
+    count, width = rows.shape[0], key_rank.shape[1]
+    text_count = captions.shape[0]
+
+    def shape(count, columns, dtype=jnp.bfloat16):
+        return jax.ShapeDtypeStruct((count, columns), dtype)
+
+    outs = [
+        shape(count, 3 * width, jnp.float32),
+        shape(text_count, width, jnp.float32),
+        shape(text_count, width, jnp.float32),
+        shape(count, width),
+        shape(count, width),
+        shape(text_count, width),
+        shape(count, width),
+        shape(count, width, jnp.float32),
+        shape(count, D, jnp.float32),
+    ]
+    whole = [qkv_rank, key_rank, value_rank, out_rank, *tables]
+    *kept, branch = item_call(attend_kernel, scalars, [rows, captions], whole, outs, [], "attend")
+    return kept, branch
+
+
+def attend_back(scalars, grad_branch, kept, qkv_rank, out_rank, tables):
+    qkv_raw, text_raw, text_value_raw, queries, keys, text_keys, _, read = kept
+    count, width = queries.shape
+    outs = [
+        jax.ShapeDtypeStruct((count, 3 * width), jnp.bfloat16),
+        jax.ShapeDtypeStruct((text_raw.shape[0], 2 * width), jnp.bfloat16),
+        jax.ShapeDtypeStruct((count, D), jnp.float32),
+    ]
+    by_item = [grad_branch, qkv_raw, text_raw, text_value_raw, queries, keys, text_keys, read]
+    summed = [jax.ShapeDtypeStruct((4, width), jnp.float32)]
+    whole = [qkv_rank, out_rank, *tables]
+    return item_call(attend_back_kernel, scalars, by_item, whole, outs, summed, "attend_back")
+
+
+def product_kernel(first_ref, left_near, left_far, right_near, right_far, out_ref):
+    near = dot_left(left_near[...], right_near[...])
+    out_ref[...] = (near + dot_left(left_far[...], right_far[...])).astype(out_ref.dtype)
+
+
+def product(left_sides, right_sides, first, lanes, dtype):
+    count, columns = right_sides[0].shape
+    block = math.gcd(lanes, 384) if lanes % 384 == 0 else math.gcd(lanes, 512)
+    cut = pl.BlockSpec((count, block), lambda i, first: (0, first[0] // block + i))
+    whole = pl.BlockSpec((count, columns), lambda i, first: (0, 0), pipeline_mode=pl.Buffered(1))
+    return pl.pallas_call(
+        product_kernel,
+        grid_spec=pltpu.PrefetchScalarGridSpec(
+            num_scalar_prefetch=1,
+            grid=(lanes // block,),
+            in_specs=[cut, cut, whole, whole],
+            out_specs=pl.BlockSpec((block, columns), lambda i, first: (i, 0)),
+        ),
+        out_shape=jax.ShapeDtypeStruct((lanes, columns), dtype),
+        compiler_params=pltpu.CompilerParams(
+            dimension_semantics=("arbitrary",), vmem_limit_bytes=48 * MIB
+        ),
+        name="product",
+    )(jnp.reshape(first, (1,)).astype(jnp.int32), *left_sides, *right_sides)
 
 
 def feed_kernel(input_ref, result_ref, gate_ref, up_ref, down_ref, hidden_ref, grad_gate_ref, grad_up_ref, grad_ref):
@@ -349,30 +456,33 @@
             return jnp.stack([block, swap(block, "hi")])
         return spread(block, "hi", self.hi)
 
+    def natural_hi(self, stacked):
+        if self.hi != 2:
+            return stacked
+        mine, other = stacked[0], stacked[1]
+        low = lax.axis_index("hi") == 0
+        return jnp.stack([jnp.where(low, mine, other), jnp.where(low, other, mine)])
+
     def natural_rows(self, stacked):
         view = stacked.reshape(self.hi, self.rep, RANKS, -1, stacked.shape[-1])
         return jnp.transpose(view, (0, 2, 1, 3, 4)).reshape(-1, stacked.shape[-1])
 
-    def product(self, left_sides, right_sides, cut):
-        near, far = [
-            dot_left(cut(left), right) for left, right in zip(left_sides, right_sides, strict=True)
-        ]
-        return near + far
-
-    def product_moved(self, left_sides, right_sides):
-        half = left_sides[0].shape[1] // 2 if self.hi == 2 else 0
-        return self.product(left_sides, right_sides, lambda left: left[:, half:]).astype(jnp.bfloat16)
+    def product_moved(self, left_sides, right_sides, first=None):
+        lanes = left_sides[0].shape[1]
+        if self.hi != 2:
+            return product(left_sides, right_sides, 0, lanes, jnp.bfloat16)
+        first = lanes // 2 if first is None else first
+        return product(left_sides, right_sides, first, lanes // 2, jnp.bfloat16)
 
     def move(self, moved):
         if self.hi == 2:
             return swap(moved, "hi")
         return fold(moved.reshape(self.hi, -1, moved.shape[1]), "hi", self.hi)
 
-    def product_kept(self, left_sides, right_sides):
+    def product_kept(self, left_sides, right_sides, first=0):
         if self.hi != 2:
             return None
-        half = left_sides[0].shape[1] // 2
-        return self.product(left_sides, right_sides, lambda left: left[:, :half])
+        return product(left_sides, right_sides, first, left_sides[0].shape[1] // 2, jnp.float32)
 
     def total(self, kept, arrived):
         if kept is None:
@@ -435,7 +545,6 @@
     def z_gather(block):
         return lax.all_gather(block.reshape(-1, block.shape[-1]), "rep", tiled=True)
 
-    down_z = z_gather(down_weight)
     qkv_mine = trade_ranks(plan.by_rank(qkv_weight, 3, plan.head_groups))
     qkv_mine = qkv_mine.reshape(RANKS * rows, 3 * rank_width)
     if plan.aligned:
@@ -485,10 +594,9 @@
     text_weight, conditions = fence(text_weight, activated_mine)
     text_mine = trade_ranks(plan.by_rank(text_weight, 2, plan.head_groups))
     partial = dot(conditions, ada_weight).astype(bf16).reshape(devices, item_count, 4 * D)
-    text_mine, partial, down_z = fence(text_mine, partial, down_z)
-    down_rank = plan.across_hi(down_z)
+    text_mine, partial = fence(text_mine, partial)
     modulation = jnp.sum(lax.all_to_all(partial, AXES, 0, 0, tiled=True).astype(f32), axis=0)
-    qkv_z, down_rank, modulation, text_mine = fence(qkv_z, down_rank, modulation, text_mine)
+    qkv_z, modulation, text_mine = fence(qkv_z, modulation, text_mine)
 
     scale_attn, gate_attn, scale_mlp, gate_mlp = jnp.split(modulation, 4, axis=1)
     captions = plan.ordered(caption.reshape(-1, TEXT_DIM))
@@ -513,10 +621,7 @@
     normed_near = pair(normed)
     if plan.aligned:
         blocks = qkv_rank.reshape(hi_count, rep_count, -1, 3 * rank_width)
-        out_rank = blocks[:, :, RANKS * rows :].reshape(hi_count, -1)
-        if hi_count == 2:
-            out_rank = jnp.where(hi_at == 0, out_rank, out_rank[::-1])
-        out_rank = out_rank.reshape(rank_width, D)
+        out_rank = plan.natural_hi(blocks[:, :, RANKS * rows :]).reshape(rank_width, D)
         qkv_rank = blocks[:, :, : RANKS * rows]
     qkv_rank = plan.natural_rows(qkv_rank)
     text_value_z, text_key_rank, normed_far, caption_sides, normed_near, qkv_rank, out_rank = fence(
@@ -528,65 +633,60 @@
     result_far = swap(grad_result, "mid")
     normed_sides = (normed_near, pair(normed_far))
     text_key_rank = plan.natural_rows(text_key_rank)
-    qkv_raw = [dot(side, qkv_rank) for side in normed_sides]
-    text_key_raw = [dot(side, text_key_rank) for side in caption_sides]
-    down_rank = down_rank.reshape(hi_count, -1)
-    if hi_count == 2:
-        down_rank = jnp.where(hi_at == 0, down_rank, down_rank[::-1])
-    down_rank = down_rank.reshape(feed_width, D)
-    gate_z, text_value_rank, result_far, normed_sides, qkv_raw, text_key_raw, down_rank = fence(
-        gate_z, text_value_rank, result_far, normed_sides, qkv_raw, text_key_raw, down_rank
+    gate_z, text_value_rank, result_far, normed_sides, text_key_rank = fence(
+        gate_z, text_value_rank, result_far, normed_sides, text_key_rank
     )
 
     up_z = z_gather(gate_up_mine[..., feed_width:])
     gate_rank = plan.across_hi(gate_z)
     text_value_rank = plan.natural_rows(text_value_rank)
-    text_value_raw = [dot(side, text_value_rank) for side in caption_sides]
-    raw_near, raw_far = zip(qkv_raw, text_key_raw, text_value_raw, strict=True)
-    kept_far = attend(*scalars[1], *raw_far, *tables)
-    up_z, gate_rank, raw_near, raw_far, kept_far = fence(
-        up_z, gate_rank, raw_near, raw_far, kept_far
-    )
-
-    across = settle_far(dot(kept_far[3], out_rank))
-    across, raw_near, up_z = fence(across, raw_near, up_z)
+    attend_weights = (qkv_rank, text_key_rank, text_value_rank, out_rank, tables)
+    kept_far, branch_far = attend(scalars[1], normed_sides[1], caption_sides[1], *attend_weights)
+    up_z, gate_rank, kept_far, branch_far, attend_weights = fence(
+        up_z, gate_rank, kept_far, branch_far, attend_weights
+    )
+
+    across = settle_far(branch_far)
+    across, normed_near, up_z = fence(across, normed_sides[0], up_z)
+    normed_sides = (normed_near, normed_sides[1])
+    down_z = z_gather(down_weight)
     up_rank = plan.across_hi(up_z)
     arrived = settle_move(across)
-    kept_near = attend(*scalars[0], *raw_near, *tables)
-    up_rank, arrived, kept_near = fence(up_rank, arrived, kept_near)
-
-    branch = settle_near(dot(kept_near[3], out_rank)) + arrived
-    branch = branch.reshape(item_count, item_len, D)
+    kept_near, branch_near = attend(scalars[0], normed_near, caption_sides[0], *attend_weights)
+    result_sides = (pair(grad_result), pair(result_far))
+    gate_rank = plan.natural_rows(gate_rank)
+    down_z, up_rank, arrived, kept_near, branch_near, result_sides, gate_rank = fence(
+        down_z, up_rank, arrived, kept_near, branch_near, result_sides, gate_rank
+    )
+
+    down_rank = plan.across_hi(down_z)
+    branch = (settle_near(branch_near) + arrived).reshape(item_count, item_len, D)
     attn_gate = jnp.tanh(gate_attn)[:, None, :]
     middle = token_rows + attn_gate * branch
     mlp_input = modulate(middle, gain_rows[4], scale_mlp)
     mlp_input = plan.ordered(mlp_input.astype(bf16).reshape(row_count, D))
-    feed_weights = (plan.natural_rows(gate_rank), plan.natural_rows(up_rank), down_rank)
-    result_sides = (pair(grad_result), pair(result_far))
+    up_rank = plan.natural_rows(up_rank)
+    input_far = swap(mlp_input, "mid")
     input_near = pair(mlp_input)
-    feed_weights, mlp_input, input_near, result_sides = fence(
-        feed_weights, mlp_input, input_near, result_sides
-    )
-
-    input_far = swap(mlp_input, "mid")
-    hidden_near, gate_near, up_near, partial_near = feed(input_near, result_sides[0], *feed_weights)
-    input_far, hidden_near, gate_near, up_near, partial_near = fence(
-        input_far, hidden_near, gate_near, up_near, partial_near
-    )
+    down_rank, input_far, input_near, up_rank = fence(down_rank, input_far, input_near, up_rank)
+
+    down_rank = plan.natural_hi(down_rank).reshape(feed_width, D)
+    feed_weights = (gate_rank, up_rank, down_rank)
     input_sides = (input_near, pair(input_far))
     hidden_far, gate_far, up_far, partial_far = feed(input_sides[1], result_sides[1], *feed_weights)
     across = settle_far(partial_far)
-    across, gate_far, up_far, hidden_far = fence(across, gate_far, up_far, hidden_far)
+    across, input_near = fence(across, input_near)
     arrived = settle_move(across)
+    hidden_near, gate_near, up_near, partial_near = feed(input_near, result_sides[0], *feed_weights)
+    input_sides = (input_near, input_sides[1])
     gate_sides, up_sides, hidden_sides = (gate_near, gate_far), (up_near, up_far), (hidden_near, hidden_far)
-    hidden_turned = [plan.ordered(side) for side in hidden_sides]
     gate_moved = plan.product_moved(input_sides, gate_sides)
-    up_moved = plan.product_moved(input_sides, up_sides)
-    near = settle_near(partial_near)
-    arrived, gate_moved, up_moved, near = fence(arrived, gate_moved, up_moved, near)
+    arrived, gate_sides, up_sides, hidden_sides, partial_near, gate_moved = fence(
+        arrived, gate_sides, up_sides, hidden_sides, partial_near, gate_moved
+    )
 
     gate_moved = plan.move(gate_moved)
-    grad_mlp_input = plan.ordered(near + arrived)
+    grad_mlp_input = plan.ordered(settle_near(partial_near) + arrived)
     _, pull_mlp_norm = jax.vjp(modulate, middle, gain_rows[4], scale_mlp)
     grad_middle_norm, grad_mlp_gain, grad_scale_mlp = pull_mlp_norm(
         grad_mlp_input.reshape(item_count, item_len, D)
@@ -595,71 +695,77 @@
     grad_attn_gate = jnp.sum(grad_middle * branch, axis=1) * (1.0 - jnp.tanh(gate_attn) ** 2)
     grad_branch = (attn_gate * grad_middle).astype(bf16).reshape(row_count, D)
     branch_near = pair(grad_branch)
-    mixed_near = dot_right(branch_near, out_rank)
+    up_moved = plan.product_moved(input_sides, up_sides)
     gate_kept = plan.product_kept(input_sides, gate_sides)
-    gate_moved, gate_kept, grad_branch, branch_near, mixed_near = fence(
-        gate_moved, gate_kept, grad_branch, branch_near, mixed_near
-    )
-
-    def attention_back(at, kept, raw, grad_mixed):
-        queries, key_rows, text_keys, _, read = kept
-        return attend_back(
-            *scalars[at], *raw, *tables, queries, key_rows, text_keys, read, grad_mixed
-        )
+    gate_moved, up_moved, gate_kept, grad_branch, branch_near = fence(
+        gate_moved, up_moved, gate_kept, grad_branch, branch_near
+    )
 
     gate_grad = plan.by_rep(plan.total(gate_kept, gate_moved))
-    gate_grad, up_moved, grad_branch, mixed_near = fence(
-        gate_grad, up_moved, grad_branch, mixed_near
+    gate_grad, up_moved, grad_branch, branch_near = fence(
+        gate_grad, up_moved, grad_branch, branch_near
     )
     gate_parts = plan.reduce(gate_grad)
     branch_far = swap(grad_branch, "mid")
     up_moved = plan.move(up_moved)
-    qkv_near, text_near, gain_near = attention_back(0, kept_near, raw_near, mixed_near)
-    branch_far, up_moved, qkv_near, text_near, gain_near = fence(
-        branch_far, up_moved, qkv_near, text_near, gain_near
+    back_weights = (qkv_rank, out_rank, tables)
+    qkv_near, text_near, rows_near, gain_near = attend_back(
+        scalars[0], branch_near, kept_near, *back_weights
+    )
+    up_kept = plan.product_kept(input_sides, up_sides)
+    hidden_first = hi_at * (feed_width // 2)
+    down_moved = plan.product_moved(hidden_sides, result_sides, feed_width // 2 - hidden_first)
+    branch_far, up_moved, qkv_near, text_near, rows_near, gain_near, up_kept, down_moved = fence(
+        branch_far, up_moved, qkv_near, text_near, rows_near, gain_near, up_kept, down_moved
     )
 
     branch_sides = (branch_near, pair(branch_far))
-    up_grad = plan.by_rep(plan.total(plan.product_kept(input_sides, up_sides), up_moved))
-    mixed_far = dot_right(branch_sides[1], out_rank)
-    down_moved = plan.product_moved(hidden_turned, result_sides)
-    up_grad, mixed_far, down_moved = fence(up_grad, mixed_far, down_moved)
+    up_grad = plan.by_rep(plan.total(up_kept, up_moved))
+    up_grad, branch_far, down_moved = fence(up_grad, branch_sides[1], down_moved)
     up_parts = plan.reduce(up_grad)
     down_moved = plan.move(down_moved)
-    qkv_far, text_far, gain_far = attention_back(1, kept_far, raw_far, mixed_far)
-    down_moved, qkv_far, text_far, gain_far = fence(down_moved, qkv_far, text_far, gain_far)
-
-    text_sides, qkv_sides, mixed_sides = (text_near, text_far), (qkv_near, qkv_far), (kept_near[3], kept_far[3])
-    mixed_sides = [plan.ordered(side) for side in mixed_sides]
-    down_kept = plan.product_kept(hidden_turned, result_sides)
+    qkv_far, text_far, rows_far, gain_far = attend_back(
+        scalars[1], branch_far, kept_far, *back_weights
+    )
+    text_sides, qkv_sides = (text_near, text_far), (qkv_near, qkv_far)
+    text_moved = plan.product_moved(caption_sides, text_sides)
+    down_moved, text_moved, text_sides, qkv_sides, rows_far, gain_far = fence(
+        down_moved, text_moved, text_sides, qkv_sides, rows_far, gain_far
+    )
+
+    text_moved = plan.move(text_moved)
+    down_kept = plan.product_kept(hidden_sides, result_sides, hidden_first)
     down_grad = plan.total(down_kept, down_moved).reshape(rep_count, -1, D)
-    across = settle_far(dot_right(qkv_far, qkv_rank))
-    text_moved = plan.product_moved(caption_sides, text_sides)
-    down_grad, across, text_moved, hidden_sides = fence(down_grad, across, text_moved, hidden_sides)
+    across = settle_far(rows_far)
+    across, down_grad, text_sides, qkv_sides = fence(across, down_grad, text_sides, qkv_sides)
     down_weight_grad = plan.reduce(down_grad).astype(f32)
     arrived = settle_move(across)
-    text_moved = plan.move(text_moved)
+    qkv_moved = plan.product_moved(normed_sides, qkv_sides)
     text_kept = plan.product_kept(caption_sides, text_sides)
-    qkv_moved = plan.product_moved(normed_sides, qkv_sides)
-    grad_normed = settle_near(dot_right(qkv_near, qkv_rank))
-    partial_result = [dot(side, down_rank) for side in hidden_sides]
-    result_near, across = settle_near(partial_result[0]), settle_far(partial_result[1])
-    if plan.aligned:
-        out_moved = plan.product_moved(mixed_sides, branch_sides)
-    if plan.aligned and hi_count == 2:
-        qkv_moved = jnp.concatenate([qkv_moved.reshape(-1), out_moved.reshape(-1)])
-        qkv_moved = qkv_moved.reshape(-1, 3 * rank_width)
-    arrived, text_moved, text_kept, qkv_moved, grad_normed, result_near, across = fence(
-        arrived, text_moved, text_kept, qkv_moved, grad_normed, result_near, across
+    qkv_kept = plan.product_kept(normed_sides, qkv_sides)
+    grad_normed = settle_near(rows_near)
+    arrived, text_moved, text_kept, qkv_moved, qkv_kept, grad_normed = fence(
+        arrived, text_moved, text_kept, qkv_moved, qkv_kept, grad_normed
     )
 
     text_grad = plan.by_rep(plan.total(text_kept, text_moved))
-    text_grad, qkv_moved, grad_normed, across = fence(text_grad, qkv_moved, grad_normed, across)
+    text_grad, qkv_moved, arrived = fence(text_grad, qkv_moved, arrived)
     text_parts = plan.reduce(text_grad)
     qkv_moved = plan.move(qkv_moved)
-    if plan.aligned and hi_count != 2:
-        out_moved = plan.move(out_moved)
-    result = (result_near + settle_move(across)).reshape(item_count, item_len, D)
+    mixed_sides = [plan.ordered(kept[6]) for kept in (kept_near, kept_far)]
+    if plan.aligned:
+        out_halves = [
+            dot_left(mixed_sides[0][:, lanes], branch_sides[0])
+            + dot_left(mixed_sides[1][:, lanes], branch_sides[1])
+            for lanes in (slice(0, rank_width // 2), slice(rank_width // 2, None))
+        ]
+        if hi_count == 2:
+            out_kept, out_moved = out_halves[0], swap(out_halves[1].astype(bf16), "hi")
+        else:
+            out_kept, out_moved = None, plan.move(jnp.concatenate(out_halves).astype(bf16))
+    partial_result = [dot(side, down_rank) for side in hidden_sides]
+    result = settle_near(partial_result[0]) + settle_move(settle_far(partial_result[1]))
+    result = result.reshape(item_count, item_len, D)
     layer_out = (middle + mlp_gate * result).astype(bf16).reshape(row_count, D)
     grad_mlp_gate = jnp.sum(grad_top * result, axis=1) * (1.0 - jnp.tanh(gate_mlp) ** 2)
     grad_normed = plan.ordered(grad_normed + arrived)
@@ -668,23 +774,18 @@
         grad_normed.reshape(item_count, item_len, D)
     )
     tokens_grad = (grad_middle + grad_token_norm).reshape(row_count, D)
-    qkv_kept = plan.product_kept(normed_sides, qkv_sides)
+    qkv_grad = plan.by_rep(plan.total(qkv_kept, qkv_moved))
     if plan.aligned:
-        out_kept = plan.product_kept(mixed_sides, branch_sides)
-        if out_kept is not None:
-            split = qkv_kept.shape[0]
-            qkv_moved, out_moved = qkv_moved[:split], qkv_moved[split:].reshape(out_kept.shape)
-        qkv_grad = plan.total(qkv_kept, qkv_moved)
-        out_grad = plan.total(out_kept, out_moved)
-        qkv_grad = jnp.concatenate(
-            [plan.by_rep(qkv_grad), out_grad.reshape(rep_count, -1, 3 * rank_width)], axis=1
-        )
+        out_grad = plan.total(out_kept, out_moved).reshape(rep_count, -1, 3 * rank_width)
+        qkv_grad = jnp.concatenate([qkv_grad, out_grad], axis=1)
     else:
-        qkv_grad = plan.by_rep(plan.total(qkv_kept, qkv_moved))
         at = (jnp.arange(RANKS) == plan.rank).astype(bf16)[:, None, None]
-        out_grad = plan.product(mixed_sides, branch_sides, lambda left: left)
+        out_grad = dot_left(mixed_sides[0], branch_sides[0]) + dot_left(mixed_sides[1], branch_sides[1])
         placed = (out_grad.astype(bf16)[None] * at).reshape(D, D)
         out_weight_grad = lax.psum_scatter(placed, AXES, scatter_dimension=0, tiled=True).astype(f32)
+    qkv_grad, grad_mlp_gate, grad_scale_attn, grad_attn_gain = fence(
+        qkv_grad, grad_mlp_gate, grad_scale_attn, grad_attn_gain
+    )
     qkv_parts = plan.reduce(qkv_grad)
     if plan.aligned:
         out_weight_grad = qkv_parts[RANKS * rows :].reshape(-1, D).astype(f32)

time: 3420 us -> 1000 us (0.29)
  local copies, waits for them, and re-layouts: 2610 us -> 116 us
  matrix products: 134 us -> 20.2 us
  Pallas kernels: 119 us -> 221 us
  waiting for transfers between devices: 279 us -> 379 us
  blocking collectives: 10.9 us -> 50.2 us
    rev x2 -> x0, local copies, waits for them, and re-layouts: 2450 us -> none  [the longest x1 2400 us: local(): down_rank = jnp.where(hi_at == 0, down_rank, down_rank[::-1])]
    reduce_scatter x5, waiting for transfers between devices: 0.01 us -> 112 us  [reduce(): return lax.psum_scatter(flat, 'rep', scatter_dimension=0, tiled=True)]
    pallas_call x4 -> x14, Pallas kernels: 72.2 us -> 174 us  [the longest x4 105 us: item_call(): pl.pallas_call(kernel, grid_spec=pltpu.PrefetchScalarGridSpec(num_scalar_...]
    dot_general x25 -> x5, matrix products: 78.8 us -> 7.67 us  [dot_left(): lax.dot_general(left, right, (((0,), (0,)), ((), ())), preferred_element_...]
    ppermute x38 -> x39, waiting for transfers between devices: 190 us -> 239 us  [swap(): return lax.ppermute(block, axis, [(at, at ^ step) for at in range(count)])]
    all_to_all x0 -> x1, blocking collectives: none -> 39.3 us  [local(): lax.all_to_all(partial, AXES, 0, 0, tiled=True).astype(f32)]
  transfers between devices with their start and end apart: 57 -> 57, of which waited for: 19 -> 23; matrix products, arithmetic and copies ran while one was open for 84% -> 23% of each run, Pallas kernels for 4% -> 20%
where the time goes in v3:
time: 1000 us; the launch traced here: 990 us
  waiting for transfers between devices  379 us (38%)
  Pallas kernels  221 us (22%)
  other arithmetic  139 us (14%)
  local copies, waits for them, and re-layouts  116 us (12%)
  blocking collectives  50.2 us (5%)
  starting transfers between devices  48.7 us (5%)
  matrix products  20.2 us (2%)
  between operations  15.9 us (2%)
    ppermute x39, waiting for transfers between devices, swap(): return lax.ppermute(block, axis, [(at, at ^ step) for at in range(count)])  239 us
    reduce_scatter x5, waiting for transfers between devices, reduce(): return lax.psum_scatter(flat, 'rep', scatter_dimension=0, tiled=True)  112 us
    pallas_call x4, Pallas kernels, item_call(): pl.pallas_call(kernel, grid_spec=pltpu.PrefetchScalarGridSpec(num_scalar_...  105 us
    pallas_call x10, Pallas kernels, product(): pl.pallas_call(product_kernel, grid_spec=pltpu.PrefetchScalarGridSpec(num...  69.7 us
    pallas_call x2, Pallas kernels, feed(): pl.pallas_call(feed_kernel, grid=(count // block,), in_specs=[cut(D), cut...  46.5 us
    all_to_all x1, blocking collectives, local(): lax.all_to_all(partial, AXES, 0, 0, tiled=True).astype(f32)  39.3 us
    concatenate x8, other arithmetic, pair(): return jnp.concatenate([rows, swap(rows, 'core')])  29.9 us
    all_to_all x6, waiting for transfers between devices, trade_ranks(): return lax.all_to_all(block, ('mid', 'core'), 0, 0, tiled=True)  28.2 us
  transfers between devices with their start and end apart: 57, of which 23 were waited for; matrix products, arithmetic and copies ran while one was open for 23% of the time, Pallas kernels for 20%

profile of v3, /device:TPU:8, one launch (start us, length us, event | category | flops | bytes accessed | tf_op | source)
XLA Modules:
  0.0 990.0 jit_solution(8870476629603470774)
XLA Ops:
  14.5 7.3 all-to-all-done
  23.9 10.8 %all_to_all.59 = bf16[32,2,194]{2,1,0:T(2,128)(2,1)S(1)} all-to-all(bf16[32,2,194]{2,1,0:T(2,128)(2,1)S(1)} %reshape.935), channel_id=1, replica_groups=mesh['hi'=2,'mid'=2,'core'=2,'rep'=4] {'hi','mid','core','rep'}, dimensions={0} | all-to-all | bytes 49664 | tf_op jit(solution)/shard_map/all_to_all | solution.py:564
  44.1 7.3 all-to-all-done.2
  51.4 39.3 %all_to_all.60 = bf16[32,2,6144]{2,1,0:T(2,128)(2,1)S(1)} all-to-all(bf16[32,2,6144]{2,1,0:T(2,128)(2,1)} %reshape.838), channel_id=1, replica_groups=mesh['hi'=2,'mid'=2,'core'=2,'rep'=4] {'hi','mid','core','rep'}, dimensions={0} | all-to-all | bytes 1572864 | tf_op jit(solution)/shard_map/all_to_all | solution.py:598
  114.5 31.5 %collective-permute-done.1 = bf16[1024,1152]{1,0:T(8,128)(2,1)} collective-permute-done((bf16[1024,1152]{1,0:T(8,128)(2,1)}, bf16[1024,1152]{1,0:T(8,128)(2,1)}, u32[]{:S(2)}, u32[]{:S(2)}) %collective-permute-start.1) | collective-permute-done | bytes 2359328 | tf_op jit(solution)/shard_map/ppermute | solution.py:369
  171.5 18.9 %collective-permute-done.2 = bf16[2048,384]{1,0:T(8,128)(2,1)} collective-permute-done((bf16[2048,384]{1,0:T(8,128)(2,1)}, bf16[2048,384]{1,0:T(8,128)(2,1)}, u32[]{:S(2)}, u32[]{:S(2)}) %collective-permute-start.2) | collective-permute-done | bytes 1572896 | tf_op jit(solution)/shard_map/ppermute | solution.py:369
  204.8 29.4 %collective-permute-done.7 = bf16[2048,384]{1,0:T(8,128)(2,1)} collective-permute-done((bf16[2048,384]{1,0:T(8,128)(2,1)}, bf16[2048,384]{1,0:T(8,128)(2,1)}, u32[]{:S(2)}, u32[]{:S(2)}) %collective-permute-start.7) | collective-permute-done | bytes 1572896 | tf_op jit(solution)/shard_map/ppermute | solution.py:369
  251.6 22.3 %attend.2 = (f32[1024,1152]{1,0:T(8,128)}, f32[512,384]{1,0:T(8,128)}, f32[512,384]{1,0:T(8,128)}, bf16[1024,384]{1,0:T(8,128)(2,1)}, bf16[1024,384]{1,0:T(8,128...) custom-call(s32[4]{0:T(128)} %maximum_convert_fusion.kind_ref, ...), custom_call_target="tpu_custom_call" | custom-call | tf_op jit(solution)/shard_map/attend/pallas_call | solution.py:249
  307.3 22.2 %attend.3 = (f32[1024,1152]{1,0:T(8,128)}, f32[512,384]{1,0:T(8,128)}, f32[512,384]{1,0:T(8,128)}, bf16[1024,384]{1,0:T(8,128)(2,1)}, bf16[1024,384]{1,0:T(8,128...) custom-call(s32[4]{0:T(128)} %maximum_convert_fusion.2.kind_ref, ...), custom_call_target="tpu_custom_call" | custom-call | tf_op jit(solution)/shard_map/attend/pallas_call | solution.py:249
  354.7 22.5 %collective-permute-done.17 = bf16[512,1536]{1,0:T(8,128)(2,1)S(1)} collective-permute-done((bf16[512,1536]{1,0:T(8,128)(2,1)}, bf16[512,1536]{1,0:T(8,128)(2,1)S(1)}, u32[]{:S(2)}, u32[]{:S(2)}) %collective-permute-start.17) | collective-permute-done | bytes 1572896 | tf_op jit(solution)/shard_map/ppermute | solution.py:369
  379.3 8.1 collective-permute-done.18
  392.5 23.3 %feed.2 = (bf16[1024,1024]{1,0:T(8,128)(2,1)}, bf16[1024,1024]{1,0:T(8,128)(2,1)}, bf16[1024,1024]{1,0:T(8,128)(2,1)}, f32[1024,1536]{1,0:T(8,128)}) custom-call(bf16[1024,1536]{1,0:T(8,128)(2,1)} %copy-done.18, bf16[1024,1536]{1,0:T(8,128)(2,1)} %pad_maximum_fusion.10.result_ref.right_far, bf16[1536,1024]{1,0:T(8,128)(2,1)} %bitcast.209, ...), custom_call_target="tpu_custom_call" | custom-call | tf_op jit(solution)/shard_map/feed/pallas_call | solution.py:355
  425.0 23.2 %feed.3 = (bf16[1024,1024]{1,0:T(8,128)(2,1)}, bf16[1024,1024]{1,0:T(8,128)(2,1)}, bf16[1024,1024]{1,0:T(8,128)(2,1)}, f32[1024,1536]{1,0:T(8,128)}) custom-call(bf16[1024,1536]{1,0:T(8,128)(2,1)} %pad_maximum_fusion.12.input_ref.left_near, bf16[1024,1536]{1,0:T(8,128)(2,1)} %pad_maximum_fusion.9.result_ref.right_near, bf16[1536,1024]{1,0:T(8,128)(2,1)} %bitcast.210, ...), custom_call_target="tpu_custom_call" | custom-call | tf_op jit(solution)/shard_map/feed/pallas_call | solution.py:355
  490.1 19.5 %collective-permute-done.27 = bf16[768,1024]{1,0:T(8,128)(2,1)S(1)} collective-permute-done((bf16[768,1024]{1,0:T(8,128)(2,1)S(1)}, bf16[768,1024]{1,0:T(8,128)(2,1)S(1)}, u32[]{:S(2)}, u32[]{:S(2)}) %collective-permute-start.27) | collective-permute-done | bytes 1572896 | tf_op jit(solution)/shard_map/ppermute | solution.py:369
  522.9 7.5 product.14
  530.4 30.3 %attend_back.2 = (bf16[1024,1152]{1,0:T(8,128)(2,1)}, bf16[512,768]{1,0:T(8,128)(2,1)}, f32[1024,1536]{1,0:T(8,128)}, f32[4,384]{1,0:T(4,128)}) custom-call(s32[4]{0:T(128)} %maximum_convert_fusion.2.kind_ref, s32[4]{0:T(128)} %maximum_convert_fusion.3.len_ref, bf16[1024,1536]{1,0:T(8,128)(2,1)} %pad_maximum_fusion.14.branch_ref, ...), custom_call_target="tpu_custom_call" | custom-call | tf_op jit(solution)/shard_map/attend_back/pallas_call | solution.py:249
  587.3 10.2 %product.16 = f32[512,1536]{1,0:T(8,128)} custom-call(s32[1]{0:T(128)} %bitcast.58.first_ref, bf16[1024,1024]{1,0:T(8,128)(2,1)S(1)} %copy-done.7, bf16[1024,1024]{1,0:T(8,128)(2,1)S(1)} %copy-done.5, bf16[1024,1536]{1,0:T(8,128)(2,1)} %pad_maximum_fusion.9.result_ref.right_near, bf16[1024,1536]{1,0:T(8,128)(2,1)} %pad_maximum_fusion.10.result_ref.right_far), custom_call_target="tpu_custom_call" | custom-call | tf_op jit(solution)/shard_map/product/pallas_call | solution.py:313
  599.1 30.1 %attend_back.3 = (bf16[1024,1152]{1,0:T(8,128)(2,1)}, bf16[512,768]{1,0:T(8,128)(2,1)}, f32[1024,1536]{1,0:T(8,128)}, f32[4,384]{1,0:T(4,128)}) custom-call(s32[4]{0:T(128)} %maximum_convert_fusion.kind_ref, s32[4]{0:T(128)} %maximum_convert_fusion.1.len_ref, bf16[1024,1536]{1,0:T(8,128)(2,1)} %copy-done.25, f32[1024,1152]{1,0:T(8,128)} %get-tuple-element.298.qkv_ref, ...), custom_call_target="tpu_custom_call" | custom-call | tf_op jit(solution)/shard_map/attend_back/pallas_call | solution.py:249
  666.8 61.0 %collective-permute-done.38 = bf16[192,1536]{1,0:T(8,128)(2,1)S(1)} collective-permute-done((bf16[192,1536]{1,0:T(8,128)(2,1)S(1)}, bf16[192,1536]{1,0:T(8,128)(2,1)S(1)}, u32[]{:S(2)}, u32[]{:S(2)}) %collective-permute-start.38) | collective-permute-done | bytes 589856 | tf_op jit(solution)/shard_map/ppermute | solution.py:369
  772.1 26.3 %collective-permute-done.37 = bf16[768,1152]{1,0:T(8,128)(2,1)S(1)} collective-permute-done((bf16[768,1152]{1,0:T(8,128)(2,1)S(1)}, bf16[768,1152]{1,0:T(8,128)(2,1)S(1)}, u32[]{:S(2)}, u32[]{:S(2)}) %collective-permute-start.37) | collective-permute-done | bytes 1769504 | tf_op jit(solution)/shard_map/ppermute | solution.py:369
  822.8 40.6 %reduce-scatter.6.cloned.1.call-done = bf16[256,1152]{1,0:T(8,128)(2,1)} async-done(((bf16[1024,1152]{1,0:T(8,128)(2,1)}), bf16[256,1152]{1,0:T(8,128)(2,1)}) %reduce-scatter.6.cloned.1.call-update) | async-done | bytes 589840 | tf_op jit(solution)/shard_map/reduce_scatter | solution.py:498
  878.6 7.7 fusion.6
  886.3 12.5 %reduce-scatter.14.cloned.1.call-done = bf16[128,1536]{1,0:T(8,128)(2,1)} async-done(((bf16[512,1536]{1,0:T(8,128)(2,1)}), bf16[128,1536]{1,0:T(8,128)(2,1)}) %reduce-scatter.14.cloned.1.call-update) | async-done | bytes 393232 | tf_op jit(solution)/shard_map/reduce_scatter | solution.py:498
  902.6 58.4 %reduce-scatter.8.cloned.1.call-done = bf16[512,768]{1,0:T(8,128)(2,1)} async-done(((bf16[2048,768]{1,0:T(8,128)(2,1)}), bf16[512,768]{1,0:T(8,128)(2,1)}) %reduce-scatter.8.cloned.1.call-update) | async-done | bytes 786448 | tf_op jit(solution)/shard_map/reduce_scatter | solution.py:498
  (518 shorter events, 403.7 us)
Async XLA Ops:
  13.8 77.6 %all-gather.7.cloned.1.call-start = ((), (), s32[]{:S(2)}) async-start(), calls=%async_computation.14 | async-start | bytes 2949120 | tf_op jit(solution)/shard_map/all_gather | solution.py:546
  39.8 114.1 %all-gather.11.cloned.1.call-start = ((), (), s32[]{:S(2)}) async-start(), calls=%async_computation.16 | async-start | bytes 1966080 | tf_op jit(solution)/shard_map/all_gather | solution.py:546
  94.3 51.6 %collective-permute-start.1 = (bf16[1024,1152]{1,0:T(8,128)(2,1)}, bf16[1024,1152]{1,0:T(8,128)(2,1)}, u32[]{:S(2)}, u32[]{:S(2)}) collective-permute-start(bf16[1024,1152]{1,0:T(8,128)(2,1)} %all-gather.7.cloned.1.call-done), channel_id=1, source_target_pairs={{0,16},{16,0},{1,17},{17,1},{2,18},{18,2},{3,19},{19,3},{4,20},{20... | collective-permute-start | bytes 7077896 | tf_op jit(solution)/shard_map/ppermute | solution.py:369
  97.2 58.7 %collective-permute-start.4 = (bf16[256,4096]{1,0:T(8,128)(2,1)}, bf16[256,4096]{1,0:T(8,128)(2,1)}, u32[]{:S(2)}, u32[]{:S(2)}) collective-permute-start(bf16[256,4096]{1,0:T(8,128)(2,1)} %maximum_select_fusion.2), channel_id=1, source_target_pairs={{0,4},{4,0},{1,5},{5,1},{2,6},{6,2},{3,7},{7,3},{8,12},{12,8},{9,1... | collective-permute-start | bytes 6291464 | tf_op jit(solution)/shard_map/ppermute | solution.py:369
  97.2 56.7 %collective-permute-start = (bf16[256,4096]{1,0:T(8,128)(2,1)}, bf16[256,4096]{1,0:T(8,128)(2,1)}, u32[]{:S(2)}, u32[]{:S(2)}) collective-permute-start(bf16[256,4096]{1,0:T(8,128)(2,1)} %maximum_select_fusion.2), channel_id=1, source_target_pairs={{0,8},{8,0},{1,9},{9,1},{2,10},{10,2},{3,11},{11,3},{4,12},{12,4},... | collective-permute-start | bytes 6291464 | tf_op jit(solution)/shard_map/ppermute | solution.py:369
  102.2 51.7 %all-to-all-start.4 = ((bf16[4,48,2048]{2,1,0:T(8,128)(2,1)}), bf16[4,48,2048]{2,1,0:T(8,128)(2,1)S(1)}, u32[]{:S(2)}, u32[]{:S(2)}) async-start(bf16[4,48,2048]{2,1,0:T(8,128)(2,1)} %reshape.842), calls=%async_computation.4 | async-start | bytes 1572864 | tf_op jit(solution)/shard_map/all_to_all | solution.py:402
  105.7 92.9 %all-gather.17.cloned.1.call-start = ((), (), s32[]{:S(2)}) async-start(), calls=%async_computation.19 | async-start | bytes 1966080 | tf_op jit(solution)/shard_map/all_gather | solution.py:546
  108.6 132.8 %all-gather.15.cloned.1.call-start = ((), (), s32[]{:S(2)}) async-start(), calls=%async_computation.18 | async-start | bytes 1966080 | tf_op jit(solution)/shard_map/all_gather | solution.py:546
  167.5 112.0 %all-gather.13.cloned.1.call-start = ((), (), s32[]{:S(2)}) async-start(), calls=%async_computation.17 | async-start | bytes 1966080 | tf_op jit(solution)/shard_map/all_gather | solution.py:546
  200.6 136.2 %all-gather.9.cloned.1.call-start = ((), (), s32[]{:S(2)}) async-start(), calls=%async_computation.15 | async-start | bytes 1966080 | tf_op jit(solution)/shard_map/all_gather | solution.py:546
  283.2 519.0 %reduce-scatter.10.cloned.1.call-start = ((), (), s32[]{:S(2)}) async-start(), calls=%async_computation.22 | async-start | bytes 1966080 | tf_op jit(solution)/shard_map/reduce_scatter | solution.py:498
  511.6 49.1 %collective-permute-start.29 = (bf16[512,1536]{1,0:T(8,128)(2,1)}, bf16[512,1536]{1,0:T(8,128)(2,1)}, u32[]{:S(2)}, u32[]{:S(2)}) collective-permute-start(bf16[512,1536]{1,0:T(8,128)(2,1)} %fusion.10), channel_id=1, source_target_pairs={{0,8},{8,0},{1,9},{9,1},{2,10},{10,2},{3,11},{11,3},{4,12},{12,4},... | collective-permute-start | bytes 4718600 | tf_op jit(solution)/shard_map/ppermute | solution.py:369
  570.4 69.0 %collective-permute-start.24 = (bf16[512,1536]{1,0:T(8,128)(2,1)}, bf16[512,1536]{1,0:T(8,128)(2,1)}, u32[]{:S(2)}, u32[]{:S(2)}) collective-permute-start(bf16[512,1536]{1,0:T(8,128)(2,1)} %slice.322), channel_id=1, source_target_pairs={{0,4},{4,0},{1,5},{5,1},{2,6},{6,2},{3,7},{7,3},{8,12},{12,8},{9,1... | collective-permute-start | bytes 4718600 | tf_op jit(solution)/shard_map/ppermute | solution.py:369
  577.4 59.7 %collective-permute-start.32 = (bf16[512,1536]{1,0:T(8,128)(2,1)}, bf16[512,1536]{1,0:T(8,128)(2,1)}, u32[]{:S(2)}, u32[]{:S(2)}) collective-permute-start(bf16[512,1536]{1,0:T(8,128)(2,1)} %product.14), channel_id=1, source_target_pairs={{0,16},{16,0},{1,17},{17,1},{2,18},{18,2},{3,19},{19,3},{4,20},{20... | collective-permute-start | bytes 4718600 | tf_op jit(solution)/shard_map/ppermute | solution.py:369
  581.2 221.0 %reduce-scatter.12.cloned.1.call-start = ((), (), s32[]{:S(2)}) async-start(), calls=%async_computation.23 | async-start | bytes 1966080 | tf_op jit(solution)/shard_map/reduce_scatter | solution.py:498
  598.9 162.0 %collective-permute-start.23 = (bf16[512,1536]{1,0:T(8,128)(2,1)}, bf16[512,1536]{1,0:T(8,128)(2,1)}, u32[]{:S(2)}, u32[]{:S(2)}) collective-permute-start(bf16[512,1536]{1,0:T(8,128)(2,1)} %slice.323), channel_id=1, source_target_pairs={{0,4},{4,0},{1,5},{5,1},{2,6},{6,2},{3,7},{7,3},{8,12},{12,8},{9,1... | collective-permute-start | bytes 4718600 | tf_op jit(solution)/shard_map/ppermute | solution.py:369
  643.6 117.2 %collective-permute-start.25 = (bf16[512,1536]{1,0:T(8,128)(2,1)}, bf16[512,1536]{1,0:T(8,128)(2,1)}, u32[]{:S(2)}, u32[]{:S(2)}) collective-permute-start(bf16[512,1536]{1,0:T(8,128)(2,1)} %fusion.16), channel_id=1, source_target_pairs={{0,8},{8,0},{1,9},{9,1},{2,10},{10,2},{3,11},{11,3},{4,12},{12,4},... | collective-permute-start | bytes 4718600 | tf_op jit(solution)/shard_map/ppermute | solution.py:369
  645.1 107.4 %collective-permute-start.35 = (bf16[2048,768]{1,0:T(8,128)(2,1)}, bf16[2048,768]{1,0:T(8,128)(2,1)}, u32[]{:S(2)}, u32[]{:S(2)}) collective-permute-start(bf16[2048,768]{1,0:T(8,128)(2,1)} %product.15), channel_id=1, source_target_pairs={{0,16},{16,0},{1,17},{17,1},{2,18},{18,2},{3,19},{19,3},{4,20},{20... | collective-permute-start | bytes 9437192 | tf_op jit(solution)/shard_map/ppermute | solution.py:369
  654.5 96.2 %collective-permute-start.34 = (bf16[512,1536]{1,0:T(8,128)(2,1)}, bf16[512,1536]{1,0:T(8,128)(2,1)}, u32[]{:S(2)}, u32[]{:S(2)}) collective-permute-start(bf16[512,1536]{1,0:T(8,128)(2,1)} %convert_add_fusion.2), channel_id=1, source_target_pairs={{0,8},{8,0},{1,9},{9,1},{2,10},{10,2},{3,11},{11,3},{4,12},{12,4},... | collective-permute-start | bytes 4718600 | tf_op jit(solution)/shard_map/ppermute | solution.py:369
  657.7 205.7 %reduce-scatter.6.cloned.1.call-start = ((), (), s32[]{:S(2)}) async-start(), calls=%async_computation.20 | async-start | bytes 2949120 | tf_op jit(solution)/shard_map/reduce_scatter | solution.py:498
  660.6 67.3 %collective-permute-start.38 = (bf16[192,1536]{1,0:T(8,128)(2,1)S(1)}, bf16[192,1536]{1,0:T(8,128)(2,1)S(1)}, u32[]{:S(2)}, u32[]{:S(2)}) collective-permute-start(bf16[192,1536]{1,0:T(8,128)(2,1)S(1)} %fusion.21), channel_id=1, source_target_pairs={{0,16},{16,0},{1,17},{17,1},{2,18},{18,2},{3,19},{19,3},{4,20},{20... | collective-permute-start | bytes 1769480 | tf_op jit(solution)/shard_map/ppermute | solution.py:369
  800.6 98.3 %reduce-scatter.14.cloned.1.call-start = ((), (), s32[]{:S(2)}) async-start(), calls=%async_computation.24 | async-start | bytes 1966080 | tf_op jit(solution)/shard_map/reduce_scatter | solution.py:498
  801.1 159.9 %reduce-scatter.8.cloned.1.call-start = ((), (), s32[]{:S(2)}) async-start(), calls=%async_computation.21 | async-start | bytes 3932160 | tf_op jit(solution)/shard_map/reduce_scatter | solution.py:498
  865.2 95.8 %all-to-all-start.6 = ((bf16[4,48,1152]{2,1,0:T(8,128)(2,1)}), bf16[4,48,1152]{2,1,0:T(8,128)(2,1)S(1)}, u32[]{:S(2)}, u32[]{:S(2)}) async-start(bf16[4,48,1152]{2,1,0:T(8,128)(2,1)} %bitcast.75), calls=%async_computation.7 | async-start | bytes 884736 | tf_op jit(solution)/shard_map/all_to_all | solution.py:402
  (128 other events, 2328.6 us)
Sparse Core Ops, SparseCore 0:
  22.8 62.3 all-gather.6
  94.3 33.4 all-gather.10
  130.0 35.9 all-gather.16
  168.0 35.9 all-gather.14
  205.4 35.9 all-gather.12
  283.3 34.5 all-gather.8
  581.3 31.6 reduce-scatter.9
  657.8 32.5 reduce-scatter.11
  800.7 62.6 reduce-scatter.5
  865.6 33.2 reduce-scatter.13
  901.2 59.8 reduce-scatter.7

commit v4 on v3

--- a/solution.py
+++ b/solution.py
@@ -95,14 +95,24 @@
 def inverse_rms(raw):
     return lax.rsqrt(head_sums(raw * raw) * (1.0 / HEAD_DIM) + EPSILON)
 
+def dot_cut(rows, mine, other):
+    half = mine.shape[0]
+    return dot(rows[:, :half], mine[...]) + dot(rows[:, half:], other[...])
+
+
 def attend_kernel(
     kind_ref,
     len_ref,
     rows_ref,
+    core_rows_ref,
     caption_ref,
-    qkv_weight_ref,
-    key_weight_ref,
-    value_weight_ref,
+    core_caption_ref,
+    qkv_mine_ref,
+    qkv_other_ref,
+    key_mine_ref,
+    key_other_ref,
+    value_mine_ref,
+    value_other_ref,
     out_weight_ref,
     gain_ref,
     cos_ref,
@@ -116,15 +126,28 @@
     mixed_ref,
     read_ref,
     branch_ref,
+    core_branch_ref,
 ):
     item = pl.program_id(0)
+    own = item < pl.num_programs(0) // 2
     kind, length = kind_ref[item], len_ref[item]
     width = q_ref.shape[1]
     cosine, sine = cos_ref[kind], sin_ref[kind]
     scaling = HEAD_DIM ** (-0.5)
-    qkv_ref[...] = dot(rows_ref[...], qkv_weight_ref[...])
-    text_ref[...] = dot(caption_ref[...], key_weight_ref[...])
-    text_value_ref[...] = dot(caption_ref[...], value_weight_ref[...])
+
+    def project(rows, captions):
+        qkv_ref[...] = dot_cut(rows, qkv_mine_ref, qkv_other_ref)
+        text_ref[...] = dot_cut(captions, key_mine_ref, key_other_ref)
+        text_value_ref[...] = dot_cut(captions, value_mine_ref, value_other_ref)
+
+    @pl.when(own)
+    def _():
+        project(rows_ref, caption_ref)
+
+    @pl.when(jnp.logical_not(own))
+    def _():
+        project(core_rows_ref, core_caption_ref)
+
     for at in range(0, width, LANES):
         lanes = slice(at, at + LANES)
         turned = []
@@ -141,9 +164,9 @@
         tk_ref[:, lanes] = text_keys
         text_values = text_value_ref[:, lanes].astype(jnp.bfloat16)
         stacked = stack_heads(queries)
-        own = dot_right(stacked, keys) * scaling
-        own = jnp.exp(own - jnp.max(own, axis=-1, keepdims=True))
-        own_out = dot(own.astype(jnp.bfloat16), values) / jnp.sum(own, axis=-1, keepdims=True)
+        scores = dot_right(stacked, keys) * scaling
+        scores = jnp.exp(scores - jnp.max(scores, axis=-1, keepdims=True))
+        own_out = dot(scores.astype(jnp.bfloat16), values) / jnp.sum(scores, axis=-1, keepdims=True)
         text = dot_right(stacked, text_keys) * scaling
         text = jnp.where(lane_index(text.shape) < length, text, -1e30)
         text = jnp.exp(text - jnp.max(text, axis=-1, keepdims=True))
@@ -151,7 +174,14 @@
         read = join_heads(text_out)
         read_ref[:, lanes] = read
         mixed_ref[:, lanes] = (join_heads(own_out) + gain_ref[3:4, lanes] * read).astype(jnp.bfloat16)
-    branch_ref[...] = dot(mixed_ref[...], out_weight_ref[...])
+
+    @pl.when(own)
+    def _():
+        branch_ref[...] = dot(mixed_ref[...], out_weight_ref[...])
+
+    @pl.when(jnp.logical_not(own))
+    def _():
+        core_branch_ref[...] = dot(mixed_ref[...], out_weight_ref[...]).astype(jnp.bfloat16)
 
 
 def head_norm_back(grad, raw, gain_row):
@@ -165,6 +195,7 @@
     kind_ref,
     len_ref,
     branch_ref,
+    core_branch_ref,
     qkv_ref,
     text_ref,
     text_value_ref,
@@ -172,22 +203,34 @@
     k_ref,
     tk_ref,
     read_ref,
-    qkv_weight_ref,
+    qkv_mine_ref,
+    qkv_other_ref,
     out_weight_ref,
     gain_ref,
     cos_ref,
     sin_ref,
     gqkv_ref,
     gtext_ref,
+    gtext_value_ref,
     grad_rows_ref,
+    core_grad_rows_ref,
     gains_ref,
+    mixed_ref,
 ):
     item = pl.program_id(0)
+    own = item < pl.num_programs(0) // 2
     kind, length = kind_ref[item], len_ref[item]
     width = q_ref.shape[1]
     cosine, sine = cos_ref[kind], sin_ref[kind]
     scaling = HEAD_DIM ** (-0.5)
-    grad_mixed = dot_right(branch_ref[...], out_weight_ref[...])
+
+    @pl.when(own)
+    def _():
+        mixed_ref[...] = dot_right(branch_ref[...], out_weight_ref[...])
+
+    @pl.when(jnp.logical_not(own))
+    def _():
+        mixed_ref[...] = dot_right(core_branch_ref[...], out_weight_ref[...])
 
     @pl.when(item == 0)
     def _():
@@ -209,7 +252,7 @@
 
     for at in range(0, width, LANES):
         lanes = slice(at, at + LANES)
-        grad = grad_mixed[:, lanes]
+        grad = mixed_ref[:, lanes]
         cross = gain_ref[3:4, lanes]
         values = qkv_ref[:, 2 * width + at : 2 * width + at + LANES].astype(jnp.bfloat16)
         text_values = text_value_ref[:, lanes].astype(jnp.bfloat16)
@@ -232,105 +275,210 @@
         grad_text, gain = head_norm_back(read_keys, text_ref[:, lanes], gain_ref[2:3, lanes])
         gtext_ref[:, lanes] = grad_text.astype(jnp.bfloat16)
         gains_ref[2:3, lanes] += gain
-        gtext_ref[:, width + at : width + at + LANES] = read_values.astype(jnp.bfloat16)
+        gtext_value_ref[:, lanes] = read_values.astype(jnp.bfloat16)
         gains_ref[3:4, lanes] += jnp.sum(grad * read_ref[:, lanes], axis=0, keepdims=True)
-    grad_rows_ref[...] = dot_right(gqkv_ref[...], qkv_weight_ref[...])
-
-def item_call(kernel, scalars, by_item, whole, outs, summed, name):
+
+    half = qkv_mine_ref.shape[0]
+
+    @pl.when(own)
+    def _():
+        grad_rows_ref[:, :half] = dot_right(gqkv_ref[...], qkv_mine_ref[...])
+        grad_rows_ref[:, half:] = dot_right(gqkv_ref[...], qkv_other_ref[...])
+
+    @pl.when(jnp.logical_not(own))
+    def _():
+        rows = gqkv_ref[...]
+        core_grad_rows_ref[:, :half] = dot_right(rows, qkv_mine_ref[...]).astype(jnp.bfloat16)
+        core_grad_rows_ref[:, half:] = dot_right(rows, qkv_other_ref[...]).astype(jnp.bfloat16)
+
+def whole_spec(array):
+    zeros = (0,) * len(array.shape)
+    return pl.BlockSpec(array.shape, lambda *_: zeros, pipeline_mode=pl.Buffered(1))
+
+
+def mine_spec(array, steps):
+    half = steps // 2
+    return pl.BlockSpec(
+        (array.shape[0] // half, array.shape[1]), lambda i, *_: (jnp.minimum(i, half - 1), 0)
+    )
+
+
+def core_spec(array, steps):
+    half = steps // 2
+    return pl.BlockSpec(
+        (array.shape[0] // half, array.shape[1]), lambda i, *_: (jnp.maximum(i - half, 0), 0)
+    )
+
+
+def pair_specs(pair_of_arrays, steps):
+    return [mine_spec(pair_of_arrays[0], steps), core_spec(pair_of_arrays[1], steps)]
+
+
+def step_spec(array, steps):
+    return pl.BlockSpec((array.shape[0] // steps, array.shape[1]), lambda i, *_: (i, 0))
+
+
+def summed_spec(array):
+    return pl.BlockSpec(array.shape, lambda i, *_: (0, 0))
+
+
+def shaped(count, columns, dtype=jnp.bfloat16):
+    return jax.ShapeDtypeStruct((count, columns), dtype)
+
+
+def parameters():
+    return pltpu.CompilerParams(dimension_semantics=("arbitrary",), vmem_limit_bytes=58 * MIB)
+
+
+def attend(scalars, rows, captions, qkv_rank, key_rank, value_rank, out_rank, tables):
     items = scalars[0].shape[0]
-
-    def cut(array):
-        return pl.BlockSpec((array.shape[0] // items, array.shape[1]), lambda i, *_: (i, 0))
-
-    def all_of(array):
-        zeros = (0,) * len(array.shape)
-        return pl.BlockSpec(array.shape, lambda i, *_: zeros, pipeline_mode=pl.Buffered(1))
+    count, width = 2 * rows[0].shape[0], out_rank.shape[0]
+    text_count = 2 * captions[0].shape[0]
+    outs = [
+        shaped(count, 3 * width, jnp.float32),
+        shaped(text_count, width, jnp.float32),
+        shaped(text_count, width, jnp.float32),
+        shaped(count, width),
+        shaped(count, width),
+        shaped(text_count, width),
+        shaped(count, width),
+        shaped(count, width, jnp.float32),
+    ]
+    branch = (shaped(count // 2, D, jnp.float32), shaped(count // 2, D))
+    whole = [*qkv_rank, *key_rank, *value_rank, out_rank, *tables]
+    *kept, branch_mine, branch_core = pl.pallas_call(
+        attend_kernel,
+        grid_spec=pltpu.PrefetchScalarGridSpec(
+            num_scalar_prefetch=2,
+            grid=(items,),
+            in_specs=pair_specs(rows, items)
+            + pair_specs(captions, items)
+            + [whole_spec(array) for array in whole],
+            out_specs=[step_spec(array, items) for array in outs] + pair_specs(branch, items),
+        ),
+        out_shape=[*outs, *branch],
+        compiler_params=parameters(),
+        name="attend",
+    )(*scalars, *rows, *captions, *whole)
+    return kept, (branch_mine, branch_core)
+
+
+def attend_back(scalars, grad_branch, kept, qkv_rank, out_rank, tables):
+    items = scalars[0].shape[0]
+    qkv_raw, text_raw, text_value_raw, queries, keys, text_keys, _, read = kept
+    count, width = queries.shape
+    outs = [
+        shaped(count, 3 * width),
+        shaped(text_raw.shape[0], width),
+        shaped(text_raw.shape[0], width),
+    ]
+    rows = (shaped(count // 2, D, jnp.float32), shaped(count // 2, D))
+    gains = shaped(4, width, jnp.float32)
+    by_item = [qkv_raw, text_raw, text_value_raw, queries, keys, text_keys, read]
+    whole = [*qkv_rank, out_rank, *tables]
+    qkv, text, text_value, rows_mine, rows_core, gains = pl.pallas_call(
+        attend_back_kernel,
+        grid_spec=pltpu.PrefetchScalarGridSpec(
+            num_scalar_prefetch=2,
+            grid=(items,),
+            in_specs=pair_specs(grad_branch, items)
+            + [step_spec(array, items) for array in by_item]
+            + [whole_spec(array) for array in whole],
+            out_specs=[step_spec(array, items) for array in outs]
+            + pair_specs(rows, items)
+            + [summed_spec(gains)],
+            scratch_shapes=[pltpu.VMEM((count // items, width), jnp.float32)],
+        ),
+        out_shape=[*outs, *rows, gains],
+        compiler_params=parameters(),
+        name="attend_back",
+    )(*scalars, *grad_branch, *by_item, *whole)
+    return qkv, text, text_value, (rows_mine, rows_core), gains
+
+
+def row_cuts(lefts, rights):
+    cuts, left, right, left_row, right_row = [], 0, 0, 0, 0
+    while left < len(lefts):
+        count = min(lefts[left].shape[0] - left_row, rights[right].shape[0] - right_row)
+        cuts.append((left, left_row, right, right_row, count))
+        left_row, right_row = left_row + count, right_row + count
+        if left_row == lefts[left].shape[0]:
+            left, left_row = left + 1, 0
+        if right_row == rights[right].shape[0]:
+            right, right_row = right + 1, 0
+    return cuts
+
+
+def product(lefts, rights, first, lanes, dtype):
+    columns = rights[0].shape[1]
+    if lanes % LANES:
+        block = lanes
+    else:
+        block = 384 if lanes % 384 == 0 else math.gcd(lanes, 512)
+    cuts = row_cuts(lefts, rights)
+
+    def kernel(first_ref, *refs):
+        left_refs, right_refs, out_ref = refs[: len(lefts)], refs[len(lefts) : -1], refs[-1]
+        total = None
+        for left, left_row, right, right_row, count in cuts:
+            term = dot_left(
+                left_refs[left][left_row : left_row + count, :],
+                right_refs[right][right_row : right_row + count, :],
+            )
+            total = term if total is None else total + term
+        out_ref[...] = total.astype(out_ref.dtype)
 
     return pl.pallas_call(
         kernel,
         grid_spec=pltpu.PrefetchScalarGridSpec(
-            num_scalar_prefetch=len(scalars),
-            grid=(items,),
-            in_specs=[cut(array) for array in by_item] + [all_of(array) for array in whole],
-            out_specs=[cut(array) for array in outs]
-            + [pl.BlockSpec(array.shape, lambda i, *_: (0, 0)) for array in summed],
-        ),
-        out_shape=outs + summed,
-        compiler_params=pltpu.CompilerParams(
-            dimension_semantics=("arbitrary",), vmem_limit_bytes=56 * MIB
-        ),
-        name=name,
-    )(*scalars, *by_item, *whole)
-
-
-def attend(scalars, rows, captions, qkv_rank, key_rank, value_rank, out_rank, tables):
-    count, width = rows.shape[0], key_rank.shape[1]
-    text_count = captions.shape[0]
-
-    def shape(count, columns, dtype=jnp.bfloat16):
-        return jax.ShapeDtypeStruct((count, columns), dtype)
-
-    outs = [
-        shape(count, 3 * width, jnp.float32),
-        shape(text_count, width, jnp.float32),
-        shape(text_count, width, jnp.float32),
-        shape(count, width),
-        shape(count, width),
-        shape(text_count, width),
-        shape(count, width),
-        shape(count, width, jnp.float32),
-        shape(count, D, jnp.float32),
-    ]
-    whole = [qkv_rank, key_rank, value_rank, out_rank, *tables]
-    *kept, branch = item_call(attend_kernel, scalars, [rows, captions], whole, outs, [], "attend")
-    return kept, branch
-
-
-def attend_back(scalars, grad_branch, kept, qkv_rank, out_rank, tables):
-    qkv_raw, text_raw, text_value_raw, queries, keys, text_keys, _, read = kept
-    count, width = queries.shape
-    outs = [
-        jax.ShapeDtypeStruct((count, 3 * width), jnp.bfloat16),
-        jax.ShapeDtypeStruct((text_raw.shape[0], 2 * width), jnp.bfloat16),
-        jax.ShapeDtypeStruct((count, D), jnp.float32),
-    ]
-    by_item = [grad_branch, qkv_raw, text_raw, text_value_raw, queries, keys, text_keys, read]
-    summed = [jax.ShapeDtypeStruct((4, width), jnp.float32)]
-    whole = [qkv_rank, out_rank, *tables]
-    return item_call(attend_back_kernel, scalars, by_item, whole, outs, summed, "attend_back")
-
-
-def product_kernel(first_ref, left_near, left_far, right_near, right_far, out_ref):
-    near = dot_left(left_near[...], right_near[...])
-    out_ref[...] = (near + dot_left(left_far[...], right_far[...])).astype(out_ref.dtype)
-
-
-def product(left_sides, right_sides, first, lanes, dtype):
-    count, columns = right_sides[0].shape
-    block = math.gcd(lanes, 384) if lanes % 384 == 0 else math.gcd(lanes, 512)
-    cut = pl.BlockSpec((count, block), lambda i, first: (0, first[0] // block + i))
-    whole = pl.BlockSpec((count, columns), lambda i, first: (0, 0), pipeline_mode=pl.Buffered(1))
-    return pl.pallas_call(
-        product_kernel,
-        grid_spec=pltpu.PrefetchScalarGridSpec(
             num_scalar_prefetch=1,
             grid=(lanes // block,),
-            in_specs=[cut, cut, whole, whole],
+            in_specs=[
+                pl.BlockSpec((array.shape[0], block), lambda i, first: (0, first[0] // block + i))
+                for array in lefts
+            ]
+            + [whole_spec(array) for array in rights],
             out_specs=pl.BlockSpec((block, columns), lambda i, first: (i, 0)),
         ),
-        out_shape=jax.ShapeDtypeStruct((lanes, columns), dtype),
-        compiler_params=pltpu.CompilerParams(
-            dimension_semantics=("arbitrary",), vmem_limit_bytes=48 * MIB
-        ),
+        out_shape=shaped(lanes, columns, dtype),
+        compiler_params=parameters(),
         name="product",
-    )(jnp.reshape(first, (1,)).astype(jnp.int32), *left_sides, *right_sides)
-
-
-def feed_kernel(input_ref, result_ref, gate_ref, up_ref, down_ref, hidden_ref, grad_gate_ref, grad_up_ref, grad_ref):
-    rows = input_ref[...]
-    gate = dot(rows, gate_ref[...])
-    up = dot(rows, up_ref[...])
-    grad_hidden = dot_right(result_ref[...], down_ref[...])
+    )(jnp.reshape(first, (1,)).astype(jnp.int32), *lefts, *rights)
+
+
+def feed_kernel(
+    rows_ref,
+    core_rows_ref,
+    result_ref,
+    core_result_ref,
+    gate_mine_ref,
+    gate_other_ref,
+    up_mine_ref,
+    up_other_ref,
+    down_ref,
+    hidden_ref,
+    grad_gate_ref,
+    grad_up_ref,
+    grad_ref,
+    core_grad_ref,
+    rows,
+    result,
+):
+    own = pl.program_id(0) < pl.num_programs(0) // 2
+
+    @pl.when(own)
+    def _():
+        rows[...] = rows_ref[...]
+        result[...] = result_ref[...]
+
+    @pl.when(jnp.logical_not(own))
+    def _():
+        rows[...] = core_rows_ref[...]
+        result[...] = core_result_ref[...]
+
+    gate = dot_cut(rows, gate_mine_ref, gate_other_ref)
+    up = dot_cut(rows, up_mine_ref, up_other_ref)
+    grad_hidden = dot_right(result[...], down_ref[...])
     sigmoid = 1.0 / (1.0 + jnp.exp(-gate))
     silu = gate * sigmoid
     hidden_ref[...] = (silu * up).astype(jnp.bfloat16)
@@ -338,31 +486,41 @@
     grad_up = (grad_hidden * silu).astype(jnp.bfloat16)
     grad_gate_ref[...] = grad_gate
     grad_up_ref[...] = grad_up
-    grad_ref[...] = dot_right(grad_gate, gate_ref[...]) + dot_right(grad_up, up_ref[...])
+    half = gate_mine_ref.shape[0]
+    low = dot_right(grad_gate, gate_mine_ref[...]) + dot_right(grad_up, up_mine_ref[...])
+    high = dot_right(grad_gate, gate_other_ref[...]) + dot_right(grad_up, up_other_ref[...])
+
+    @pl.when(own)
+    def _():
+        grad_ref[:, :half] = low
+        grad_ref[:, half:] = high
+
+    @pl.when(jnp.logical_not(own))
+    def _():
+        core_grad_ref[:, :half] = low.astype(jnp.bfloat16)
+        core_grad_ref[:, half:] = high.astype(jnp.bfloat16)
 
 
 def feed(rows, grad_result, gate_rank, up_rank, down_rank):
-    count, width = rows.shape[0], gate_rank.shape[1]
+    count, width = 2 * rows[0].shape[0], down_rank.shape[0]
     block = 256
-
-    def cut(columns):
-        return pl.BlockSpec((block, columns), lambda i: (i, 0))
-
-    def whole(array):
-        return pl.BlockSpec(array.shape, lambda i: (0, 0), pipeline_mode=pl.Buffered(1))
-
-    hidden = jax.ShapeDtypeStruct((count, width), jnp.bfloat16)
-    return pl.pallas_call(
+    steps = count // block
+    outs = [shaped(count, width)] * 3
+    grads = (shaped(count // 2, D, jnp.float32), shaped(count // 2, D))
+    whole = [*gate_rank, *up_rank, down_rank]
+    hidden, grad_gate, grad_up, grad_mine, grad_core = pl.pallas_call(
         feed_kernel,
-        grid=(count // block,),
-        in_specs=[cut(D), cut(D), whole(gate_rank), whole(up_rank), whole(down_rank)],
-        out_specs=[cut(width), cut(width), cut(width), cut(D)],
-        out_shape=[hidden, hidden, hidden, jax.ShapeDtypeStruct((count, D), jnp.float32)],
-        compiler_params=pltpu.CompilerParams(
-            dimension_semantics=("arbitrary",), vmem_limit_bytes=56 * MIB
-        ),
+        grid=(steps,),
+        in_specs=pair_specs(rows, steps)
+        + pair_specs(grad_result, steps)
+        + [whole_spec(array) for array in whole],
+        out_specs=[step_spec(array, steps) for array in outs] + pair_specs(grads, steps),
+        out_shape=[*outs, *grads],
+        scratch_shapes=[pltpu.VMEM((block, D), jnp.bfloat16)] * 2,
+        compiler_params=parameters(),
         name="feed",
-    )(rows, grad_result, gate_rank, up_rank, down_rank)
+    )(*rows, *grad_result, *whole)
+    return hidden, grad_gate, grad_up, (grad_mine, grad_core)
 
 
 def swap(block, axis, count=2, step=1):
@@ -407,21 +565,16 @@
 
 
 def pair(rows):
-    return jnp.concatenate([rows, swap(rows, "core")])
-
-
-def settle_far(far):
-    half = far.shape[0] // 2
-    return far[:half] + swap(far[half:].astype(jnp.bfloat16), "core").astype(jnp.float32)
-
-
-def settle_near(near):
-    half = near.shape[0] // 2
-    return near[:half] + swap(near[half:].astype(jnp.bfloat16), "core").astype(jnp.float32)
+    return (rows, swap(rows, "core"))
+
+
+def settle(partial):
+    mine, core = partial
+    return mine + swap(core, "core").astype(jnp.float32)
 
 
 def settle_move(across):
-    return swap(across.astype(jnp.bfloat16), "mid").astype(jnp.float32)
+    return swap(across, "mid").astype(jnp.float32)
 
 
 class Layout:
@@ -453,36 +606,40 @@
 
     def across_hi(self, block):
         if self.hi == 2:
-            return jnp.stack([block, swap(block, "hi")])
+            return (block, swap(block, "hi"))
         return spread(block, "hi", self.hi)
 
-    def natural_hi(self, stacked):
+    def natural_hi(self, blocks):
         if self.hi != 2:
-            return stacked
-        mine, other = stacked[0], stacked[1]
+            return blocks
+        mine, other = blocks
         low = lax.axis_index("hi") == 0
         return jnp.stack([jnp.where(low, mine, other), jnp.where(low, other, mine)])
 
+    def halves(self, blocks):
+        if self.hi == 2:
+            return tuple(self.natural_rows(block[None]) for block in blocks)
+        return tuple(jnp.split(self.natural_rows(blocks), 2))
+
     def natural_rows(self, stacked):
-        view = stacked.reshape(self.hi, self.rep, RANKS, -1, stacked.shape[-1])
+        view = stacked.reshape(stacked.shape[0], self.rep, RANKS, -1, stacked.shape[-1])
         return jnp.transpose(view, (0, 2, 1, 3, 4)).reshape(-1, stacked.shape[-1])
 
-    def product_moved(self, left_sides, right_sides, first=None):
-        lanes = left_sides[0].shape[1]
+    def product_moved(self, lefts, rights, first=None):
+        lanes = lefts[0].shape[1]
         if self.hi != 2:
-            return product(left_sides, right_sides, 0, lanes, jnp.bfloat16)
-        first = lanes // 2 if first is None else first
-        return product(left_sides, right_sides, first, lanes // 2, jnp.bfloat16)
+            return product(lefts, rights, 0, lanes, jnp.bfloat16)
+        return product(lefts, rights, lanes // 2 if first is None else first, lanes // 2, jnp.bfloat16)
 
     def move(self, moved):
         if self.hi == 2:
             return swap(moved, "hi")
         return fold(moved.reshape(self.hi, -1, moved.shape[1]), "hi", self.hi)
 
-    def product_kept(self, left_sides, right_sides, first=0):
+    def product_kept(self, lefts, rights, first=0):
         if self.hi != 2:
             return None
-        return product(left_sides, right_sides, first, left_sides[0].shape[1] // 2, jnp.float32)
+        return product(lefts, rights, first, lefts[0].shape[1] // 2, jnp.float32)
 
     def total(self, kept, arrived):
         if kept is None:
@@ -591,102 +748,107 @@
     tables = (head_gains, cosine, sine)
     scalars = list(zip(kinds_sides, lengths_sides, strict=True))
 
-    text_weight, conditions = fence(text_weight, activated_mine)
+    captions = plan.ordered(caption.reshape(-1, TEXT_DIM))
+    text_weight, conditions, captions = fence(text_weight, activated_mine, captions)
     text_mine = trade_ranks(plan.by_rank(text_weight, 2, plan.head_groups))
+    captions_near = pair(captions)
     partial = dot(conditions, ada_weight).astype(bf16).reshape(devices, item_count, 4 * D)
-    text_mine, partial = fence(text_mine, partial)
+    text_mine, partial, captions_near = fence(text_mine, partial, captions_near)
+    text_key_mine, text_value_mine = text_mine[..., :rank_width], text_mine[..., rank_width:]
     modulation = jnp.sum(lax.all_to_all(partial, AXES, 0, 0, tiled=True).astype(f32), axis=0)
-    qkv_z, modulation, text_mine = fence(qkv_z, modulation, text_mine)
+    qkv_z, modulation, text_key_mine, text_value_mine = fence(
+        qkv_z, modulation, text_key_mine, text_value_mine
+    )
 
     scale_attn, gate_attn, scale_mlp, gate_mlp = jnp.split(modulation, 4, axis=1)
-    captions = plan.ordered(caption.reshape(-1, TEXT_DIM))
-    text_key_z = z_gather(text_mine[..., :rank_width])
+    text_key_z = z_gather(text_key_mine)
     captions_far = swap(captions, "mid")
     qkv_rank = plan.across_hi(qkv_z)
     gate_up_mine = trade_ranks(plan.by_rank(gate_up_weight, 2, hi_count))
+    gate_mine, up_mine = gate_up_mine[..., :feed_width], gate_up_mine[..., feed_width:]
     token_rows = tokens.astype(f32).reshape(item_count, item_len, D)
     normed = modulate(token_rows, gain_rows[0], scale_attn)
     normed = plan.ordered(normed.astype(bf16).reshape(row_count, D))
     mlp_gate = jnp.tanh(gate_mlp)[:, None, :]
     grad_top = out_cotangent.astype(f32).reshape(item_count, item_len, D)
     grad_result = (mlp_gate * grad_top).astype(bf16).reshape(row_count, D)
-    text_key_z, captions_far, qkv_rank, gate_up_mine, normed, grad_result = fence(
-        text_key_z, captions_far, qkv_rank, gate_up_mine, normed, grad_result
-    )
-
-    text_value_z = z_gather(text_mine[..., rank_width:])
+    normed_near, result_near = pair(normed), pair(grad_result)
+    text_key_z, captions_far, qkv_rank, gate_mine, up_mine, normed_near, result_near = fence(
+        text_key_z, captions_far, qkv_rank, gate_mine, up_mine, normed_near, result_near
+    )
+
+    text_value_z = z_gather(text_value_mine)
     text_key_rank = plan.across_hi(text_key_z)
-    normed_far = swap(normed, "mid")
-    caption_sides = (pair(captions), pair(captions_far))
-    normed_near = pair(normed)
+    normed_far = swap(normed_near[0], "mid")
+    captions_far = pair(captions_far)
+    text_value_z, text_key_rank, normed_far, captions_far = fence(
+        text_value_z, text_key_rank, normed_far, captions_far
+    )
+
+    gate_z = z_gather(gate_mine)
+    text_value_rank = plan.across_hi(text_value_z)
+    result_far = swap(result_near[0], "mid")
+    normed_far = pair(normed_far)
     if plan.aligned:
-        blocks = qkv_rank.reshape(hi_count, rep_count, -1, 3 * rank_width)
-        out_rank = plan.natural_hi(blocks[:, :, RANKS * rows :]).reshape(rank_width, D)
-        qkv_rank = blocks[:, :, : RANKS * rows]
-    qkv_rank = plan.natural_rows(qkv_rank)
-    text_value_z, text_key_rank, normed_far, caption_sides, normed_near, qkv_rank, out_rank = fence(
-        text_value_z, text_key_rank, normed_far, caption_sides, normed_near, qkv_rank, out_rank
-    )
-
-    gate_z = z_gather(gate_up_mine[..., :feed_width])
-    text_value_rank = plan.across_hi(text_value_z)
-    result_far = swap(grad_result, "mid")
-    normed_sides = (normed_near, pair(normed_far))
-    text_key_rank = plan.natural_rows(text_key_rank)
-    gate_z, text_value_rank, result_far, normed_sides, text_key_rank = fence(
-        gate_z, text_value_rank, result_far, normed_sides, text_key_rank
-    )
-
-    up_z = z_gather(gate_up_mine[..., feed_width:])
+        blocks = [block.reshape(rep_count, -1, 3 * rank_width) for block in qkv_rank]
+        out_rank = plan.natural_hi([block[:, RANKS * rows :].reshape(-1, D) for block in blocks])
+        out_rank = out_rank.reshape(rank_width, D)
+        qkv_rank = [block[:, : RANKS * rows].reshape(-1, 3 * rank_width) for block in blocks]
+        qkv_rank = qkv_rank if hi_count == 2 else jnp.stack(qkv_rank)
+    qkv_rank, text_key_rank = plan.halves(qkv_rank), plan.halves(text_key_rank)
+    gate_z, text_value_rank, result_far, normed_far, qkv_rank, out_rank, text_key_rank = fence(
+        gate_z, text_value_rank, result_far, normed_far, qkv_rank, out_rank, text_key_rank
+    )
+
+    up_z = z_gather(up_mine)
     gate_rank = plan.across_hi(gate_z)
-    text_value_rank = plan.natural_rows(text_value_rank)
-    attend_weights = (qkv_rank, text_key_rank, text_value_rank, out_rank, tables)
-    kept_far, branch_far = attend(scalars[1], normed_sides[1], caption_sides[1], *attend_weights)
-    up_z, gate_rank, kept_far, branch_far, attend_weights = fence(
-        up_z, gate_rank, kept_far, branch_far, attend_weights
-    )
-
-    across = settle_far(branch_far)
-    across, normed_near, up_z = fence(across, normed_sides[0], up_z)
-    normed_sides = (normed_near, normed_sides[1])
+    attend_weights = (qkv_rank, text_key_rank, plan.halves(text_value_rank), out_rank, tables)
+    kept_far, partial_far = attend(scalars[1], normed_far, captions_far, *attend_weights)
+    up_z, gate_rank, kept_far, partial_far, attend_weights = fence(
+        up_z, gate_rank, kept_far, partial_far, attend_weights
+    )
+
+    across = settle(partial_far).astype(bf16)
+    across, normed_near, up_z = fence(across, normed_near, up_z)
     down_z = z_gather(down_weight)
     up_rank = plan.across_hi(up_z)
     arrived = settle_move(across)
-    kept_near, branch_near = attend(scalars[0], normed_near, caption_sides[0], *attend_weights)
-    result_sides = (pair(grad_result), pair(result_far))
-    gate_rank = plan.natural_rows(gate_rank)
-    down_z, up_rank, arrived, kept_near, branch_near, result_sides, gate_rank = fence(
-        down_z, up_rank, arrived, kept_near, branch_near, result_sides, gate_rank
+    kept_near, partial_near = attend(scalars[0], normed_near, captions_near, *attend_weights)
+    result_far = pair(result_far)
+    down_z, up_rank, arrived, kept_near, partial_near, result_far = fence(
+        down_z, up_rank, arrived, kept_near, partial_near, result_far
     )
 
     down_rank = plan.across_hi(down_z)
-    branch = (settle_near(branch_near) + arrived).reshape(item_count, item_len, D)
+    branch = (settle(partial_near) + arrived).reshape(item_count, item_len, D)
     attn_gate = jnp.tanh(gate_attn)[:, None, :]
     middle = token_rows + attn_gate * branch
     mlp_input = modulate(middle, gain_rows[4], scale_mlp)
     mlp_input = plan.ordered(mlp_input.astype(bf16).reshape(row_count, D))
-    up_rank = plan.natural_rows(up_rank)
     input_far = swap(mlp_input, "mid")
     input_near = pair(mlp_input)
-    down_rank, input_far, input_near, up_rank = fence(down_rank, input_far, input_near, up_rank)
+    gate_rank, up_rank = plan.halves(gate_rank), plan.halves(up_rank)
+    down_rank, input_far, input_near, gate_rank, up_rank = fence(
+        down_rank, input_far, input_near, gate_rank, up_rank
+    )
 
     down_rank = plan.natural_hi(down_rank).reshape(feed_width, D)
     feed_weights = (gate_rank, up_rank, down_rank)
-    input_sides = (input_near, pair(input_far))
-    hidden_far, gate_far, up_far, partial_far = feed(input_sides[1], result_sides[1], *feed_weights)
-    across = settle_far(partial_far)
+    input_far = pair(input_far)
+    hidden_far, gate_far, up_far, partial_far = feed(input_far, result_far, *feed_weights)
+    across = settle(partial_far).astype(bf16)
     across, input_near = fence(across, input_near)
     arrived = settle_move(across)
-    hidden_near, gate_near, up_near, partial_near = feed(input_near, result_sides[0], *feed_weights)
-    input_sides = (input_near, input_sides[1])
-    gate_sides, up_sides, hidden_sides = (gate_near, gate_far), (up_near, up_far), (hidden_near, hidden_far)
-    gate_moved = plan.product_moved(input_sides, gate_sides)
-    arrived, gate_sides, up_sides, hidden_sides, partial_near, gate_moved = fence(
-        arrived, gate_sides, up_sides, hidden_sides, partial_near, gate_moved
+    hidden_near, gate_near, up_near, partial_near = feed(input_near, result_near, *feed_weights)
+    inputs, results = (*input_near, *input_far), (*result_near, *result_far)
+    gate_rows, up_rows, hidden_rows = (gate_near, gate_far), (up_near, up_far), (hidden_near, hidden_far)
+    gate_moved = plan.product_moved(inputs, gate_rows)
+    arrived, gate_rows, up_rows, hidden_rows, partial_near, gate_moved = fence(
+        arrived, gate_rows, up_rows, hidden_rows, partial_near, gate_moved
     )
 
     gate_moved = plan.move(gate_moved)
-    grad_mlp_input = plan.ordered(settle_near(partial_near) + arrived)
+    grad_mlp_input = plan.ordered(settle(partial_near) + arrived)
     _, pull_mlp_norm = jax.vjp(modulate, middle, gain_rows[4], scale_mlp)
     grad_middle_norm, grad_mlp_gain, grad_scale_mlp = pull_mlp_norm(
         grad_mlp_input.reshape(item_count, item_len, D)
@@ -695,80 +857,94 @@
     grad_attn_gate = jnp.sum(grad_middle * branch, axis=1) * (1.0 - jnp.tanh(gate_attn) ** 2)
     grad_branch = (attn_gate * grad_middle).astype(bf16).reshape(row_count, D)
     branch_near = pair(grad_branch)
-    up_moved = plan.product_moved(input_sides, up_sides)
-    gate_kept = plan.product_kept(input_sides, gate_sides)
-    gate_moved, up_moved, gate_kept, grad_branch, branch_near = fence(
-        gate_moved, up_moved, gate_kept, grad_branch, branch_near
+    up_moved = plan.product_moved(inputs, up_rows)
+    gate_kept = plan.product_kept(inputs, gate_rows)
+    hidden_first = hi_at * (feed_width // 2)
+    down_moved = plan.product_moved(hidden_rows, results, feed_width // 2 - hidden_first)
+    gate_moved, up_moved, gate_kept, branch_near, down_moved = fence(
+        gate_moved, up_moved, gate_kept, branch_near, down_moved
     )
 
     gate_grad = plan.by_rep(plan.total(gate_kept, gate_moved))
-    gate_grad, up_moved, grad_branch, branch_near = fence(
-        gate_grad, up_moved, grad_branch, branch_near
-    )
+    gate_grad, up_moved, branch_near = fence(gate_grad, up_moved, branch_near)
     gate_parts = plan.reduce(gate_grad)
-    branch_far = swap(grad_branch, "mid")
+    branch_far = swap(branch_near[0], "mid")
     up_moved = plan.move(up_moved)
     back_weights = (qkv_rank, out_rank, tables)
-    qkv_near, text_near, rows_near, gain_near = attend_back(
+    qkv_near, key_near, value_near, rows_near, gain_near = attend_back(
         scalars[0], branch_near, kept_near, *back_weights
     )
-    up_kept = plan.product_kept(input_sides, up_sides)
-    hidden_first = hi_at * (feed_width // 2)
-    down_moved = plan.product_moved(hidden_sides, result_sides, feed_width // 2 - hidden_first)
-    branch_far, up_moved, qkv_near, text_near, rows_near, gain_near, up_kept, down_moved = fence(
-        branch_far, up_moved, qkv_near, text_near, rows_near, gain_near, up_kept, down_moved
-    )
-
-    branch_sides = (branch_near, pair(branch_far))
+    up_kept = plan.product_kept(inputs, up_rows)
+    gate_parts, branch_far, up_moved, qkv_near, key_near, value_near, rows_near, gain_near, up_kept = fence(
+        gate_parts, branch_far, up_moved, qkv_near, key_near, value_near, rows_near, gain_near, up_kept
+    )
+
+    branch_far = pair(branch_far)
     up_grad = plan.by_rep(plan.total(up_kept, up_moved))
-    up_grad, branch_far, down_moved = fence(up_grad, branch_sides[1], down_moved)
+    up_grad, branch_far, down_moved = fence(up_grad, branch_far, down_moved)
     up_parts = plan.reduce(up_grad)
     down_moved = plan.move(down_moved)
-    qkv_far, text_far, rows_far, gain_far = attend_back(
+    qkv_far, key_far, value_far, rows_far, gain_far = attend_back(
         scalars[1], branch_far, kept_far, *back_weights
     )
-    text_sides, qkv_sides = (text_near, text_far), (qkv_near, qkv_far)
-    text_moved = plan.product_moved(caption_sides, text_sides)
-    down_moved, text_moved, text_sides, qkv_sides, rows_far, gain_far = fence(
-        down_moved, text_moved, text_sides, qkv_sides, rows_far, gain_far
-    )
-
-    text_moved = plan.move(text_moved)
-    down_kept = plan.product_kept(hidden_sides, result_sides, hidden_first)
+    qkv_rows, key_rows, value_rows = (qkv_near, qkv_far), (key_near, key_far), (value_near, value_far)
+    all_captions, all_normed = (*captions_near, *captions_far), (*normed_near, *normed_far)
+    key_moved = plan.product_moved(all_captions, key_rows)
+    down_kept = plan.product_kept(hidden_rows, results, hidden_first)
+    up_parts, down_moved, key_moved, down_kept, qkv_rows, value_rows, rows_far, gain_far = fence(
+        up_parts, down_moved, key_moved, down_kept, qkv_rows, value_rows, rows_far, gain_far
+    )
+
+    across = settle(rows_far).astype(bf16)
     down_grad = plan.total(down_kept, down_moved).reshape(rep_count, -1, D)
-    across = settle_far(rows_far)
-    across, down_grad, text_sides, qkv_sides = fence(across, down_grad, text_sides, qkv_sides)
-    down_weight_grad = plan.reduce(down_grad).astype(f32)
+    across, down_grad, key_moved, qkv_rows, value_rows = fence(
+        across, down_grad, key_moved, qkv_rows, value_rows
+    )
+    down_parts = plan.reduce(down_grad)
     arrived = settle_move(across)
-    qkv_moved = plan.product_moved(normed_sides, qkv_sides)
-    text_kept = plan.product_kept(caption_sides, text_sides)
-    qkv_kept = plan.product_kept(normed_sides, qkv_sides)
-    grad_normed = settle_near(rows_near)
-    arrived, text_moved, text_kept, qkv_moved, qkv_kept, grad_normed = fence(
-        arrived, text_moved, text_kept, qkv_moved, qkv_kept, grad_normed
-    )
-
-    text_grad = plan.by_rep(plan.total(text_kept, text_moved))
-    text_grad, qkv_moved, arrived = fence(text_grad, qkv_moved, arrived)
-    text_parts = plan.reduce(text_grad)
-    qkv_moved = plan.move(qkv_moved)
-    mixed_sides = [plan.ordered(kept[6]) for kept in (kept_near, kept_far)]
+    key_moved = plan.move(key_moved)
+    value_moved = plan.product_moved(all_captions, value_rows)
+    key_kept = plan.product_kept(all_captions, key_rows)
+    qkv_moved = plan.product_moved(all_normed, qkv_rows)
+    value_kept = plan.product_kept(all_captions, value_rows)
+    down_parts, arrived, key_moved, value_moved, key_kept, qkv_moved, value_kept, rows_near = fence(
+        down_parts, arrived, key_moved, value_moved, key_kept, qkv_moved, value_kept, rows_near
+    )
+
+    key_grad = plan.by_rep(plan.total(key_kept, key_moved))
+    key_grad, value_moved, qkv_moved, hidden_rows = fence(key_grad, value_moved, qkv_moved, hidden_rows)
+    key_parts = plan.reduce(key_grad)
+    value_moved = plan.move(value_moved)
+    qkv_kept = plan.product_kept(all_normed, qkv_rows)
+    mixed_rows = [plan.ordered(kept[6]) for kept in (kept_near, kept_far)]
+    branches = (*branch_near, *branch_far)
     if plan.aligned:
         out_halves = [
-            dot_left(mixed_sides[0][:, lanes], branch_sides[0])
-            + dot_left(mixed_sides[1][:, lanes], branch_sides[1])
+            product([rows[:, lanes] for rows in mixed_rows], branches, 0, rank_width // 2, bf16)
             for lanes in (slice(0, rank_width // 2), slice(rank_width // 2, None))
         ]
+    result_far = [dot(rows, down_rank) for rows in jnp.split(hidden_rows[1], 2)]
+    across = settle((result_far[0], result_far[1].astype(bf16))).astype(bf16)
+    grad_normed = plan.ordered(settle(rows_near) + arrived)
+    key_parts, value_moved, qkv_kept, across, grad_normed = fence(
+        key_parts, value_moved, qkv_kept, across, grad_normed
+    )
+
+    value_grad = plan.by_rep(plan.total(value_kept, value_moved))
+    value_grad, qkv_moved, across = fence(value_grad, qkv_moved, across)
+    value_parts = plan.reduce(value_grad)
+    qkv_moved = plan.move(qkv_moved)
+    result = settle_move(across)
+    if plan.aligned:
         if hi_count == 2:
-            out_kept, out_moved = out_halves[0], swap(out_halves[1].astype(bf16), "hi")
+            out_kept, out_moved = out_halves[0].astype(f32), swap(out_halves[1], "hi")
         else:
-            out_kept, out_moved = None, plan.move(jnp.concatenate(out_halves).astype(bf16))
-    partial_result = [dot(side, down_rank) for side in hidden_sides]
-    result = settle_near(partial_result[0]) + settle_move(settle_far(partial_result[1]))
+            out_kept, out_moved = None, plan.move(jnp.concatenate(out_halves))
+    result_near = [dot(rows, down_rank) for rows in jnp.split(hidden_rows[0], 2)]
+    result = result + settle((result_near[0], result_near[1].astype(bf16)))
     result = result.reshape(item_count, item_len, D)
     layer_out = (middle + mlp_gate * result).astype(bf16).reshape(row_count, D)
     grad_mlp_gate = jnp.sum(grad_top * result, axis=1) * (1.0 - jnp.tanh(gate_mlp) ** 2)
-    grad_normed = plan.ordered(grad_normed + arrived)
     _, pull_attn_norm = jax.vjp(modulate, token_rows, gain_rows[0], scale_attn)
     grad_token_norm, grad_attn_gain, grad_scale_attn = pull_attn_norm(
         grad_normed.reshape(item_count, item_len, D)
@@ -780,11 +956,11 @@
         qkv_grad = jnp.concatenate([qkv_grad, out_grad], axis=1)
     else:
         at = (jnp.arange(RANKS) == plan.rank).astype(bf16)[:, None, None]
-        out_grad = dot_left(mixed_sides[0], branch_sides[0]) + dot_left(mixed_sides[1], branch_sides[1])
-        placed = (out_grad.astype(bf16)[None] * at).reshape(D, D)
+        out_grad = product(mixed_rows, branches, 0, rank_width, bf16)
+        placed = (out_grad[None] * at).reshape(D, D)
         out_weight_grad = lax.psum_scatter(placed, AXES, scatter_dimension=0, tiled=True).astype(f32)
-    qkv_grad, grad_mlp_gate, grad_scale_attn, grad_attn_gain = fence(
-        qkv_grad, grad_mlp_gate, grad_scale_attn, grad_attn_gain
+    value_parts, qkv_grad, grad_mlp_gate, grad_scale_attn, grad_attn_gain = fence(
+        value_parts, qkv_grad, grad_mlp_gate, grad_scale_attn, grad_attn_gain
     )
     qkv_parts = plan.reduce(qkv_grad)
     if plan.aligned:
@@ -815,8 +991,11 @@
     gate_up_weight_grad = whole(
         jnp.concatenate([gate_parts, up_parts], axis=-1), gate_up_weight, 2, hi_count
     )
-    text_weight_grad = whole(text_parts, text_weight, 2, plan.head_groups)
+    text_weight_grad = whole(
+        jnp.concatenate([key_parts, value_parts], axis=-1), text_weight, 2, plan.head_groups
+    )
     qkv_weight_grad = whole(qkv_parts, qkv_weight, 3, plan.head_groups)
+    down_weight_grad = down_parts.astype(f32)
     return (
         layer_out,
         tokens_grad,

time: 1000 us -> 871 us (0.87)
  waiting for transfers between devices: 379 us -> 258 us
  Pallas kernels: 221 us -> 280 us
  other arithmetic: 139 us -> 85.5 us
  local copies, waits for them, and re-layouts: 116 us -> 98.2 us
    reduce_scatter x5 -> x6, waiting for transfers between devices: 112 us -> 0.04 us  [reduce(): return lax.psum_scatter(flat, 'rep', scatter_dimension=0, tiled=True)]
    ppermute x39 -> x40, waiting for transfers between devices: 239 us -> 143 us  [swap(): return lax.ppermute(block, axis, [(at, at ^ step) for at in range(count)])]
    pallas_call x16 -> x20, Pallas kernels: 221 us -> 280 us  [the longest x14 101 us: product(): pl.pallas_call(kernel, grid_spec=pltpu.PrefetchScalarGridSpec(num_scalar_...]
    all_to_all x0 -> x2, waiting for transfers between devices: none -> 42.6 us  [the longest x1 39.8 us: local(): lax.all_to_all(partial, AXES, 0, 0, tiled=True).astype(f32)]
    all_to_all x1, waiting for transfers between devices: 0.01 us -> 32 us  [local(): lax.all_to_all(jnp.concatenate([modulations, gain_blocks], axis=1), AXES,...]
    concatenate x8 -> x1, other arithmetic: 29.9 us -> 0.94 us  [local(): jnp.concatenate([key_parts, value_parts], axis=-1)]
    another operation x8 -> x2, other arithmetic: 19.5 us -> 0.09 us  [the longest x6 19.4 us: across_hi(): return jnp.stack([block, swap(block, 'hi')])]
    add x7 -> x3, other arithmetic: 22 us -> 3.06 us  [the longest x1 2.29 us: local(): grad_normed = plan.ordered(settle(rows_near) + arrived)]
  transfers between devices with their start and end apart: 57 -> 60, of which waited for: 23 -> 24; matrix products, arithmetic and copies ran while one was open for 23% -> 20% of each run, Pallas kernels for 20% -> 30%
where the time goes in v4:
time: 871 us; the launch traced here: 860 us
  Pallas kernels  280 us (32%)
  waiting for transfers between devices  258 us (30%)
  local copies, waits for them, and re-layouts  98.2 us (11%)
  other arithmetic  85.5 us (10%)
  starting transfers between devices  57.5 us (7%)
  blocking collectives  42 us (5%)
  matrix products  22.9 us (3%)
  between operations  16.1 us (2%)
    ppermute x40, waiting for transfers between devices, swap(): return lax.ppermute(block, axis, [(at, at ^ step) for at in range(count)])  143 us
    pallas_call x14, Pallas kernels, product(): pl.pallas_call(kernel, grid_spec=pltpu.PrefetchScalarGridSpec(num_scalar_...  101 us
    pallas_call x2, Pallas kernels, attend(): pl.pallas_call(attend_kernel, grid_spec=pltpu.PrefetchScalarGridSpec(num_...  65.1 us
    pallas_call x2, Pallas kernels, attend_back(): pl.pallas_call(attend_back_kernel, grid_spec=pltpu.PrefetchScalarGridSpec...  62.6 us
    pallas_call x2, Pallas kernels, feed(): pl.pallas_call(feed_kernel, grid=(steps,), in_specs=pair_specs(rows, step...  51.1 us
    all_to_all x1, blocking collectives, trade_ranks(): return lax.all_to_all(block, ('mid', 'core'), 0, 0, tiled=True)  42 us
    all_to_all x1, waiting for transfers between devices, local(): lax.all_to_all(partial, AXES, 0, 0, tiled=True).astype(f32)  39.8 us
    all_to_all x1, waiting for transfers between devices, local(): lax.all_to_all(jnp.concatenate([modulations, gain_blocks], axis=1), AXES,...  32 us
  transfers between devices with their start and end apart: 60, of which 24 were waited for; matrix products, arithmetic and copies ran while one was open for 20% of the time, Pallas kernels for 30%

profile of v4, /device:TPU:8, one launch (start us, length us, event | category | flops | bytes accessed | tf_op | source)
XLA Modules:
  0.0 860.2 jit_solution(16294424308594755862)
XLA Ops:
  60.8 39.8 %all-to-all-done.3 = bf16[32,2,6144]{2,1,0:T(2,128)(2,1)} async-done(((bf16[32,2,6144]{2,1,0:T(2,128)(2,1)}), bf16[32,2,6144]{2,1,0:T(2,128)(2,1)}, u32[]{:S(2)}, u32[]{:S(2)}) %all-to-all-start.3) | async-done | bytes 786464 | tf_op jit(solution)/shard_map/all_to_all | solution.py:758
  118.8 42.0 %all_to_all.59 = bf16[4,48,2048]{2,1,0:T(8,128)(2,1)S(1)} all-to-all(bf16[4,48,2048]{2,1,0:T(8,128)(2,1)} %reshape.894), channel_id=1, replica_groups=mesh['hi'=2,'mid'=2,'core'=2,'rep'=4] {'mid','core'}, dimensions={0} | all-to-all | bytes 1572864 | tf_op jit(solution)/shard_map/all_to_all | solution.py:560
  165.8 12.6 %all-gather.17.cloned.1.call-done = bf16[2048,384]{1,0:T(8,128)(2,1)} async-done(((bf16[512,384]{1,0:T(8,128)(2,1)}), bf16[2048,384]{1,0:T(8,128)(2,1)}) %all-gather.17.cloned.1.call-update) | async-done | bytes 1572880 | tf_op jit(solution)/shard_map/all_gather | solution.py:703
  178.4 20.8 %collective-permute-done.5 = bf16[2048,384]{1,0:T(8,128)(2,1)} collective-permute-done((bf16[2048,384]{1,0:T(8,128)(2,1)}, bf16[2048,384]{1,0:T(8,128)(2,1)}, u32[]{:S(2)}, u32[]{:S(2)}) %collective-permute-start.5) | collective-permute-done | bytes 1572896 | tf_op jit(solution)/shard_map/ppermute | solution.py:527
  216.1 18.3 %collective-permute-done.9.result_ref.refs_4_ = bf16[512,1536]{1,0:T(8,128)(2,1)} collective-permute-done((bf16[512,1536]{1,0:T(8,128)(2,1)}, bf16[512,1536]{1,0:T(8,128)(2,1)}, u32[]{:S(2)}, u32[]{:S(2)}) %collective-permute-start.9) | collective-permute-done | bytes 1572896 | tf_op jit(solution)/shard_map/ppermute | solution.py:527
  246.2 32.5 %attend.2 = (f32[1024,1152]{1,0:T(8,128)}, f32[512,384]{1,0:T(8,128)}, f32[512,384]{1,0:T(8,128)}, bf16[1024,384]{1,0:T(8,128)(2,1)}, bf16[1024,384]{1,0:T(8,128...) custom-call(s32[4]{0:T(128)} %maximum_convert_fusion.kind_ref, ...), custom_call_target="tpu_custom_call" | custom-call | tf_op jit(solution)/shard_map/attend/pallas_call | solution.py:349
  291.4 32.6 %attend.3 = (f32[1024,1152]{1,0:T(8,128)}, f32[512,384]{1,0:T(8,128)}, f32[512,384]{1,0:T(8,128)}, bf16[1024,384]{1,0:T(8,128)(2,1)}, bf16[1024,384]{1,0:T(8,128...) custom-call(s32[4]{0:T(128)} %maximum_convert_fusion.2.kind_ref, ...), custom_call_target="tpu_custom_call" | custom-call | tf_op jit(solution)/shard_map/attend/pallas_call | solution.py:349
  350.5 14.2 %collective-permute-done.17 = bf16[512,1536]{1,0:T(8,128)(2,1)S(1)} collective-permute-done((bf16[512,1536]{1,0:T(8,128)(2,1)}, bf16[512,1536]{1,0:T(8,128)(2,1)S(1)}, u32[]{:S(2)}, u32[]{:S(2)}) %collective-permute-start.17) | collective-permute-done | bytes 1572896 | tf_op jit(solution)/shard_map/ppermute | solution.py:527
  364.7 11.8 %collective-permute-done.18.rows_ref.refs_2_ = bf16[512,1536]{1,0:T(8,128)(2,1)S(1)} collective-permute-done((bf16[512,1536]{1,0:T(8,128)(2,1)S(1)}, bf16[512,1536]{1,0:T(8,128)(2,1)S(1)}, u32[]{:S(2)}, u32[]{:S(2)}) %collective-permute-start.18) | collective-permute-done | bytes 1572896 | tf_op jit(solution)/shard_map/ppermute | solution.py:527
  381.1 25.8 %feed.2 = (bf16[1024,1024]{1,0:T(8,128)(2,1)}, bf16[1024,1024]{1,0:T(8,128)(2,1)}, bf16[1024,1024]{1,0:T(8,128)(2,1)}, f32[512,1536]{1,0:T(8,128)}, bf16[512,1536]{1,0:T(8,128)(2,1)}) custom-call(bf16[512,1536]{1,0:T(8,128)(2,1)} %copy-done.11, bf16[512,1536]{1,0:T(8,128)(2,1)} %copy-done.12, bf16[512,1536]{1,0:T(8,128)(2,1)} %collective-permute-done.9.result_ref.refs_4_, ...), custom_call_target="tpu_custom_call" | custom-call | tf_op jit(solution)/shard_map/feed/pallas_call | solution.py:511
  413.8 25.4 %feed.3 = (bf16[1024,1024]{1,0:T(8,128)(2,1)}, bf16[1024,1024]{1,0:T(8,128)(2,1)}, bf16[1024,1024]{1,0:T(8,128)(2,1)}, f32[512,1536]{1,0:T(8,128)}, bf16[512,1536]{1,0:T(8,128)(2,1)}) custom-call(bf16[512,1536]{1,0:T(8,128)(2,1)} %copy-done.4, bf16[512,1536]{1,0:T(8,128)(2,1)} %copy-done.10, bf16[512,1536]{1,0:T(8,128)(2,1)} %fusion.12.result_ref.refs_2_, ...), custom_call_target="tpu_custom_call" | custom-call | tf_op jit(solution)/shard_map/feed/pallas_call | solution.py:511
  460.9 8.1 product.17
  494.4 7.9 product.18
  502.4 31.2 %attend_back.2 = (bf16[1024,1152]{1,0:T(8,128)(2,1)}, bf16[512,384]{1,0:T(8,128)(2,1)}, bf16[512,384]{1,0:T(8,128)(2,1)}, f32[512,1536]{1,0:T(8,128)}, bf16[512,1536]{1,0:T(8,128)(2,1)}, /*index=5*/f32[4,384]{1,0:T(4,128)}) custom-call(s32[4]{0:T(128)} %maximum_convert_fusion.2.kind_ref, s32[4]{0:T(128)} %maximum_convert_fusion.3.len_ref, ...), custom_call_target="tpu_custom_call" | custom-call | tf_op jit(solution)/shard_map/attend_back/pallas_call | solution.py:379
  539.4 8.6 %product.20 = f32[512,1536]{1,0:T(8,128)} custom-call(s32[1]{0:T(128)} %bitcast.67.first_ref, bf16[1024,1024]{1,0:T(8,128)(2,1)} %get-tuple-element.435.refs_0_, bf16[1024,1024]{1,0:T(8,128)(2,1)} %get-tuple-element.427.refs_1_, bf16[512,1536]{1,0:T(8,128)(2,1)} %fusion.12.result_ref.refs_2_, ...), custom_call_target="tpu_custom_call" | custom-call | tf_op jit(solution)/shard_map/product/pallas_call | solution.py:431
  548.0 31.4 %attend_back.3 = (bf16[1024,1152]{1,0:T(8,128)(2,1)}, bf16[512,384]{1,0:T(8,128)(2,1)}, bf16[512,384]{1,0:T(8,128)(2,1)}, f32[512,1536]{1,0:T(8,128)}, bf16[512,1536]{1,0:T(8,128)(2,1)}, /*index=5*/f32[4,384]{1,0:T(4,128)}) custom-call(s32[4]{0:T(128)} %maximum_convert_fusion.kind_ref, s32[4]{0:T(128)} %maximum_convert_fusion.1.len_ref, ...), custom_call_target="tpu_custom_call" | custom-call | tf_op jit(solution)/shard_map/attend_back/pallas_call | solution.py:379
  611.9 8.5 product.23
  620.5 8.8 %product.25 = f32[768,1152]{1,0:T(8,128)} custom-call(s32[1]{0:T(128)} %constant.579.clone.1.first_ref, bf16[512,1536]{1,0:T(8,128)(2,1)} %maximum_select_fusion.3.rows_ref.refs_0_, bf16[512,1536]{1,0:T(8,128)(2,1)} %collective-permute-done.3.core_rows_ref.refs_1_, bf16[512,1536]{1,0:T(8,128)(2,1)} %collective-permute-done.6.rows_ref.refs_2_, ...), custom_call_target="tpu_custom_call" | custom-call | tf_op jit(solution)/shard_map/product/pallas_call | solution.py:431
  665.4 27.2 %collective-permute-done.33 = bf16[2048,384]{1,0:T(8,128)(2,1)} collective-permute-done((bf16[2048,384]{1,0:T(8,128)(2,1)S(1)}, bf16[2048,384]{1,0:T(8,128)(2,1)}, u32[]{:S(2)}, u32[]{:S(2)}) %collective-permute-start.33) | collective-permute-done | bytes 1572896 | tf_op jit(solution)/shard_map/ppermute | solution.py:527
  720.2 14.0 %collective-permute-done.36 = bf16[512,1536]{1,0:T(8,128)(2,1)} collective-permute-done((bf16[512,1536]{1,0:T(8,128)(2,1)}, bf16[512,1536]{1,0:T(8,128)(2,1)}, u32[]{:S(2)}, u32[]{:S(2)}) %collective-permute-start.36) | collective-permute-done | bytes 1572896 | tf_op jit(solution)/shard_map/ppermute | solution.py:527
  734.3 10.2 %fusion.6 = (f32[512,1536]{1,0:T(8,128)}, bf16[512,1536]{1,0:T(8,128)(2,1)}, f32[512,1536]{1,0:T(8,128)S(1)}) fusion(bf16[512,1536]{1,0:T(8,128)(2,1)S(1)} %copy-done.3, f32[512,1536]{1,0:T(8,128)S(1)} %copy-done.6, f32[512]{0:T(512)S(1)} %multiply_multiply_fusion.1, f32[2,1536]{1,0:T(2,128)S(1)} %copy-done.47, f32[1536]{0:T(1024)S(1)} %copy-done.45, ...), kind=kOutput, calls=%fused_computation.24 | convolution fusion | flops 1628700672 | bytes 27844608 | tf_op jit(solution)/shard_map/dot_general | solution.py:59
  748.0 12.7 %collective-permute-done.38 = bf16[768,1152]{1,0:T(8,128)(2,1)S(1)} collective-permute-done((bf16[768,1152]{1,0:T(8,128)(2,1)}, bf16[768,1152]{1,0:T(8,128)(2,1)S(1)}, u32[]{:S(2)}, u32[]{:S(2)}) %collective-permute-start.38) | collective-permute-done | bytes 1769504 | tf_op jit(solution)/shard_map/ppermute | solution.py:527
  772.2 8.6 all-to-all-done.7
  796.6 32.0 %all-to-all-done.5 = bf16[32,2,6288]{2,1,0:T(2,128)(2,1)} async-done(((bf16[32,2,6288]{2,1,0:T(2,128)(2,1)}), bf16[32,2,6288]{2,1,0:T(2,128)(2,1)}, u32[]{:S(2)}, u32[]{:S(2)}) %all-to-all-start.5) | async-done | bytes 804896 | tf_op jit(solution)/shard_map/all_to_all | solution.py:981
  (447 shorter events, 359.3 us)
Async XLA Ops:
  31.5 70.9 %all-gather.7.cloned.1.call-start = ((), (), s32[]{:S(2)}) async-start(), calls=%async_computation.15 | async-start | bytes 2949120 | tf_op jit(solution)/shard_map/all_gather | solution.py:703
  60.0 101.8 %all-gather.11.cloned.1.call-start = ((), (), s32[]{:S(2)}) async-start(), calls=%async_computation.17 | async-start | bytes 1966080 | tf_op jit(solution)/shard_map/all_gather | solution.py:703
  104.4 74.0 %all-gather.17.cloned.1.call-start = ((), (), s32[]{:S(2)}) async-start(), calls=%async_computation.20 | async-start | bytes 1966080 | tf_op jit(solution)/shard_map/all_gather | solution.py:703
  106.3 55.5 %collective-permute-start.1 = (bf16[256,4096]{1,0:T(8,128)(2,1)S(1)}, bf16[256,4096]{1,0:T(8,128)(2,1)}, u32[]{:S(2)}, u32[]{:S(2)}) collective-permute-start(bf16[256,4096]{1,0:T(8,128)(2,1)S(1)} %maximum_select_fusion.2.caption_ref.refs_0_), channel_id=1, source_target_pairs={{0,8},{8,0},{1,9},{9,1},{2,10},{10,2},{3,11},{11,3},{4,12},{12,4},... | collective-permute-start | bytes 6291464 | tf_op jit(solution)/shard_map/ppermute | solution.py:527
  107.6 54.1 %collective-permute-start.2 = (bf16[1024,1152]{1,0:T(8,128)(2,1)}, bf16[1024,1152]{1,0:T(8,128)(2,1)}, u32[]{:S(2)}, u32[]{:S(2)}) collective-permute-start(bf16[1024,1152]{1,0:T(8,128)(2,1)} %all-gather.7.cloned.1.call-done), channel_id=1, source_target_pairs={{0,16},{16,0},{1,17},{17,1},{2,18},{18,2},{3,19},{19,3},{4,20},{20... | collective-permute-start | bytes 7077896 | tf_op jit(solution)/shard_map/ppermute | solution.py:527
  108.8 125.5 %all-gather.15.cloned.1.call-start = ((), (), s32[]{:S(2)}) async-start(), calls=%async_computation.19 | async-start | bytes 1966080 | tf_op jit(solution)/shard_map/all_gather | solution.py:703
  112.5 49.2 %collective-permute-start.3 = (bf16[512,1536]{1,0:T(8,128)(2,1)}, bf16[512,1536]{1,0:T(8,128)(2,1)}, u32[]{:S(2)}, u32[]{:S(2)}) collective-permute-start(bf16[512,1536]{1,0:T(8,128)(2,1)} %maximum_select_fusion.3.rows_ref.refs_0_), channel_id=1, source_target_pairs={{0,4},{4,0},{1,5},{5,1},{2,6},{6,2},{3,7},{7,3},{8,12},{12,8},{9,1... | collective-permute-start | bytes 4718600 | tf_op jit(solution)/shard_map/ppermute | solution.py:527
  114.2 47.5 %collective-permute-start.4 = (bf16[512,1536]{1,0:T(8,128)(2,1)}, bf16[512,1536]{1,0:T(8,128)(2,1)}, u32[]{:S(2)}, u32[]{:S(2)}) collective-permute-start(bf16[512,1536]{1,0:T(8,128)(2,1)} %fusion.12.result_ref.refs_2_), channel_id=1, source_target_pairs={{0,4},{4,0},{1,5},{5,1},{2,6},{6,2},{3,7},{7,3},{8,12},{12,8},{9,1... | collective-permute-start | bytes 4718600 | tf_op jit(solution)/shard_map/ppermute | solution.py:527
  161.9 116.9 %all-gather.13.cloned.1.call-start = ((), (), s32[]{:S(2)}) async-start(), calls=%async_computation.18 | async-start | bytes 1966080 | tf_op jit(solution)/shard_map/all_gather | solution.py:703
  165.0 69.4 %collective-permute-start.9 = (bf16[512,1536]{1,0:T(8,128)(2,1)}, bf16[512,1536]{1,0:T(8,128)(2,1)}, u32[]{:S(2)}, u32[]{:S(2)}) collective-permute-start(bf16[512,1536]{1,0:T(8,128)(2,1)} %fusion.12.result_ref.refs_2_), channel_id=1, source_target_pairs={{0,8},{8,0},{1,9},{9,1},{2,10},{10,2},{3,11},{11,3},{4,12},{12,4},... | collective-permute-start | bytes 4718600 | tf_op jit(solution)/shard_map/ppermute | solution.py:527
  208.2 119.3 %all-gather.9.cloned.1.call-start = ((), (), s32[]{:S(2)}) async-start(), calls=%async_computation.16 | async-start | bytes 1966080 | tf_op jit(solution)/shard_map/all_gather | solution.py:703
  278.9 254.7 %reduce-scatter.7.cloned.1.call-start = ((), (), s32[]{:S(2)}) async-start(), calls=%async_computation.21 | async-start | bytes 1966080 | tf_op jit(solution)/shard_map/reduce_scatter | solution.py:655
  492.8 92.7 %reduce-scatter.9.cloned.1.call-start = ((), (), s32[]{:S(2)}) async-start(), calls=%async_computation.22 | async-start | bytes 1966080 | tf_op jit(solution)/shard_map/reduce_scatter | solution.py:655
  537.9 105.9 %reduce-scatter.11.cloned.1.call-start = ((), (), s32[]{:S(2)}) async-start(), calls=%async_computation.23 | async-start | bytes 1966080 | tf_op jit(solution)/shard_map/reduce_scatter | solution.py:655
  538.0 47.5 %collective-permute-start.29 = (bf16[512,1536]{1,0:T(8,128)(2,1)}, bf16[512,1536]{1,0:T(8,128)(2,1)}, u32[]{:S(2)}, u32[]{:S(2)}) collective-permute-start(bf16[512,1536]{1,0:T(8,128)(2,1)} %product.17), channel_id=1, source_target_pairs={{0,16},{16,0},{1,17},{17,1},{2,18},{18,2},{3,19},{19,3},{4,20},{20... | collective-permute-start | bytes 4718600 | tf_op jit(solution)/shard_map/ppermute | solution.py:527
  591.6 101.0 %reduce-scatter.13.cloned.1.call-start = ((), (), s32[]{:S(2)}) async-start(), calls=%async_computation.24 | async-start | bytes 1966080 | tf_op jit(solution)/shard_map/reduce_scatter | solution.py:655
  591.7 50.1 %collective-permute-start.31 = (bf16[512,1536]{1,0:T(8,128)(2,1)}, bf16[512,1536]{1,0:T(8,128)(2,1)S(1)}, u32[]{:S(2)}, u32[]{:S(2)}) collective-permute-start(bf16[512,1536]{1,0:T(8,128)(2,1)} %add_convert_fusion.5), channel_id=1, source_target_pairs={{0,8},{8,0},{1,9},{9,1},{2,10},{10,2},{3,11},{11,3},{4,12},{12,4},... | collective-permute-start | bytes 4718600 | tf_op jit(solution)/shard_map/ppermute | solution.py:527
  592.9 51.0 %collective-permute-start.32 = (bf16[2048,384]{1,0:T(8,128)(2,1)}, bf16[2048,384]{1,0:T(8,128)(2,1)}, u32[]{:S(2)}, u32[]{:S(2)}) collective-permute-start(bf16[2048,384]{1,0:T(8,128)(2,1)} %product.19), channel_id=1, source_target_pairs={{0,16},{16,0},{1,17},{17,1},{2,18},{18,2},{3,19},{19,3},{4,20},{20... | collective-permute-start | bytes 4718600 | tf_op jit(solution)/shard_map/ppermute | solution.py:527
  610.6 92.4 %collective-permute-start.39 = (bf16[192,1536]{1,0:T(8,128)(2,1)}, bf16[192,1536]{1,0:T(8,128)(2,1)}, u32[]{:S(2)}, u32[]{:S(2)}) collective-permute-start(bf16[192,1536]{1,0:T(8,128)(2,1)} %product.27), channel_id=1, source_target_pairs={{0,16},{16,0},{1,17},{17,1},{2,18},{18,2},{3,19},{19,3},{4,20},{20... | collective-permute-start | bytes 1769480 | tf_op jit(solution)/shard_map/ppermute | solution.py:527
  655.7 64.5 %collective-permute-start.37 = (bf16[512,1536]{1,0:T(8,128)(2,1)}, bf16[512,1536]{1,0:T(8,128)(2,1)}, u32[]{:S(2)}, u32[]{:S(2)}) collective-permute-start(bf16[512,1536]{1,0:T(8,128)(2,1)} %convolution_convert_fusion.1), channel_id=1, source_target_pairs={{0,4},{4,0},{1,5},{5,1},{2,6},{6,2},{3,7},{7,3},{8,12},{12,8},{9,1... | collective-permute-start | bytes 4718600 | tf_op jit(solution)/shard_map/ppermute | solution.py:527
  710.5 55.2 %all-to-all-start.8 = ((bf16[4,48,2048]{2,1,0:T(8,128)(2,1)}), bf16[4,48,2048]{2,1,0:T(8,128)(2,1)}, u32[]{:S(2)}, u32[]{:S(2)}) async-start(bf16[4,48,2048]{2,1,0:T(8,128)(2,1)} %bitcast.266), calls=%async_computation.14 | async-start | bytes 1572864 | tf_op jit(solution)/shard_map/all_to_all | solution.py:560
  714.7 48.9 %reduce-scatter.15.cloned.1.call-start = ((), (), s32[]{:S(2)}) async-start(), calls=%async_computation.25 | async-start | bytes 1966080 | tf_op jit(solution)/shard_map/reduce_scatter | solution.py:655
  715.5 120.9 %reduce-scatter.17.cloned.1.call-start = ((), (), s32[]{:S(2)}) async-start(), calls=%async_computation.26 | async-start | bytes 2949120 | tf_op jit(solution)/shard_map/reduce_scatter | solution.py:655
  780.8 47.7 %all-to-all-start.5 = ((bf16[32,2,6288]{2,1,0:T(2,128)(2,1)}), bf16[32,2,6288]{2,1,0:T(2,128)(2,1)}, u32[]{:S(2)}, u32[]{:S(2)}) async-start(bf16[32,2,6288]{2,1,0:T(2,128)(2,1)} %reshape.993), calls=%async_computation.10 | async-start | bytes 1638400 | tf_op jit(solution)/shard_map/all_to_all | solution.py:981
  (99 other events, 1472.4 us)
Sparse Core Ops, SparseCore 0:
  38.0 61.5 all-gather.6
  104.5 35.7 all-gather.10
  142.4 35.9 all-gather.16
  180.4 35.9 all-gather.14
  217.8 35.9 all-gather.12
  279.0 36.8 all-gather.8
  492.9 33.5 reduce-scatter.6
  538.0 34.9 reduce-scatter.8
  591.7 34.1 reduce-scatter.10
  648.1 33.7 reduce-scatter.12
  717.9 34.6 reduce-scatter.14
  763.8 64.7 reduce-scatter.16

commit v5 on v4

--- a/solution.py
+++ b/solution.py
@@ -117,6 +117,8 @@
     gain_ref,
     cos_ref,
     sin_ref,
+    rows_out_ref,
+    caption_out_ref,
     qkv_ref,
     text_ref,
     text_value_ref,
@@ -135,19 +137,19 @@
     cosine, sine = cos_ref[kind], sin_ref[kind]
     scaling = HEAD_DIM ** (-0.5)
 
-    def project(rows, captions):
-        qkv_ref[...] = dot_cut(rows, qkv_mine_ref, qkv_other_ref)
-        text_ref[...] = dot_cut(captions, key_mine_ref, key_other_ref)
-        text_value_ref[...] = dot_cut(captions, value_mine_ref, value_other_ref)
-
     @pl.when(own)
     def _():
-        project(rows_ref, caption_ref)
+        rows_out_ref[...] = rows_ref[...]
+        caption_out_ref[...] = caption_ref[...]
 
     @pl.when(jnp.logical_not(own))
     def _():
-        project(core_rows_ref, core_caption_ref)
-
+        rows_out_ref[...] = core_rows_ref[...]
+        caption_out_ref[...] = core_caption_ref[...]
+
+    qkv_ref[...] = dot_cut(rows_out_ref, qkv_mine_ref, qkv_other_ref)
+    text_ref[...] = dot_cut(caption_out_ref, key_mine_ref, key_other_ref)
+    text_value_ref[...] = dot_cut(caption_out_ref, value_mine_ref, value_other_ref)
     for at in range(0, width, LANES):
         lanes = slice(at, at + LANES)
         turned = []
@@ -175,13 +177,15 @@
         read_ref[:, lanes] = read
         mixed_ref[:, lanes] = (join_heads(own_out) + gain_ref[3:4, lanes] * read).astype(jnp.bfloat16)
 
+    branch = dot(mixed_ref[...], out_weight_ref[...])
+
     @pl.when(own)
     def _():
-        branch_ref[...] = dot(mixed_ref[...], out_weight_ref[...])
+        branch_ref[...] = branch
 
     @pl.when(jnp.logical_not(own))
     def _():
-        core_branch_ref[...] = dot(mixed_ref[...], out_weight_ref[...]).astype(jnp.bfloat16)
+        core_branch_ref[...] = branch.astype(jnp.bfloat16)
 
 
 def head_norm_back(grad, raw, gain_row):
@@ -209,9 +213,9 @@
     gain_ref,
     cos_ref,
     sin_ref,
+    branch_out_ref,
     gqkv_ref,
     gtext_ref,
-    gtext_value_ref,
     grad_rows_ref,
     core_grad_rows_ref,
     gains_ref,
@@ -226,11 +230,13 @@
 
     @pl.when(own)
     def _():
-        mixed_ref[...] = dot_right(branch_ref[...], out_weight_ref[...])
+        branch_out_ref[...] = branch_ref[...]
 
     @pl.when(jnp.logical_not(own))
     def _():
-        mixed_ref[...] = dot_right(core_branch_ref[...], out_weight_ref[...])
+        branch_out_ref[...] = core_branch_ref[...]
+
+    mixed_ref[...] = dot_right(branch_out_ref[...], out_weight_ref[...])
 
     @pl.when(item == 0)
     def _():
@@ -275,21 +281,23 @@
         grad_text, gain = head_norm_back(read_keys, text_ref[:, lanes], gain_ref[2:3, lanes])
         gtext_ref[:, lanes] = grad_text.astype(jnp.bfloat16)
         gains_ref[2:3, lanes] += gain
-        gtext_value_ref[:, lanes] = read_values.astype(jnp.bfloat16)
+        gtext_ref[:, width + at : width + at + LANES] = read_values.astype(jnp.bfloat16)
         gains_ref[3:4, lanes] += jnp.sum(grad * read_ref[:, lanes], axis=0, keepdims=True)
 
     half = qkv_mine_ref.shape[0]
+    low = dot_right(gqkv_ref[...], qkv_mine_ref[...])
+    high = dot_right(gqkv_ref[...], qkv_other_ref[...])
 
     @pl.when(own)
     def _():
-        grad_rows_ref[:, :half] = dot_right(gqkv_ref[...], qkv_mine_ref[...])
-        grad_rows_ref[:, half:] = dot_right(gqkv_ref[...], qkv_other_ref[...])
+        grad_rows_ref[:, :half] = low
+        grad_rows_ref[:, half:] = high
 
     @pl.when(jnp.logical_not(own))
     def _():
-        rows = gqkv_ref[...]
-        core_grad_rows_ref[:, :half] = dot_right(rows, qkv_mine_ref[...]).astype(jnp.bfloat16)
-        core_grad_rows_ref[:, half:] = dot_right(rows, qkv_other_ref[...]).astype(jnp.bfloat16)
+        core_grad_rows_ref[:, :half] = low.astype(jnp.bfloat16)
+        core_grad_rows_ref[:, half:] = high.astype(jnp.bfloat16)
+
 
 def whole_spec(array):
     zeros = (0,) * len(array.shape)
@@ -335,6 +343,8 @@
     count, width = 2 * rows[0].shape[0], out_rank.shape[0]
     text_count = 2 * captions[0].shape[0]
     outs = [
+        shaped(count, D),
+        shaped(text_count, TEXT_DIM),
         shaped(count, 3 * width, jnp.float32),
         shaped(text_count, width, jnp.float32),
         shaped(text_count, width, jnp.float32),
@@ -346,7 +356,7 @@
     ]
     branch = (shaped(count // 2, D, jnp.float32), shaped(count // 2, D))
     whole = [*qkv_rank, *key_rank, *value_rank, out_rank, *tables]
-    *kept, branch_mine, branch_core = pl.pallas_call(
+    rows, captions, *kept, branch_mine, branch_core = pl.pallas_call(
         attend_kernel,
         grid_spec=pltpu.PrefetchScalarGridSpec(
             num_scalar_prefetch=2,
@@ -360,7 +370,7 @@
         compiler_params=parameters(),
         name="attend",
     )(*scalars, *rows, *captions, *whole)
-    return kept, (branch_mine, branch_core)
+    return rows, captions, kept, (branch_mine, branch_core)
 
 
 def attend_back(scalars, grad_branch, kept, qkv_rank, out_rank, tables):
@@ -368,15 +378,15 @@
     qkv_raw, text_raw, text_value_raw, queries, keys, text_keys, _, read = kept
     count, width = queries.shape
     outs = [
+        shaped(count, D),
         shaped(count, 3 * width),
-        shaped(text_raw.shape[0], width),
-        shaped(text_raw.shape[0], width),
+        shaped(text_raw.shape[0], 2 * width),
     ]
     rows = (shaped(count // 2, D, jnp.float32), shaped(count // 2, D))
     gains = shaped(4, width, jnp.float32)
     by_item = [qkv_raw, text_raw, text_value_raw, queries, keys, text_keys, read]
     whole = [*qkv_rank, out_rank, *tables]
-    qkv, text, text_value, rows_mine, rows_core, gains = pl.pallas_call(
+    branch, qkv, text, rows_mine, rows_core, gains = pl.pallas_call(
         attend_back_kernel,
         grid_spec=pltpu.PrefetchScalarGridSpec(
             num_scalar_prefetch=2,
@@ -393,7 +403,7 @@
         compiler_params=parameters(),
         name="attend_back",
     )(*scalars, *grad_branch, *by_item, *whole)
-    return qkv, text, text_value, (rows_mine, rows_core), gains
+    return branch, qkv, text, (rows_mine, rows_core), gains
 
 
 def row_cuts(lefts, rights):
@@ -456,13 +466,13 @@
     up_mine_ref,
     up_other_ref,
     down_ref,
+    rows,
+    result,
     hidden_ref,
     grad_gate_ref,
     grad_up_ref,
     grad_ref,
     core_grad_ref,
-    rows,
-    result,
 ):
     own = pl.program_id(0) < pl.num_programs(0) // 2
 
@@ -505,10 +515,10 @@
     count, width = 2 * rows[0].shape[0], down_rank.shape[0]
     block = 256
     steps = count // block
-    outs = [shaped(count, width)] * 3
+    outs = [shaped(count, D)] * 2 + [shaped(count, width)] * 3
     grads = (shaped(count // 2, D, jnp.float32), shaped(count // 2, D))
     whole = [*gate_rank, *up_rank, down_rank]
-    hidden, grad_gate, grad_up, grad_mine, grad_core = pl.pallas_call(
+    *outs, grad_mine, grad_core = pl.pallas_call(
         feed_kernel,
         grid=(steps,),
         in_specs=pair_specs(rows, steps)
@@ -516,11 +526,10 @@
         + [whole_spec(array) for array in whole],
         out_specs=[step_spec(array, steps) for array in outs] + pair_specs(grads, steps),
         out_shape=[*outs, *grads],
-        scratch_shapes=[pltpu.VMEM((block, D), jnp.bfloat16)] * 2,
         compiler_params=parameters(),
         name="feed",
     )(*rows, *grad_result, *whole)
-    return hidden, grad_gate, grad_up, (grad_mine, grad_core)
+    return *outs, (grad_mine, grad_core)
 
 
 def swap(block, axis, count=2, step=1):
@@ -702,6 +711,7 @@
     def z_gather(block):
         return lax.all_gather(block.reshape(-1, block.shape[-1]), "rep", tiled=True)
 
+    down_z = z_gather(down_weight)
     qkv_mine = trade_ranks(plan.by_rank(qkv_weight, 3, plan.head_groups))
     qkv_mine = qkv_mine.reshape(RANKS * rows, 3 * rank_width)
     if plan.aligned:
@@ -709,6 +719,8 @@
     else:
         out_whole = lax.all_gather(out_weight, AXES, axis=0, tiled=True)
         out_rank = pick(out_whole.reshape(RANKS, rank_width, D), plan.rank)
+    text_mine = trade_ranks(plan.by_rank(text_weight, 2, plan.head_groups))
+    captions_near = pair(plan.ordered(caption.reshape(-1, TEXT_DIM)))
 
     head = condition.reshape(item_count, devices, rows)
     head = jnp.transpose(head, (1, 0, 2)).reshape(devices, -1)
@@ -716,8 +728,6 @@
         [norm_gains.reshape(-1), caption_len.astype(bf16), item_kind.astype(bf16)]
     )
     small = jnp.concatenate([head, jnp.broadcast_to(rest, (devices, rest.size))], axis=1)
-    qkv_mine, small = fence(qkv_mine, small)
-    qkv_z = z_gather(qkv_mine)
     small = lax.all_to_all(small, AXES, 0, 0, tiled=True)
     cut = [head.shape[1], head.shape[1] + norm_gains.size]
     cut.append(cut[1] + item_count)
@@ -748,24 +758,25 @@
     tables = (head_gains, cosine, sine)
     scalars = list(zip(kinds_sides, lengths_sides, strict=True))
 
-    captions = plan.ordered(caption.reshape(-1, TEXT_DIM))
-    text_weight, conditions, captions = fence(text_weight, activated_mine, captions)
-    text_mine = trade_ranks(plan.by_rank(text_weight, 2, plan.head_groups))
-    captions_near = pair(captions)
-    partial = dot(conditions, ada_weight).astype(bf16).reshape(devices, item_count, 4 * D)
-    text_mine, partial, captions_near = fence(text_mine, partial, captions_near)
+    partial = dot(activated_mine, ada_weight).astype(bf16).reshape(devices, item_count, 4 * D)
     text_key_mine, text_value_mine = text_mine[..., :rank_width], text_mine[..., rank_width:]
+    down_z, qkv_mine, text_key_mine, text_value_mine, captions_near, partial = fence(
+        down_z, qkv_mine, text_key_mine, text_value_mine, captions_near, partial
+    )
+    qkv_z = z_gather(qkv_mine)
+    down_rank = plan.across_hi(down_z)
+    gate_up_mine = trade_ranks(plan.by_rank(gate_up_weight, 2, hi_count))
+    gate_mine, up_mine = gate_up_mine[..., :feed_width], gate_up_mine[..., feed_width:]
     modulation = jnp.sum(lax.all_to_all(partial, AXES, 0, 0, tiled=True).astype(f32), axis=0)
-    qkv_z, modulation, text_key_mine, text_value_mine = fence(
-        qkv_z, modulation, text_key_mine, text_value_mine
+    qkv_z, down_rank, modulation, gate_mine, up_mine = fence(
+        qkv_z, down_rank, modulation, gate_mine, up_mine
     )
 
     scale_attn, gate_attn, scale_mlp, gate_mlp = jnp.split(modulation, 4, axis=1)
     text_key_z = z_gather(text_key_mine)
-    captions_far = swap(captions, "mid")
+    captions_far = swap(captions_near[0], "mid")
     qkv_rank = plan.across_hi(qkv_z)
-    gate_up_mine = trade_ranks(plan.by_rank(gate_up_weight, 2, hi_count))
-    gate_mine, up_mine = gate_up_mine[..., :feed_width], gate_up_mine[..., feed_width:]
+    down_rank = plan.natural_hi(down_rank).reshape(feed_width, D)
     token_rows = tokens.astype(f32).reshape(item_count, item_len, D)
     normed = modulate(token_rows, gain_rows[0], scale_attn)
     normed = plan.ordered(normed.astype(bf16).reshape(row_count, D))
@@ -773,8 +784,8 @@
     grad_top = out_cotangent.astype(f32).reshape(item_count, item_len, D)
     grad_result = (mlp_gate * grad_top).astype(bf16).reshape(row_count, D)
     normed_near, result_near = pair(normed), pair(grad_result)
-    text_key_z, captions_far, qkv_rank, gate_mine, up_mine, normed_near, result_near = fence(
-        text_key_z, captions_far, qkv_rank, gate_mine, up_mine, normed_near, result_near
+    text_key_z, captions_far, qkv_rank, down_rank, normed_near, result_near = fence(
+        text_key_z, captions_far, qkv_rank, down_rank, normed_near, result_near
     )
 
     text_value_z = z_gather(text_value_mine)
@@ -803,51 +814,60 @@
     up_z = z_gather(up_mine)
     gate_rank = plan.across_hi(gate_z)
     attend_weights = (qkv_rank, text_key_rank, plan.halves(text_value_rank), out_rank, tables)
-    kept_far, partial_far = attend(scalars[1], normed_far, captions_far, *attend_weights)
-    up_z, gate_rank, kept_far, partial_far, attend_weights = fence(
-        up_z, gate_rank, kept_far, partial_far, attend_weights
+    normed_far, captions_far, kept_far, partial_far = attend(
+        scalars[1], normed_far, captions_far, *attend_weights
+    )
+    up_z, gate_rank, normed_far, captions_far, kept_far, partial_far, attend_weights = fence(
+        up_z, gate_rank, normed_far, captions_far, kept_far, partial_far, attend_weights
     )
 
     across = settle(partial_far).astype(bf16)
     across, normed_near, up_z = fence(across, normed_near, up_z)
-    down_z = z_gather(down_weight)
     up_rank = plan.across_hi(up_z)
     arrived = settle_move(across)
-    kept_near, partial_near = attend(scalars[0], normed_near, captions_near, *attend_weights)
+    normed_near, captions_near, kept_near, partial_near = attend(
+        scalars[0], normed_near, captions_near, *attend_weights
+    )
     result_far = pair(result_far)
-    down_z, up_rank, arrived, kept_near, partial_near, result_far = fence(
-        down_z, up_rank, arrived, kept_near, partial_near, result_far
-    )
-
-    down_rank = plan.across_hi(down_z)
+    gate_rank = plan.halves(gate_rank)
+    up_rank, arrived, normed_near, captions_near, kept_near, partial_near, result_far, gate_rank = fence(
+        up_rank, arrived, normed_near, captions_near, kept_near, partial_near, result_far, gate_rank
+    )
+
     branch = (settle(partial_near) + arrived).reshape(item_count, item_len, D)
     attn_gate = jnp.tanh(gate_attn)[:, None, :]
     middle = token_rows + attn_gate * branch
     mlp_input = modulate(middle, gain_rows[4], scale_mlp)
     mlp_input = plan.ordered(mlp_input.astype(bf16).reshape(row_count, D))
+    up_rank = plan.halves(up_rank)
+    mlp_input, up_rank = fence(mlp_input, up_rank)
+
+    feed_weights = (gate_rank, up_rank, down_rank)
     input_far = swap(mlp_input, "mid")
-    input_near = pair(mlp_input)
-    gate_rank, up_rank = plan.halves(gate_rank), plan.halves(up_rank)
-    down_rank, input_far, input_near, gate_rank, up_rank = fence(
-        down_rank, input_far, input_near, gate_rank, up_rank
-    )
-
-    down_rank = plan.natural_hi(down_rank).reshape(feed_width, D)
-    feed_weights = (gate_rank, up_rank, down_rank)
-    input_far = pair(input_far)
-    hidden_far, gate_far, up_far, partial_far = feed(input_far, result_far, *feed_weights)
+    input_near, result_near, hidden_near, gate_near, up_near, partial_near = feed(
+        pair(mlp_input), result_near, *feed_weights
+    )
+    input_far, input_near, result_near, hidden_near, gate_near, up_near, partial_near = fence(
+        input_far, input_near, result_near, hidden_near, gate_near, up_near, partial_near
+    )
+    input_far, result_far, hidden_far, gate_far, up_far, partial_far = feed(
+        pair(input_far), result_far, *feed_weights
+    )
     across = settle(partial_far).astype(bf16)
-    across, input_near = fence(across, input_near)
+    inputs, results = (input_near, input_far), (result_near, result_far)
+    gate_rows, up_rows, hidden_rows = (gate_near, gate_far), (up_near, up_far), (hidden_near, hidden_far)
+    across, gate_rows, up_rows, hidden_rows = fence(across, gate_rows, up_rows, hidden_rows)
     arrived = settle_move(across)
-    hidden_near, gate_near, up_near, partial_near = feed(input_near, result_near, *feed_weights)
-    inputs, results = (*input_near, *input_far), (*result_near, *result_far)
-    gate_rows, up_rows, hidden_rows = (gate_near, gate_far), (up_near, up_far), (hidden_near, hidden_far)
     gate_moved = plan.product_moved(inputs, gate_rows)
-    arrived, gate_rows, up_rows, hidden_rows, partial_near, gate_moved = fence(
-        arrived, gate_rows, up_rows, hidden_rows, partial_near, gate_moved
-    )
-
-    gate_moved = plan.move(gate_moved)
+    up_moved = plan.product_moved(inputs, up_rows)
+    hidden_first = hi_at * (feed_width // 2)
+    down_moved = plan.product_moved(hidden_rows, results, feed_width // 2 - hidden_first)
+    gate_kept = plan.product_kept(inputs, gate_rows)
+    arrived, gate_moved, up_moved, down_moved, gate_kept, partial_near = fence(
+        arrived, gate_moved, up_moved, down_moved, gate_kept, partial_near
+    )
+
+    gate_moved, up_moved = plan.move(gate_moved), plan.move(up_moved)
     grad_mlp_input = plan.ordered(settle(partial_near) + arrived)
     _, pull_mlp_norm = jax.vjp(modulate, middle, gain_rows[4], scale_mlp)
     grad_middle_norm, grad_mlp_gain, grad_scale_mlp = pull_mlp_norm(
@@ -856,91 +876,71 @@
     grad_middle = grad_top + grad_middle_norm
     grad_attn_gate = jnp.sum(grad_middle * branch, axis=1) * (1.0 - jnp.tanh(gate_attn) ** 2)
     grad_branch = (attn_gate * grad_middle).astype(bf16).reshape(row_count, D)
-    branch_near = pair(grad_branch)
-    up_moved = plan.product_moved(inputs, up_rows)
-    gate_kept = plan.product_kept(inputs, gate_rows)
-    hidden_first = hi_at * (feed_width // 2)
-    down_moved = plan.product_moved(hidden_rows, results, feed_width // 2 - hidden_first)
-    gate_moved, up_moved, gate_kept, branch_near, down_moved = fence(
-        gate_moved, up_moved, gate_kept, branch_near, down_moved
+    (grad_branch,) = fence(grad_branch)
+
+    branch_far = swap(grad_branch, "mid")
+    back_weights = (qkv_rank, out_rank, tables)
+    branch_near, qkv_near, text_near, rows_near, gain_near = attend_back(
+        scalars[0], pair(grad_branch), kept_near, *back_weights
+    )
+    up_kept = plan.product_kept(inputs, up_rows)
+    branch_far, gate_moved, branch_near, qkv_near, text_near, rows_near, gain_near, up_kept = fence(
+        branch_far, gate_moved, branch_near, qkv_near, text_near, rows_near, gain_near, up_kept
     )
 
     gate_grad = plan.by_rep(plan.total(gate_kept, gate_moved))
-    gate_grad, up_moved, branch_near = fence(gate_grad, up_moved, branch_near)
+    gate_grad, branch_far, down_moved = fence(gate_grad, pair(branch_far), down_moved)
     gate_parts = plan.reduce(gate_grad)
-    branch_far = swap(branch_near[0], "mid")
-    up_moved = plan.move(up_moved)
-    back_weights = (qkv_rank, out_rank, tables)
-    qkv_near, key_near, value_near, rows_near, gain_near = attend_back(
-        scalars[0], branch_near, kept_near, *back_weights
-    )
-    up_kept = plan.product_kept(inputs, up_rows)
-    gate_parts, branch_far, up_moved, qkv_near, key_near, value_near, rows_near, gain_near, up_kept = fence(
-        gate_parts, branch_far, up_moved, qkv_near, key_near, value_near, rows_near, gain_near, up_kept
-    )
-
-    branch_far = pair(branch_far)
+    down_moved = plan.move(down_moved)
+    branch_far, qkv_far, text_far, rows_far, gain_far = attend_back(
+        scalars[1], branch_far, kept_far, *back_weights
+    )
+    down_kept = plan.product_kept(hidden_rows, results, hidden_first)
+    captions, normed_rows = (captions_near, captions_far), (normed_near, normed_far)
+    text_rows, qkv_rows, branches = (text_near, text_far), (qkv_near, qkv_far), (branch_near, branch_far)
+    text_moved = plan.product_moved(captions, text_rows)
+    gate_parts, up_moved, text_rows, qkv_rows, branches, rows_far, gain_far, down_kept, text_moved = fence(
+        gate_parts, up_moved, text_rows, qkv_rows, branches, rows_far, gain_far, down_kept, text_moved
+    )
+
+    across = settle(rows_far).astype(bf16)
     up_grad = plan.by_rep(plan.total(up_kept, up_moved))
-    up_grad, branch_far, down_moved = fence(up_grad, branch_far, down_moved)
+    across, up_grad, text_moved, text_rows, qkv_rows, hidden_rows = fence(
+        across, up_grad, text_moved, text_rows, qkv_rows, hidden_rows
+    )
+    text_moved = plan.move(text_moved)
     up_parts = plan.reduce(up_grad)
-    down_moved = plan.move(down_moved)
-    qkv_far, key_far, value_far, rows_far, gain_far = attend_back(
-        scalars[1], branch_far, kept_far, *back_weights
-    )
-    qkv_rows, key_rows, value_rows = (qkv_near, qkv_far), (key_near, key_far), (value_near, value_far)
-    all_captions, all_normed = (*captions_near, *captions_far), (*normed_near, *normed_far)
-    key_moved = plan.product_moved(all_captions, key_rows)
-    down_kept = plan.product_kept(hidden_rows, results, hidden_first)
-    up_parts, down_moved, key_moved, down_kept, qkv_rows, value_rows, rows_far, gain_far = fence(
-        up_parts, down_moved, key_moved, down_kept, qkv_rows, value_rows, rows_far, gain_far
-    )
-
-    across = settle(rows_far).astype(bf16)
+    arrived = settle_move(across)
     down_grad = plan.total(down_kept, down_moved).reshape(rep_count, -1, D)
-    across, down_grad, key_moved, qkv_rows, value_rows = fence(
-        across, down_grad, key_moved, qkv_rows, value_rows
-    )
     down_parts = plan.reduce(down_grad)
-    arrived = settle_move(across)
-    key_moved = plan.move(key_moved)
-    value_moved = plan.product_moved(all_captions, value_rows)
-    key_kept = plan.product_kept(all_captions, key_rows)
-    qkv_moved = plan.product_moved(all_normed, qkv_rows)
-    value_kept = plan.product_kept(all_captions, value_rows)
-    down_parts, arrived, key_moved, value_moved, key_kept, qkv_moved, value_kept, rows_near = fence(
-        down_parts, arrived, key_moved, value_moved, key_kept, qkv_moved, value_kept, rows_near
-    )
-
-    key_grad = plan.by_rep(plan.total(key_kept, key_moved))
-    key_grad, value_moved, qkv_moved, hidden_rows = fence(key_grad, value_moved, qkv_moved, hidden_rows)
-    key_parts = plan.reduce(key_grad)
-    value_moved = plan.move(value_moved)
-    qkv_kept = plan.product_kept(all_normed, qkv_rows)
+    qkv_moved = plan.product_moved(normed_rows, qkv_rows)
+    text_kept = plan.product_kept(captions, text_rows)
+    qkv_kept = plan.product_kept(normed_rows, qkv_rows)
     mixed_rows = [plan.ordered(kept[6]) for kept in (kept_near, kept_far)]
-    branches = (*branch_near, *branch_far)
     if plan.aligned:
         out_halves = [
-            product([rows[:, lanes] for rows in mixed_rows], branches, 0, rank_width // 2, bf16)
+            product([side[:, lanes] for side in mixed_rows], branches, 0, rank_width // 2, bf16)
             for lanes in (slice(0, rank_width // 2), slice(rank_width // 2, None))
         ]
-    result_far = [dot(rows, down_rank) for rows in jnp.split(hidden_rows[1], 2)]
-    across = settle((result_far[0], result_far[1].astype(bf16))).astype(bf16)
+    else:
+        out_halves = []
+    result_far = [dot(side, down_rank) for side in jnp.split(hidden_rows[1], 2)]
+    result_across = settle((result_far[0], result_far[1].astype(bf16))).astype(bf16)
     grad_normed = plan.ordered(settle(rows_near) + arrived)
-    key_parts, value_moved, qkv_kept, across, grad_normed = fence(
-        key_parts, value_moved, qkv_kept, across, grad_normed
-    )
-
-    value_grad = plan.by_rep(plan.total(value_kept, value_moved))
-    value_grad, qkv_moved, across = fence(value_grad, qkv_moved, across)
-    value_parts = plan.reduce(value_grad)
+    text_moved, up_parts, down_parts, grad_normed, qkv_moved, text_kept, qkv_kept, out_halves, result_across = fence(
+        text_moved, up_parts, down_parts, grad_normed, qkv_moved, text_kept, qkv_kept, out_halves, result_across
+    )
+
     qkv_moved = plan.move(qkv_moved)
-    result = settle_move(across)
+    result = settle_move(result_across)
     if plan.aligned:
         if hi_count == 2:
             out_kept, out_moved = out_halves[0].astype(f32), swap(out_halves[1], "hi")
         else:
             out_kept, out_moved = None, plan.move(jnp.concatenate(out_halves))
-    result_near = [dot(rows, down_rank) for rows in jnp.split(hidden_rows[0], 2)]
+    text_grad = plan.by_rep(plan.total(text_kept, text_moved))
+    text_parts = plan.reduce(text_grad)
+    result_near = [dot(side, down_rank) for side in jnp.split(hidden_rows[0], 2)]
     result = result + settle((result_near[0], result_near[1].astype(bf16)))
     result = result.reshape(item_count, item_len, D)
     layer_out = (middle + mlp_gate * result).astype(bf16).reshape(row_count, D)
@@ -959,8 +959,8 @@
         out_grad = product(mixed_rows, branches, 0, rank_width, bf16)
         placed = (out_grad[None] * at).reshape(D, D)
         out_weight_grad = lax.psum_scatter(placed, AXES, scatter_dimension=0, tiled=True).astype(f32)
-    value_parts, qkv_grad, grad_mlp_gate, grad_scale_attn, grad_attn_gain = fence(
-        value_parts, qkv_grad, grad_mlp_gate, grad_scale_attn, grad_attn_gain
+    text_parts, qkv_grad, grad_mlp_gate, grad_scale_attn, grad_attn_gain = fence(
+        text_parts, qkv_grad, grad_mlp_gate, grad_scale_attn, grad_attn_gain
     )
     qkv_parts = plan.reduce(qkv_grad)
     if plan.aligned:
@@ -991,9 +991,7 @@
     gate_up_weight_grad = whole(
         jnp.concatenate([gate_parts, up_parts], axis=-1), gate_up_weight, 2, hi_count
     )
-    text_weight_grad = whole(
-        jnp.concatenate([key_parts, value_parts], axis=-1), text_weight, 2, plan.head_groups
-    )
+    text_weight_grad = whole(text_parts, text_weight, 2, plan.head_groups)
     qkv_weight_grad = whole(qkv_parts, qkv_weight, 3, plan.head_groups)
     down_weight_grad = down_parts.astype(f32)
     return (

time: 871 us -> 875 us (level)
  blocking collectives: 42 us -> 15.1 us
  Pallas kernels: 280 us -> 254 us
  waiting for transfers between devices: 258 us -> 284 us
  local copies, waits for them, and re-layouts: 98.2 us -> 115 us
    all_to_all x1, blocking collectives: 42 us -> 15.1 us  [trade_ranks(): return lax.all_to_all(block, ('mid', 'core'), 0, 0, tiled=True)]
    all_gather x6, waiting for transfers between devices: 12.6 us -> 34.1 us  [z_gather(): return lax.all_gather(block.reshape(-1, block.shape[-1]), 'rep', tiled=True)]
    pallas_call x2, Pallas kernels: 65.1 us -> 50.1 us  [attend(): pl.pallas_call(attend_kernel, grid_spec=pltpu.PrefetchScalarGridSpec(num_...]
    pallas_call x14 -> x12, Pallas kernels: 101 us -> 89.6 us  [product(): pl.pallas_call(kernel, grid_spec=pltpu.PrefetchScalarGridSpec(num_scalar_...]
    all_to_all x1, waiting for transfers between devices: 39.8 us -> 28.7 us  [local(): lax.all_to_all(partial, AXES, 0, 0, tiled=True).astype(f32)]
    mul x8, local copies, waits for them, and re-layouts: 0.67 us -> 10.9 us  [place_lanes(): return (view * at).reshape(-1)]
    ppermute x40 -> x39, waiting for transfers between devices: 143 us -> 153 us  [swap(): return lax.ppermute(block, axis, [(at, at ^ step) for at in range(count)])]
    ppermute x40 -> x39, starting transfers between devices: 22.7 us -> 27.8 us  [swap(): return lax.ppermute(block, axis, [(at, at ^ step) for at in range(count)])]
  transfers between devices with their start and end apart: 60 -> 58, of which waited for: 24 -> 28; matrix products, arithmetic and copies ran while one was open for 20% -> 22% of each run, Pallas kernels for 30% -> 26%
where the time goes in v5:
time: 875 us; the launch traced here: 864 us
  waiting for transfers between devices  284 us (32%)
  Pallas kernels  254 us (29%)
  local copies, waits for them, and re-layouts  115 us (13%)
  other arithmetic  90.6 us (10%)
  starting transfers between devices  63 us (7%)
  matrix products  26.8 us (3%)
  between operations  15.6 us (2%)
  blocking collectives  15.1 us (2%)
    ppermute x39, waiting for transfers between devices, swap(): return lax.ppermute(block, axis, [(at, at ^ step) for at in range(count)])  153 us
    pallas_call x12, Pallas kernels, product(): pl.pallas_call(kernel, grid_spec=pltpu.PrefetchScalarGridSpec(num_scalar_...  89.6 us
    pallas_call x2, Pallas kernels, attend_back(): pl.pallas_call(attend_back_kernel, grid_spec=pltpu.PrefetchScalarGridSpec...  62.6 us
    pallas_call x2, Pallas kernels, feed(): pl.pallas_call(feed_kernel, grid=(steps,), in_specs=pair_specs(rows, step...  51.9 us
    pallas_call x2, Pallas kernels, attend(): pl.pallas_call(attend_kernel, grid_spec=pltpu.PrefetchScalarGridSpec(num_...  50.1 us
    all_to_all x1, waiting for transfers between devices, local(): lax.all_to_all(jnp.concatenate([modulations, gain_blocks], axis=1), AXES,...  34.9 us
    all_gather x6, waiting for transfers between devices, z_gather(): return lax.all_gather(block.reshape(-1, block.shape[-1]), 'rep', tiled=True)  34.1 us
    all_to_all x5, waiting for transfers between devices, trade_ranks(): return lax.all_to_all(block, ('mid', 'core'), 0, 0, tiled=True)  29.8 us
  transfers between devices with their start and end apart: 58, of which 28 were waited for; matrix products, arithmetic and copies ran while one was open for 22% of the time, Pallas kernels for 26%

profile of v5, /device:TPU:8, one launch (start us, length us, event | category | flops | bytes accessed | tf_op | source)
XLA Modules:
  0.0 864.5 jit_solution(2071082794085806863)
XLA Ops:
  47.3 8.8 %all-to-all-done.1 = bf16[4,128,768]{1,2,0:T(8,128)(2,1)S(1)} async-done(((bf16[4,128,768]{1,2,0:T(8,128)(2,1)}), bf16[4,128,768]{1,2,0:T(8,128)(2,1)S(1)}, u32[]{:S(2)}, u32[]{:S(2)}) %all-to-all-start.1) | async-done | bytes 786464 | tf_op jit(solution)/shard_map/all_to_all | solution.py:569
  59.6 15.1 %all_to_all.59 = bf16[4,48,2048]{2,1,0:T(8,128)(2,1)S(1)} all-to-all(bf16[4,48,2048]{2,1,0:T(8,128)(2,1)} %reshape.872), channel_id=1, replica_groups=mesh['hi'=2,'mid'=2,'core'=2,'rep'=4] {'mid','core'}, dimensions={0} | all-to-all | bytes 1572864 | tf_op jit(solution)/shard_map/all_to_all | solution.py:569
  90.8 28.7 %all-to-all-done.3 = bf16[32,2,6144]{2,1,0:T(2,128)(2,1)S(1)} async-done(((bf16[32,2,6144]{2,1,0:T(2,128)(2,1)}), bf16[32,2,6144]{2,1,0:T(2,128)(2,1)S(1)}, u32[]{:S(2)}, u32[]{:S(2)}) %all-to-all-start.3) | async-done | bytes 786464 | tf_op jit(solution)/shard_map/all_to_all | solution.py:770
  140.5 17.8 %all-gather.17.cloned.1.call-done = bf16[2048,384]{1,0:T(8,128)(2,1)} async-done(((bf16[512,384]{1,0:T(8,128)(2,1)}), bf16[2048,384]{1,0:T(8,128)(2,1)}) %all-gather.17.cloned.1.call-update) | async-done | bytes 1572880 | tf_op jit(solution)/shard_map/all_gather | solution.py:712
  158.2 19.1 %collective-permute-done.3 = bf16[1024,1152]{1,0:T(8,128)(2,1)} collective-permute-done((bf16[1024,1152]{1,0:T(8,128)(2,1)}, bf16[1024,1152]{1,0:T(8,128)(2,1)}, u32[]{:S(2)}, u32[]{:S(2)}) %collective-permute-start.3) | collective-permute-done | bytes 2359328 | tf_op jit(solution)/shard_map/ppermute | solution.py:536
  180.0 16.3 %all-gather.15.cloned.1.call-done = bf16[2048,384]{1,0:T(8,128)(2,1)} async-done(((bf16[512,384]{1,0:T(8,128)(2,1)}), bf16[2048,384]{1,0:T(8,128)(2,1)}) %all-gather.15.cloned.1.call-update) | async-done | bytes 1572880 | tf_op jit(solution)/shard_map/all_gather | solution.py:712
  196.2 18.4 %collective-permute-done.6 = bf16[2048,384]{1,0:T(8,128)(2,1)} collective-permute-done((bf16[2048,384]{1,0:T(8,128)(2,1)}, bf16[2048,384]{1,0:T(8,128)(2,1)}, u32[]{:S(2)}, u32[]{:S(2)}) %collective-permute-start.6) | collective-permute-done | bytes 1572896 | tf_op jit(solution)/shard_map/ppermute | solution.py:536
  235.8 12.6 %collective-permute-done.10.result_ref = bf16[512,1536]{1,0:T(8,128)(2,1)} collective-permute-done((bf16[512,1536]{1,0:T(8,128)(2,1)}, bf16[512,1536]{1,0:T(8,128)(2,1)}, u32[]{:S(2)}, u32[]{:S(2)}) %collective-permute-start.10) | collective-permute-done | bytes 1572896 | tf_op jit(solution)/shard_map/ppermute | solution.py:536
  262.9 25.2 %attend.2 = (bf16[1024,1536]{1,0:T(8,128)(2,1)}, bf16[512,4096]{1,0:T(8,128)(2,1)}, f32[1024,1152]{1,0:T(8,128)}, f32[512,384]{1,0:T(8,128)}, f32[512,384]{1,0:T...) custom-call(s32[4]{0:T(128)} %maximum_convert_fusion.kind_ref, ...), custom_call_target="tpu_custom_call" | custom-call | tf_op jit(solution)/shard_map/attend/pallas_call | solution.py:359
  306.2 25.0 %attend.3 = (bf16[1024,1536]{1,0:T(8,128)(2,1)}, bf16[512,4096]{1,0:T(8,128)(2,1)}, f32[1024,1152]{1,0:T(8,128)}, f32[512,384]{1,0:T(8,128)}, f32[512,384]{1,0:T...) custom-call(s32[4]{0:T(128)} %maximum_convert_fusion.2.kind_ref, ...), custom_call_target="tpu_custom_call" | custom-call | tf_op jit(solution)/shard_map/attend/pallas_call | solution.py:359
  353.4 26.1 %feed.2 = (bf16[1024,1536]{1,0:T(8,128)(2,1)}, bf16[1024,1536]{1,0:T(8,128)(2,1)}, bf16[1024,1024]{1,0:T(8,128)(2,1)}, bf16[1024,1024]{1,0:T(8,128)(2,1)}, bf16[...) custom-call(bf16[512,1536]{1,0:T(8,128)(2,1)} %copy-done.18, ...), custom_call_target="tpu_custom_call" | custom-call | tf_op jit(solution)/shard_map/feed/pallas_call | solution.py:521
  391.5 25.8 %feed.3 = (bf16[1024,1536]{1,0:T(8,128)(2,1)}, bf16[1024,1536]{1,0:T(8,128)(2,1)}, bf16[1024,1024]{1,0:T(8,128)(2,1)}, bf16[1024,1024]{1,0:T(8,128)(2,1)}, bf16[...) custom-call(bf16[512,1536]{1,0:T(8,128)(2,1)} %collective-permute-done.18.rows_ref, ...), custom_call_target="tpu_custom_call" | custom-call | tf_op jit(solution)/shard_map/feed/pallas_call | solution.py:521
  448.9 8.0 product.14
  483.1 31.4 %attend_back.2 = (bf16[1024,1536]{1,0:T(8,128)(2,1)}, bf16[1024,1152]{1,0:T(8,128)(2,1)}, bf16[512,768]{1,0:T(8,128)(2,1)}, f32[512,1536]{1,0:T(8,128)}, bf16[512,1536]{1,0:T(8,128)(2,1)}, /*index=5*/f32[4,384]{1,0:T(4,128)}) custom-call(s32[4]{0:T(128)} %maximum_convert_fusion.2.kind_ref, s32[4]{0:T(128)} %maximum_convert_fusion.3.len_ref, ...), custom_call_target="tpu_custom_call" | custom-call | tf_op jit(solution)/shard_map/attend_back/pallas_call | solution.py:389
  521.0 8.6 product.17
  529.6 31.2 %attend_back.3 = (bf16[1024,1536]{1,0:T(8,128)(2,1)}, bf16[1024,1152]{1,0:T(8,128)(2,1)}, bf16[512,768]{1,0:T(8,128)(2,1)}, f32[512,1536]{1,0:T(8,128)}, bf16[512,1536]{1,0:T(8,128)(2,1)}, /*index=5*/f32[4,384]{1,0:T(4,128)}) custom-call(s32[4]{0:T(128)} %maximum_convert_fusion.kind_ref, s32[4]{0:T(128)} %maximum_convert_fusion.1.len_ref, ...), custom_call_target="tpu_custom_call" | custom-call | tf_op jit(solution)/shard_map/attend_back/pallas_call | solution.py:389
  568.0 21.8 %collective-permute-done.31 = bf16[512,1536]{1,0:T(8,128)(2,1)} collective-permute-done((bf16[512,1536]{1,0:T(8,128)(2,1)}, bf16[512,1536]{1,0:T(8,128)(2,1)}, u32[]{:S(2)}, u32[]{:S(2)}) %collective-permute-start.31) | collective-permute-done | bytes 1572896 | tf_op jit(solution)/shard_map/ppermute | solution.py:536
  624.6 8.7 %product.21 = f32[768,1152]{1,0:T(8,128)} custom-call(s32[1]{0:T(128)} %constant.580.clone.1.first_ref, bf16[1024,1536]{1,0:T(8,128)(2,1)} %get-tuple-element.415.refs_0_, bf16[1024,1536]{1,0:T(8,128)(2,1)} %get-tuple-element.416.refs_1_, bf16[1024,1152]{1,0:T(8,128)(2,1)} %get-tuple-element.417.refs_2_, bf16[1024,1152]{1,0:T(8,128)(2,1)} %get-tuple-element.418.refs_3_), custom_call_target="tpu_custom_call" | custom-call | tf_op jit(solution)/shard_map/product/pallas_call | solution.py:441
  633.3 8.4 product.19
  660.7 15.6 %collective-permute-done.30 = bf16[2048,768]{1,0:T(8,128)(2,1)} collective-permute-done((bf16[2048,768]{1,0:T(8,128)(2,1)}, bf16[2048,768]{1,0:T(8,128)(2,1)}, u32[]{:S(2)}, u32[]{:S(2)}) %collective-permute-start.30) | collective-permute-done | bytes 3145760 | tf_op jit(solution)/shard_map/ppermute | solution.py:536
  727.0 11.7 %fusion.6 = (f32[512,1536]{1,0:T(8,128)}, bf16[512,1536]{1,0:T(8,128)(2,1)}, f32[512,1536]{1,0:T(8,128)S(1)}) fusion(bf16[512,1536]{1,0:T(8,128)(2,1)} %param.15, f32[512,1536]{1,0:T(8,128)} %maximum_select_fusion.1, f32[512]{0:T(512)S(1)} %multiply_multiply_fusion.1, f32[2,1536]{1,0:T(2,128)S(1)} %copy-done.55, f32[1536]{0:T(1024)S(1)} %copy-done.49, ...), kind=kOutput, calls=%fused_computation.27 | convolution fusion | flops 1628700672 | bytes 27844608 | tf_op jit(solution)/shard_map/dot_general | solution.py:59
  742.2 20.2 %collective-permute-done.37 = bf16[768,1152]{1,0:T(8,128)(2,1)} collective-permute-done((bf16[768,1152]{1,0:T(8,128)(2,1)}, bf16[768,1152]{1,0:T(8,128)(2,1)}, u32[]{:S(2)}, u32[]{:S(2)}) %collective-permute-start.37) | collective-permute-done | bytes 1769504 | tf_op jit(solution)/shard_map/ppermute | solution.py:536
  776.3 8.4 all-to-all-done.7
  798.5 34.9 %all-to-all-done.5 = bf16[32,2,6288]{2,1,0:T(2,128)(2,1)} async-done(((bf16[32,2,6288]{2,1,0:T(2,128)(2,1)}), bf16[32,2,6288]{2,1,0:T(2,128)(2,1)}, u32[]{:S(2)}, u32[]{:S(2)}) %all-to-all-start.5) | async-done | bytes 804896 | tf_op jit(solution)/shard_map/all_to_all | solution.py:981
  (483 shorter events, 401.3 us)
Async XLA Ops:
  7.2 49.0 %all-gather.7.cloned.1.call-start = ((), (), s32[]{:S(2)}) async-start(), calls=%async_computation.14 | async-start | bytes 1966080 | tf_op jit(solution)/shard_map/all_gather | solution.py:712
  44.5 79.1 %all-gather.9.cloned.1.call-start = ((), (), s32[]{:S(2)}) async-start(), calls=%async_computation.15 | async-start | bytes 2949120 | tf_op jit(solution)/shard_map/all_gather | solution.py:712
  56.2 102.0 %all-gather.17.cloned.1.call-start = ((), (), s32[]{:S(2)}) async-start(), calls=%async_computation.19 | async-start | bytes 1966080 | tf_op jit(solution)/shard_map/all_gather | solution.py:712
  74.8 44.7 %all-to-all-start.3 = ((bf16[32,2,6144]{2,1,0:T(2,128)(2,1)}), bf16[32,2,6144]{2,1,0:T(2,128)(2,1)S(1)}, u32[]{:S(2)}, u32[]{:S(2)}) async-start(bf16[32,2,6144]{2,1,0:T(2,128)(2,1)} %reshape.870), calls=%async_computation.3 | async-start | bytes 1572864 | tf_op jit(solution)/shard_map/all_to_all | solution.py:770
  78.8 117.4 %all-gather.15.cloned.1.call-start = ((), (), s32[]{:S(2)}) async-start(), calls=%async_computation.18 | async-start | bytes 1966080 | tf_op jit(solution)/shard_map/all_gather | solution.py:712
  78.9 44.8 %collective-permute-start.1 = (bf16[512,1536]{1,0:T(8,128)(2,1)}, bf16[512,1536]{1,0:T(8,128)(2,1)}, u32[]{:S(2)}, u32[]{:S(2)}) collective-permute-start(bf16[512,1536]{1,0:T(8,128)(2,1)} %all-gather.7.cloned.1.call-done), channel_id=1, source_target_pairs={{0,16},{16,0},{1,17},{17,1},{2,18},{18,2},{3,19},{19,3},{4,20},{20... | collective-permute-start | bytes 4718600 | tf_op jit(solution)/shard_map/ppermute | solution.py:536
  88.3 52.2 %collective-permute-start.2 = (bf16[256,4096]{1,0:T(8,128)(2,1)}, bf16[256,4096]{1,0:T(8,128)(2,1)}, u32[]{:S(2)}, u32[]{:S(2)}) collective-permute-start(bf16[256,4096]{1,0:T(8,128)(2,1)} %maximum_select_fusion.2.caption_ref), channel_id=1, source_target_pairs={{0,8},{8,0},{1,9},{9,1},{2,10},{10,2},{3,11},{11,3},{4,12},{12,4},... | collective-permute-start | bytes 6291464 | tf_op jit(solution)/shard_map/ppermute | solution.py:536
  90.7 145.1 %all-gather.13.cloned.1.call-start = ((), (), s32[]{:S(2)}) async-start(), calls=%async_computation.17 | async-start | bytes 1966080 | tf_op jit(solution)/shard_map/all_gather | solution.py:712
  124.3 53.1 %collective-permute-start.3 = (bf16[1024,1152]{1,0:T(8,128)(2,1)}, bf16[1024,1152]{1,0:T(8,128)(2,1)}, u32[]{:S(2)}, u32[]{:S(2)}) collective-permute-start(bf16[1024,1152]{1,0:T(8,128)(2,1)} %all-gather.9.cloned.1.call-done), channel_id=1, source_target_pairs={{0,16},{16,0},{1,17},{17,1},{2,18},{18,2},{3,19},{19,3},{4,20},{20... | collective-permute-start | bytes 7077896 | tf_op jit(solution)/shard_map/ppermute | solution.py:536
  177.4 110.7 %all-gather.11.cloned.1.call-start = ((), (), s32[]{:S(2)}) async-start(), calls=%async_computation.16 | async-start | bytes 1966080 | tf_op jit(solution)/shard_map/all_gather | solution.py:712
  179.8 68.6 %collective-permute-start.10 = (bf16[512,1536]{1,0:T(8,128)(2,1)}, bf16[512,1536]{1,0:T(8,128)(2,1)}, u32[]{:S(2)}, u32[]{:S(2)}) collective-permute-start(bf16[512,1536]{1,0:T(8,128)(2,1)} %fusion.12.result_ref), channel_id=1, source_target_pairs={{0,8},{8,0},{1,9},{9,1},{2,10},{10,2},{3,11},{11,3},{4,12},{12,4},... | collective-permute-start | bytes 4718600 | tf_op jit(solution)/shard_map/ppermute | solution.py:536
  216.9 351.1 %reduce-scatter.6.cloned.1.call-start = ((), (), s32[]{:S(2)}) async-start(), calls=%async_computation.20 | async-start | bytes 1966080 | tf_op jit(solution)/shard_map/reduce_scatter | solution.py:664
  472.4 42.1 %collective-permute-start.25 = (bf16[768,1024]{1,0:T(8,128)(2,1)}, bf16[768,1024]{1,0:T(8,128)(2,1)}, u32[]{:S(2)}, u32[]{:S(2)}) collective-permute-start(bf16[768,1024]{1,0:T(8,128)(2,1)} %product.12), channel_id=1, source_target_pairs={{0,16},{16,0},{1,17},{17,1},{2,18},{18,2},{3,19},{19,3},{4,20},{20... | collective-permute-start | bytes 4718600 | tf_op jit(solution)/shard_map/ppermute | solution.py:536
  518.9 141.9 %reduce-scatter.10.cloned.1.call-start = ((), (), s32[]{:S(2)}) async-start(), calls=%async_computation.22 | async-start | bytes 1966080 | tf_op jit(solution)/shard_map/reduce_scatter | solution.py:664
  518.9 49.1 %collective-permute-start.28 = (bf16[768,1024]{1,0:T(8,128)(2,1)}, bf16[768,1024]{1,0:T(8,128)(2,1)}, u32[]{:S(2)}, u32[]{:S(2)}) collective-permute-start(bf16[768,1024]{1,0:T(8,128)(2,1)} %product.13), channel_id=1, source_target_pairs={{0,16},{16,0},{1,17},{17,1},{2,18},{18,2},{3,19},{19,3},{4,20},{20... | collective-permute-start | bytes 4718600 | tf_op jit(solution)/shard_map/ppermute | solution.py:536
  519.6 70.2 %collective-permute-start.31 = (bf16[512,1536]{1,0:T(8,128)(2,1)}, bf16[512,1536]{1,0:T(8,128)(2,1)}, u32[]{:S(2)}, u32[]{:S(2)}) collective-permute-start(bf16[512,1536]{1,0:T(8,128)(2,1)} %product.14), channel_id=1, source_target_pairs={{0,16},{16,0},{1,17},{17,1},{2,18},{18,2},{3,19},{19,3},{4,20},{20... | collective-permute-start | bytes 4718600 | tf_op jit(solution)/shard_map/ppermute | solution.py:536
  593.8 82.6 %reduce-scatter.8.cloned.1.call-start = ((), (), s32[]{:S(2)}) async-start(), calls=%async_computation.21 | async-start | bytes 1966080 | tf_op jit(solution)/shard_map/reduce_scatter | solution.py:664
  595.4 54.2 %collective-permute-start.32 = (bf16[512,1536]{1,0:T(8,128)(2,1)}, bf16[512,1536]{1,0:T(8,128)(2,1)}, u32[]{:S(2)}, u32[]{:S(2)}) collective-permute-start(bf16[512,1536]{1,0:T(8,128)(2,1)} %get-tuple-element.413), channel_id=1, source_target_pairs={{0,4},{4,0},{1,5},{5,1},{2,6},{6,2},{3,7},{7,3},{8,12},{12,8},{9,1... | collective-permute-start | bytes 4718600 | tf_op jit(solution)/shard_map/ppermute | solution.py:536
  603.0 46.5 %collective-permute-start.33 = (bf16[512,1536]{1,0:T(8,128)(2,1)}, bf16[512,1536]{1,0:T(8,128)(2,1)}, u32[]{:S(2)}, u32[]{:S(2)}) collective-permute-start(bf16[512,1536]{1,0:T(8,128)(2,1)} %add_convert_fusion.4), channel_id=1, source_target_pairs={{0,8},{8,0},{1,9},{9,1},{2,10},{10,2},{3,11},{11,3},{4,12},{12,4},... | collective-permute-start | bytes 4718600 | tf_op jit(solution)/shard_map/ppermute | solution.py:536
  606.2 70.1 %collective-permute-start.30 = (bf16[2048,768]{1,0:T(8,128)(2,1)}, bf16[2048,768]{1,0:T(8,128)(2,1)}, u32[]{:S(2)}, u32[]{:S(2)}) collective-permute-start(bf16[2048,768]{1,0:T(8,128)(2,1)} %product.18), channel_id=1, source_target_pairs={{0,16},{16,0},{1,17},{17,1},{2,18},{18,2},{3,19},{19,3},{4,20},{20... | collective-permute-start | bytes 9437192 | tf_op jit(solution)/shard_map/ppermute | solution.py:536
  606.6 160.3 %reduce-scatter.12.cloned.1.call-start = ((), (), s32[]{:S(2)}) async-start(), calls=%async_computation.23 | async-start | bytes 3932160 | tf_op jit(solution)/shard_map/reduce_scatter | solution.py:664
  712.6 57.0 %all-to-all-start.8 = ((bf16[4,48,2048]{2,1,0:T(8,128)(2,1)}), bf16[4,48,2048]{2,1,0:T(8,128)(2,1)}, u32[]{:S(2)}, u32[]{:S(2)}) async-start(bf16[4,48,2048]{2,1,0:T(8,128)(2,1)} %bitcast.257), calls=%async_computation.13 | async-start | bytes 1572864 | tf_op jit(solution)/shard_map/all_to_all | solution.py:569
  717.0 124.2 %reduce-scatter.14.cloned.1.call-start = ((), (), s32[]{:S(2)}) async-start(), calls=%async_computation.24 | async-start | bytes 2949120 | tf_op jit(solution)/shard_map/reduce_scatter | solution.py:664
  784.7 48.6 %all-to-all-start.5 = ((bf16[32,2,6288]{2,1,0:T(2,128)(2,1)}), bf16[32,2,6288]{2,1,0:T(2,128)(2,1)}, u32[]{:S(2)}, u32[]{:S(2)}) async-start(bf16[32,2,6288]{2,1,0:T(2,128)(2,1)} %reshape.965), calls=%async_computation.9 | async-start | bytes 1638400 | tf_op jit(solution)/shard_map/all_to_all | solution.py:981
  (120 other events, 1897.2 us)
Sparse Core Ops, SparseCore 0:
  9.6 37.7 all-gather.6
  56.4 61.2 all-gather.8
  119.8 38.3 all-gather.16
  160.2 35.9 all-gather.14
  198.2 35.9 all-gather.12
  235.6 35.9 all-gather.10
  519.0 33.5 reduce-scatter.5
  593.9 33.3 reduce-scatter.9
  629.6 34.2 reduce-scatter.7
  682.8 59.9 reduce-scatter.11
  769.7 65.6 reduce-scatter.13

commit v6 on v5

--- a/solution.py
+++ b/solution.py
@@ -719,8 +719,6 @@
     else:
         out_whole = lax.all_gather(out_weight, AXES, axis=0, tiled=True)
         out_rank = pick(out_whole.reshape(RANKS, rank_width, D), plan.rank)
-    text_mine = trade_ranks(plan.by_rank(text_weight, 2, plan.head_groups))
-    captions_near = pair(plan.ordered(caption.reshape(-1, TEXT_DIM)))
 
     head = condition.reshape(item_count, devices, rows)
     head = jnp.transpose(head, (1, 0, 2)).reshape(devices, -1)
@@ -758,18 +756,20 @@
     tables = (head_gains, cosine, sine)
     scalars = list(zip(kinds_sides, lengths_sides, strict=True))
 
-    partial = dot(activated_mine, ada_weight).astype(bf16).reshape(devices, item_count, 4 * D)
-    text_key_mine, text_value_mine = text_mine[..., :rank_width], text_mine[..., rank_width:]
-    down_z, qkv_mine, text_key_mine, text_value_mine, captions_near, partial = fence(
-        down_z, qkv_mine, text_key_mine, text_value_mine, captions_near, partial
+    down_z, qkv_mine, text_weight, activated_mine = fence(
+        down_z, qkv_mine, text_weight, activated_mine
     )
     qkv_z = z_gather(qkv_mine)
     down_rank = plan.across_hi(down_z)
+    text_mine = trade_ranks(plan.by_rank(text_weight, 2, plan.head_groups))
+    captions_near = pair(plan.ordered(caption.reshape(-1, TEXT_DIM)))
+    partial = dot(activated_mine, ada_weight).astype(bf16).reshape(devices, item_count, 4 * D)
     gate_up_mine = trade_ranks(plan.by_rank(gate_up_weight, 2, hi_count))
+    modulation = jnp.sum(lax.all_to_all(partial, AXES, 0, 0, tiled=True).astype(f32), axis=0)
+    text_key_mine, text_value_mine = text_mine[..., :rank_width], text_mine[..., rank_width:]
     gate_mine, up_mine = gate_up_mine[..., :feed_width], gate_up_mine[..., feed_width:]
-    modulation = jnp.sum(lax.all_to_all(partial, AXES, 0, 0, tiled=True).astype(f32), axis=0)
-    qkv_z, down_rank, modulation, gate_mine, up_mine = fence(
-        qkv_z, down_rank, modulation, gate_mine, up_mine
+    qkv_z, down_rank, modulation, text_key_mine, text_value_mine, gate_mine, up_mine, captions_near = fence(
+        qkv_z, down_rank, modulation, text_key_mine, text_value_mine, gate_mine, up_mine, captions_near
     )
 
     scale_attn, gate_attn, scale_mlp, gate_mlp = jnp.split(modulation, 4, axis=1)
@@ -853,12 +853,15 @@
     input_far, result_far, hidden_far, gate_far, up_far, partial_far = feed(
         pair(input_far), result_far, *feed_weights
     )
-    across = settle(partial_far).astype(bf16)
     inputs, results = (input_near, input_far), (result_near, result_far)
     gate_rows, up_rows, hidden_rows = (gate_near, gate_far), (up_near, up_far), (hidden_near, hidden_far)
-    across, gate_rows, up_rows, hidden_rows = fence(across, gate_rows, up_rows, hidden_rows)
+    across = settle(partial_far).astype(bf16)
+    gate_moved = plan.product_moved(inputs, gate_rows)
+    across, gate_moved, gate_rows, up_rows, hidden_rows = fence(
+        across, gate_moved, gate_rows, up_rows, hidden_rows
+    )
     arrived = settle_move(across)
-    gate_moved = plan.product_moved(inputs, gate_rows)
+    gate_moved = plan.move(gate_moved)
     up_moved = plan.product_moved(inputs, up_rows)
     hidden_first = hi_at * (feed_width // 2)
     down_moved = plan.product_moved(hidden_rows, results, feed_width // 2 - hidden_first)
@@ -867,7 +870,9 @@
         arrived, gate_moved, up_moved, down_moved, gate_kept, partial_near
     )
 
-    gate_moved, up_moved = plan.move(gate_moved), plan.move(up_moved)
+    up_moved = plan.move(up_moved)
+    gate_grad = plan.by_rep(plan.total(gate_kept, gate_moved))
+    gate_parts = plan.reduce(gate_grad)
     grad_mlp_input = plan.ordered(settle(partial_near) + arrived)
     _, pull_mlp_norm = jax.vjp(modulate, middle, gain_rows[4], scale_mlp)
     grad_middle_norm, grad_mlp_gain, grad_scale_mlp = pull_mlp_norm(
@@ -876,7 +881,7 @@
     grad_middle = grad_top + grad_middle_norm
     grad_attn_gate = jnp.sum(grad_middle * branch, axis=1) * (1.0 - jnp.tanh(gate_attn) ** 2)
     grad_branch = (attn_gate * grad_middle).astype(bf16).reshape(row_count, D)
-    (grad_branch,) = fence(grad_branch)
+    grad_branch, up_rows = fence(grad_branch, up_rows)
 
     branch_far = swap(grad_branch, "mid")
     back_weights = (qkv_rank, out_rank, tables)
@@ -884,35 +889,33 @@
         scalars[0], pair(grad_branch), kept_near, *back_weights
     )
     up_kept = plan.product_kept(inputs, up_rows)
-    branch_far, gate_moved, branch_near, qkv_near, text_near, rows_near, gain_near, up_kept = fence(
-        branch_far, gate_moved, branch_near, qkv_near, text_near, rows_near, gain_near, up_kept
-    )
-
-    gate_grad = plan.by_rep(plan.total(gate_kept, gate_moved))
-    gate_grad, branch_far, down_moved = fence(gate_grad, pair(branch_far), down_moved)
-    gate_parts = plan.reduce(gate_grad)
+    branch_far, up_moved, gate_parts, branch_near, qkv_near, text_near, rows_near, gain_near, up_kept = fence(
+        branch_far, up_moved, gate_parts, branch_near, qkv_near, text_near, rows_near, gain_near, up_kept
+    )
+
+    up_grad = plan.by_rep(plan.total(up_kept, up_moved))
+    up_grad, branch_far, down_moved = fence(up_grad, pair(branch_far), down_moved)
+    up_parts = plan.reduce(up_grad)
     down_moved = plan.move(down_moved)
     branch_far, qkv_far, text_far, rows_far, gain_far = attend_back(
         scalars[1], branch_far, kept_far, *back_weights
     )
-    down_kept = plan.product_kept(hidden_rows, results, hidden_first)
     captions, normed_rows = (captions_near, captions_far), (normed_near, normed_far)
     text_rows, qkv_rows, branches = (text_near, text_far), (qkv_near, qkv_far), (branch_near, branch_far)
     text_moved = plan.product_moved(captions, text_rows)
-    gate_parts, up_moved, text_rows, qkv_rows, branches, rows_far, gain_far, down_kept, text_moved = fence(
-        gate_parts, up_moved, text_rows, qkv_rows, branches, rows_far, gain_far, down_kept, text_moved
-    )
-
+    down_moved, up_parts, text_rows, qkv_rows, branches, rows_far, gain_far, text_moved, hidden_rows = fence(
+        down_moved, up_parts, text_rows, qkv_rows, branches, rows_far, gain_far, text_moved, hidden_rows
+    )
+
+    text_moved = plan.move(text_moved)
+    down_kept = plan.product_kept(hidden_rows, results, hidden_first)
+    down_grad = plan.total(down_kept, down_moved).reshape(rep_count, -1, D)
     across = settle(rows_far).astype(bf16)
-    up_grad = plan.by_rep(plan.total(up_kept, up_moved))
-    across, up_grad, text_moved, text_rows, qkv_rows, hidden_rows = fence(
-        across, up_grad, text_moved, text_rows, qkv_rows, hidden_rows
-    )
-    text_moved = plan.move(text_moved)
-    up_parts = plan.reduce(up_grad)
+    across, down_grad, text_rows, qkv_rows, hidden_rows, branches = fence(
+        across, down_grad, text_rows, qkv_rows, hidden_rows, branches
+    )
+    down_parts = plan.reduce(down_grad)
     arrived = settle_move(across)
-    down_grad = plan.total(down_kept, down_moved).reshape(rep_count, -1, D)
-    down_parts = plan.reduce(down_grad)
     qkv_moved = plan.product_moved(normed_rows, qkv_rows)
     text_kept = plan.product_kept(captions, text_rows)
     qkv_kept = plan.product_kept(normed_rows, qkv_rows)
@@ -927,10 +930,15 @@
     result_far = [dot(side, down_rank) for side in jnp.split(hidden_rows[1], 2)]
     result_across = settle((result_far[0], result_far[1].astype(bf16))).astype(bf16)
     grad_normed = plan.ordered(settle(rows_near) + arrived)
-    text_moved, up_parts, down_parts, grad_normed, qkv_moved, text_kept, qkv_kept, out_halves, result_across = fence(
-        text_moved, up_parts, down_parts, grad_normed, qkv_moved, text_kept, qkv_kept, out_halves, result_across
-    )
-
+    text_moved, down_parts, grad_normed, qkv_moved, text_kept, qkv_kept, out_halves, result_across = fence(
+        text_moved, down_parts, grad_normed, qkv_moved, text_kept, qkv_kept, out_halves, result_across
+    )
+
+    text_grad = plan.by_rep(plan.total(text_kept, text_moved))
+    text_grad, qkv_moved, out_halves, result_across, hidden_rows = fence(
+        text_grad, qkv_moved, out_halves, result_across, hidden_rows
+    )
+    text_parts = plan.reduce(text_grad)
     qkv_moved = plan.move(qkv_moved)
     result = settle_move(result_across)
     if plan.aligned:
@@ -938,8 +946,6 @@
             out_kept, out_moved = out_halves[0].astype(f32), swap(out_halves[1], "hi")
         else:
             out_kept, out_moved = None, plan.move(jnp.concatenate(out_halves))
-    text_grad = plan.by_rep(plan.total(text_kept, text_moved))
-    text_parts = plan.reduce(text_grad)
     result_near = [dot(side, down_rank) for side in jnp.split(hidden_rows[0], 2)]
     result = result + settle((result_near[0], result_near[1].astype(bf16)))
     result = result.reshape(item_count, item_len, D)

time: 875 us -> 840 us (0.960)
  waiting for transfers between devices: 284 us -> 264 us
  blocking collectives: 15.1 us -> 0 us
    all_to_all x1 -> x0, blocking collectives: 15.1 us -> none  [trade_ranks(): return lax.all_to_all(block, ('mid', 'core'), 0, 0, tiled=True)]
    all_gather x6, waiting for transfers between devices: 34.1 us -> 21.6 us  [z_gather(): return lax.all_gather(block.reshape(-1, block.shape[-1]), 'rep', tiled=True)]
    mul x8, local copies, waits for them, and re-layouts: 10.9 us -> 0.68 us  [place_lanes(): return (view * at).reshape(-1)]
    all_to_all x5 -> x6, waiting for transfers between devices: 29.8 us -> 22.9 us  [trade_ranks(): return lax.all_to_all(block, ('mid', 'core'), 0, 0, tiled=True)]
    all_to_all x5 -> x6, starting transfers between devices: 18.2 us -> 23.1 us  [trade_ranks(): return lax.all_to_all(block, ('mid', 'core'), 0, 0, tiled=True)]
    unnamed x186 -> x173, local copies, waits for them, and re-layouts: 20.4 us -> 21.3 us
  transfers between devices with their start and end apart: 58 -> 59, of which waited for: 28 -> 29; matrix products, arithmetic and copies ran while one was open for 22% -> 23% of each run, Pallas kernels for 26% -> 28%
where the time goes in v6:
time: 840 us; the launch traced here: 830 us
  waiting for transfers between devices  264 us (31%)
  Pallas kernels  254 us (30%)
  local copies, waits for them, and re-layouts  107 us (13%)
  other arithmetic  94 us (11%)
  starting transfers between devices  68.1 us (8%)
  matrix products  26.6 us (3%)
  between operations  15.4 us (2%)
    ppermute x39, waiting for transfers between devices, swap(): return lax.ppermute(block, axis, [(at, at ^ step) for at in range(count)])  145 us
    pallas_call x12, Pallas kernels, product(): pl.pallas_call(kernel, grid_spec=pltpu.PrefetchScalarGridSpec(num_scalar_...  90.2 us
    pallas_call x2, Pallas kernels, attend_back(): pl.pallas_call(attend_back_kernel, grid_spec=pltpu.PrefetchScalarGridSpec...  62.3 us
    pallas_call x2, Pallas kernels, feed(): pl.pallas_call(feed_kernel, grid=(steps,), in_specs=pair_specs(rows, step...  52 us
    pallas_call x2, Pallas kernels, attend(): pl.pallas_call(attend_kernel, grid_spec=pltpu.PrefetchScalarGridSpec(num_...  50 us
    all_to_all x1, waiting for transfers between devices, local(): lax.all_to_all(partial, AXES, 0, 0, tiled=True).astype(f32)  36.9 us
    all_to_all x1, waiting for transfers between devices, local(): lax.all_to_all(jnp.concatenate([modulations, gain_blocks], axis=1), AXES,...  33.6 us
    ppermute x39, starting transfers between devices, swap(): return lax.ppermute(block, axis, [(at, at ^ step) for at in range(count)])  29.1 us
  transfers between devices with their start and end apart: 59, of which 29 were waited for; matrix products, arithmetic and copies ran while one was open for 23% of the time, Pallas kernels for 28%

profile of v6, /device:TPU:8, one launch (start us, length us, event | category | flops | bytes accessed | tf_op | source)
XLA Modules:
  0.0 829.6 jit_solution(11150857527819420912)
XLA Ops:
  77.0 36.9 %all-to-all-done.2 = bf16[32,2,6144]{2,1,0:T(2,128)(2,1)S(1)} async-done(((bf16[32,2,6144]{2,1,0:T(2,128)(2,1)}), bf16[32,2,6144]{2,1,0:T(2,128)(2,1)S(1)}, u32[]{:S(2)}, u32[]{:S(2)}) %all-to-all-start.2) | async-done | bytes 786464 | tf_op jit(solution)/shard_map/all_to_all | solution.py:768
  134.5 34.3 %collective-permute-done.2.caption_ref = bf16[256,4096]{1,0:T(8,128)(2,1)} collective-permute-done((bf16[256,4096]{1,0:T(8,128)(2,1)}, bf16[256,4096]{1,0:T(8,128)(2,1)}, u32[]{:S(2)}, u32[]{:S(2)}) %collective-permute-start.2) | collective-permute-done | bytes 2097184 | tf_op jit(solution)/shard_map/ppermute | solution.py:536
  176.8 16.5 %all-gather.15.cloned.1.call-done = bf16[2048,384]{1,0:T(8,128)(2,1)} async-done(((bf16[512,384]{1,0:T(8,128)(2,1)}), bf16[2048,384]{1,0:T(8,128)(2,1)}) %all-gather.15.cloned.1.call-update) | async-done | bytes 1572880 | tf_op jit(solution)/shard_map/all_gather | solution.py:712
  193.3 18.0 %collective-permute-done.6 = bf16[2048,384]{1,0:T(8,128)(2,1)S(1)} collective-permute-done((bf16[2048,384]{1,0:T(8,128)(2,1)}, bf16[2048,384]{1,0:T(8,128)(2,1)S(1)}, u32[]{:S(2)}, u32[]{:S(2)}) %collective-permute-start.6) | collective-permute-done | bytes 1572896 | tf_op jit(solution)/shard_map/ppermute | solution.py:536
  231.3 13.9 %collective-permute-done.10.result_ref = bf16[512,1536]{1,0:T(8,128)(2,1)} collective-permute-done((bf16[512,1536]{1,0:T(8,128)(2,1)}, bf16[512,1536]{1,0:T(8,128)(2,1)}, u32[]{:S(2)}, u32[]{:S(2)}) %collective-permute-start.10) | collective-permute-done | bytes 1572896 | tf_op jit(solution)/shard_map/ppermute | solution.py:536
  259.6 25.0 %attend.2 = (bf16[1024,1536]{1,0:T(8,128)(2,1)}, bf16[512,4096]{1,0:T(8,128)(2,1)}, f32[1024,1152]{1,0:T(8,128)}, f32[512,384]{1,0:T(8,128)}, f32[512,384]{1,0:T...) custom-call(s32[4]{0:T(128)} %maximum_convert_fusion.kind_ref, ...), custom_call_target="tpu_custom_call" | custom-call | tf_op jit(solution)/shard_map/attend/pallas_call | solution.py:359
  303.1 25.0 %attend.3 = (bf16[1024,1536]{1,0:T(8,128)(2,1)}, bf16[512,4096]{1,0:T(8,128)(2,1)}, f32[1024,1152]{1,0:T(8,128)}, f32[512,384]{1,0:T(8,128)}, f32[512,384]{1,0:T...) custom-call(s32[4]{0:T(128)} %maximum_convert_fusion.2.kind_ref, ...), custom_call_target="tpu_custom_call" | custom-call | tf_op jit(solution)/shard_map/attend/pallas_call | solution.py:359
  350.2 26.2 %feed.2 = (bf16[1024,1536]{1,0:T(8,128)(2,1)}, bf16[1024,1536]{1,0:T(8,128)(2,1)}, bf16[1024,1024]{1,0:T(8,128)(2,1)}, bf16[1024,1024]{1,0:T(8,128)(2,1)}, bf16[...) custom-call(bf16[512,1536]{1,0:T(8,128)(2,1)} %copy-done.19, ...), custom_call_target="tpu_custom_call" | custom-call | tf_op jit(solution)/shard_map/feed/pallas_call | solution.py:521
  388.3 25.8 %feed.3 = (bf16[1024,1536]{1,0:T(8,128)(2,1)}, bf16[1024,1536]{1,0:T(8,128)(2,1)}, bf16[1024,1024]{1,0:T(8,128)(2,1)}, bf16[1024,1024]{1,0:T(8,128)(2,1)}, bf16[...) custom-call(bf16[512,1536]{1,0:T(8,128)(2,1)} %collective-permute-done.18.rows_ref, ...), custom_call_target="tpu_custom_call" | custom-call | tf_op jit(solution)/shard_map/feed/pallas_call | solution.py:521
  435.5 7.8 product.15
  443.3 8.0 product.14
  451.4 10.7 %collective-permute-done.22 = bf16[512,1536]{1,0:T(8,128)(2,1)} collective-permute-done((bf16[512,1536]{1,0:T(8,128)(2,1)}, bf16[512,1536]{1,0:T(8,128)(2,1)}, u32[]{:S(2)}, u32[]{:S(2)}) %collective-permute-start.22) | collective-permute-done | bytes 1572896 | tf_op jit(solution)/shard_map/ppermute | solution.py:536
  482.6 8.0 product.16
  490.7 31.1 %attend_back.2 = (bf16[1024,1536]{1,0:T(8,128)(2,1)}, bf16[1024,1152]{1,0:T(8,128)(2,1)}, bf16[512,768]{1,0:T(8,128)(2,1)}, f32[512,1536]{1,0:T(8,128)}, bf16[512,1536]{1,0:T(8,128)(2,1)}, /*index=5*/f32[4,384]{1,0:T(4,128)}) custom-call(s32[4]{0:T(128)} %maximum_convert_fusion.2.kind_ref, s32[4]{0:T(128)} %maximum_convert_fusion.3.len_ref, ...), custom_call_target="tpu_custom_call" | custom-call | tf_op jit(solution)/shard_map/attend_back/pallas_call | solution.py:389
  526.9 31.1 %attend_back.3 = (bf16[1024,1536]{1,0:T(8,128)(2,1)}, bf16[1024,1152]{1,0:T(8,128)(2,1)}, bf16[512,768]{1,0:T(8,128)(2,1)}, f32[512,1536]{1,0:T(8,128)}, bf16[512,1536]{1,0:T(8,128)(2,1)}, /*index=5*/f32[4,384]{1,0:T(4,128)}) custom-call(s32[4]{0:T(128)} %maximum_convert_fusion.kind_ref, s32[4]{0:T(128)} %maximum_convert_fusion.1.len_ref, ...), custom_call_target="tpu_custom_call" | custom-call | tf_op jit(solution)/shard_map/attend_back/pallas_call | solution.py:389
  567.5 8.6 %product.18 = f32[512,1536]{1,0:T(8,128)} custom-call(s32[1]{0:T(128)} %bitcast.66.first_ref, bf16[1024,1024]{1,0:T(8,128)(2,1)} %get-tuple-element.454.refs_0_, bf16[1024,1024]{1,0:T(8,128)(2,1)} %get-tuple-element.445.refs_1_, bf16[1024,1536]{1,0:T(8,128)(2,1)} %get-tuple-element.365.refs_2_, bf16[1024,1536]{1,0:T(8,128)(2,1)} %get-tuple-element.366.refs_3_), custom_call_target="tpu_custom_call" | custom-call | tf_op jit(solution)/shard_map/product/pallas_call | solution.py:441
  593.4 8.9 %product.21 = f32[768,1152]{1,0:T(8,128)} custom-call(s32[1]{0:T(128)} %constant.580.clone.1.first_ref, bf16[1024,1536]{1,0:T(8,128)(2,1)} %get-tuple-element.435.refs_0_, bf16[1024,1536]{1,0:T(8,128)(2,1)} %get-tuple-element.436.refs_1_, bf16[1024,1152]{1,0:T(8,128)(2,1)} %get-tuple-element.437.refs_2_, bf16[1024,1152]{1,0:T(8,128)(2,1)} %get-tuple-element.438.refs_3_), custom_call_target="tpu_custom_call" | custom-call | tf_op jit(solution)/shard_map/product/pallas_call | solution.py:441
  602.3 8.3 %product.19 = bf16[768,1152]{1,0:T(8,128)(2,1)} custom-call(s32[1]{0:T(128)} %constant.578.clone.1.first_ref, bf16[1024,1536]{1,0:T(8,128)(2,1)} %get-tuple-element.435.refs_0_, bf16[1024,1536]{1,0:T(8,128)(2,1)} %get-tuple-element.436.refs_1_, bf16[1024,1152]{1,0:T(8,128)(2,1)} %get-tuple-element.437.refs_2_, bf16[1024,1152]{1,0:T(8,128)(2,1)} %get-tuple-element.438.refs_3_), custom_call_target="tpu_custom_call" | custom-call | tf_op jit(solution)/shard_map/product/pallas_call | solution.py:441
  640.4 14.9 %collective-permute-done.30 = bf16[2048,768]{1,0:T(8,128)(2,1)} collective-permute-done((bf16[2048,768]{1,0:T(8,128)(2,1)}, bf16[2048,768]{1,0:T(8,128)(2,1)}, u32[]{:S(2)}, u32[]{:S(2)}) %collective-permute-start.30) | collective-permute-done | bytes 3145760 | tf_op jit(solution)/shard_map/ppermute | solution.py:536
  695.0 9.3 %collective-permute-done.35 = bf16[512,1536]{1,0:T(8,128)(2,1)} collective-permute-done((bf16[512,1536]{1,0:T(8,128)(2,1)}, bf16[512,1536]{1,0:T(8,128)(2,1)}, u32[]{:S(2)}, u32[]{:S(2)}) %collective-permute-start.35) | collective-permute-done | bytes 1572896 | tf_op jit(solution)/shard_map/ppermute | solution.py:536
  704.3 11.5 %fusion.6 = (f32[512,1536]{1,0:T(8,128)}, bf16[512,1536]{1,0:T(8,128)(2,1)}, f32[512,1536]{1,0:T(8,128)S(1)}) fusion(bf16[512,1536]{1,0:T(8,128)(2,1)} %param.15, f32[512,1536]{1,0:T(8,128)} %maximum_select_fusion.1, f32[512]{0:T(512)S(1)} %multiply_multiply_fusion.1, f32[2,1536]{1,0:T(2,128)S(1)} %copy-done.58, f32[1536]{0:T(1024)S(1)} %copy-done.52, ...), kind=kOutput, calls=%fused_computation.27 | convolution fusion | flops 1628700672 | bytes 27844608 | tf_op jit(solution)/shard_map/dot_general | solution.py:59
  719.3 11.4 %collective-permute-done.37 = bf16[768,1152]{1,0:T(8,128)(2,1)} collective-permute-done((bf16[768,1152]{1,0:T(8,128)(2,1)}, bf16[768,1152]{1,0:T(8,128)(2,1)}, u32[]{:S(2)}, u32[]{:S(2)}) %collective-permute-start.37) | collective-permute-done | bytes 1769504 | tf_op jit(solution)/shard_map/ppermute | solution.py:536
  742.2 8.5 %all-to-all-done.7 = bf16[4,128,768]{2,1,0:T(8,128)(2,1)S(1)} async-done(((bf16[4,128,768]{2,1,0:T(8,128)(2,1)}), bf16[4,128,768]{2,1,0:T(8,128)(2,1)S(1)}, u32[]{:S(2)}, u32[]{:S(2)}) %all-to-all-start.7) | async-done | bytes 786464 | tf_op jit(solution)/shard_map/all_to_all | solution.py:569
  764.8 33.6 %all-to-all-done.5 = bf16[32,2,6288]{2,1,0:T(2,128)(2,1)} async-done(((bf16[32,2,6288]{2,1,0:T(2,128)(2,1)}), bf16[32,2,6288]{2,1,0:T(2,128)(2,1)}, u32[]{:S(2)}, u32[]{:S(2)}) %all-to-all-start.5) | async-done | bytes 804896 | tf_op jit(solution)/shard_map/all_to_all | solution.py:987
  (471 shorter events, 380.9 us)
Async XLA Ops:
  40.6 77.5 %all-gather.9.cloned.1.call-start = ((), (), s32[]{:S(2)}) async-start(), calls=%async_computation.15 | async-start | bytes 2949120 | tf_op jit(solution)/shard_map/all_gather | solution.py:712
  61.2 53.3 %collective-permute-start.1 = (bf16[256,4096]{1,0:T(8,128)(2,1)}, bf16[256,4096]{1,0:T(8,128)(2,1)}, u32[]{:S(2)}, u32[]{:S(2)}) collective-permute-start(bf16[256,4096]{1,0:T(8,128)(2,1)} %maximum_select_fusion.2.caption_ref), channel_id=1, source_target_pairs={{0,4},{4,0},{1,5},{5,1},{2,6},{6,2},{3,7},{7,3},{8,12},{12,8},{9,1... | collective-permute-start | bytes 6291464 | tf_op jit(solution)/shard_map/ppermute | solution.py:536
  69.2 44.7 %all-to-all-start.2 = ((bf16[32,2,6144]{2,1,0:T(2,128)(2,1)}), bf16[32,2,6144]{2,1,0:T(2,128)(2,1)S(1)}, u32[]{:S(2)}, u32[]{:S(2)}) async-start(bf16[32,2,6144]{2,1,0:T(2,128)(2,1)} %reshape.873), calls=%async_computation.2 | async-start | bytes 1572864 | tf_op jit(solution)/shard_map/all_to_all | solution.py:768
  73.2 100.9 %all-gather.17.cloned.1.call-start = ((), (), s32[]{:S(2)}) async-start(), calls=%async_computation.19 | async-start | bytes 1966080 | tf_op jit(solution)/shard_map/all_gather | solution.py:712
  73.3 44.8 %collective-permute-start = (bf16[512,1536]{1,0:T(8,128)(2,1)}, bf16[512,1536]{1,0:T(8,128)(2,1)}, u32[]{:S(2)}, u32[]{:S(2)}) collective-permute-start(bf16[512,1536]{1,0:T(8,128)(2,1)} %all-gather.7.cloned.1.call-done), channel_id=1, source_target_pairs={{0,16},{16,0},{1,17},{17,1},{2,18},{18,2},{3,19},{19,3},{4,20},{20... | collective-permute-start | bytes 4718600 | tf_op jit(solution)/shard_map/ppermute | solution.py:536
  119.0 74.3 %all-gather.15.cloned.1.call-start = ((), (), s32[]{:S(2)}) async-start(), calls=%async_computation.18 | async-start | bytes 1966080 | tf_op jit(solution)/shard_map/all_gather | solution.py:712
  121.0 53.2 %collective-permute-start.3 = (bf16[1024,1152]{1,0:T(8,128)(2,1)}, bf16[1024,1152]{1,0:T(8,128)(2,1)}, u32[]{:S(2)}, u32[]{:S(2)}) collective-permute-start(bf16[1024,1152]{1,0:T(8,128)(2,1)} %all-gather.9.cloned.1.call-done), channel_id=1, source_target_pairs={{0,16},{16,0},{1,17},{17,1},{2,18},{18,2},{3,19},{19,3},{4,20},{20... | collective-permute-start | bytes 7077896 | tf_op jit(solution)/shard_map/ppermute | solution.py:536
  121.6 47.2 %collective-permute-start.2 = (bf16[256,4096]{1,0:T(8,128)(2,1)}, bf16[256,4096]{1,0:T(8,128)(2,1)}, u32[]{:S(2)}, u32[]{:S(2)}) collective-permute-start(bf16[256,4096]{1,0:T(8,128)(2,1)} %maximum_select_fusion.2.caption_ref), channel_id=1, source_target_pairs={{0,8},{8,0},{1,9},{9,1},{2,10},{10,2},{3,11},{11,3},{4,12},{12,4},... | collective-permute-start | bytes 6291464 | tf_op jit(solution)/shard_map/ppermute | solution.py:536
  124.6 106.7 %all-gather.13.cloned.1.call-start = ((), (), s32[]{:S(2)}) async-start(), calls=%async_computation.17 | async-start | bytes 1966080 | tf_op jit(solution)/shard_map/all_gather | solution.py:712
  174.2 110.4 %all-gather.11.cloned.1.call-start = ((), (), s32[]{:S(2)}) async-start(), calls=%async_computation.16 | async-start | bytes 1966080 | tf_op jit(solution)/shard_map/all_gather | solution.py:712
  176.6 68.6 %collective-permute-start.10 = (bf16[512,1536]{1,0:T(8,128)(2,1)}, bf16[512,1536]{1,0:T(8,128)(2,1)}, u32[]{:S(2)}, u32[]{:S(2)}) collective-permute-start(bf16[512,1536]{1,0:T(8,128)(2,1)} %fusion.12.result_ref), channel_id=1, source_target_pairs={{0,8},{8,0},{1,9},{9,1},{2,10},{10,2},{3,11},{11,3},{4,12},{12,4},... | collective-permute-start | bytes 4718600 | tf_op jit(solution)/shard_map/ppermute | solution.py:536
  213.7 308.1 %reduce-scatter.6.cloned.1.call-start = ((), (), s32[]{:S(2)}) async-start(), calls=%async_computation.20 | async-start | bytes 1966080 | tf_op jit(solution)/shard_map/reduce_scatter | solution.py:664
  469.0 96.4 %reduce-scatter.8.cloned.1.call-start = ((), (), s32[]{:S(2)}) async-start(), calls=%async_computation.21 | async-start | bytes 1966080 | tf_op jit(solution)/shard_map/reduce_scatter | solution.py:664
  479.5 42.3 %collective-permute-start.26 = (bf16[768,1024]{1,0:T(8,128)(2,1)S(1)}, bf16[768,1024]{1,0:T(8,128)(2,1)}, u32[]{:S(2)}, u32[]{:S(2)}) collective-permute-start(bf16[768,1024]{1,0:T(8,128)(2,1)S(1)} %copy-done.32), channel_id=1, source_target_pairs={{0,16},{16,0},{1,17},{17,1},{2,18},{18,2},{3,19},{19,3},{4,20},{20... | collective-permute-start | bytes 4718600 | tf_op jit(solution)/shard_map/ppermute | solution.py:536
  526.2 129.1 %reduce-scatter.10.cloned.1.call-start = ((), (), s32[]{:S(2)}) async-start(), calls=%async_computation.22 | async-start | bytes 1966080 | tf_op jit(solution)/shard_map/reduce_scatter | solution.py:664
  567.1 62.2 %collective-permute-start.32 = (bf16[512,1536]{1,0:T(8,128)(2,1)}, bf16[512,1536]{1,0:T(8,128)(2,1)}, u32[]{:S(2)}, u32[]{:S(2)}) collective-permute-start(bf16[512,1536]{1,0:T(8,128)(2,1)} %get-tuple-element.433), channel_id=1, source_target_pairs={{0,4},{4,0},{1,5},{5,1},{2,6},{6,2},{3,7},{7,3},{8,12},{12,8},{9,1... | collective-permute-start | bytes 4718600 | tf_op jit(solution)/shard_map/ppermute | solution.py:536
  581.9 47.3 %collective-permute-start.33 = (bf16[512,1536]{1,0:T(8,128)(2,1)}, bf16[512,1536]{1,0:T(8,128)(2,1)}, u32[]{:S(2)}, u32[]{:S(2)}) collective-permute-start(bf16[512,1536]{1,0:T(8,128)(2,1)} %add_convert_fusion.3), channel_id=1, source_target_pairs={{0,8},{8,0},{1,9},{9,1},{2,10},{10,2},{3,11},{11,3},{4,12},{12,4},... | collective-permute-start | bytes 4718600 | tf_op jit(solution)/shard_map/ppermute | solution.py:536
  585.0 70.2 %collective-permute-start.30 = (bf16[2048,768]{1,0:T(8,128)(2,1)}, bf16[2048,768]{1,0:T(8,128)(2,1)}, u32[]{:S(2)}, u32[]{:S(2)}) collective-permute-start(bf16[2048,768]{1,0:T(8,128)(2,1)} %product.17), channel_id=1, source_target_pairs={{0,16},{16,0},{1,17},{17,1},{2,18},{18,2},{3,19},{19,3},{4,20},{20... | collective-permute-start | bytes 9437192 | tf_op jit(solution)/shard_map/ppermute | solution.py:536
  586.5 148.6 %reduce-scatter.12.cloned.1.call-start = ((), (), s32[]{:S(2)}) async-start(), calls=%async_computation.23 | async-start | bytes 3932160 | tf_op jit(solution)/shard_map/reduce_scatter | solution.py:664
  591.9 41.2 %collective-permute-start.34 = (bf16[512,1536]{1,0:T(8,128)(2,1)}, bf16[512,1536]{1,0:T(8,128)(2,1)S(1)}, u32[]{:S(2)}, u32[]{:S(2)}) collective-permute-start(bf16[512,1536]{1,0:T(8,128)(2,1)} %convolution_convert_fusion.2), channel_id=1, source_target_pairs={{0,4},{4,0},{1,5},{5,1},{2,6},{6,2},{3,7},{7,3},{8,12},{12,8},{9,1... | collective-permute-start | bytes 4718600 | tf_op jit(solution)/shard_map/ppermute | solution.py:536
  678.2 57.4 %all-to-all-start.8 = ((bf16[4,48,2048]{2,1,0:T(8,128)(2,1)}), bf16[4,48,2048]{2,1,0:T(8,128)(2,1)}, u32[]{:S(2)}, u32[]{:S(2)}) async-start(bf16[4,48,2048]{2,1,0:T(8,128)(2,1)} %bitcast.259), calls=%async_computation.13 | async-start | bytes 1572864 | tf_op jit(solution)/shard_map/all_to_all | solution.py:569
  682.5 123.8 %reduce-scatter.14.cloned.1.call-start = ((), (), s32[]{:S(2)}) async-start(), calls=%async_computation.24 | async-start | bytes 2949120 | tf_op jit(solution)/shard_map/reduce_scatter | solution.py:664
  689.4 41.3 %collective-permute-start.37 = (bf16[768,1152]{1,0:T(8,128)(2,1)}, bf16[768,1152]{1,0:T(8,128)(2,1)}, u32[]{:S(2)}, u32[]{:S(2)}) collective-permute-start(bf16[768,1152]{1,0:T(8,128)(2,1)} %product.19), channel_id=1, source_target_pairs={{0,16},{16,0},{1,17},{17,1},{2,18},{18,2},{3,19},{19,3},{4,20},{20... | collective-permute-start | bytes 5308424 | tf_op jit(solution)/shard_map/ppermute | solution.py:536
  750.7 47.8 %all-to-all-start.5 = ((bf16[32,2,6288]{2,1,0:T(2,128)(2,1)}), bf16[32,2,6288]{2,1,0:T(2,128)(2,1)}, u32[]{:S(2)}, u32[]{:S(2)}) async-start(bf16[32,2,6288]{2,1,0:T(2,128)(2,1)} %reshape.973), calls=%async_computation.9 | async-start | bytes 1638400 | tf_op jit(solution)/shard_map/all_to_all | solution.py:987
  (115 other events, 2019.9 us)
Sparse Core Ops, SparseCore 0:
  9.6 37.7 all-gather.6
  49.6 63.3 all-gather.8
  119.1 36.1 all-gather.16
  157.3 35.9 all-gather.14
  195.3 35.9 all-gather.12
  232.7 35.9 all-gather.10
  469.1 35.5 reduce-scatter.5
  526.3 33.4 reduce-scatter.7
  586.6 34.4 reduce-scatter.9
  661.7 60.9 reduce-scatter.11
  735.7 64.7 reduce-scatter.13

commit v7 on v6

--- a/solution.py
+++ b/solution.py
@@ -532,6 +532,34 @@
     return *outs, (grad_mine, grad_core)
 
 
+def result_kernel(hidden_ref, down_ref, result_ref, core_result_ref):
+    own = pl.program_id(0) < pl.num_programs(0) // 2
+    rows = dot(hidden_ref[...], down_ref[...])
+
+    @pl.when(own)
+    def _():
+        result_ref[...] = rows
+
+    @pl.when(jnp.logical_not(own))
+    def _():
+        core_result_ref[...] = rows.astype(jnp.bfloat16)
+
+
+def result_part(hidden, down_rank):
+    count = hidden.shape[0]
+    steps = count // 256
+    outs = (shaped(count // 2, D, jnp.float32), shaped(count // 2, D))
+    return pl.pallas_call(
+        result_kernel,
+        grid=(steps,),
+        in_specs=[step_spec(hidden, steps), whole_spec(down_rank)],
+        out_specs=pair_specs(outs, steps),
+        out_shape=outs,
+        compiler_params=parameters(),
+        name="result",
+    )(hidden, down_rank)
+
+
 def swap(block, axis, count=2, step=1):
     return lax.ppermute(block, axis, [(at, at ^ step) for at in range(count)])
 
@@ -583,7 +611,7 @@
 
 
 def settle_move(across):
-    return swap(across, "mid").astype(jnp.float32)
+    return swap(across, "mid")
 
 
 class Layout:
@@ -612,6 +640,18 @@
         half = values.shape[-1] // 2
         turned = jnp.concatenate([values[..., half:], values[..., :half]], axis=-1)
         return jnp.where(lax.axis_index("hi") == 0, values, turned)
+
+    def ordered_text(self, values):
+        if self.hi != 2:
+            return values
+        view = values.reshape(values.shape[0], self.hi, RANKS, self.rep, -1)
+        return self.ordered(jnp.swapaxes(view, 2, 3).reshape(values.shape))
+
+    def text_halves(self, blocks):
+        return tuple(blocks) if self.hi == 2 else self.halves(blocks)
+
+    def text_by_rep(self, summed):
+        return summed.reshape(self.rep, -1, summed.shape[1]) if self.hi == 2 else self.by_rep(summed)
 
     def across_hi(self, block):
         if self.hi == 2:
@@ -762,7 +802,7 @@
     qkv_z = z_gather(qkv_mine)
     down_rank = plan.across_hi(down_z)
     text_mine = trade_ranks(plan.by_rank(text_weight, 2, plan.head_groups))
-    captions_near = pair(plan.ordered(caption.reshape(-1, TEXT_DIM)))
+    captions_near = pair(plan.ordered_text(caption.reshape(-1, TEXT_DIM)))
     partial = dot(activated_mine, ada_weight).astype(bf16).reshape(devices, item_count, 4 * D)
     gate_up_mine = trade_ranks(plan.by_rank(gate_up_weight, 2, hi_count))
     modulation = jnp.sum(lax.all_to_all(partial, AXES, 0, 0, tiled=True).astype(f32), axis=0)
@@ -806,14 +846,14 @@
         out_rank = out_rank.reshape(rank_width, D)
         qkv_rank = [block[:, : RANKS * rows].reshape(-1, 3 * rank_width) for block in blocks]
         qkv_rank = qkv_rank if hi_count == 2 else jnp.stack(qkv_rank)
-    qkv_rank, text_key_rank = plan.halves(qkv_rank), plan.halves(text_key_rank)
+    qkv_rank, text_key_rank = plan.halves(qkv_rank), plan.text_halves(text_key_rank)
     gate_z, text_value_rank, result_far, normed_far, qkv_rank, out_rank, text_key_rank = fence(
         gate_z, text_value_rank, result_far, normed_far, qkv_rank, out_rank, text_key_rank
     )
 
     up_z = z_gather(up_mine)
     gate_rank = plan.across_hi(gate_z)
-    attend_weights = (qkv_rank, text_key_rank, plan.halves(text_value_rank), out_rank, tables)
+    attend_weights = (qkv_rank, text_key_rank, plan.text_halves(text_value_rank), out_rank, tables)
     normed_far, captions_far, kept_far, partial_far = attend(
         scalars[1], normed_far, captions_far, *attend_weights
     )
@@ -834,7 +874,7 @@
         up_rank, arrived, normed_near, captions_near, kept_near, partial_near, result_far, gate_rank
     )
 
-    branch = (settle(partial_near) + arrived).reshape(item_count, item_len, D)
+    branch = (settle(partial_near) + arrived.astype(f32)).reshape(item_count, item_len, D)
     attn_gate = jnp.tanh(gate_attn)[:, None, :]
     middle = token_rows + attn_gate * branch
     mlp_input = modulate(middle, gain_rows[4], scale_mlp)
@@ -847,8 +887,9 @@
     input_near, result_near, hidden_near, gate_near, up_near, partial_near = feed(
         pair(mlp_input), result_near, *feed_weights
     )
-    input_far, input_near, result_near, hidden_near, gate_near, up_near, partial_near = fence(
-        input_far, input_near, result_near, hidden_near, gate_near, up_near, partial_near
+    result_part_near = result_part(hidden_near, down_rank)
+    input_far, input_near, result_near, hidden_near, gate_near, up_near, partial_near, result_part_near = fence(
+        input_far, input_near, result_near, hidden_near, gate_near, up_near, partial_near, result_part_near
     )
     input_far, result_far, hidden_far, gate_far, up_far, partial_far = feed(
         pair(input_far), result_far, *feed_weights
@@ -866,14 +907,16 @@
     hidden_first = hi_at * (feed_width // 2)
     down_moved = plan.product_moved(hidden_rows, results, feed_width // 2 - hidden_first)
     gate_kept = plan.product_kept(inputs, gate_rows)
-    arrived, gate_moved, up_moved, down_moved, gate_kept, partial_near = fence(
-        arrived, gate_moved, up_moved, down_moved, gate_kept, partial_near
+    up_kept = plan.product_kept(inputs, up_rows)
+    result_part_far = result_part(hidden_rows[1], down_rank)
+    arrived, gate_moved, up_moved, down_moved, gate_kept, up_kept, result_part_far, partial_near = fence(
+        arrived, gate_moved, up_moved, down_moved, gate_kept, up_kept, result_part_far, partial_near
     )
 
     up_moved = plan.move(up_moved)
     gate_grad = plan.by_rep(plan.total(gate_kept, gate_moved))
     gate_parts = plan.reduce(gate_grad)
-    grad_mlp_input = plan.ordered(settle(partial_near) + arrived)
+    grad_mlp_input = plan.ordered(settle(partial_near) + arrived.astype(f32))
     _, pull_mlp_norm = jax.vjp(modulate, middle, gain_rows[4], scale_mlp)
     grad_middle_norm, grad_mlp_gain, grad_scale_mlp = pull_mlp_norm(
         grad_mlp_input.reshape(item_count, item_len, D)
@@ -881,44 +924,45 @@
     grad_middle = grad_top + grad_middle_norm
     grad_attn_gate = jnp.sum(grad_middle * branch, axis=1) * (1.0 - jnp.tanh(gate_attn) ** 2)
     grad_branch = (attn_gate * grad_middle).astype(bf16).reshape(row_count, D)
-    grad_branch, up_rows = fence(grad_branch, up_rows)
+    grad_branch, result_part_far = fence(grad_branch, result_part_far)
 
     branch_far = swap(grad_branch, "mid")
     back_weights = (qkv_rank, out_rank, tables)
     branch_near, qkv_near, text_near, rows_near, gain_near = attend_back(
         scalars[0], pair(grad_branch), kept_near, *back_weights
     )
-    up_kept = plan.product_kept(inputs, up_rows)
-    branch_far, up_moved, gate_parts, branch_near, qkv_near, text_near, rows_near, gain_near, up_kept = fence(
-        branch_far, up_moved, gate_parts, branch_near, qkv_near, text_near, rows_near, gain_near, up_kept
+    result_across = settle(result_part_far).astype(bf16)
+    branch_far, up_moved, gate_parts, branch_near, qkv_near, text_near, rows_near, gain_near, result_across = fence(
+        branch_far, up_moved, gate_parts, branch_near, qkv_near, text_near, rows_near, gain_near, result_across
     )
 
     up_grad = plan.by_rep(plan.total(up_kept, up_moved))
-    up_grad, branch_far, down_moved = fence(up_grad, pair(branch_far), down_moved)
+    up_grad, branch_far, down_moved, result_across = fence(
+        up_grad, pair(branch_far), down_moved, result_across
+    )
     up_parts = plan.reduce(up_grad)
     down_moved = plan.move(down_moved)
+    result_arrived = settle_move(result_across)
     branch_far, qkv_far, text_far, rows_far, gain_far = attend_back(
         scalars[1], branch_far, kept_far, *back_weights
     )
     captions, normed_rows = (captions_near, captions_far), (normed_near, normed_far)
     text_rows, qkv_rows, branches = (text_near, text_far), (qkv_near, qkv_far), (branch_near, branch_far)
     text_moved = plan.product_moved(captions, text_rows)
-    down_moved, up_parts, text_rows, qkv_rows, branches, rows_far, gain_far, text_moved, hidden_rows = fence(
-        down_moved, up_parts, text_rows, qkv_rows, branches, rows_far, gain_far, text_moved, hidden_rows
+    down_moved, up_parts, result_arrived, text_rows, qkv_rows, branches, rows_far, gain_far, text_moved = fence(
+        down_moved, up_parts, result_arrived, text_rows, qkv_rows, branches, rows_far, gain_far, text_moved
     )
 
     text_moved = plan.move(text_moved)
     down_kept = plan.product_kept(hidden_rows, results, hidden_first)
     down_grad = plan.total(down_kept, down_moved).reshape(rep_count, -1, D)
     across = settle(rows_far).astype(bf16)
-    across, down_grad, text_rows, qkv_rows, hidden_rows, branches = fence(
-        across, down_grad, text_rows, qkv_rows, hidden_rows, branches
+    across, down_grad, text_rows, qkv_rows, branches = fence(
+        across, down_grad, text_rows, qkv_rows, branches
     )
     down_parts = plan.reduce(down_grad)
     arrived = settle_move(across)
     qkv_moved = plan.product_moved(normed_rows, qkv_rows)
-    text_kept = plan.product_kept(captions, text_rows)
-    qkv_kept = plan.product_kept(normed_rows, qkv_rows)
     mixed_rows = [plan.ordered(kept[6]) for kept in (kept_near, kept_far)]
     if plan.aligned:
         out_halves = [
@@ -927,34 +971,36 @@
         ]
     else:
         out_halves = []
-    result_far = [dot(side, down_rank) for side in jnp.split(hidden_rows[1], 2)]
-    result_across = settle((result_far[0], result_far[1].astype(bf16))).astype(bf16)
-    grad_normed = plan.ordered(settle(rows_near) + arrived)
-    text_moved, down_parts, grad_normed, qkv_moved, text_kept, qkv_kept, out_halves, result_across = fence(
-        text_moved, down_parts, grad_normed, qkv_moved, text_kept, qkv_kept, out_halves, result_across
-    )
-
-    text_grad = plan.by_rep(plan.total(text_kept, text_moved))
-    text_grad, qkv_moved, out_halves, result_across, hidden_rows = fence(
-        text_grad, qkv_moved, out_halves, result_across, hidden_rows
-    )
-    text_parts = plan.reduce(text_grad)
+    text_kept = plan.product_kept(captions, text_rows)
+    qkv_kept = plan.product_kept(normed_rows, qkv_rows)
+    text_moved, down_parts, arrived, qkv_moved, text_kept, qkv_kept, out_halves = fence(
+        text_moved, down_parts, arrived, qkv_moved, text_kept, qkv_kept, out_halves
+    )
+
     qkv_moved = plan.move(qkv_moved)
-    result = settle_move(result_across)
     if plan.aligned:
         if hi_count == 2:
             out_kept, out_moved = out_halves[0].astype(f32), swap(out_halves[1], "hi")
         else:
             out_kept, out_moved = None, plan.move(jnp.concatenate(out_halves))
-    result_near = [dot(side, down_rank) for side in jnp.split(hidden_rows[0], 2)]
-    result = result + settle((result_near[0], result_near[1].astype(bf16)))
-    result = result.reshape(item_count, item_len, D)
-    layer_out = (middle + mlp_gate * result).astype(bf16).reshape(row_count, D)
-    grad_mlp_gate = jnp.sum(grad_top * result, axis=1) * (1.0 - jnp.tanh(gate_mlp) ** 2)
+    else:
+        out_moved = ()
+    text_grad = plan.text_by_rep(plan.total(text_kept, text_moved))
+    text_parts = plan.reduce(text_grad)
+    grad_normed = plan.ordered(settle(rows_near) + arrived.astype(f32))
     _, pull_attn_norm = jax.vjp(modulate, token_rows, gain_rows[0], scale_attn)
     grad_token_norm, grad_attn_gain, grad_scale_attn = pull_attn_norm(
         grad_normed.reshape(item_count, item_len, D)
     )
+    result = settle(result_part_near) + result_arrived.astype(f32)
+    result = result.reshape(item_count, item_len, D)
+    grad_mlp_gate = jnp.sum(grad_top * result, axis=1) * (1.0 - jnp.tanh(gate_mlp) ** 2)
+    gate_up_parts = jnp.concatenate([gate_parts, up_parts], axis=-1)
+    gate_up_parts = trade_ranks(gate_up_parts.reshape(RANKS, rows, -1))
+    text_parts, qkv_moved, out_moved, grad_mlp_gate, grad_scale_attn, grad_attn_gain, gate_up_parts = fence(
+        text_parts, qkv_moved, out_moved, grad_mlp_gate, grad_scale_attn, grad_attn_gain, gate_up_parts
+    )
+    layer_out = (middle + mlp_gate * result).astype(bf16).reshape(row_count, D)
     tokens_grad = (grad_middle + grad_token_norm).reshape(row_count, D)
     qkv_grad = plan.by_rep(plan.total(qkv_kept, qkv_moved))
     if plan.aligned:
@@ -965,9 +1011,7 @@
         out_grad = product(mixed_rows, branches, 0, rank_width, bf16)
         placed = (out_grad[None] * at).reshape(D, D)
         out_weight_grad = lax.psum_scatter(placed, AXES, scatter_dimension=0, tiled=True).astype(f32)
-    text_parts, qkv_grad, grad_mlp_gate, grad_scale_attn, grad_attn_gain = fence(
-        text_parts, qkv_grad, grad_mlp_gate, grad_scale_attn, grad_attn_gain
-    )
+    qkv_grad, grad_mlp_gate, text_parts = fence(qkv_grad, grad_mlp_gate, text_parts)
     qkv_parts = plan.reduce(qkv_grad)
     if plan.aligned:
         out_weight_grad = qkv_parts[RANKS * rows :].reshape(-1, D).astype(f32)
@@ -982,21 +1026,25 @@
     gains_grad = jnp.stack(
         [grad_attn_gain, gain_terms[0], gain_terms[1], gain_terms[2], grad_mlp_gain, gain_terms[3]]
     ).astype(bf16)
-    gain_blocks = jnp.moveaxis(gains_grad.reshape(6, devices, -1), 1, 0).reshape(devices, -1)
-    modulations = jnp.broadcast_to(grad_modulation.reshape(-1), (devices, grad_modulation.size))
+    gain_blocks = jnp.moveaxis(gains_grad.reshape(6, devices, -1), 1, 0)
+    gain_blocks = gain_blocks.reshape(devices, item_count, -1)
+    modulations = jnp.broadcast_to(grad_modulation, (devices,) + grad_modulation.shape)
     both = lax.all_to_all(
-        jnp.concatenate([modulations, gain_blocks], axis=1), AXES, 0, 0, tiled=True
-    )
-    ada_weight_grad = dot_left(activated_mine, both[:, : modulations.shape[1]].reshape(-1, 4 * D))
-    norm_gains_grad = jnp.sum(both[:, modulations.shape[1] :].astype(f32), axis=0).reshape(6, -1)
+        jnp.concatenate([modulations, gain_blocks], axis=2), AXES, 0, 0, tiled=True
+    )
+    ada_weight_grad = lax.dot_general(
+        activated_mine.reshape(devices, item_count, rows),
+        both[:, :, : 4 * D],
+        (((0, 1), (0, 1)), ((), ())),
+        preferred_element_type=f32,
+    )
+    norm_gains_grad = jnp.sum(both[:, :, 4 * D :].astype(f32), axis=0).reshape(6, -1)
 
     def whole(parts, weight, sections, groups):
         blocks = trade_ranks(parts.reshape(RANKS, weight.shape[0], -1))
         return plan.from_ranks(blocks, sections, groups).astype(f32)
 
-    gate_up_weight_grad = whole(
-        jnp.concatenate([gate_parts, up_parts], axis=-1), gate_up_weight, 2, hi_count
-    )
+    gate_up_weight_grad = plan.from_ranks(gate_up_parts, 2, hi_count).astype(f32)
     text_weight_grad = whole(text_parts, text_weight, 2, plan.head_groups)
     qkv_weight_grad = whole(qkv_parts, qkv_weight, 3, plan.head_groups)
     down_weight_grad = down_parts.astype(f32)

time: 840 us -> 847 us (level)
  Pallas kernels: 254 us -> 279 us
  matrix products: 26.6 us -> 1.74 us
  other arithmetic: 94 us -> 107 us
  waiting for transfers between devices: 264 us -> 251 us
    dot_general x5 -> x1, matrix products: 25.2 us -> 0.34 us  [dot(): return jnp.dot(left, right, preferred_element_type=jnp.float32)]
    pallas_call x0 -> x2, Pallas kernels: none -> 16.5 us  [result_part(): pl.pallas_call(result_kernel, grid=(steps,), in_specs=[step_spec(hidden,...]
    all_to_all x1, waiting for transfers between devices: 33.6 us -> 20.5 us  [local(): lax.all_to_all(jnp.concatenate([modulations, gain_blocks], axis=2), AXES,...]
    ppermute x39, waiting for transfers between devices: 145 us -> 156 us  [swap(): return lax.ppermute(block, axis, [(at, at ^ step) for at in range(count)])]
    unnamed x173 -> x139, local copies, waits for them, and re-layouts: 21.3 us -> 14.9 us
    transpose x10 -> x6, local copies, waits for them, and re-layouts: 19.1 us -> 13 us  [natural_rows(): return jnp.transpose(view, (0, 2, 1, 3, 4)).reshape(-1, stacked.shape[-1])]
  transfers between devices with their start and end apart: 59 -> 59, of which waited for: 29 -> 25; matrix products, arithmetic and copies ran while one was open for 23% -> 22% of each run, Pallas kernels for 28% -> 30%
where the time goes in v7:
time: 847 us; the launch traced here: 836 us
  Pallas kernels  279 us (33%)
  waiting for transfers between devices  251 us (30%)
  local copies, waits for them, and re-layouts  113 us (13%)
  other arithmetic  107 us (13%)
  starting transfers between devices  68 us (8%)
  between operations  15.4 us (2%)
    ppermute x39, waiting for transfers between devices, swap(): return lax.ppermute(block, axis, [(at, at ^ step) for at in range(count)])  156 us
    pallas_call x12, Pallas kernels, product(): pl.pallas_call(kernel, grid_spec=pltpu.PrefetchScalarGridSpec(num_scalar_...  89.7 us
    pallas_call x2, Pallas kernels, attend_back(): pl.pallas_call(attend_back_kernel, grid_spec=pltpu.PrefetchScalarGridSpec...  62.6 us
    pallas_call x2, Pallas kernels, feed(): pl.pallas_call(feed_kernel, grid=(steps,), in_specs=pair_specs(rows, step...  60 us
    pallas_call x2, Pallas kernels, attend(): pl.pallas_call(attend_kernel, grid_spec=pltpu.PrefetchScalarGridSpec(num_...  50.2 us
    all_to_all x1, waiting for transfers between devices, local(): lax.all_to_all(partial, AXES, 0, 0, tiled=True).astype(f32)  34.6 us
    ppermute x39, starting transfers between devices, swap(): return lax.ppermute(block, axis, [(at, at ^ step) for at in range(count)])  27.7 us
    all_to_all x6, starting transfers between devices, trade_ranks(): return lax.all_to_all(block, ('mid', 'core'), 0, 0, tiled=True)  23.8 us
  transfers between devices with their start and end apart: 59, of which 25 were waited for; matrix products, arithmetic and copies ran while one was open for 22% of the time, Pallas kernels for 30%

profile of v7, /device:TPU:8, one launch (start us, length us, event | category | flops | bytes accessed | tf_op | source)
XLA Modules:
  0.0 835.9 jit_solution(17394908219924659823)
XLA Ops:
  83.1 34.6 %all-to-all-done.2 = bf16[32,2,6144]{2,1,0:T(2,128)(2,1)S(1)} async-done(((bf16[32,2,6144]{2,1,0:T(2,128)(2,1)}), bf16[32,2,6144]{2,1,0:T(2,128)(2,1)S(1)}, u32[]{:S(2)}, u32[]{:S(2)}) %all-to-all-start.2) | async-done | bytes 786464 | tf_op jit(solution)/shard_map/all_to_all | solution.py:808
  138.7 35.7 %collective-permute-done.2.caption_ref = bf16[256,4096]{1,0:T(8,128)(2,1)} collective-permute-done((bf16[256,4096]{1,0:T(8,128)(2,1)}, bf16[256,4096]{1,0:T(8,128)(2,1)}, u32[]{:S(2)}, u32[]{:S(2)}) %collective-permute-start.2) | collective-permute-done | bytes 2097184 | tf_op jit(solution)/shard_map/ppermute | solution.py:564
  182.4 17.1 %all-gather.15.cloned.1.call-done.value_mine_ref = bf16[2048,384]{1,0:T(8,128)(2,1)} async-done(((bf16[512,384]{1,0:T(8,128)(2,1)}), bf16[2048,384]{1,0:T(8,128)(2,1)}) %all-gather.15.cloned.1.call-update) | async-done | bytes 1572880 | tf_op jit(solution)/shard_map/all_gather | solution.py:752
  199.5 17.4 %collective-permute-done.6.key_other_ref = bf16[2048,384]{1,0:T(8,128)(2,1)S(1)} collective-permute-done((bf16[2048,384]{1,0:T(8,128)(2,1)}, bf16[2048,384]{1,0:T(8,128)(2,1)S(1)}, u32[]{:S(2)}, u32[]{:S(2)}) %collective-permute-start.6) | collective-permute-done | bytes 1572896 | tf_op jit(solution)/shard_map/ppermute | solution.py:564
  237.5 13.3 %collective-permute-done.10.result_ref = bf16[512,1536]{1,0:T(8,128)(2,1)} collective-permute-done((bf16[512,1536]{1,0:T(8,128)(2,1)}, bf16[512,1536]{1,0:T(8,128)(2,1)}, u32[]{:S(2)}, u32[]{:S(2)}) %collective-permute-start.10) | collective-permute-done | bytes 1572896 | tf_op jit(solution)/shard_map/ppermute | solution.py:564
  261.1 25.0 %attend.2 = (bf16[1024,1536]{1,0:T(8,128)(2,1)}, bf16[512,4096]{1,0:T(8,128)(2,1)}, f32[1024,1152]{1,0:T(8,128)}, f32[512,384]{1,0:T(8,128)}, f32[512,384]{1,0:T...) custom-call(s32[4]{0:T(128)} %maximum_convert_fusion.kind_ref, ...), custom_call_target="tpu_custom_call" | custom-call | tf_op jit(solution)/shard_map/attend/pallas_call | solution.py:359
  310.8 25.2 %attend.3 = (bf16[1024,1536]{1,0:T(8,128)(2,1)}, bf16[512,4096]{1,0:T(8,128)(2,1)}, f32[1024,1152]{1,0:T(8,128)}, f32[512,384]{1,0:T(8,128)}, f32[512,384]{1,0:T...) custom-call(s32[4]{0:T(128)} %maximum_convert_fusion.2.kind_ref, ...), custom_call_target="tpu_custom_call" | custom-call | tf_op jit(solution)/shard_map/attend/pallas_call | solution.py:359
  353.2 34.2 %feed.2 = (bf16[1024,1536]{1,0:T(8,128)(2,1)}, bf16[1024,1536]{1,0:T(8,128)(2,1)}, bf16[1024,1024]{1,0:T(8,128)(2,1)}, bf16[1024,1024]{1,0:T(8,128)(2,1)}, bf16[...) custom-call(bf16[512,1536]{1,0:T(8,128)(2,1)} %copy-done.19, ...), custom_call_target="tpu_custom_call" | custom-call | tf_op jit(solution)/shard_map/feed/pallas_call | solution.py:521
  387.4 8.1 result.2
  400.4 25.8 %feed.3 = (bf16[1024,1536]{1,0:T(8,128)(2,1)}, bf16[1024,1536]{1,0:T(8,128)(2,1)}, bf16[1024,1024]{1,0:T(8,128)(2,1)}, bf16[1024,1024]{1,0:T(8,128)(2,1)}, bf16[...) custom-call(bf16[512,1536]{1,0:T(8,128)(2,1)} %collective-permute-done.18.rows_ref, ...), custom_call_target="tpu_custom_call" | custom-call | tf_op jit(solution)/shard_map/feed/pallas_call | solution.py:521
  439.5 8.3 result.3
  455.2 7.6 product.16
  462.9 7.6 product.15
  470.5 8.1 product.14
  496.0 31.4 %attend_back.2 = (bf16[1024,1536]{1,0:T(8,128)(2,1)}, bf16[1024,1152]{1,0:T(8,128)(2,1)}, bf16[512,768]{1,0:T(8,128)(2,1)}, f32[512,1536]{1,0:T(8,128)}, bf16[512,1536]{1,0:T(8,128)(2,1)}, /*index=5*/f32[4,384]{1,0:T(4,128)}) custom-call(s32[4]{0:T(128)} %maximum_convert_fusion.2.kind_ref, s32[4]{0:T(128)} %maximum_convert_fusion.3.len_ref, ...), custom_call_target="tpu_custom_call" | custom-call | tf_op jit(solution)/shard_map/attend_back/pallas_call | solution.py:389
  538.1 31.2 %attend_back.3 = (bf16[1024,1536]{1,0:T(8,128)(2,1)}, bf16[1024,1152]{1,0:T(8,128)(2,1)}, bf16[512,768]{1,0:T(8,128)(2,1)}, f32[512,1536]{1,0:T(8,128)}, bf16[512,1536]{1,0:T(8,128)(2,1)}, /*index=5*/f32[4,384]{1,0:T(4,128)}) custom-call(s32[4]{0:T(128)} %maximum_convert_fusion.kind_ref, s32[4]{0:T(128)} %maximum_convert_fusion.1.len_ref, ...), custom_call_target="tpu_custom_call" | custom-call | tf_op jit(solution)/shard_map/attend_back/pallas_call | solution.py:389
  576.7 8.6 %product.18 = f32[512,1536]{1,0:T(8,128)} custom-call(s32[1]{0:T(128)} %bitcast.54.first_ref, bf16[1024,1024]{1,0:T(8,128)(2,1)} %get-tuple-element.372.hidden_ref.refs_0_, bf16[1024,1024]{1,0:T(8,128)(2,1)} %get-tuple-element.373.refs_1_.hidden_ref, bf16[1024,1536]{1,0:T(8,128)(2,1)} %get-tuple-element.374.refs_2_, ...), custom_call_target="tpu_custom_call" | custom-call | tf_op jit(solution)/shard_map/product/pallas_call | solution.py:441
  599.6 8.8 %product.21 = f32[768,1152]{1,0:T(8,128)} custom-call(s32[1]{0:T(128)} %constant.580.clone.1.first_ref, bf16[1024,1536]{1,0:T(8,128)(2,1)} %get-tuple-element.449.refs_0_, bf16[1024,1536]{1,0:T(8,128)(2,1)} %get-tuple-element.450.refs_1_, bf16[1024,1152]{1,0:T(8,128)(2,1)} %get-tuple-element.451.refs_2_, bf16[1024,1152]{1,0:T(8,128)(2,1)} %get-tuple-element.452.refs_3_), custom_call_target="tpu_custom_call" | custom-call | tf_op jit(solution)/shard_map/product/pallas_call | solution.py:441
  608.4 8.4 %product.19 = bf16[768,1152]{1,0:T(8,128)(2,1)} custom-call(s32[1]{0:T(128)} %constant.578.clone.1.first_ref, bf16[1024,1536]{1,0:T(8,128)(2,1)} %get-tuple-element.449.refs_0_, bf16[1024,1536]{1,0:T(8,128)(2,1)} %get-tuple-element.450.refs_1_, bf16[1024,1152]{1,0:T(8,128)(2,1)} %get-tuple-element.451.refs_2_, bf16[1024,1152]{1,0:T(8,128)(2,1)} %get-tuple-element.452.refs_3_), custom_call_target="tpu_custom_call" | custom-call | tf_op jit(solution)/shard_map/product/pallas_call | solution.py:441
  627.6 7.8 product.20
  635.4 20.7 %collective-permute-done.34 = bf16[2048,768]{1,0:T(8,128)(2,1)} collective-permute-done((bf16[2048,768]{1,0:T(8,128)(2,1)}, bf16[2048,768]{1,0:T(8,128)(2,1)}, u32[]{:S(2)}, u32[]{:S(2)}) %collective-permute-start.34) | collective-permute-done | bytes 3145760 | tf_op jit(solution)/shard_map/ppermute | solution.py:564
  686.1 8.5 %fusion.9 = (f32[2,1536]{1,0:T(2,128)S(1)}, bf16[2,1536]{1,0:T(2,128)(2,1)}, f32[2,1536]{1,0:T(2,128)S(1)}, bf16[2,1536]{1,0:T(2,128)(2,1)}, f32[512,1536]{1,0:T(8,128)S(1)}, /*index=5*/f32[512,1536]{1,0:T(8,128)}) fusion(bf16[512,1536]{1,0:T(8,128)(2,1)S(1)} %copy-done.4, f32[2,256]{1,0:T(2,128)S(1)} %copy-done.62, f32[2,256]{1,0:T(2,128)S(1)} %copy-done.61, ...), kind=kLoop, calls=%fused_computation.29 | loop fusion | flops 25939968 | bytes 31537152 | tf_op jit(solution)/shard_map/reduce_sum | solution.py:925
  697.0 33.0 %collective-permute-done.38 = bf16[192,1536]{1,0:T(8,128)(2,1)} collective-permute-done((bf16[192,1536]{1,0:T(8,128)(2,1)}, bf16[192,1536]{1,0:T(8,128)(2,1)}, u32[]{:S(2)}, u32[]{:S(2)}) %collective-permute-start.38) | collective-permute-done | bytes 589856 | tf_op jit(solution)/shard_map/ppermute | solution.py:564
  787.2 20.5 %all-to-all-done.6 = bf16[32,2,6288]{2,1,0:T(2,128)(2,1)} async-done(((bf16[32,2,6288]{2,1,0:T(2,128)(2,1)}), bf16[32,2,6288]{2,1,0:T(2,128)(2,1)}, u32[]{:S(2)}, u32[]{:S(2)}) %all-to-all-start.6) | async-done | bytes 804896 | tf_op jit(solution)/shard_map/all_to_all | solution.py:1032
  (431 shorter events, 373.5 us)
Async XLA Ops:
  7.2 42.7 %all-gather.7.cloned.1.call-start = ((), (), s32[]{:S(2)}) async-start(), calls=%async_computation.14 | async-start | bytes 1966080 | tf_op jit(solution)/shard_map/all_gather | solution.py:752
  47.9 76.4 %all-gather.9.cloned.1.call-start = ((), (), s32[]{:S(2)}) async-start(), calls=%async_computation.15 | async-start | bytes 2949120 | tf_op jit(solution)/shard_map/all_gather | solution.py:752
  67.4 51.1 %collective-permute-start.1 = (bf16[256,4096]{1,0:T(8,128)(2,1)}, bf16[256,4096]{1,0:T(8,128)(2,1)}, u32[]{:S(2)}, u32[]{:S(2)}) collective-permute-start(bf16[256,4096]{1,0:T(8,128)(2,1)} %maximum_select_fusion.2.caption_ref), channel_id=1, source_target_pairs={{0,4},{4,0},{1,5},{5,1},{2,6},{6,2},{3,7},{7,3},{8,12},{12,8},{9,1... | collective-permute-start | bytes 6291464 | tf_op jit(solution)/shard_map/ppermute | solution.py:564
  75.4 42.4 %all-to-all-start.2 = ((bf16[32,2,6144]{2,1,0:T(2,128)(2,1)}), bf16[32,2,6144]{2,1,0:T(2,128)(2,1)S(1)}, u32[]{:S(2)}, u32[]{:S(2)}) async-start(bf16[32,2,6144]{2,1,0:T(2,128)(2,1)} %reshape.847), calls=%async_computation.2 | async-start | bytes 1572864 | tf_op jit(solution)/shard_map/all_to_all | solution.py:808
  79.4 100.3 %all-gather.17.cloned.1.call-start = ((), (), s32[]{:S(2)}) async-start(), calls=%async_computation.19 | async-start | bytes 1966080 | tf_op jit(solution)/shard_map/all_gather | solution.py:752
  79.5 44.8 %collective-permute-start = (bf16[512,1536]{1,0:T(8,128)(2,1)}, bf16[512,1536]{1,0:T(8,128)(2,1)}, u32[]{:S(2)}, u32[]{:S(2)}) collective-permute-start(bf16[512,1536]{1,0:T(8,128)(2,1)} %all-gather.7.cloned.1.call-done), channel_id=1, source_target_pairs={{0,16},{16,0},{1,17},{17,1},{2,18},{18,2},{3,19},{19,3},{4,20},{20... | collective-permute-start | bytes 4718600 | tf_op jit(solution)/shard_map/ppermute | solution.py:564
  125.2 74.3 %all-gather.15.cloned.1.call-start = ((), (), s32[]{:S(2)}) async-start(), calls=%async_computation.18 | async-start | bytes 1966080 | tf_op jit(solution)/shard_map/all_gather | solution.py:752
  126.6 53.2 %collective-permute-start.3 = (bf16[1024,1152]{1,0:T(8,128)(2,1)}, bf16[1024,1152]{1,0:T(8,128)(2,1)}, u32[]{:S(2)}, u32[]{:S(2)}) collective-permute-start(bf16[1024,1152]{1,0:T(8,128)(2,1)} %all-gather.9.cloned.1.call-done), channel_id=1, source_target_pairs={{0,16},{16,0},{1,17},{17,1},{2,18},{18,2},{3,19},{19,3},{4,20},{20... | collective-permute-start | bytes 7077896 | tf_op jit(solution)/shard_map/ppermute | solution.py:564
  127.3 47.1 %collective-permute-start.2 = (bf16[256,4096]{1,0:T(8,128)(2,1)}, bf16[256,4096]{1,0:T(8,128)(2,1)}, u32[]{:S(2)}, u32[]{:S(2)}) collective-permute-start(bf16[256,4096]{1,0:T(8,128)(2,1)} %maximum_select_fusion.2.caption_ref), channel_id=1, source_target_pairs={{0,8},{8,0},{1,9},{9,1},{2,10},{10,2},{3,11},{11,3},{4,12},{12,4},... | collective-permute-start | bytes 6291464 | tf_op jit(solution)/shard_map/ppermute | solution.py:564
  130.2 107.3 %all-gather.13.cloned.1.call-start = ((), (), s32[]{:S(2)}) async-start(), calls=%async_computation.17 | async-start | bytes 1966080 | tf_op jit(solution)/shard_map/all_gather | solution.py:752
  179.8 106.3 %all-gather.11.cloned.1.call-start = ((), (), s32[]{:S(2)}) async-start(), calls=%async_computation.16 | async-start | bytes 1966080 | tf_op jit(solution)/shard_map/all_gather | solution.py:752
  182.2 68.6 %collective-permute-start.10 = (bf16[512,1536]{1,0:T(8,128)(2,1)}, bf16[512,1536]{1,0:T(8,128)(2,1)}, u32[]{:S(2)}, u32[]{:S(2)}) collective-permute-start(bf16[512,1536]{1,0:T(8,128)(2,1)} %copy-done.20), channel_id=1, source_target_pairs={{0,8},{8,0},{1,9},{9,1},{2,10},{10,2},{3,11},{11,3},{4,12},{12,4},... | collective-permute-start | bytes 4718600 | tf_op jit(solution)/shard_map/ppermute | solution.py:564
  219.8 311.6 %reduce-scatter.6.cloned.1.call-start = ((), (), s32[]{:S(2)}) async-start(), calls=%async_computation.20 | async-start | bytes 1966080 | tf_op jit(solution)/shard_map/reduce_scatter | solution.py:704
  291.1 44.9 %collective-permute-start.16 = (bf16[512,1536]{1,0:T(8,128)(2,1)}, bf16[512,1536]{1,0:T(8,128)(2,1)}, u32[]{:S(2)}, u32[]{:S(2)}) collective-permute-start(bf16[512,1536]{1,0:T(8,128)(2,1)} %collective-permute-done.10.result_ref), channel_id=1, source_target_pairs={{0,4},{4,0},{1,5},{5,1},{2,6},{6,2},{3,7},{7,3},{8,12},{12,8},{9,1... | collective-permute-start | bytes 4718600 | tf_op jit(solution)/shard_map/ppermute | solution.py:564
  349.8 45.7 %collective-permute-start.18 = (bf16[512,1536]{1,0:T(8,128)(2,1)S(1)}, bf16[512,1536]{1,0:T(8,128)(2,1)}, u32[]{:S(2)}, u32[]{:S(2)}) collective-permute-start(bf16[512,1536]{1,0:T(8,128)(2,1)S(1)} %maximum_select_fusion.4.rows_ref), channel_id=1, source_target_pairs={{0,8},{8,0},{1,9},{9,1},{2,10},{10,2},{3,11},{11,3},{4,12},{12,4},... | collective-permute-start | bytes 4718600 | tf_op jit(solution)/shard_map/ppermute | solution.py:564
  482.9 93.7 %reduce-scatter.8.cloned.1.call-start = ((), (), s32[]{:S(2)}) async-start(), calls=%async_computation.21 | async-start | bytes 1966080 | tf_op jit(solution)/shard_map/reduce_scatter | solution.py:704
  536.2 119.9 %reduce-scatter.10.cloned.1.call-start = ((), (), s32[]{:S(2)}) async-start(), calls=%async_computation.22 | async-start | bytes 1966080 | tf_op jit(solution)/shard_map/reduce_scatter | solution.py:704
  585.3 70.8 %collective-permute-start.34 = (bf16[2048,768]{1,0:T(8,128)(2,1)}, bf16[2048,768]{1,0:T(8,128)(2,1)}, u32[]{:S(2)}, u32[]{:S(2)}) collective-permute-start(bf16[2048,768]{1,0:T(8,128)(2,1)} %product.17), channel_id=1, source_target_pairs={{0,16},{16,0},{1,17},{17,1},{2,18},{18,2},{3,19},{19,3},{4,20},{20... | collective-permute-start | bytes 9437192 | tf_op jit(solution)/shard_map/ppermute | solution.py:564
  591.8 138.2 %reduce-scatter.12.cloned.1.call-start = ((), (), s32[]{:S(2)}) async-start(), calls=%async_computation.23 | async-start | bytes 3932160 | tf_op jit(solution)/shard_map/reduce_scatter | solution.py:704
  591.8 43.6 %collective-permute-start.36 = (bf16[512,1536]{1,0:T(8,128)(2,1)}, bf16[512,1536]{1,0:T(8,128)(2,1)}, u32[]{:S(2)}, u32[]{:S(2)}) collective-permute-start(bf16[512,1536]{1,0:T(8,128)(2,1)} %add_convert_fusion.3), channel_id=1, source_target_pairs={{0,8},{8,0},{1,9},{9,1},{2,10},{10,2},{3,11},{11,3},{4,12},{12,4},... | collective-permute-start | bytes 4718600 | tf_op jit(solution)/shard_map/ppermute | solution.py:564
  675.3 137.0 %reduce-scatter.14.cloned.1.call-start = ((), (), s32[]{:S(2)}) async-start(), calls=%async_computation.24 | async-start | bytes 2949120 | tf_op jit(solution)/shard_map/reduce_scatter | solution.py:704
  676.0 53.9 %collective-permute-start.37 = (bf16[768,1152]{1,0:T(8,128)(2,1)}, bf16[768,1152]{1,0:T(8,128)(2,1)}, u32[]{:S(2)}, u32[]{:S(2)}) collective-permute-start(bf16[768,1152]{1,0:T(8,128)(2,1)} %product.19), channel_id=1, source_target_pairs={{0,16},{16,0},{1,17},{17,1},{2,18},{18,2},{3,19},{19,3},{4,20},{20... | collective-permute-start | bytes 5308424 | tf_op jit(solution)/shard_map/ppermute | solution.py:564
  676.4 53.5 %collective-permute-start.38 = (bf16[192,1536]{1,0:T(8,128)(2,1)}, bf16[192,1536]{1,0:T(8,128)(2,1)}, u32[]{:S(2)}, u32[]{:S(2)}) collective-permute-start(bf16[192,1536]{1,0:T(8,128)(2,1)} %product.23), channel_id=1, source_target_pairs={{0,16},{16,0},{1,17},{17,1},{2,18},{18,2},{3,19},{19,3},{4,20},{20... | collective-permute-start | bytes 1769480 | tf_op jit(solution)/shard_map/ppermute | solution.py:564
  764.1 43.6 %all-to-all-start.6 = ((bf16[32,2,6288]{2,1,0:T(2,128)(2,1)}), bf16[32,2,6288]{2,1,0:T(2,128)(2,1)}, u32[]{:S(2)}, u32[]{:S(2)}) async-start(bf16[32,2,6288]{2,1,0:T(2,128)(2,1)} %pad_maximum_fusion.3), calls=%async_computation.10 | async-start | bytes 1638400 | tf_op jit(solution)/shard_map/all_to_all | solution.py:1032
  (100 other events, 1773.7 us)
Sparse Core Ops, SparseCore 0:
  9.6 37.7 all-gather.6
  50.9 63.0 all-gather.8
  125.3 36.1 all-gather.16
  163.5 35.9 all-gather.14
  201.5 35.9 all-gather.12
  238.9 35.9 all-gather.10
  483.0 34.3 reduce-scatter.5
  536.3 34.1 reduce-scatter.7
  591.9 35.3 reduce-scatter.9
  662.3 60.1 reduce-scatter.11
  742.1 64.2 reduce-scatter.13

commit v8 on v7

--- a/solution.py
+++ b/solution.py
@@ -94,6 +94,10 @@
 
 def inverse_rms(raw):
     return lax.rsqrt(head_sums(raw * raw) * (1.0 / HEAD_DIM) + EPSILON)
+
+def rows_of(ref):
+    return ref.shape[0]
+
 
 def dot_cut(rows, mine, other):
     half = mine.shape[0]
@@ -134,7 +138,8 @@
     own = item < pl.num_programs(0) // 2
     kind, length = kind_ref[item], len_ref[item]
     width = q_ref.shape[1]
-    cosine, sine = cos_ref[kind], sin_ref[kind]
+    positions = pl.ds(kind * rows_of(q_ref), rows_of(q_ref))
+    cosine, sine = cos_ref[positions, :], sin_ref[positions, :]
     scaling = HEAD_DIM ** (-0.5)
 
     @pl.when(own)
@@ -225,7 +230,8 @@
     own = item < pl.num_programs(0) // 2
     kind, length = kind_ref[item], len_ref[item]
     width = q_ref.shape[1]
-    cosine, sine = cos_ref[kind], sin_ref[kind]
+    positions = pl.ds(kind * rows_of(q_ref), rows_of(q_ref))
+    cosine, sine = cos_ref[positions, :], sin_ref[positions, :]
     scaling = HEAD_DIM ** (-0.5)
 
     @pl.when(own)
@@ -789,12 +795,15 @@
     kinds_sides = group_items(kinds)
     cosine, sine = rope_tables(jnp.arange(2), item_len)
     signs = jnp.where(jnp.arange(HEAD_DIM) % (HEAD_DIM // 2) < HEAD_DIM // 4, -1.0, 1.0)
-    cosine, sine = jnp.tile(cosine, (1, 1, 2)), jnp.tile(sine * signs, (1, 1, 2))
+    cosine, sine = [
+        jnp.tile(table, (1, 1, LANES // HEAD_DIM)).reshape(-1, LANES) for table in (cosine, sine * signs)
+    ]
     head_gains = plan.rank_lanes(gain_rows, plan.head_groups)
     cross_gate = jnp.tanh(head_gains[5])
     head_gains = jnp.concatenate([head_gains[1:4], cross_gate[None]])
     tables = (head_gains, cosine, sine)
     scalars = list(zip(kinds_sides, lengths_sides, strict=True))
+    tables, scalars = fence(tables, scalars)
 
     down_z, qkv_mine, text_weight, activated_mine = fence(
         down_z, qkv_mine, text_weight, activated_mine
@@ -853,9 +862,9 @@
 
     up_z = z_gather(up_mine)
     gate_rank = plan.across_hi(gate_z)
-    attend_weights = (qkv_rank, text_key_rank, plan.text_halves(text_value_rank), out_rank, tables)
+    attend_weights = (qkv_rank, text_key_rank, plan.text_halves(text_value_rank), out_rank)
     normed_far, captions_far, kept_far, partial_far = attend(
-        scalars[1], normed_far, captions_far, *attend_weights
+        scalars[1], normed_far, captions_far, *attend_weights, tables
     )
     up_z, gate_rank, normed_far, captions_far, kept_far, partial_far, attend_weights = fence(
         up_z, gate_rank, normed_far, captions_far, kept_far, partial_far, attend_weights
@@ -866,7 +875,7 @@
     up_rank = plan.across_hi(up_z)
     arrived = settle_move(across)
     normed_near, captions_near, kept_near, partial_near = attend(
-        scalars[0], normed_near, captions_near, *attend_weights
+        scalars[0], normed_near, captions_near, *attend_weights, tables
     )
     result_far = pair(result_far)
     gate_rank = plan.halves(gate_rank)
@@ -887,9 +896,8 @@
     input_near, result_near, hidden_near, gate_near, up_near, partial_near = feed(
         pair(mlp_input), result_near, *feed_weights
     )
-    result_part_near = result_part(hidden_near, down_rank)
-    input_far, input_near, result_near, hidden_near, gate_near, up_near, partial_near, result_part_near = fence(
-        input_far, input_near, result_near, hidden_near, gate_near, up_near, partial_near, result_part_near
+    input_far, input_near, result_near, hidden_near, gate_near, up_near, partial_near = fence(
+        input_far, input_near, result_near, hidden_near, gate_near, up_near, partial_near
     )
     input_far, result_far, hidden_far, gate_far, up_far, partial_far = feed(
         pair(input_far), result_far, *feed_weights
@@ -908,15 +916,16 @@
     down_moved = plan.product_moved(hidden_rows, results, feed_width // 2 - hidden_first)
     gate_kept = plan.product_kept(inputs, gate_rows)
     up_kept = plan.product_kept(inputs, up_rows)
-    result_part_far = result_part(hidden_rows[1], down_rank)
-    arrived, gate_moved, up_moved, down_moved, gate_kept, up_kept, result_part_far, partial_near = fence(
-        arrived, gate_moved, up_moved, down_moved, gate_kept, up_kept, result_part_far, partial_near
+    down_kept = plan.product_kept(hidden_rows, results, hidden_first)
+    near = settle(partial_near)
+    arrived, gate_moved, up_moved, down_moved, gate_kept, up_kept, down_kept, near = fence(
+        arrived, gate_moved, up_moved, down_moved, gate_kept, up_kept, down_kept, near
     )
 
     up_moved = plan.move(up_moved)
     gate_grad = plan.by_rep(plan.total(gate_kept, gate_moved))
     gate_parts = plan.reduce(gate_grad)
-    grad_mlp_input = plan.ordered(settle(partial_near) + arrived.astype(f32))
+    grad_mlp_input = plan.ordered(near + arrived.astype(f32))
     _, pull_mlp_norm = jax.vjp(modulate, middle, gain_rows[4], scale_mlp)
     grad_middle_norm, grad_mlp_gain, grad_scale_mlp = pull_mlp_norm(
         grad_mlp_input.reshape(item_count, item_len, D)
@@ -924,98 +933,91 @@
     grad_middle = grad_top + grad_middle_norm
     grad_attn_gate = jnp.sum(grad_middle * branch, axis=1) * (1.0 - jnp.tanh(gate_attn) ** 2)
     grad_branch = (attn_gate * grad_middle).astype(bf16).reshape(row_count, D)
-    grad_branch, result_part_far = fence(grad_branch, result_part_far)
+    (grad_branch,) = fence(grad_branch)
 
     branch_far = swap(grad_branch, "mid")
     back_weights = (qkv_rank, out_rank, tables)
     branch_near, qkv_near, text_near, rows_near, gain_near = attend_back(
         scalars[0], pair(grad_branch), kept_near, *back_weights
     )
-    result_across = settle(result_part_far).astype(bf16)
-    branch_far, up_moved, gate_parts, branch_near, qkv_near, text_near, rows_near, gain_near, result_across = fence(
-        branch_far, up_moved, gate_parts, branch_near, qkv_near, text_near, rows_near, gain_near, result_across
+    branch_far, up_moved, gate_parts, branch_near, qkv_near, text_near, rows_near, gain_near = fence(
+        branch_far, up_moved, gate_parts, branch_near, qkv_near, text_near, rows_near, gain_near
     )
 
     up_grad = plan.by_rep(plan.total(up_kept, up_moved))
-    up_grad, branch_far, down_moved, result_across = fence(
-        up_grad, pair(branch_far), down_moved, result_across
-    )
+    up_grad, branch_far, down_moved = fence(up_grad, pair(branch_far), down_moved)
     up_parts = plan.reduce(up_grad)
     down_moved = plan.move(down_moved)
-    result_arrived = settle_move(result_across)
     branch_far, qkv_far, text_far, rows_far, gain_far = attend_back(
         scalars[1], branch_far, kept_far, *back_weights
     )
     captions, normed_rows = (captions_near, captions_far), (normed_near, normed_far)
     text_rows, qkv_rows, branches = (text_near, text_far), (qkv_near, qkv_far), (branch_near, branch_far)
     text_moved = plan.product_moved(captions, text_rows)
-    down_moved, up_parts, result_arrived, text_rows, qkv_rows, branches, rows_far, gain_far, text_moved = fence(
-        down_moved, up_parts, result_arrived, text_rows, qkv_rows, branches, rows_far, gain_far, text_moved
+    down_moved, up_parts, text_rows, qkv_rows, branches, rows_far, gain_far, text_moved = fence(
+        down_moved, up_parts, text_rows, qkv_rows, branches, rows_far, gain_far, text_moved
     )
 
     text_moved = plan.move(text_moved)
-    down_kept = plan.product_kept(hidden_rows, results, hidden_first)
     down_grad = plan.total(down_kept, down_moved).reshape(rep_count, -1, D)
     across = settle(rows_far).astype(bf16)
-    across, down_grad, text_rows, qkv_rows, branches = fence(
-        across, down_grad, text_rows, qkv_rows, branches
+    mixed_rows = [plan.ordered(kept[6]) for kept in (kept_near, kept_far)]
+    if plan.aligned:
+        halves = [slice(0, rank_width // 2), slice(rank_width // 2, None)]
+        out_kept, out_moved = [
+            product([side[:, lanes] for side in mixed_rows], branches, 0, rank_width // 2, bf16)
+            for lanes in halves
+        ]
+    else:
+        out_kept, out_moved = (), ()
+    across, down_grad, text_rows, qkv_rows, out_kept, out_moved, hidden_rows = fence(
+        across, down_grad, text_rows, qkv_rows, out_kept, out_moved, hidden_rows
     )
     down_parts = plan.reduce(down_grad)
     arrived = settle_move(across)
+    if plan.aligned:
+        if hi_count == 2:
+            out_grad = plan.total(out_kept.astype(f32), swap(out_moved, "hi"))
+        else:
+            out_grad = plan.move(jnp.concatenate([out_kept, out_moved]))
+        out_parts = plan.reduce(out_grad.reshape(rep_count, -1, D))
+    else:
+        at = (jnp.arange(RANKS) == plan.rank).astype(bf16)[:, None, None]
+        out_grad = product(mixed_rows, branches, 0, rank_width, bf16)
+        placed = (out_grad[None] * at).reshape(D, D)
+        out_parts = lax.psum_scatter(placed, AXES, scatter_dimension=0, tiled=True)
     qkv_moved = plan.product_moved(normed_rows, qkv_rows)
-    mixed_rows = [plan.ordered(kept[6]) for kept in (kept_near, kept_far)]
-    if plan.aligned:
-        out_halves = [
-            product([side[:, lanes] for side in mixed_rows], branches, 0, rank_width // 2, bf16)
-            for lanes in (slice(0, rank_width // 2), slice(rank_width // 2, None))
-        ]
-    else:
-        out_halves = []
     text_kept = plan.product_kept(captions, text_rows)
     qkv_kept = plan.product_kept(normed_rows, qkv_rows)
-    text_moved, down_parts, arrived, qkv_moved, text_kept, qkv_kept, out_halves = fence(
-        text_moved, down_parts, arrived, qkv_moved, text_kept, qkv_kept, out_halves
+    result_far = result_part(hidden_rows[1], down_rank)
+    result_near = result_part(hidden_rows[0], down_rank)
+    text_moved, down_parts, out_parts, arrived, qkv_moved, text_kept, qkv_kept, result_far, result_near = fence(
+        text_moved, down_parts, out_parts, arrived, qkv_moved, text_kept, qkv_kept, result_far, result_near
     )
 
     qkv_moved = plan.move(qkv_moved)
-    if plan.aligned:
-        if hi_count == 2:
-            out_kept, out_moved = out_halves[0].astype(f32), swap(out_halves[1], "hi")
-        else:
-            out_kept, out_moved = None, plan.move(jnp.concatenate(out_halves))
-    else:
-        out_moved = ()
     text_grad = plan.text_by_rep(plan.total(text_kept, text_moved))
     text_parts = plan.reduce(text_grad)
+    result_arrived = settle_move(settle(result_far).astype(bf16))
     grad_normed = plan.ordered(settle(rows_near) + arrived.astype(f32))
     _, pull_attn_norm = jax.vjp(modulate, token_rows, gain_rows[0], scale_attn)
     grad_token_norm, grad_attn_gain, grad_scale_attn = pull_attn_norm(
         grad_normed.reshape(item_count, item_len, D)
     )
-    result = settle(result_part_near) + result_arrived.astype(f32)
-    result = result.reshape(item_count, item_len, D)
-    grad_mlp_gate = jnp.sum(grad_top * result, axis=1) * (1.0 - jnp.tanh(gate_mlp) ** 2)
+    result_near = settle(result_near)
     gate_up_parts = jnp.concatenate([gate_parts, up_parts], axis=-1)
     gate_up_parts = trade_ranks(gate_up_parts.reshape(RANKS, rows, -1))
-    text_parts, qkv_moved, out_moved, grad_mlp_gate, grad_scale_attn, grad_attn_gain, gate_up_parts = fence(
-        text_parts, qkv_moved, out_moved, grad_mlp_gate, grad_scale_attn, grad_attn_gain, gate_up_parts
-    )
+    text_parts, qkv_moved, result_arrived, result_near, grad_scale_attn, grad_attn_gain, gate_up_parts = fence(
+        text_parts, qkv_moved, result_arrived, result_near, grad_scale_attn, grad_attn_gain, gate_up_parts
+    )
+
+    qkv_grad = plan.by_rep(plan.total(qkv_kept, qkv_moved))
+    qkv_grad, result_near, text_parts = fence(qkv_grad, result_near, text_parts)
+    qkv_parts = plan.reduce(qkv_grad)
+    result = (result_near + result_arrived.astype(f32)).reshape(item_count, item_len, D)
+    grad_mlp_gate = jnp.sum(grad_top * result, axis=1) * (1.0 - jnp.tanh(gate_mlp) ** 2)
     layer_out = (middle + mlp_gate * result).astype(bf16).reshape(row_count, D)
     tokens_grad = (grad_middle + grad_token_norm).reshape(row_count, D)
-    qkv_grad = plan.by_rep(plan.total(qkv_kept, qkv_moved))
-    if plan.aligned:
-        out_grad = plan.total(out_kept, out_moved).reshape(rep_count, -1, 3 * rank_width)
-        qkv_grad = jnp.concatenate([qkv_grad, out_grad], axis=1)
-    else:
-        at = (jnp.arange(RANKS) == plan.rank).astype(bf16)[:, None, None]
-        out_grad = product(mixed_rows, branches, 0, rank_width, bf16)
-        placed = (out_grad[None] * at).reshape(D, D)
-        out_weight_grad = lax.psum_scatter(placed, AXES, scatter_dimension=0, tiled=True).astype(f32)
-    qkv_grad, grad_mlp_gate, text_parts = fence(qkv_grad, grad_mlp_gate, text_parts)
-    qkv_parts = plan.reduce(qkv_grad)
-    if plan.aligned:
-        out_weight_grad = qkv_parts[RANKS * rows :].reshape(-1, D).astype(f32)
-        qkv_parts = qkv_parts[: RANKS * rows]
 
     grad_modulation = jnp.concatenate(
         [grad_scale_attn, grad_attn_gate, grad_scale_mlp, grad_mlp_gate], axis=1
@@ -1047,7 +1049,7 @@
     gate_up_weight_grad = plan.from_ranks(gate_up_parts, 2, hi_count).astype(f32)
     text_weight_grad = whole(text_parts, text_weight, 2, plan.head_groups)
     qkv_weight_grad = whole(qkv_parts, qkv_weight, 3, plan.head_groups)
-    down_weight_grad = down_parts.astype(f32)
+    down_weight_grad, out_weight_grad = down_parts.astype(f32), out_parts.astype(f32)
     return (
         layer_out,
         tokens_grad,

time: 847 us -> 849 us (level)
  local copies, waits for them, and re-layouts: 113 us -> 100 us
  waiting for transfers between devices: 251 us -> 264 us
    ppermute x39, waiting for transfers between devices: 156 us -> 175 us  [swap(): return lax.ppermute(block, axis, [(at, at ^ step) for at in range(count)])]
  transfers between devices with their start and end apart: 59 -> 60, of which waited for: 25 -> 31; matrix products, arithmetic and copies ran while one was open for 22% -> 21% of each run, Pallas kernels for 30% -> 30%
where the time goes in v8:
time: 849 us; the launch traced here: 839 us
  Pallas kernels  278 us (33%)
  waiting for transfers between devices  264 us (31%)
  other arithmetic  111 us (13%)
  local copies, waits for them, and re-layouts  100 us (12%)
  starting transfers between devices  67.2 us (8%)
  between operations  15.9 us (2%)
    ppermute x39, waiting for transfers between devices, swap(): return lax.ppermute(block, axis, [(at, at ^ step) for at in range(count)])  175 us
    pallas_call x12, Pallas kernels, product(): pl.pallas_call(kernel, grid_spec=pltpu.PrefetchScalarGridSpec(num_scalar_...  89.6 us
    pallas_call x2, Pallas kernels, attend_back(): pl.pallas_call(attend_back_kernel, grid_spec=pltpu.PrefetchScalarGridSpec...  62.1 us
    pallas_call x2, Pallas kernels, attend(): pl.pallas_call(attend_kernel, grid_spec=pltpu.PrefetchScalarGridSpec(num_...  58 us
    pallas_call x2, Pallas kernels, feed(): pl.pallas_call(feed_kernel, grid=(steps,), in_specs=pair_specs(rows, step...  51.7 us
    all_to_all x1, waiting for transfers between devices, local(): lax.all_to_all(partial, AXES, 0, 0, tiled=True).astype(f32)  34.7 us
    ppermute x39, starting transfers between devices, swap(): return lax.ppermute(block, axis, [(at, at ^ step) for at in range(count)])  25.5 us
    all_to_all x6, starting transfers between devices, trade_ranks(): return lax.all_to_all(block, ('mid', 'core'), 0, 0, tiled=True)  24 us
  transfers between devices with their start and end apart: 60, of which 31 were waited for; matrix products, arithmetic and copies ran while one was open for 21% of the time, Pallas kernels for 30%

profile of v8, /device:TPU:8, one launch (start us, length us, event | category | flops | bytes accessed | tf_op | source)
XLA Modules:
  0.0 838.5 jit_solution(13064639038028000662)
XLA Ops:
  83.1 34.7 %all-to-all-done.2 = bf16[32,2,6144]{2,1,0:T(2,128)(2,1)S(1)} async-done(((bf16[32,2,6144]{2,1,0:T(2,128)(2,1)}), bf16[32,2,6144]{2,1,0:T(2,128)(2,1)S(1)}, u32[]{:S(2)}, u32[]{:S(2)}) %all-to-all-start.2) | async-done | bytes 786464 | tf_op jit(solution)/shard_map/all_to_all | solution.py:817
  138.6 35.7 %collective-permute-done.2.caption_ref = bf16[256,4096]{1,0:T(8,128)(2,1)} collective-permute-done((bf16[256,4096]{1,0:T(8,128)(2,1)}, bf16[256,4096]{1,0:T(8,128)(2,1)}, u32[]{:S(2)}, u32[]{:S(2)}) %collective-permute-start.2) | collective-permute-done | bytes 2097184 | tf_op jit(solution)/shard_map/ppermute | solution.py:570
  182.4 17.1 %all-gather.15.cloned.1.call-done.value_mine_ref = bf16[2048,384]{1,0:T(8,128)(2,1)} async-done(((bf16[512,384]{1,0:T(8,128)(2,1)}), bf16[2048,384]{1,0:T(8,128)(2,1)}) %all-gather.15.cloned.1.call-update) | async-done | bytes 1572880 | tf_op jit(solution)/shard_map/all_gather | solution.py:758
  199.5 17.4 %collective-permute-done.6.key_other_ref = bf16[2048,384]{1,0:T(8,128)(2,1)S(1)} collective-permute-done((bf16[2048,384]{1,0:T(8,128)(2,1)}, bf16[2048,384]{1,0:T(8,128)(2,1)S(1)}, u32[]{:S(2)}, u32[]{:S(2)}) %collective-permute-start.6) | collective-permute-done | bytes 1572896 | tf_op jit(solution)/shard_map/ppermute | solution.py:570
  237.5 13.3 %collective-permute-done.10.result_ref = bf16[512,1536]{1,0:T(8,128)(2,1)} collective-permute-done((bf16[512,1536]{1,0:T(8,128)(2,1)}, bf16[512,1536]{1,0:T(8,128)(2,1)}, u32[]{:S(2)}, u32[]{:S(2)}) %collective-permute-start.10) | collective-permute-done | bytes 1572896 | tf_op jit(solution)/shard_map/ppermute | solution.py:570
  264.3 25.0 %attend.2 = (bf16[1024,1536]{1,0:T(8,128)(2,1)}, bf16[512,4096]{1,0:T(8,128)(2,1)}, f32[1024,1152]{1,0:T(8,128)}, f32[512,384]{1,0:T(8,128)}, f32[512,384]{1,0:T...) custom-call(s32[4]{0:T(128)} %maximum_convert_fusion.2.kind_ref, ...), custom_call_target="tpu_custom_call" | custom-call | tf_op jit(solution)/shard_map/attend/pallas_call | solution.py:365
  305.8 33.0 %attend.3 = (bf16[1024,1536]{1,0:T(8,128)(2,1)}, bf16[512,4096]{1,0:T(8,128)(2,1)}, f32[1024,1152]{1,0:T(8,128)}, f32[512,384]{1,0:T(8,128)}, f32[512,384]{1,0:T...) custom-call(s32[4]{0:T(128)} %maximum_convert_fusion.kind_ref, ...), custom_call_target="tpu_custom_call" | custom-call | tf_op jit(solution)/shard_map/attend/pallas_call | solution.py:365
  352.3 25.8 %feed.2 = (bf16[1024,1536]{1,0:T(8,128)(2,1)}, bf16[1024,1536]{1,0:T(8,128)(2,1)}, bf16[1024,1024]{1,0:T(8,128)(2,1)}, bf16[1024,1024]{1,0:T(8,128)(2,1)}, bf16[...) custom-call(bf16[512,1536]{1,0:T(8,128)(2,1)} %copy-done.13, ...), custom_call_target="tpu_custom_call" | custom-call | tf_op jit(solution)/shard_map/feed/pallas_call | solution.py:527
  390.4 25.9 %feed.3 = (bf16[1024,1536]{1,0:T(8,128)(2,1)}, bf16[1024,1536]{1,0:T(8,128)(2,1)}, bf16[1024,1024]{1,0:T(8,128)(2,1)}, bf16[1024,1024]{1,0:T(8,128)(2,1)}, bf16[...) custom-call(bf16[512,1536]{1,0:T(8,128)(2,1)} %collective-permute-done.18.rows_ref, ...), custom_call_target="tpu_custom_call" | custom-call | tf_op jit(solution)/shard_map/feed/pallas_call | solution.py:527
  416.9 7.6 product.12
  448.1 8.6 %product.17 = f32[512,1536]{1,0:T(8,128)} custom-call(s32[1]{0:T(128)} %bitcast.45.first_ref, bf16[1024,1024]{1,0:T(8,128)(2,1)} %get-tuple-element.449.refs_0_.hidden_ref, bf16[1024,1024]{1,0:T(8,128)(2,1)} %get-tuple-element.446.refs_1_.hidden_ref, bf16[1024,1536]{1,0:T(8,128)(2,1)} %get-tuple-element.373.refs_2_, ...), custom_call_target="tpu_custom_call" | custom-call | tf_op jit(solution)/shard_map/product/pallas_call | solution.py:447
  456.7 8.1 product.14
  488.2 31.1 %attend_back.2 = (bf16[1024,1536]{1,0:T(8,128)(2,1)}, bf16[1024,1152]{1,0:T(8,128)(2,1)}, bf16[512,768]{1,0:T(8,128)(2,1)}, f32[512,1536]{1,0:T(8,128)}, bf16[512,1536]{1,0:T(8,128)(2,1)}, /*index=5*/f32[4,384]{1,0:T(4,128)}) custom-call(s32[4]{0:T(128)} %maximum_convert_fusion.kind_ref, s32[4]{0:T(128)} %maximum_convert_fusion.1.len_ref, ...), custom_call_target="tpu_custom_call" | custom-call | tf_op jit(solution)/shard_map/attend_back/pallas_call | solution.py:395
  533.2 31.0 %attend_back.3 = (bf16[1024,1536]{1,0:T(8,128)(2,1)}, bf16[1024,1152]{1,0:T(8,128)(2,1)}, bf16[512,768]{1,0:T(8,128)(2,1)}, f32[512,1536]{1,0:T(8,128)}, bf16[512,1536]{1,0:T(8,128)(2,1)}, /*index=5*/f32[4,384]{1,0:T(4,128)}) custom-call(s32[4]{0:T(128)} %maximum_convert_fusion.2.kind_ref, s32[4]{0:T(128)} %maximum_convert_fusion.3.len_ref, ...), custom_call_target="tpu_custom_call" | custom-call | tf_op jit(solution)/shard_map/attend_back/pallas_call | solution.py:395
  593.9 15.5 %collective-permute-done.32 = bf16[192,1536]{1,0:T(8,128)(2,1)S(1)} collective-permute-done((bf16[192,1536]{1,0:T(8,128)(2,1)S(1)}, bf16[192,1536]{1,0:T(8,128)(2,1)S(1)}, u32[]{:S(2)}, u32[]{:S(2)}) %collective-permute-start.32) | collective-permute-done | bytes 589856 | tf_op jit(solution)/shard_map/ppermute | solution.py:570
  611.9 8.6 %product.23 = f32[768,1152]{1,0:T(8,128)} custom-call(s32[1]{0:T(128)} %constant.580.clone.1.first_ref, bf16[1024,1536]{1,0:T(8,128)(2,1)} %get-tuple-element.440.refs_0_, bf16[1024,1536]{1,0:T(8,128)(2,1)} %get-tuple-element.441.refs_1_, bf16[1024,1152]{1,0:T(8,128)(2,1)} %get-tuple-element.442.refs_2_, bf16[1024,1152]{1,0:T(8,128)(2,1)} %get-tuple-element.443.refs_3_), custom_call_target="tpu_custom_call" | custom-call | tf_op jit(solution)/shard_map/product/pallas_call | solution.py:447
  620.5 8.4 product.21
  628.9 8.1 result.3
  637.0 8.4 %result.2 = (f32[512,1536]{1,0:T(8,128)}, bf16[512,1536]{1,0:T(8,128)(2,1)}) custom-call(bf16[1024,1024]{1,0:T(8,128)(2,1)} %get-tuple-element.446.refs_1_.hidden_ref, bf16[1024,1536]{1,0:T(8,128)(2,1)} %bitcast.188), custom_call_target="tpu_custom_call" | custom-call | tf_op jit(solution)/shard_map/result/pallas_call | solution.py:558
  645.4 7.8 product.22
  653.2 27.1 %collective-permute-done.30 = bf16[2048,768]{1,0:T(8,128)(2,1)} collective-permute-done((bf16[2048,768]{1,0:T(8,128)(2,1)}, bf16[2048,768]{1,0:T(8,128)(2,1)}, u32[]{:S(2)}, u32[]{:S(2)}) %collective-permute-start.30) | collective-permute-done | bytes 3145760 | tf_op jit(solution)/shard_map/ppermute | solution.py:570
  720.2 23.5 %collective-permute-done.34 = bf16[768,1152]{1,0:T(8,128)(2,1)} collective-permute-done((bf16[768,1152]{1,0:T(8,128)(2,1)}, bf16[768,1152]{1,0:T(8,128)(2,1)}, u32[]{:S(2)}, u32[]{:S(2)}) %collective-permute-start.34) | collective-permute-done | bytes 1769504 | tf_op jit(solution)/shard_map/ppermute | solution.py:570
  757.9 8.8 %fusion.9 = (f32[2,1536]{1,0:T(2,128)S(1)}, bf16[2,1536]{1,0:T(2,128)(2,1)S(1)}, f32[2,1536]{1,0:T(2,128)S(1)}, f32[512,1536]{1,0:T(8,128)}) fusion(bf16[512,1536]{1,0:T(8,128)(2,1)} %param.15, f32[2,256]{1,0:T(2,128)S(1)} %copy-done.69, f32[2,256]{1,0:T(2,128)S(1)} %copy-done.68, f32[1536]{0:T(1024)S(1)} %copy-done.40, ...), kind=kLoop, calls=%fused_computation.29 | loop fusion | flops 19651584 | bytes 20512768 | tf_op jit(solution)/shard_map/reduce_sum | solution.py:934
  795.4 20.7 %all-to-all-done.6 = bf16[32,2,6288]{2,1,0:T(2,128)(2,1)} async-done(((bf16[32,2,6288]{2,1,0:T(2,128)(2,1)}), bf16[32,2,6288]{2,1,0:T(2,128)(2,1)}, u32[]{:S(2)}, u32[]{:S(2)}) %all-to-all-start.6) | async-done | bytes 804896 | tf_op jit(solution)/shard_map/all_to_all | solution.py:1034
  (452 shorter events, 371.3 us)
Async XLA Ops:
  7.2 42.7 %all-gather.7.cloned.1.call-start = ((), (), s32[]{:S(2)}) async-start(), calls=%async_computation.15 | async-start | bytes 1966080 | tf_op jit(solution)/shard_map/all_gather | solution.py:758
  47.9 76.4 %all-gather.9.cloned.1.call-start = ((), (), s32[]{:S(2)}) async-start(), calls=%async_computation.16 | async-start | bytes 2949120 | tf_op jit(solution)/shard_map/all_gather | solution.py:758
  67.4 51.0 %collective-permute-start.1 = (bf16[256,4096]{1,0:T(8,128)(2,1)}, bf16[256,4096]{1,0:T(8,128)(2,1)}, u32[]{:S(2)}, u32[]{:S(2)}) collective-permute-start(bf16[256,4096]{1,0:T(8,128)(2,1)} %maximum_select_fusion.2.caption_ref), channel_id=1, source_target_pairs={{0,4},{4,0},{1,5},{5,1},{2,6},{6,2},{3,7},{7,3},{8,12},{12,8},{9,1... | collective-permute-start | bytes 6291464 | tf_op jit(solution)/shard_map/ppermute | solution.py:570
  75.4 42.4 %all-to-all-start.2 = ((bf16[32,2,6144]{2,1,0:T(2,128)(2,1)}), bf16[32,2,6144]{2,1,0:T(2,128)(2,1)S(1)}, u32[]{:S(2)}, u32[]{:S(2)}) async-start(bf16[32,2,6144]{2,1,0:T(2,128)(2,1)} %reshape.841), calls=%async_computation.2 | async-start | bytes 1572864 | tf_op jit(solution)/shard_map/all_to_all | solution.py:817
  79.4 100.3 %all-gather.17.cloned.1.call-start = ((), (), s32[]{:S(2)}) async-start(), calls=%async_computation.20 | async-start | bytes 1966080 | tf_op jit(solution)/shard_map/all_gather | solution.py:758
  79.4 44.8 %collective-permute-start = (bf16[512,1536]{1,0:T(8,128)(2,1)}, bf16[512,1536]{1,0:T(8,128)(2,1)}, u32[]{:S(2)}, u32[]{:S(2)}) collective-permute-start(bf16[512,1536]{1,0:T(8,128)(2,1)} %all-gather.7.cloned.1.call-done), channel_id=1, source_target_pairs={{0,16},{16,0},{1,17},{17,1},{2,18},{18,2},{3,19},{19,3},{4,20},{20... | collective-permute-start | bytes 4718600 | tf_op jit(solution)/shard_map/ppermute | solution.py:570
  125.2 74.3 %all-gather.15.cloned.1.call-start = ((), (), s32[]{:S(2)}) async-start(), calls=%async_computation.19 | async-start | bytes 1966080 | tf_op jit(solution)/shard_map/all_gather | solution.py:758
  126.6 53.2 %collective-permute-start.3 = (bf16[1024,1152]{1,0:T(8,128)(2,1)}, bf16[1024,1152]{1,0:T(8,128)(2,1)}, u32[]{:S(2)}, u32[]{:S(2)}) collective-permute-start(bf16[1024,1152]{1,0:T(8,128)(2,1)} %all-gather.9.cloned.1.call-done), channel_id=1, source_target_pairs={{0,16},{16,0},{1,17},{17,1},{2,18},{18,2},{3,19},{19,3},{4,20},{20... | collective-permute-start | bytes 7077896 | tf_op jit(solution)/shard_map/ppermute | solution.py:570
  127.3 47.1 %collective-permute-start.2 = (bf16[256,4096]{1,0:T(8,128)(2,1)}, bf16[256,4096]{1,0:T(8,128)(2,1)}, u32[]{:S(2)}, u32[]{:S(2)}) collective-permute-start(bf16[256,4096]{1,0:T(8,128)(2,1)} %maximum_select_fusion.2.caption_ref), channel_id=1, source_target_pairs={{0,8},{8,0},{1,9},{9,1},{2,10},{10,2},{3,11},{11,3},{4,12},{12,4},... | collective-permute-start | bytes 6291464 | tf_op jit(solution)/shard_map/ppermute | solution.py:570
  130.2 107.3 %all-gather.13.cloned.1.call-start = ((), (), s32[]{:S(2)}) async-start(), calls=%async_computation.18 | async-start | bytes 1966080 | tf_op jit(solution)/shard_map/all_gather | solution.py:758
  179.8 109.6 %all-gather.11.cloned.1.call-start = ((), (), s32[]{:S(2)}) async-start(), calls=%async_computation.17 | async-start | bytes 1966080 | tf_op jit(solution)/shard_map/all_gather | solution.py:758
  182.2 68.6 %collective-permute-start.10 = (bf16[512,1536]{1,0:T(8,128)(2,1)}, bf16[512,1536]{1,0:T(8,128)(2,1)}, u32[]{:S(2)}, u32[]{:S(2)}) collective-permute-start(bf16[512,1536]{1,0:T(8,128)(2,1)} %copy-done.14), channel_id=1, source_target_pairs={{0,8},{8,0},{1,9},{9,1},{2,10},{10,2},{3,11},{11,3},{4,12},{12,4},... | collective-permute-start | bytes 4718600 | tf_op jit(solution)/shard_map/ppermute | solution.py:570
  220.9 302.4 %reduce-scatter.7.cloned.1.call-start = ((), (), s32[]{:S(2)}) async-start(), calls=%async_computation.21 | async-start | bytes 1966080 | tf_op jit(solution)/shard_map/reduce_scatter | solution.py:710
  291.1 47.8 %collective-permute-start.16 = (bf16[512,1536]{1,0:T(8,128)(2,1)}, bf16[512,1536]{1,0:T(8,128)(2,1)}, u32[]{:S(2)}, u32[]{:S(2)}) collective-permute-start(bf16[512,1536]{1,0:T(8,128)(2,1)} %collective-permute-done.10.result_ref), channel_id=1, source_target_pairs={{0,4},{4,0},{1,5},{5,1},{2,6},{6,2},{3,7},{7,3},{8,12},{12,8},{9,1... | collective-permute-start | bytes 4718600 | tf_op jit(solution)/shard_map/ppermute | solution.py:570
  427.9 44.5 %collective-permute-start.22 = (bf16[512,1536]{1,0:T(8,128)(2,1)}, bf16[512,1536]{1,0:T(8,128)(2,1)}, u32[]{:S(2)}, u32[]{:S(2)}) collective-permute-start(bf16[512,1536]{1,0:T(8,128)(2,1)} %add_convert_fusion.7), channel_id=1, source_target_pairs={{0,8},{8,0},{1,9},{9,1},{2,10},{10,2},{3,11},{11,3},{4,12},{12,4},... | collective-permute-start | bytes 4718600 | tf_op jit(solution)/shard_map/ppermute | solution.py:570
  428.3 44.2 %collective-permute-start.23 = (bf16[768,1024]{1,0:T(8,128)(2,1)}, bf16[768,1024]{1,0:T(8,128)(2,1)}, u32[]{:S(2)}, u32[]{:S(2)}) collective-permute-start(bf16[768,1024]{1,0:T(8,128)(2,1)} %product.12), channel_id=1, source_target_pairs={{0,16},{16,0},{1,17},{17,1},{2,18},{18,2},{3,19},{19,3},{4,20},{20... | collective-permute-start | bytes 4718600 | tf_op jit(solution)/shard_map/ppermute | solution.py:570
  476.7 94.7 %reduce-scatter.9.cloned.1.call-start = ((), (), s32[]{:S(2)}) async-start(), calls=%async_computation.22 | async-start | bytes 1966080 | tf_op jit(solution)/shard_map/reduce_scatter | solution.py:710
  527.5 152.8 %reduce-scatter.13.cloned.1.call-start = ((), (), s32[]{:S(2)}) async-start(), calls=%async_computation.24 | async-start | bytes 737280 | tf_op jit(solution)/shard_map/reduce_scatter | solution.py:710
  527.8 43.7 %collective-permute-start.29 = (bf16[512,1536]{1,0:T(8,128)(2,1)}, bf16[512,1536]{1,0:T(8,128)(2,1)}, u32[]{:S(2)}, u32[]{:S(2)}) collective-permute-start(bf16[512,1536]{1,0:T(8,128)(2,1)} %product.14), channel_id=1, source_target_pairs={{0,16},{16,0},{1,17},{17,1},{2,18},{18,2},{3,19},{19,3},{4,20},{20... | collective-permute-start | bytes 4718600 | tf_op jit(solution)/shard_map/ppermute | solution.py:570
  610.4 69.9 %reduce-scatter.11.cloned.1.call-start = ((), (), s32[]{:S(2)}) async-start(), calls=%async_computation.23 | async-start | bytes 1966080 | tf_op jit(solution)/shard_map/reduce_scatter | solution.py:710
  610.4 69.9 %collective-permute-start.30 = (bf16[2048,768]{1,0:T(8,128)(2,1)}, bf16[2048,768]{1,0:T(8,128)(2,1)}, u32[]{:S(2)}, u32[]{:S(2)}) collective-permute-start(bf16[2048,768]{1,0:T(8,128)(2,1)} %product.18), channel_id=1, source_target_pairs={{0,16},{16,0},{1,17},{17,1},{2,18},{18,2},{3,19},{19,3},{4,20},{20... | collective-permute-start | bytes 9437192 | tf_op jit(solution)/shard_map/ppermute | solution.py:570
  611.0 134.6 %reduce-scatter.15.cloned.1.call-start = ((), (), s32[]{:S(2)}) async-start(), calls=%async_computation.25 | async-start | bytes 3932160 | tf_op jit(solution)/shard_map/reduce_scatter | solution.py:710
  757.3 58.9 %reduce-scatter.17.cloned.1.call-start = ((), (), s32[]{:S(2)}) async-start(), calls=%async_computation.26 | async-start | bytes 2211840 | tf_op jit(solution)/shard_map/reduce_scatter | solution.py:710
  769.0 47.1 %all-to-all-start.6 = ((bf16[32,2,6288]{2,1,0:T(2,128)(2,1)}), bf16[32,2,6288]{2,1,0:T(2,128)(2,1)}, u32[]{:S(2)}, u32[]{:S(2)}) async-start(bf16[32,2,6288]{2,1,0:T(2,128)(2,1)} %pad_maximum_fusion.2), calls=%async_computation.11 | async-start | bytes 1638400 | tf_op jit(solution)/shard_map/all_to_all | solution.py:1034
  (111 other events, 1884.9 us)
Sparse Core Ops, SparseCore 0:
  9.6 37.7 all-gather.6
  50.8 63.0 all-gather.8
  125.3 36.1 all-gather.16
  163.5 35.9 all-gather.14
  201.5 35.9 all-gather.12
  238.9 35.9 all-gather.10
  476.8 35.3 reduce-scatter.6
  527.7 34.3 reduce-scatter.8
  610.5 18.4 reduce-scatter.12
  631.1 35.2 reduce-scatter.10
  686.6 59.0 reduce-scatter.14
  760.1 56.0 reduce-scatter.16

commit v9 on v8

--- a/solution.py
+++ b/solution.py
@@ -803,7 +803,6 @@
     head_gains = jnp.concatenate([head_gains[1:4], cross_gate[None]])
     tables = (head_gains, cosine, sine)
     scalars = list(zip(kinds_sides, lengths_sides, strict=True))
-    tables, scalars = fence(tables, scalars)
 
     down_z, qkv_mine, text_weight, activated_mine = fence(
         down_z, qkv_mine, text_weight, activated_mine
@@ -833,8 +832,8 @@
     grad_top = out_cotangent.astype(f32).reshape(item_count, item_len, D)
     grad_result = (mlp_gate * grad_top).astype(bf16).reshape(row_count, D)
     normed_near, result_near = pair(normed), pair(grad_result)
-    text_key_z, captions_far, qkv_rank, down_rank, normed_near, result_near = fence(
-        text_key_z, captions_far, qkv_rank, down_rank, normed_near, result_near
+    text_key_z, captions_far, qkv_rank, down_rank, normed_near, result_near, tables, scalars = fence(
+        text_key_z, captions_far, qkv_rank, down_rank, normed_near, result_near, tables, scalars
     )
 
     text_value_z = z_gather(text_value_mine)
@@ -954,13 +953,21 @@
     captions, normed_rows = (captions_near, captions_far), (normed_near, normed_far)
     text_rows, qkv_rows, branches = (text_near, text_far), (qkv_near, qkv_far), (branch_near, branch_far)
     text_moved = plan.product_moved(captions, text_rows)
-    down_moved, up_parts, text_rows, qkv_rows, branches, rows_far, gain_far, text_moved = fence(
-        down_moved, up_parts, text_rows, qkv_rows, branches, rows_far, gain_far, text_moved
-    )
-
-    text_moved = plan.move(text_moved)
     down_grad = plan.total(down_kept, down_moved).reshape(rep_count, -1, D)
     across = settle(rows_far).astype(bf16)
+    down_grad, up_parts, across, text_rows, qkv_rows, branches, gain_far, text_moved, hidden_rows = fence(
+        down_grad, up_parts, across, text_rows, qkv_rows, branches, gain_far, text_moved, hidden_rows
+    )
+
+    text_moved = plan.move(text_moved)
+    down_parts = plan.reduce(down_grad)
+    arrived = settle_move(across)
+    result_far = result_part(hidden_rows[1], down_rank)
+    result_arrived = settle_move(settle(result_far).astype(bf16))
+    result_near = result_part(hidden_rows[0], down_rank)
+    qkv_moved = plan.product_moved(normed_rows, qkv_rows)
+    text_kept = plan.product_kept(captions, text_rows)
+    qkv_kept = plan.product_kept(normed_rows, qkv_rows)
     mixed_rows = [plan.ordered(kept[6]) for kept in (kept_near, kept_far)]
     if plan.aligned:
         halves = [slice(0, rank_width // 2), slice(rank_width // 2, None)]
@@ -970,52 +977,65 @@
         ]
     else:
         out_kept, out_moved = (), ()
-    across, down_grad, text_rows, qkv_rows, out_kept, out_moved, hidden_rows = fence(
-        across, down_grad, text_rows, qkv_rows, out_kept, out_moved, hidden_rows
-    )
-    down_parts = plan.reduce(down_grad)
-    arrived = settle_move(across)
+    (
+        text_moved,
+        down_parts,
+        arrived,
+        result_arrived,
+        result_near,
+        qkv_moved,
+        text_kept,
+        qkv_kept,
+        out_kept,
+        out_moved,
+    ) = fence(
+        text_moved,
+        down_parts,
+        arrived,
+        result_arrived,
+        result_near,
+        qkv_moved,
+        text_kept,
+        qkv_kept,
+        out_kept,
+        out_moved,
+    )
+
+    qkv_moved = plan.move(qkv_moved)
     if plan.aligned:
         if hi_count == 2:
-            out_grad = plan.total(out_kept.astype(f32), swap(out_moved, "hi"))
+            out_moved = swap(out_moved, "hi")
         else:
-            out_grad = plan.move(jnp.concatenate([out_kept, out_moved]))
-        out_parts = plan.reduce(out_grad.reshape(rep_count, -1, D))
-    else:
-        at = (jnp.arange(RANKS) == plan.rank).astype(bf16)[:, None, None]
-        out_grad = product(mixed_rows, branches, 0, rank_width, bf16)
-        placed = (out_grad[None] * at).reshape(D, D)
-        out_parts = lax.psum_scatter(placed, AXES, scatter_dimension=0, tiled=True)
-    qkv_moved = plan.product_moved(normed_rows, qkv_rows)
-    text_kept = plan.product_kept(captions, text_rows)
-    qkv_kept = plan.product_kept(normed_rows, qkv_rows)
-    result_far = result_part(hidden_rows[1], down_rank)
-    result_near = result_part(hidden_rows[0], down_rank)
-    text_moved, down_parts, out_parts, arrived, qkv_moved, text_kept, qkv_kept, result_far, result_near = fence(
-        text_moved, down_parts, out_parts, arrived, qkv_moved, text_kept, qkv_kept, result_far, result_near
-    )
-
-    qkv_moved = plan.move(qkv_moved)
+            out_moved = plan.move(jnp.concatenate([out_kept, out_moved]))
     text_grad = plan.text_by_rep(plan.total(text_kept, text_moved))
     text_parts = plan.reduce(text_grad)
-    result_arrived = settle_move(settle(result_far).astype(bf16))
     grad_normed = plan.ordered(settle(rows_near) + arrived.astype(f32))
     _, pull_attn_norm = jax.vjp(modulate, token_rows, gain_rows[0], scale_attn)
     grad_token_norm, grad_attn_gain, grad_scale_attn = pull_attn_norm(
         grad_normed.reshape(item_count, item_len, D)
     )
-    result_near = settle(result_near)
-    gate_up_parts = jnp.concatenate([gate_parts, up_parts], axis=-1)
-    gate_up_parts = trade_ranks(gate_up_parts.reshape(RANKS, rows, -1))
-    text_parts, qkv_moved, result_arrived, result_near, grad_scale_attn, grad_attn_gain, gate_up_parts = fence(
-        text_parts, qkv_moved, result_arrived, result_near, grad_scale_attn, grad_attn_gain, gate_up_parts
+    result = (settle(result_near) + result_arrived.astype(f32)).reshape(item_count, item_len, D)
+    grad_mlp_gate = jnp.sum(grad_top * result, axis=1) * (1.0 - jnp.tanh(gate_mlp) ** 2)
+    text_parts, qkv_moved, out_moved, grad_mlp_gate, grad_scale_attn, grad_attn_gain = fence(
+        text_parts, qkv_moved, out_moved, grad_mlp_gate, grad_scale_attn, grad_attn_gain
     )
 
     qkv_grad = plan.by_rep(plan.total(qkv_kept, qkv_moved))
-    qkv_grad, result_near, text_parts = fence(qkv_grad, result_near, text_parts)
+    if plan.aligned:
+        out_grad = plan.total(out_kept.astype(f32), out_moved) if hi_count == 2 else out_moved
+        out_grad = out_grad.reshape(rep_count, -1, D)
+    else:
+        at = (jnp.arange(RANKS) == plan.rank).astype(bf16)[:, None, None]
+        out_grad = product(mixed_rows, branches, 0, rank_width, bf16)
+        out_grad = (out_grad[None] * at).reshape(D, D)
+    qkv_grad, out_grad, grad_mlp_gate, text_parts = fence(
+        qkv_grad, out_grad, grad_mlp_gate, text_parts
+    )
     qkv_parts = plan.reduce(qkv_grad)
-    result = (result_near + result_arrived.astype(f32)).reshape(item_count, item_len, D)
-    grad_mlp_gate = jnp.sum(grad_top * result, axis=1) * (1.0 - jnp.tanh(gate_mlp) ** 2)
+    if plan.aligned:
+        out_parts = plan.reduce(out_grad)
+    else:
+        out_parts = lax.psum_scatter(out_grad, AXES, scatter_dimension=0, tiled=True)
     layer_out = (middle + mlp_gate * result).astype(bf16).reshape(row_count, D)
     tokens_grad = (grad_middle + grad_token_norm).reshape(row_count, D)
 
@@ -1046,7 +1066,9 @@
         blocks = trade_ranks(parts.reshape(RANKS, weight.shape[0], -1))
         return plan.from_ranks(blocks, sections, groups).astype(f32)
 
-    gate_up_weight_grad = plan.from_ranks(gate_up_parts, 2, hi_count).astype(f32)
+    gate_up_weight_grad = whole(
+        jnp.concatenate([gate_parts, up_parts], axis=-1), gate_up_weight, 2, hi_count
+    )
     text_weight_grad = whole(text_parts, text_weight, 2, plan.head_groups)
     qkv_weight_grad = whole(qkv_parts, qkv_weight, 3, plan.head_groups)
     down_weight_grad, out_weight_grad = down_parts.astype(f32), out_parts.astype(f32)

time: 849 us -> 868 us (1.022)
  waiting for transfers between devices: 264 us -> 290 us
    ppermute x39, waiting for transfers between devices: 175 us -> 198 us  [swap(): return lax.ppermute(block, axis, [(at, at ^ step) for at in range(count)])]
    convert_element_type x3 -> x0, local copies, waits for them, and re-layouts: 9.84 us -> none  [local(): plan.from_ranks(gate_up_parts, 2, hi_count).astype(f32)]
    convert_element_type x4 -> x7, local copies, waits for them, and re-layouts: 3.45 us -> 13.3 us  [whole(): return plan.from_ranks(blocks, sections, groups).astype(f32)]
    all_to_all x6, waiting for transfers between devices: 9.91 us -> 19.3 us  [trade_ranks(): return lax.all_to_all(block, ('mid', 'core'), 0, 0, tiled=True)]
    reduce_scatter x6, waiting for transfers between devices: 0.85 us -> 9.82 us  [reduce(): return lax.psum_scatter(flat, 'rep', scatter_dimension=0, tiled=True)]
  transfers between devices with their start and end apart: 60 -> 60, of which waited for: 31 -> 30; matrix products, arithmetic and copies ran while one was open for 21% -> 22% of each run, Pallas kernels for 30% -> 28%
where the time goes in v9:
time: 868 us; the launch traced here: 854 us
  waiting for transfers between devices  290 us (33%)
  Pallas kernels  271 us (31%)
  other arithmetic  110 us (13%)
  local copies, waits for them, and re-layouts  97 us (11%)
  starting transfers between devices  68.9 us (8%)
  between operations  15.5 us (2%)
    ppermute x39, waiting for transfers between devices, swap(): return lax.ppermute(block, axis, [(at, at ^ step) for at in range(count)])  198 us
    pallas_call x12, Pallas kernels, product(): pl.pallas_call(kernel, grid_spec=pltpu.PrefetchScalarGridSpec(num_scalar_...  90.2 us
    pallas_call x2, Pallas kernels, attend_back(): pl.pallas_call(attend_back_kernel, grid_spec=pltpu.PrefetchScalarGridSpec...  62.3 us
    pallas_call x2, Pallas kernels, feed(): pl.pallas_call(feed_kernel, grid=(steps,), in_specs=pair_specs(rows, step...  51.9 us
    pallas_call x2, Pallas kernels, attend(): pl.pallas_call(attend_kernel, grid_spec=pltpu.PrefetchScalarGridSpec(num_...  50.2 us
    all_to_all x1, waiting for transfers between devices, local(): lax.all_to_all(partial, AXES, 0, 0, tiled=True).astype(f32)  34 us
    ppermute x39, starting transfers between devices, swap(): return lax.ppermute(block, axis, [(at, at ^ step) for at in range(count)])  29.3 us
    all_to_all x6, starting transfers between devices, trade_ranks(): return lax.all_to_all(block, ('mid', 'core'), 0, 0, tiled=True)  23.9 us
  transfers between devices with their start and end apart: 60, of which 30 were waited for; matrix products, arithmetic and copies ran while one was open for 22% of the time, Pallas kernels for 28%

profile of v9, /device:TPU:8, one launch (start us, length us, event | category | flops | bytes accessed | tf_op | source)
XLA Modules:
  0.0 854.1 jit_solution(9239892501367071226)
XLA Ops:
  84.4 34.0 %all-to-all-done.2 = bf16[32,2,6144]{2,1,0:T(2,128)(2,1)S(1)} async-done(((bf16[32,2,6144]{2,1,0:T(2,128)(2,1)}), bf16[32,2,6144]{2,1,0:T(2,128)(2,1)S(1)}, u32[]{:S(2)}, u32[]{:S(2)}) %all-to-all-start.2) | async-done | bytes 786464 | tf_op jit(solution)/shard_map/all_to_all | solution.py:816
  152.5 31.5 %collective-permute-done.2.caption_ref = bf16[256,4096]{1,0:T(8,128)(2,1)} collective-permute-done((bf16[256,4096]{1,0:T(8,128)(2,1)}, bf16[256,4096]{1,0:T(8,128)(2,1)}, u32[]{:S(2)}, u32[]{:S(2)}) %collective-permute-start.2) | collective-permute-done | bytes 2097184 | tf_op jit(solution)/shard_map/ppermute | solution.py:570
  189.0 11.1 %all-gather.15.cloned.1.call-done.value_mine_ref = bf16[2048,384]{1,0:T(8,128)(2,1)} async-done(((bf16[512,384]{1,0:T(8,128)(2,1)}), bf16[2048,384]{1,0:T(8,128)(2,1)}) %all-gather.15.cloned.1.call-update) | async-done | bytes 1572880 | tf_op jit(solution)/shard_map/all_gather | solution.py:758
  200.1 23.4 %collective-permute-done.6.key_other_ref = bf16[2048,384]{1,0:T(8,128)(2,1)S(1)} collective-permute-done((bf16[2048,384]{1,0:T(8,128)(2,1)}, bf16[2048,384]{1,0:T(8,128)(2,1)S(1)}, u32[]{:S(2)}, u32[]{:S(2)}) %collective-permute-start.6) | collective-permute-done | bytes 1572896 | tf_op jit(solution)/shard_map/ppermute | solution.py:570
  240.3 17.3 %collective-permute-done.10.result_ref = bf16[512,1536]{1,0:T(8,128)(2,1)} collective-permute-done((bf16[512,1536]{1,0:T(8,128)(2,1)}, bf16[512,1536]{1,0:T(8,128)(2,1)}, u32[]{:S(2)}, u32[]{:S(2)}) %collective-permute-start.10) | collective-permute-done | bytes 1572896 | tf_op jit(solution)/shard_map/ppermute | solution.py:570
  264.8 25.2 %attend.2 = (bf16[1024,1536]{1,0:T(8,128)(2,1)}, bf16[512,4096]{1,0:T(8,128)(2,1)}, f32[1024,1152]{1,0:T(8,128)}, f32[512,384]{1,0:T(8,128)}, f32[512,384]{1,0:T...) custom-call(s32[4]{0:T(128)} %maximum_convert_fusion.2.kind_ref, ...), custom_call_target="tpu_custom_call" | custom-call | tf_op jit(solution)/shard_map/attend/pallas_call | solution.py:365
  290.0 7.8 collective-permute-done.12
  312.6 25.1 %attend.3 = (bf16[1024,1536]{1,0:T(8,128)(2,1)}, bf16[512,4096]{1,0:T(8,128)(2,1)}, f32[1024,1152]{1,0:T(8,128)}, f32[512,384]{1,0:T(8,128)}, f32[512,384]{1,0:T...) custom-call(s32[4]{0:T(128)} %maximum_convert_fusion.kind_ref, ...), custom_call_target="tpu_custom_call" | custom-call | tf_op jit(solution)/shard_map/attend/pallas_call | solution.py:365
  357.0 26.1 %feed.2 = (bf16[1024,1536]{1,0:T(8,128)(2,1)}, bf16[1024,1536]{1,0:T(8,128)(2,1)}, bf16[1024,1024]{1,0:T(8,128)(2,1)}, bf16[1024,1024]{1,0:T(8,128)(2,1)}, bf16[...) custom-call(bf16[512,1536]{1,0:T(8,128)(2,1)} %copy-done.17, ...), custom_call_target="tpu_custom_call" | custom-call | tf_op jit(solution)/shard_map/feed/pallas_call | solution.py:527
  395.1 25.9 %feed.3 = (bf16[1024,1536]{1,0:T(8,128)(2,1)}, bf16[1024,1536]{1,0:T(8,128)(2,1)}, bf16[1024,1024]{1,0:T(8,128)(2,1)}, bf16[1024,1024]{1,0:T(8,128)(2,1)}, bf16[...) custom-call(bf16[512,1536]{1,0:T(8,128)(2,1)} %collective-permute-done.18.rows_ref, ...), custom_call_target="tpu_custom_call" | custom-call | tf_op jit(solution)/shard_map/feed/pallas_call | solution.py:527
  454.9 8.6 %product.17 = f32[512,1536]{1,0:T(8,128)} custom-call(s32[1]{0:T(128)} %bitcast.45.first_ref, bf16[1024,1024]{1,0:T(8,128)(2,1)} %get-tuple-element.421.refs_0_.hidden_ref, bf16[1024,1024]{1,0:T(8,128)(2,1)} %get-tuple-element.418.refs_1_.hidden_ref, bf16[1024,1536]{1,0:T(8,128)(2,1)} %get-tuple-element.364.refs_2_, ...), custom_call_target="tpu_custom_call" | custom-call | tf_op jit(solution)/shard_map/product/pallas_call | solution.py:447
  463.5 8.1 product.14
  494.6 31.2 %attend_back.2 = (bf16[1024,1536]{1,0:T(8,128)(2,1)}, bf16[1024,1152]{1,0:T(8,128)(2,1)}, bf16[512,768]{1,0:T(8,128)(2,1)}, f32[512,1536]{1,0:T(8,128)}, bf16[512,1536]{1,0:T(8,128)(2,1)}, /*index=5*/f32[4,384]{1,0:T(4,128)}) custom-call(s32[4]{0:T(128)} %maximum_convert_fusion.kind_ref, s32[4]{0:T(128)} %maximum_convert_fusion.1.len_ref, ...), custom_call_target="tpu_custom_call" | custom-call | tf_op jit(solution)/shard_map/attend_back/pallas_call | solution.py:395
  532.6 31.1 %attend_back.3 = (bf16[1024,1536]{1,0:T(8,128)(2,1)}, bf16[1024,1152]{1,0:T(8,128)(2,1)}, bf16[512,768]{1,0:T(8,128)(2,1)}, f32[512,1536]{1,0:T(8,128)}, bf16[512,1536]{1,0:T(8,128)(2,1)}, /*index=5*/f32[4,384]{1,0:T(4,128)}) custom-call(s32[4]{0:T(128)} %maximum_convert_fusion.2.kind_ref, s32[4]{0:T(128)} %maximum_convert_fusion.3.len_ref, ...), custom_call_target="tpu_custom_call" | custom-call | tf_op jit(solution)/shard_map/attend_back/pallas_call | solution.py:395
  576.6 24.2 %collective-permute-done.29 = bf16[512,1536]{1,0:T(8,128)(2,1)} collective-permute-done((bf16[512,1536]{1,0:T(8,128)(2,1)S(1)}, bf16[512,1536]{1,0:T(8,128)(2,1)}, u32[]{:S(2)}, u32[]{:S(2)}) %collective-permute-start.29) | collective-permute-done | bytes 1572896 | tf_op jit(solution)/shard_map/ppermute | solution.py:570
  603.9 8.1 result.2
  624.1 9.1 %product.21 = f32[768,1152]{1,0:T(8,128)} custom-call(s32[1]{0:T(128)} %constant.580.clone.1.first_ref, bf16[1024,1536]{1,0:T(8,128)(2,1)} %get-tuple-element.424.refs_0_, bf16[1024,1536]{1,0:T(8,128)(2,1)} %get-tuple-element.425.refs_1_, bf16[1024,1152]{1,0:T(8,128)(2,1)} %get-tuple-element.426.refs_2_, bf16[1024,1152]{1,0:T(8,128)(2,1)} %get-tuple-element.427.refs_3_), custom_call_target="tpu_custom_call" | custom-call | tf_op jit(solution)/shard_map/product/pallas_call | solution.py:447
  633.1 8.4 product.19
  641.5 8.2 result.3
  668.2 15.4 %collective-permute-done.34 = bf16[512,1536]{1,0:T(8,128)(2,1)} collective-permute-done((bf16[512,1536]{1,0:T(8,128)(2,1)S(1)}, bf16[512,1536]{1,0:T(8,128)(2,1)}, u32[]{:S(2)}, u32[]{:S(2)}) %collective-permute-start.34) | collective-permute-done | bytes 1572896 | tf_op jit(solution)/shard_map/ppermute | solution.py:570
  722.5 35.1 %collective-permute-done.38 = bf16[192,1536]{1,0:T(8,128)(2,1)} collective-permute-done((bf16[192,1536]{1,0:T(8,128)(2,1)}, bf16[192,1536]{1,0:T(8,128)(2,1)}, u32[]{:S(2)}, u32[]{:S(2)}) %collective-permute-start.38) | collective-permute-done | bytes 589856 | tf_op jit(solution)/shard_map/ppermute | solution.py:570
  773.8 9.7 %all-to-all-done.7 = bf16[4,128,768]{1,2,0:T(8,128)(2,1)} async-done(((bf16[4,128,768]{1,2,0:T(8,128)(2,1)}), bf16[4,128,768]{1,2,0:T(8,128)(2,1)}, u32[]{:S(2)}, u32[]{:S(2)}) %all-to-all-start.7) | async-done | bytes 786464 | tf_op jit(solution)/shard_map/all_to_all | solution.py:603
  807.3 13.6 %all-to-all-done.5 = bf16[32,2,6288]{2,1,0:T(2,128)(2,1)} async-done(((bf16[32,2,6288]{2,1,0:T(2,128)(2,1)}), bf16[32,2,6288]{2,1,0:T(2,128)(2,1)}, u32[]{:S(2)}, u32[]{:S(2)}) %all-to-all-start.5) | async-done | bytes 804896 | tf_op jit(solution)/shard_map/all_to_all | solution.py:1054
  827.6 9.8 %reduce-scatter.17.cloned.1.call-done = bf16[48,1536]{1,0:T(8,128)(2,1)} async-done(((bf16[192,1536]{1,0:T(8,128)(2,1)}), bf16[48,1536]{1,0:T(8,128)(2,1)}) %reduce-scatter.17.cloned.1.call-update) | async-done | bytes 147472 | tf_op jit(solution)/shard_map/reduce_scatter | solution.py:710
  (433 shorter events, 390.8 us)
Async XLA Ops:
  48.5 76.4 %all-gather.9.cloned.1.call-start = ((), (), s32[]{:S(2)}) async-start(), calls=%async_computation.16 | async-start | bytes 2949120 | tf_op jit(solution)/shard_map/all_gather | solution.py:758
  68.0 51.0 %collective-permute-start.1 = (bf16[256,4096]{1,0:T(8,128)(2,1)}, bf16[256,4096]{1,0:T(8,128)(2,1)}, u32[]{:S(2)}, u32[]{:S(2)}) collective-permute-start(bf16[256,4096]{1,0:T(8,128)(2,1)} %maximum_select_fusion.2.caption_ref), channel_id=1, source_target_pairs={{0,4},{4,0},{1,5},{5,1},{2,6},{6,2},{3,7},{7,3},{8,12},{12,8},{9,1... | collective-permute-start | bytes 6291464 | tf_op jit(solution)/shard_map/ppermute | solution.py:570
  80.0 106.3 %all-gather.17.cloned.1.call-start = ((), (), s32[]{:S(2)}) async-start(), calls=%async_computation.20 | async-start | bytes 1966080 | tf_op jit(solution)/shard_map/all_gather | solution.py:758
  80.0 44.8 %collective-permute-start = (bf16[512,1536]{1,0:T(8,128)(2,1)}, bf16[512,1536]{1,0:T(8,128)(2,1)}, u32[]{:S(2)}, u32[]{:S(2)}) collective-permute-start(bf16[512,1536]{1,0:T(8,128)(2,1)} %all-gather.7.cloned.1.call-done), channel_id=1, source_target_pairs={{0,16},{16,0},{1,17},{17,1},{2,18},{18,2},{3,19},{19,3},{4,20},{20... | collective-permute-start | bytes 4718600 | tf_op jit(solution)/shard_map/ppermute | solution.py:570
  125.8 74.3 %all-gather.15.cloned.1.call-start = ((), (), s32[]{:S(2)}) async-start(), calls=%async_computation.19 | async-start | bytes 1966080 | tf_op jit(solution)/shard_map/all_gather | solution.py:758
  133.2 53.1 %collective-permute-start.3 = (bf16[1024,1152]{1,0:T(8,128)(2,1)}, bf16[1024,1152]{1,0:T(8,128)(2,1)}, u32[]{:S(2)}, u32[]{:S(2)}) collective-permute-start(bf16[1024,1152]{1,0:T(8,128)(2,1)} %all-gather.9.cloned.1.call-done), channel_id=1, source_target_pairs={{0,16},{16,0},{1,17},{17,1},{2,18},{18,2},{3,19},{19,3},{4,20},{20... | collective-permute-start | bytes 7077896 | tf_op jit(solution)/shard_map/ppermute | solution.py:570
  137.0 47.1 %collective-permute-start.2 = (bf16[256,4096]{1,0:T(8,128)(2,1)}, bf16[256,4096]{1,0:T(8,128)(2,1)}, u32[]{:S(2)}, u32[]{:S(2)}) collective-permute-start(bf16[256,4096]{1,0:T(8,128)(2,1)} %maximum_select_fusion.2.caption_ref), channel_id=1, source_target_pairs={{0,8},{8,0},{1,9},{9,1},{2,10},{10,2},{3,11},{11,3},{4,12},{12,4},... | collective-permute-start | bytes 6291464 | tf_op jit(solution)/shard_map/ppermute | solution.py:570
  139.2 101.0 %all-gather.13.cloned.1.call-start = ((), (), s32[]{:S(2)}) async-start(), calls=%async_computation.18 | async-start | bytes 1966080 | tf_op jit(solution)/shard_map/all_gather | solution.py:758
  186.3 103.7 %all-gather.11.cloned.1.call-start = ((), (), s32[]{:S(2)}) async-start(), calls=%async_computation.17 | async-start | bytes 1966080 | tf_op jit(solution)/shard_map/all_gather | solution.py:758
  188.7 68.8 %collective-permute-start.10 = (bf16[512,1536]{1,0:T(8,128)(2,1)}, bf16[512,1536]{1,0:T(8,128)(2,1)}, u32[]{:S(2)}, u32[]{:S(2)}) collective-permute-start(bf16[512,1536]{1,0:T(8,128)(2,1)} %fusion.12.result_ref), channel_id=1, source_target_pairs={{0,8},{8,0},{1,9},{9,1},{2,10},{10,2},{3,11},{11,3},{4,12},{12,4},... | collective-permute-start | bytes 4718600 | tf_op jit(solution)/shard_map/ppermute | solution.py:570
  226.0 302.3 %reduce-scatter.7.cloned.1.call-start = ((), (), s32[]{:S(2)}) async-start(), calls=%async_computation.21 | async-start | bytes 1966080 | tf_op jit(solution)/shard_map/reduce_scatter | solution.py:710
  432.4 46.8 %collective-permute-start.22 = (bf16[512,1536]{1,0:T(8,128)(2,1)}, bf16[512,1536]{1,0:T(8,128)(2,1)}, u32[]{:S(2)}, u32[]{:S(2)}) collective-permute-start(bf16[512,1536]{1,0:T(8,128)(2,1)} %add_convert_fusion.7), channel_id=1, source_target_pairs={{0,8},{8,0},{1,9},{9,1},{2,10},{10,2},{3,11},{11,3},{4,12},{12,4},... | collective-permute-start | bytes 4718600 | tf_op jit(solution)/shard_map/ppermute | solution.py:570
  434.1 45.2 %collective-permute-start.23 = (bf16[768,1024]{1,0:T(8,128)(2,1)}, bf16[768,1024]{1,0:T(8,128)(2,1)}, u32[]{:S(2)}, u32[]{:S(2)}) collective-permute-start(bf16[768,1024]{1,0:T(8,128)(2,1)} %product.12), channel_id=1, source_target_pairs={{0,16},{16,0},{1,17},{17,1},{2,18},{18,2},{3,19},{19,3},{4,20},{20... | collective-permute-start | bytes 4718600 | tf_op jit(solution)/shard_map/ppermute | solution.py:570
  483.5 120.4 %reduce-scatter.9.cloned.1.call-start = ((), (), s32[]{:S(2)}) async-start(), calls=%async_computation.22 | async-start | bytes 1966080 | tf_op jit(solution)/shard_map/reduce_scatter | solution.py:710
  532.6 151.1 %reduce-scatter.11.cloned.1.call-start = ((), (), s32[]{:S(2)}) async-start(), calls=%async_computation.23 | async-start | bytes 1966080 | tf_op jit(solution)/shard_map/reduce_scatter | solution.py:710
  612.0 71.6 %collective-permute-start.31 = (bf16[2048,768]{1,0:T(8,128)(2,1)}, bf16[2048,768]{1,0:T(8,128)(2,1)}, u32[]{:S(2)}, u32[]{:S(2)}) collective-permute-start(bf16[2048,768]{1,0:T(8,128)(2,1)} %product.18), channel_id=1, source_target_pairs={{0,16},{16,0},{1,17},{17,1},{2,18},{18,2},{3,19},{19,3},{4,20},{20... | collective-permute-start | bytes 9437192 | tf_op jit(solution)/shard_map/ppermute | solution.py:570
  613.0 144.7 %reduce-scatter.13.cloned.1.call-start = ((), (), s32[]{:S(2)}) async-start(), calls=%async_computation.24 | async-start | bytes 3932160 | tf_op jit(solution)/shard_map/reduce_scatter | solution.py:710
  613.0 55.2 %collective-permute-start.32 = (bf16[512,1536]{1,0:T(8,128)(2,1)}, bf16[512,1536]{1,0:T(8,128)(2,1)}, u32[]{:S(2)}, u32[]{:S(2)}) collective-permute-start(bf16[512,1536]{1,0:T(8,128)(2,1)} %add_convert_fusion.3), channel_id=1, source_target_pairs={{0,8},{8,0},{1,9},{9,1},{2,10},{10,2},{3,11},{11,3},{4,12},{12,4},... | collective-permute-start | bytes 4718600 | tf_op jit(solution)/shard_map/ppermute | solution.py:570
  618.7 65.0 %collective-permute-start.34 = (bf16[512,1536]{1,0:T(8,128)(2,1)S(1)}, bf16[512,1536]{1,0:T(8,128)(2,1)}, u32[]{:S(2)}, u32[]{:S(2)}) collective-permute-start(bf16[512,1536]{1,0:T(8,128)(2,1)S(1)} %add_convert_fusion.2), channel_id=1, source_target_pairs={{0,8},{8,0},{1,9},{9,1},{2,10},{10,2},{3,11},{11,3},{4,12},{12,4},... | collective-permute-start | bytes 4718600 | tf_op jit(solution)/shard_map/ppermute | solution.py:570
  698.8 68.7 %all-to-all-start.8 = ((bf16[4,48,2048]{2,1,0:T(8,128)(2,1)}), bf16[4,48,2048]{2,1,0:T(8,128)(2,1)}, u32[]{:S(2)}, u32[]{:S(2)}) async-start(bf16[4,48,2048]{2,1,0:T(8,128)(2,1)} %bitcast.223), calls=%async_computation.14 | async-start | bytes 1572864 | tf_op jit(solution)/shard_map/all_to_all | solution.py:603
  703.0 117.9 %reduce-scatter.15.cloned.1.call-start = ((), (), s32[]{:S(2)}) async-start(), calls=%async_computation.25 | async-start | bytes 2211840 | tf_op jit(solution)/shard_map/reduce_scatter | solution.py:710
  703.7 53.9 %collective-permute-start.37 = (bf16[768,1152]{1,0:T(8,128)(2,1)}, bf16[768,1152]{1,0:T(8,128)(2,1)}, u32[]{:S(2)}, u32[]{:S(2)}) collective-permute-start(bf16[768,1152]{1,0:T(8,128)(2,1)} %product.19), channel_id=1, source_target_pairs={{0,16},{16,0},{1,17},{17,1},{2,18},{18,2},{3,19},{19,3},{4,20},{20... | collective-permute-start | bytes 5308424 | tf_op jit(solution)/shard_map/ppermute | solution.py:570
  704.8 52.8 %collective-permute-start.38 = (bf16[192,1536]{1,0:T(8,128)(2,1)}, bf16[192,1536]{1,0:T(8,128)(2,1)}, u32[]{:S(2)}, u32[]{:S(2)}) collective-permute-start(bf16[192,1536]{1,0:T(8,128)(2,1)} %product.23), channel_id=1, source_target_pairs={{0,16},{16,0},{1,17},{17,1},{2,18},{18,2},{3,19},{19,3},{4,20},{20... | collective-permute-start | bytes 1769480 | tf_op jit(solution)/shard_map/ppermute | solution.py:570
  788.1 49.4 %reduce-scatter.17.cloned.1.call-start = ((), (), s32[]{:S(2)}) async-start(), calls=%async_computation.26 | async-start | bytes 737280 | tf_op jit(solution)/shard_map/reduce_scatter | solution.py:710
  (102 other events, 1795.4 us)
Sparse Core Ops, SparseCore 0:
  9.6 37.7 all-gather.6
  51.4 63.0 all-gather.8
  125.9 36.1 all-gather.16
  164.1 35.9 all-gather.14
  202.1 35.9 all-gather.12
  239.5 35.9 all-gather.10
  483.6 33.7 reduce-scatter.6
  532.7 34.9 reduce-scatter.8
  613.1 34.9 reduce-scatter.10
  689.9 60.5 reduce-scatter.12
  764.1 52.1 reduce-scatter.14
  819.1 18.2 reduce-scatter.16

commit v10 on v8

--- a/solution.py
+++ b/solution.py
@@ -803,7 +803,6 @@
     head_gains = jnp.concatenate([head_gains[1:4], cross_gate[None]])
     tables = (head_gains, cosine, sine)
     scalars = list(zip(kinds_sides, lengths_sides, strict=True))
-    tables, scalars = fence(tables, scalars)
 
     down_z, qkv_mine, text_weight, activated_mine = fence(
         down_z, qkv_mine, text_weight, activated_mine
@@ -833,8 +832,8 @@
     grad_top = out_cotangent.astype(f32).reshape(item_count, item_len, D)
     grad_result = (mlp_gate * grad_top).astype(bf16).reshape(row_count, D)
     normed_near, result_near = pair(normed), pair(grad_result)
-    text_key_z, captions_far, qkv_rank, down_rank, normed_near, result_near = fence(
-        text_key_z, captions_far, qkv_rank, down_rank, normed_near, result_near
+    text_key_z, captions_far, qkv_rank, down_rank, normed_near, result_near, tables, scalars = fence(
+        text_key_z, captions_far, qkv_rank, down_rank, normed_near, result_near, tables, scalars
     )
 
     text_value_z = z_gather(text_value_mine)
@@ -847,7 +846,6 @@
 
     gate_z = z_gather(gate_mine)
     text_value_rank = plan.across_hi(text_value_z)
-    result_far = swap(result_near[0], "mid")
     normed_far = pair(normed_far)
     if plan.aligned:
         blocks = [block.reshape(rep_count, -1, 3 * rank_width) for block in qkv_rank]
@@ -856,8 +854,8 @@
         qkv_rank = [block[:, : RANKS * rows].reshape(-1, 3 * rank_width) for block in blocks]
         qkv_rank = qkv_rank if hi_count == 2 else jnp.stack(qkv_rank)
     qkv_rank, text_key_rank = plan.halves(qkv_rank), plan.text_halves(text_key_rank)
-    gate_z, text_value_rank, result_far, normed_far, qkv_rank, out_rank, text_key_rank = fence(
-        gate_z, text_value_rank, result_far, normed_far, qkv_rank, out_rank, text_key_rank
+    gate_z, text_value_rank, normed_far, qkv_rank, out_rank, text_key_rank = fence(
+        gate_z, text_value_rank, normed_far, qkv_rank, out_rank, text_key_rank
     )
 
     up_z = z_gather(up_mine)
@@ -866,8 +864,9 @@
     normed_far, captions_far, kept_far, partial_far = attend(
         scalars[1], normed_far, captions_far, *attend_weights, tables
     )
-    up_z, gate_rank, normed_far, captions_far, kept_far, partial_far, attend_weights = fence(
-        up_z, gate_rank, normed_far, captions_far, kept_far, partial_far, attend_weights
+    result_far = swap(result_near[0], "mid")
+    up_z, gate_rank, result_far, normed_far, captions_far, kept_far, partial_far, attend_weights = fence(
+        up_z, gate_rank, result_far, normed_far, captions_far, kept_far, partial_far, attend_weights
     )
 
     across = settle(partial_far).astype(bf16)
@@ -953,68 +952,95 @@
     )
     captions, normed_rows = (captions_near, captions_far), (normed_near, normed_far)
     text_rows, qkv_rows, branches = (text_near, text_far), (qkv_near, qkv_far), (branch_near, branch_far)
-    text_moved = plan.product_moved(captions, text_rows)
-    down_moved, up_parts, text_rows, qkv_rows, branches, rows_far, gain_far, text_moved = fence(
-        down_moved, up_parts, text_rows, qkv_rows, branches, rows_far, gain_far, text_moved
-    )
-
-    text_moved = plan.move(text_moved)
+    qkv_moved = plan.product_moved(normed_rows, qkv_rows)
+    down_moved, up_parts, text_rows, qkv_rows, branches, rows_far, gain_far, qkv_moved, hidden_rows = fence(
+        down_moved, up_parts, text_rows, qkv_rows, branches, rows_far, gain_far, qkv_moved, hidden_rows
+    )
+
+    qkv_moved = plan.move(qkv_moved)
     down_grad = plan.total(down_kept, down_moved).reshape(rep_count, -1, D)
     across = settle(rows_far).astype(bf16)
-    mixed_rows = [plan.ordered(kept[6]) for kept in (kept_near, kept_far)]
+    mixed_rows = (kept_near[6], kept_far[6])
+    across, down_grad, text_rows, qkv_rows, branches, hidden_rows, mixed_rows = fence(
+        across, down_grad, text_rows, qkv_rows, branches, hidden_rows, mixed_rows
+    )
+    down_parts = plan.reduce(down_grad)
+    arrived = settle_move(across)
+    mixed_rows = [plan.ordered(rows) for rows in mixed_rows]
     if plan.aligned:
         halves = [slice(0, rank_width // 2), slice(rank_width // 2, None)]
         out_kept, out_moved = [
             product([side[:, lanes] for side in mixed_rows], branches, 0, rank_width // 2, bf16)
             for lanes in halves
         ]
+        if hi_count == 2:
+            out_moved = swap(out_moved, "hi")
+        else:
+            out_moved = plan.move(jnp.concatenate([out_kept, out_moved]))
     else:
         out_kept, out_moved = (), ()
-    across, down_grad, text_rows, qkv_rows, out_kept, out_moved, hidden_rows = fence(
-        across, down_grad, text_rows, qkv_rows, out_kept, out_moved, hidden_rows
-    )
-    down_parts = plan.reduce(down_grad)
-    arrived = settle_move(across)
-    if plan.aligned:
-        if hi_count == 2:
-            out_grad = plan.total(out_kept.astype(f32), swap(out_moved, "hi"))
-        else:
-            out_grad = plan.move(jnp.concatenate([out_kept, out_moved]))
-        out_parts = plan.reduce(out_grad.reshape(rep_count, -1, D))
-    else:
-        at = (jnp.arange(RANKS) == plan.rank).astype(bf16)[:, None, None]
-        out_grad = product(mixed_rows, branches, 0, rank_width, bf16)
-        placed = (out_grad[None] * at).reshape(D, D)
-        out_parts = lax.psum_scatter(placed, AXES, scatter_dimension=0, tiled=True)
-    qkv_moved = plan.product_moved(normed_rows, qkv_rows)
+    text_moved = plan.product_moved(captions, text_rows)
     text_kept = plan.product_kept(captions, text_rows)
     qkv_kept = plan.product_kept(normed_rows, qkv_rows)
     result_far = result_part(hidden_rows[1], down_rank)
     result_near = result_part(hidden_rows[0], down_rank)
-    text_moved, down_parts, out_parts, arrived, qkv_moved, text_kept, qkv_kept, result_far, result_near = fence(
-        text_moved, down_parts, out_parts, arrived, qkv_moved, text_kept, qkv_kept, result_far, result_near
-    )
-
-    qkv_moved = plan.move(qkv_moved)
-    text_grad = plan.text_by_rep(plan.total(text_kept, text_moved))
-    text_parts = plan.reduce(text_grad)
+    qkv_moved, down_parts, arrived, text_moved, out_kept, out_moved, text_kept, qkv_kept, result_far, result_near = fence(
+        qkv_moved, down_parts, arrived, text_moved, out_kept, out_moved, text_kept, qkv_kept, result_far, result_near
+    )
+
+    text_moved = plan.move(text_moved)
+    qkv_grad = plan.by_rep(plan.total(qkv_kept, qkv_moved))
+    if plan.aligned:
+        out_grad = plan.total(out_kept.astype(f32), out_moved) if hi_count == 2 else out_moved
+        out_grad = out_grad.reshape(rep_count, -1, 3 * rank_width)
+        qkv_grad = jnp.concatenate([qkv_grad, out_grad], axis=1)
+    else:
+        at = (jnp.arange(RANKS) == plan.rank).astype(bf16)[:, None, None]
+        out_grad = product(mixed_rows, branches, 0, rank_width, bf16)
+        out_grad = (out_grad[None] * at).reshape(D, D)
+    qkv_parts = plan.reduce(qkv_grad)
     result_arrived = settle_move(settle(result_far).astype(bf16))
     grad_normed = plan.ordered(settle(rows_near) + arrived.astype(f32))
     _, pull_attn_norm = jax.vjp(modulate, token_rows, gain_rows[0], scale_attn)
     grad_token_norm, grad_attn_gain, grad_scale_attn = pull_attn_norm(
         grad_normed.reshape(item_count, item_len, D)
     )
-    result_near = settle(result_near)
     gate_up_parts = jnp.concatenate([gate_parts, up_parts], axis=-1)
     gate_up_parts = trade_ranks(gate_up_parts.reshape(RANKS, rows, -1))
-    text_parts, qkv_moved, result_arrived, result_near, grad_scale_attn, grad_attn_gain, gate_up_parts = fence(
-        text_parts, qkv_moved, result_arrived, result_near, grad_scale_attn, grad_attn_gain, gate_up_parts
-    )
-
-    qkv_grad = plan.by_rep(plan.total(qkv_kept, qkv_moved))
-    qkv_grad, result_near, text_parts = fence(qkv_grad, result_near, text_parts)
-    qkv_parts = plan.reduce(qkv_grad)
-    result = (result_near + result_arrived.astype(f32)).reshape(item_count, item_len, D)
+    gain_terms = gain_near + gain_far
+    gain_terms = gain_terms.at[3].multiply(1.0 - cross_gate**2)
+    gain_terms = [plan.place_lanes(row) for row in gain_terms]
+    (
+        text_moved,
+        qkv_parts,
+        result_arrived,
+        result_near,
+        grad_scale_attn,
+        grad_attn_gain,
+        gate_up_parts,
+        gain_terms,
+    ) = fence(
+        text_moved,
+        qkv_parts,
+        result_arrived,
+        result_near,
+        grad_scale_attn,
+        grad_attn_gain,
+        gate_up_parts,
+        gain_terms,
+    )
+
+    text_grad = plan.text_by_rep(plan.total(text_kept, text_moved))
+    text_grad, result_near, result_arrived, qkv_parts, gate_up_parts = fence(
+        text_grad, result_near, result_arrived, qkv_parts, gate_up_parts
+    )
+    text_parts = plan.reduce(text_grad)
+    if plan.aligned:
+        out_parts = qkv_parts[RANKS * rows :].reshape(-1, D)
+        qkv_parts = qkv_parts[: RANKS * rows]
+    else:
+        out_parts = lax.psum_scatter(out_grad, AXES, scatter_dimension=0, tiled=True)
+    result = (settle(result_near) + result_arrived.astype(f32)).reshape(item_count, item_len, D)
     grad_mlp_gate = jnp.sum(grad_top * result, axis=1) * (1.0 - jnp.tanh(gate_mlp) ** 2)
     layer_out = (middle + mlp_gate * result).astype(bf16).reshape(row_count, D)
     tokens_grad = (grad_middle + grad_token_norm).reshape(row_count, D)
@@ -1022,9 +1048,6 @@
     grad_modulation = jnp.concatenate(
         [grad_scale_attn, grad_attn_gate, grad_scale_mlp, grad_mlp_gate], axis=1
     ).astype(bf16)
-    gain_terms = gain_near + gain_far
-    gain_terms = gain_terms.at[3].multiply(1.0 - cross_gate**2)
-    gain_terms = [plan.place_lanes(row) for row in gain_terms]
     gains_grad = jnp.stack(
         [grad_attn_gain, gain_terms[0], gain_terms[1], gain_terms[2], grad_mlp_gain, gain_terms[3]]
     ).astype(bf16)
@@ -1047,8 +1070,10 @@
         return plan.from_ranks(blocks, sections, groups).astype(f32)
 
     gate_up_weight_grad = plan.from_ranks(gate_up_parts, 2, hi_count).astype(f32)
+    both, qkv_parts = fence(both, qkv_parts)
+    qkv_weight_grad = whole(qkv_parts, qkv_weight, 3, plan.head_groups)
+    qkv_weight_grad, text_parts = fence(qkv_weight_grad, text_parts)
     text_weight_grad = whole(text_parts, text_weight, 2, plan.head_groups)
-    qkv_weight_grad = whole(qkv_parts, qkv_weight, 3, plan.head_groups)
     down_weight_grad, out_weight_grad = down_parts.astype(f32), out_parts.astype(f32)
     return (
         layer_out,

time: 849 us -> 859 us (1.012)
  local copies, waits for them, and re-layouts: 100 us -> 112 us
    ppermute x39, waiting for transfers between devices: 175 us -> 130 us  [swap(): return lax.ppermute(block, axis, [(at, at ^ step) for at in range(count)])]
    all_to_all x6, waiting for transfers between devices: 9.91 us -> 37.9 us  [trade_ranks(): return lax.all_to_all(block, ('mid', 'core'), 0, 0, tiled=True)]
    all_to_all x1, waiting for transfers between devices: 20.7 us -> 42.1 us  [local(): lax.all_to_all(jnp.concatenate([modulations, gain_blocks], axis=2), AXES,...]
  transfers between devices with their start and end apart: 60 -> 59, of which waited for: 31 -> 26; matrix products, arithmetic and copies ran while one was open for 21% -> 23% of each run, Pallas kernels for 30% -> 29%
where the time goes in v10:
time: 859 us; the launch traced here: 848 us
  Pallas kernels  271 us (32%)
  waiting for transfers between devices  259 us (30%)
  other arithmetic  119 us (14%)
  local copies, waits for them, and re-layouts  112 us (13%)
  starting transfers between devices  70.2 us (8%)
  between operations  15.2 us (2%)
    ppermute x39, waiting for transfers between devices, swap(): return lax.ppermute(block, axis, [(at, at ^ step) for at in range(count)])  130 us
    pallas_call x12, Pallas kernels, product(): pl.pallas_call(kernel, grid_spec=pltpu.PrefetchScalarGridSpec(num_scalar_...  89.9 us
    pallas_call x2, Pallas kernels, attend_back(): pl.pallas_call(attend_back_kernel, grid_spec=pltpu.PrefetchScalarGridSpec...  62 us
    pallas_call x2, Pallas kernels, feed(): pl.pallas_call(feed_kernel, grid=(steps,), in_specs=pair_specs(rows, step...  51.9 us
    pallas_call x2, Pallas kernels, attend(): pl.pallas_call(attend_kernel, grid_spec=pltpu.PrefetchScalarGridSpec(num_...  50.4 us
    all_to_all x1, waiting for transfers between devices, local(): lax.all_to_all(jnp.concatenate([modulations, gain_blocks], axis=2), AXES,...  42.1 us
    all_to_all x6, waiting for transfers between devices, trade_ranks(): return lax.all_to_all(block, ('mid', 'core'), 0, 0, tiled=True)  37.9 us
    all_to_all x1, waiting for transfers between devices, local(): lax.all_to_all(partial, AXES, 0, 0, tiled=True).astype(f32)  34 us
  transfers between devices with their start and end apart: 59, of which 26 were waited for; matrix products, arithmetic and copies ran while one was open for 23% of the time, Pallas kernels for 29%

profile of v10, /device:TPU:8, one launch (start us, length us, event | category | flops | bytes accessed | tf_op | source)
XLA Modules:
  0.0 848.2 jit_solution(17637849843737167416)
XLA Ops:
  84.4 34.0 %all-to-all-done.2 = bf16[32,2,6144]{2,1,0:T(2,128)(2,1)S(1)} async-done(((bf16[32,2,6144]{2,1,0:T(2,128)(2,1)}), bf16[32,2,6144]{2,1,0:T(2,128)(2,1)S(1)}, u32[]{:S(2)}, u32[]{:S(2)}) %all-to-all-start.2) | async-done | bytes 786464 | tf_op jit(solution)/shard_map/all_to_all | solution.py:816
  152.3 31.7 %collective-permute-done.2.caption_ref = bf16[256,4096]{1,0:T(8,128)(2,1)} collective-permute-done((bf16[256,4096]{1,0:T(8,128)(2,1)}, bf16[256,4096]{1,0:T(8,128)(2,1)}, u32[]{:S(2)}, u32[]{:S(2)}) %collective-permute-start.2) | collective-permute-done | bytes 2097184 | tf_op jit(solution)/shard_map/ppermute | solution.py:570
  188.7 11.4 %all-gather.15.cloned.1.call-done.value_mine_ref = bf16[2048,384]{1,0:T(8,128)(2,1)} async-done(((bf16[512,384]{1,0:T(8,128)(2,1)}), bf16[2048,384]{1,0:T(8,128)(2,1)}) %all-gather.15.cloned.1.call-update) | async-done | bytes 1572880 | tf_op jit(solution)/shard_map/all_gather | solution.py:758
  200.1 23.3 %collective-permute-done.6.key_other_ref = bf16[2048,384]{1,0:T(8,128)(2,1)S(1)} collective-permute-done((bf16[2048,384]{1,0:T(8,128)(2,1)}, bf16[2048,384]{1,0:T(8,128)(2,1)S(1)}, u32[]{:S(2)}, u32[]{:S(2)}) %collective-permute-start.6) | collective-permute-done | bytes 1572896 | tf_op jit(solution)/shard_map/ppermute | solution.py:570
  241.3 19.6 %collective-permute-done.9.value_other_ref = bf16[2048,384]{1,0:T(8,128)(2,1)} collective-permute-done((bf16[2048,384]{1,0:T(8,128)(2,1)}, bf16[2048,384]{1,0:T(8,128)(2,1)}, u32[]{:S(2)}, u32[]{:S(2)}) %collective-permute-start.9) | collective-permute-done | bytes 1572896 | tf_op jit(solution)/shard_map/ppermute | solution.py:570
  265.0 25.2 %attend.2 = (bf16[1024,1536]{1,0:T(8,128)(2,1)}, bf16[512,4096]{1,0:T(8,128)(2,1)}, f32[1024,1152]{1,0:T(8,128)}, f32[512,384]{1,0:T(8,128)}, f32[512,384]{1,0:T...) custom-call(s32[4]{0:T(128)} %maximum_convert_fusion.2.kind_ref, ...), custom_call_target="tpu_custom_call" | custom-call | tf_op jit(solution)/shard_map/attend/pallas_call | solution.py:365
  311.8 25.2 %attend.3 = (bf16[1024,1536]{1,0:T(8,128)(2,1)}, bf16[512,4096]{1,0:T(8,128)(2,1)}, f32[1024,1152]{1,0:T(8,128)}, f32[512,384]{1,0:T(8,128)}, f32[512,384]{1,0:T...) custom-call(s32[4]{0:T(128)} %maximum_convert_fusion.kind_ref, ...), custom_call_target="tpu_custom_call" | custom-call | tf_op jit(solution)/shard_map/attend/pallas_call | solution.py:365
  356.2 26.0 %feed.2 = (bf16[1024,1536]{1,0:T(8,128)(2,1)}, bf16[1024,1536]{1,0:T(8,128)(2,1)}, bf16[1024,1024]{1,0:T(8,128)(2,1)}, bf16[1024,1024]{1,0:T(8,128)(2,1)}, bf16[...) custom-call(bf16[512,1536]{1,0:T(8,128)(2,1)} %copy-done.11, ...), custom_call_target="tpu_custom_call" | custom-call | tf_op jit(solution)/shard_map/feed/pallas_call | solution.py:527
  394.3 25.8 %feed.3 = (bf16[1024,1536]{1,0:T(8,128)(2,1)}, bf16[1024,1536]{1,0:T(8,128)(2,1)}, bf16[1024,1024]{1,0:T(8,128)(2,1)}, bf16[1024,1024]{1,0:T(8,128)(2,1)}, bf16[...) custom-call(bf16[512,1536]{1,0:T(8,128)(2,1)} %collective-permute-done.18.rows_ref, ...), custom_call_target="tpu_custom_call" | custom-call | tf_op jit(solution)/shard_map/feed/pallas_call | solution.py:527
  438.8 7.8 product.13
  446.6 7.6 product.16
  454.1 8.6 %product.17 = f32[512,1536]{1,0:T(8,128)} custom-call(s32[1]{0:T(128)} %bitcast.45.first_ref, bf16[1024,1024]{1,0:T(8,128)(2,1)} %get-tuple-element.469.refs_0_.hidden_ref, bf16[1024,1024]{1,0:T(8,128)(2,1)} %get-tuple-element.466.refs_1_.hidden_ref, bf16[1024,1536]{1,0:T(8,128)(2,1)} %get-tuple-element.389.refs_2_, ...), custom_call_target="tpu_custom_call" | custom-call | tf_op jit(solution)/shard_map/product/pallas_call | solution.py:447
  462.7 8.1 product.14
  493.8 31.1 %attend_back.2 = (bf16[1024,1536]{1,0:T(8,128)(2,1)}, bf16[1024,1152]{1,0:T(8,128)(2,1)}, bf16[512,768]{1,0:T(8,128)(2,1)}, f32[512,1536]{1,0:T(8,128)}, bf16[512,1536]{1,0:T(8,128)(2,1)}, /*index=5*/f32[4,384]{1,0:T(4,128)}) custom-call(s32[4]{0:T(128)} %maximum_convert_fusion.kind_ref, s32[4]{0:T(128)} %maximum_convert_fusion.1.len_ref, ...), custom_call_target="tpu_custom_call" | custom-call | tf_op jit(solution)/shard_map/attend_back/pallas_call | solution.py:395
  532.8 30.9 %attend_back.3 = (bf16[1024,1536]{1,0:T(8,128)(2,1)}, bf16[1024,1152]{1,0:T(8,128)(2,1)}, bf16[512,768]{1,0:T(8,128)(2,1)}, f32[512,1536]{1,0:T(8,128)}, bf16[512,1536]{1,0:T(8,128)(2,1)}, /*index=5*/f32[4,384]{1,0:T(4,128)}) custom-call(s32[4]{0:T(128)} %maximum_convert_fusion.2.kind_ref, s32[4]{0:T(128)} %maximum_convert_fusion.3.len_ref, ...), custom_call_target="tpu_custom_call" | custom-call | tf_op jit(solution)/shard_map/attend_back/pallas_call | solution.py:395
  563.7 8.4 product.18
  592.6 8.4 result.3
  601.0 8.1 result.2
  609.1 7.8 product.22
  624.3 8.6 %product.23 = f32[768,1152]{1,0:T(8,128)} custom-call(s32[1]{0:T(128)} %constant.580.clone.1.first_ref, bf16[1024,1536]{1,0:T(8,128)(2,1)} %get-tuple-element.437.refs_0_, bf16[1024,1536]{1,0:T(8,128)(2,1)} %get-tuple-element.438.refs_1_, bf16[1024,1152]{1,0:T(8,128)(2,1)} %get-tuple-element.464.refs_2_, bf16[1024,1152]{1,0:T(8,128)(2,1)} %get-tuple-element.465.refs_3_), custom_call_target="tpu_custom_call" | custom-call | tf_op jit(solution)/shard_map/product/pallas_call | solution.py:447
  684.3 28.3 %all-to-all-done.5 = bf16[4,48,2048]{2,1,0:T(8,128)(2,1)} async-done(((bf16[4,48,2048]{2,1,0:T(8,128)(2,1)}), bf16[4,48,2048]{2,1,0:T(8,128)(2,1)}, u32[]{:S(2)}, u32[]{:S(2)}) %all-to-all-start.5) | async-done | bytes 786464 | tf_op jit(solution)/shard_map/all_to_all | solution.py:603
  712.6 8.9 %collective-permute-done.34 = bf16[2048,768]{1,0:T(8,128)(2,1)} collective-permute-done((bf16[2048,768]{1,0:T(8,128)(2,1)}, bf16[2048,768]{1,0:T(8,128)(2,1)}, u32[]{:S(2)}, u32[]{:S(2)}) %collective-permute-start.34) | collective-permute-done | bytes 3145760 | tf_op jit(solution)/shard_map/ppermute | solution.py:570
  731.4 10.3 %fusion.9 = (f32[2,1536]{1,0:T(2,128)S(1)}, bf16[2,1536]{1,0:T(2,128)(2,1)S(1)}, f32[2,1536]{1,0:T(2,128)S(1)}, f32[512,1536]{1,0:T(8,128)}) fusion(bf16[512,1536]{1,0:T(8,128)(2,1)} %param.15, f32[2,256]{1,0:T(2,128)S(1)} %get-tuple-element.614, f32[2,256]{1,0:T(2,128)S(1)} %get-tuple-element.613, f32[1536]{0:T(1024)S(1)} %copy-done.35, ...), kind=kLoop, calls=%fused_computation.29 | loop fusion | flops 21224448 | bytes 22085632 | tf_op jit(solution)/shard_map/reduce_sum | solution.py:933
  751.1 42.1 %all-to-all-done.6 = bf16[32,2,6288]{2,1,0:T(2,128)(2,1)} async-done(((bf16[32,2,6288]{2,1,0:T(2,128)(2,1)}), bf16[32,2,6288]{2,1,0:T(2,128)(2,1)}, u32[]{:S(2)}, u32[]{:S(2)}) %all-to-all-start.6) | async-done | bytes 804896 | tf_op jit(solution)/shard_map/all_to_all | solution.py:1057
  (445 shorter events, 385.7 us)
Async XLA Ops:
  48.5 76.4 %all-gather.9.cloned.1.call-start = ((), (), s32[]{:S(2)}) async-start(), calls=%async_computation.15 | async-start | bytes 2949120 | tf_op jit(solution)/shard_map/all_gather | solution.py:758
  68.0 51.0 %collective-permute-start.1 = (bf16[256,4096]{1,0:T(8,128)(2,1)}, bf16[256,4096]{1,0:T(8,128)(2,1)}, u32[]{:S(2)}, u32[]{:S(2)}) collective-permute-start(bf16[256,4096]{1,0:T(8,128)(2,1)} %maximum_select_fusion.2.caption_ref), channel_id=1, source_target_pairs={{0,4},{4,0},{1,5},{5,1},{2,6},{6,2},{3,7},{7,3},{8,12},{12,8},{9,1... | collective-permute-start | bytes 6291464 | tf_op jit(solution)/shard_map/ppermute | solution.py:570
  80.0 106.2 %all-gather.17.cloned.1.call-start = ((), (), s32[]{:S(2)}) async-start(), calls=%async_computation.19 | async-start | bytes 1966080 | tf_op jit(solution)/shard_map/all_gather | solution.py:758
  80.0 44.8 %collective-permute-start = (bf16[512,1536]{1,0:T(8,128)(2,1)}, bf16[512,1536]{1,0:T(8,128)(2,1)}, u32[]{:S(2)}, u32[]{:S(2)}) collective-permute-start(bf16[512,1536]{1,0:T(8,128)(2,1)} %all-gather.7.cloned.1.call-done), channel_id=1, source_target_pairs={{0,16},{16,0},{1,17},{17,1},{2,18},{18,2},{3,19},{19,3},{4,20},{20... | collective-permute-start | bytes 4718600 | tf_op jit(solution)/shard_map/ppermute | solution.py:570
  125.8 74.3 %all-gather.15.cloned.1.call-start = ((), (), s32[]{:S(2)}) async-start(), calls=%async_computation.18 | async-start | bytes 1966080 | tf_op jit(solution)/shard_map/all_gather | solution.py:758
  133.1 53.1 %collective-permute-start.3 = (bf16[1024,1152]{1,0:T(8,128)(2,1)}, bf16[1024,1152]{1,0:T(8,128)(2,1)}, u32[]{:S(2)}, u32[]{:S(2)}) collective-permute-start(bf16[1024,1152]{1,0:T(8,128)(2,1)} %all-gather.9.cloned.1.call-done), channel_id=1, source_target_pairs={{0,16},{16,0},{1,17},{17,1},{2,18},{18,2},{3,19},{19,3},{4,20},{20... | collective-permute-start | bytes 7077896 | tf_op jit(solution)/shard_map/ppermute | solution.py:570
  136.9 47.1 %collective-permute-start.2 = (bf16[256,4096]{1,0:T(8,128)(2,1)}, bf16[256,4096]{1,0:T(8,128)(2,1)}, u32[]{:S(2)}, u32[]{:S(2)}) collective-permute-start(bf16[256,4096]{1,0:T(8,128)(2,1)} %maximum_select_fusion.2.caption_ref), channel_id=1, source_target_pairs={{0,8},{8,0},{1,9},{9,1},{2,10},{10,2},{3,11},{11,3},{4,12},{12,4},... | collective-permute-start | bytes 6291464 | tf_op jit(solution)/shard_map/ppermute | solution.py:570
  139.2 102.1 %all-gather.13.cloned.1.call-start = ((), (), s32[]{:S(2)}) async-start(), calls=%async_computation.17 | async-start | bytes 1966080 | tf_op jit(solution)/shard_map/all_gather | solution.py:758
  186.3 103.9 %all-gather.11.cloned.1.call-start = ((), (), s32[]{:S(2)}) async-start(), calls=%async_computation.16 | async-start | bytes 1966080 | tf_op jit(solution)/shard_map/all_gather | solution.py:758
  225.3 302.2 %reduce-scatter.6.cloned.1.call-start = ((), (), s32[]{:S(2)}) async-start(), calls=%async_computation.20 | async-start | bytes 1966080 | tf_op jit(solution)/shard_map/reduce_scatter | solution.py:710
  238.5 51.8 %collective-permute-start.12 = (bf16[512,1536]{1,0:T(8,128)(2,1)}, bf16[512,1536]{1,0:T(8,128)(2,1)S(1)}, u32[]{:S(2)}, u32[]{:S(2)}) collective-permute-start(bf16[512,1536]{1,0:T(8,128)(2,1)} %fusion.12.result_ref), channel_id=1, source_target_pairs={{0,8},{8,0},{1,9},{9,1},{2,10},{10,2},{3,11},{11,3},{4,12},{12,4},... | collective-permute-start | bytes 4718600 | tf_op jit(solution)/shard_map/ppermute | solution.py:570
  431.5 46.8 %collective-permute-start.22 = (bf16[512,1536]{1,0:T(8,128)(2,1)}, bf16[512,1536]{1,0:T(8,128)(2,1)}, u32[]{:S(2)}, u32[]{:S(2)}) collective-permute-start(bf16[512,1536]{1,0:T(8,128)(2,1)} %add_convert_fusion.7), channel_id=1, source_target_pairs={{0,8},{8,0},{1,9},{9,1},{2,10},{10,2},{3,11},{11,3},{4,12},{12,4},... | collective-permute-start | bytes 4718600 | tf_op jit(solution)/shard_map/ppermute | solution.py:570
  433.2 45.1 %collective-permute-start.23 = (bf16[768,1024]{1,0:T(8,128)(2,1)}, bf16[768,1024]{1,0:T(8,128)(2,1)}, u32[]{:S(2)}, u32[]{:S(2)}) collective-permute-start(bf16[768,1024]{1,0:T(8,128)(2,1)} %product.12), channel_id=1, source_target_pairs={{0,16},{16,0},{1,17},{17,1},{2,18},{18,2},{3,19},{19,3},{4,20},{20... | collective-permute-start | bytes 4718600 | tf_op jit(solution)/shard_map/ppermute | solution.py:570
  482.6 89.5 %reduce-scatter.8.cloned.1.call-start = ((), (), s32[]{:S(2)}) async-start(), calls=%async_computation.21 | async-start | bytes 1966080 | tf_op jit(solution)/shard_map/reduce_scatter | solution.py:710
  531.7 106.6 %reduce-scatter.10.cloned.1.call-start = ((), (), s32[]{:S(2)}) async-start(), calls=%async_computation.22 | async-start | bytes 1966080 | tf_op jit(solution)/shard_map/reduce_scatter | solution.py:710
  578.2 143.3 %reduce-scatter.12.cloned.1.call-start = ((), (), s32[]{:S(2)}) async-start(), calls=%async_computation.23 | async-start | bytes 2949120 | tf_op jit(solution)/shard_map/reduce_scatter | solution.py:710
  578.3 60.0 %collective-permute-start.30 = (bf16[768,1152]{1,0:T(8,128)(2,1)}, bf16[768,1152]{1,0:T(8,128)(2,1)}, u32[]{:S(2)}, u32[]{:S(2)}) collective-permute-start(bf16[768,1152]{1,0:T(8,128)(2,1)} %product.18), channel_id=1, source_target_pairs={{0,16},{16,0},{1,17},{17,1},{2,18},{18,2},{3,19},{19,3},{4,20},{20... | collective-permute-start | bytes 5308424 | tf_op jit(solution)/shard_map/ppermute | solution.py:570
  579.5 58.8 %collective-permute-start.32 = (bf16[512,1536]{1,0:T(8,128)(2,1)}, bf16[512,1536]{1,0:T(8,128)(2,1)}, u32[]{:S(2)}, u32[]{:S(2)}) collective-permute-start(bf16[512,1536]{1,0:T(8,128)(2,1)} %add_convert_fusion.4), channel_id=1, source_target_pairs={{0,8},{8,0},{1,9},{9,1},{2,10},{10,2},{3,11},{11,3},{4,12},{12,4},... | collective-permute-start | bytes 4718600 | tf_op jit(solution)/shard_map/ppermute | solution.py:570
  592.6 45.7 %collective-permute-start.33 = (bf16[192,1536]{1,0:T(8,128)(2,1)}, bf16[192,1536]{1,0:T(8,128)(2,1)}, u32[]{:S(2)}, u32[]{:S(2)}) collective-permute-start(bf16[192,1536]{1,0:T(8,128)(2,1)} %product.21), channel_id=1, source_target_pairs={{0,16},{16,0},{1,17},{17,1},{2,18},{18,2},{3,19},{19,3},{4,20},{20... | collective-permute-start | bytes 1769480 | tf_op jit(solution)/shard_map/ppermute | solution.py:570
  650.4 71.1 %collective-permute-start.34 = (bf16[2048,768]{1,0:T(8,128)(2,1)}, bf16[2048,768]{1,0:T(8,128)(2,1)}, u32[]{:S(2)}, u32[]{:S(2)}) collective-permute-start(bf16[2048,768]{1,0:T(8,128)(2,1)} %product.19), channel_id=1, source_target_pairs={{0,16},{16,0},{1,17},{17,1},{2,18},{18,2},{3,19},{19,3},{4,20},{20... | collective-permute-start | bytes 9437192 | tf_op jit(solution)/shard_map/ppermute | solution.py:570
  667.2 45.3 %collective-permute-start.36 = (bf16[512,1536]{1,0:T(8,128)(2,1)}, bf16[512,1536]{1,0:T(8,128)(2,1)}, u32[]{:S(2)}, u32[]{:S(2)}) collective-permute-start(bf16[512,1536]{1,0:T(8,128)(2,1)} %add_convert_fusion.2), channel_id=1, source_target_pairs={{0,8},{8,0},{1,9},{9,1},{2,10},{10,2},{3,11},{11,3},{4,12},{12,4},... | collective-permute-start | bytes 4718600 | tf_op jit(solution)/shard_map/ppermute | solution.py:570
  668.1 44.4 %all-to-all-start.5 = ((bf16[4,48,2048]{2,1,0:T(8,128)(2,1)}), bf16[4,48,2048]{2,1,0:T(8,128)(2,1)}, u32[]{:S(2)}, u32[]{:S(2)}) async-start(bf16[4,48,2048]{2,1,0:T(8,128)(2,1)} %bitcast.224), calls=%async_computation.9 | async-start | bytes 1572864 | tf_op jit(solution)/shard_map/all_to_all | solution.py:603
  672.3 145.8 %reduce-scatter.14.cloned.1.call-start = ((), (), s32[]{:S(2)}) async-start(), calls=%async_computation.24 | async-start | bytes 3932160 | tf_op jit(solution)/shard_map/reduce_scatter | solution.py:710
  743.9 49.3 %all-to-all-start.6 = ((bf16[32,2,6288]{2,1,0:T(2,128)(2,1)}), bf16[32,2,6288]{2,1,0:T(2,128)(2,1)}, u32[]{:S(2)}, u32[]{:S(2)}) async-start(bf16[32,2,6288]{2,1,0:T(2,128)(2,1)} %pad_maximum_fusion.3), calls=%async_computation.10 | async-start | bytes 1638400 | tf_op jit(solution)/shard_map/all_to_all | solution.py:1057
  (105 other events, 1789.6 us)
Sparse Core Ops, SparseCore 0:
  9.6 37.7 all-gather.6
  51.4 63.0 all-gather.8
  125.9 36.1 all-gather.16
  164.1 35.9 all-gather.14
  202.1 35.9 all-gather.12
  239.5 35.9 all-gather.10
  482.7 33.7 reduce-scatter.5
  531.8 34.9 reduce-scatter.7
  578.4 35.0 reduce-scatter.9
  650.5 47.6 reduce-scatter.11
  727.8 77.9 reduce-scatter.13

commit v11 on v10

--- a/solution.py
+++ b/solution.py
@@ -980,12 +980,9 @@
     else:
         out_kept, out_moved = (), ()
     text_moved = plan.product_moved(captions, text_rows)
-    text_kept = plan.product_kept(captions, text_rows)
     qkv_kept = plan.product_kept(normed_rows, qkv_rows)
-    result_far = result_part(hidden_rows[1], down_rank)
-    result_near = result_part(hidden_rows[0], down_rank)
-    qkv_moved, down_parts, arrived, text_moved, out_kept, out_moved, text_kept, qkv_kept, result_far, result_near = fence(
-        qkv_moved, down_parts, arrived, text_moved, out_kept, out_moved, text_kept, qkv_kept, result_far, result_near
+    qkv_moved, arrived, text_moved, out_kept, out_moved, qkv_kept, text_rows, hidden_rows = fence(
+        qkv_moved, arrived, text_moved, out_kept, out_moved, qkv_kept, text_rows, hidden_rows
     )
 
     text_moved = plan.move(text_moved)
@@ -998,41 +995,45 @@
         at = (jnp.arange(RANKS) == plan.rank).astype(bf16)[:, None, None]
         out_grad = product(mixed_rows, branches, 0, rank_width, bf16)
         out_grad = (out_grad[None] * at).reshape(D, D)
+    qkv_grad, text_rows, hidden_rows, rows_near = fence(qkv_grad, text_rows, hidden_rows, rows_near)
     qkv_parts = plan.reduce(qkv_grad)
+    result_far = result_part(hidden_rows[1], down_rank)
+    result_near = result_part(hidden_rows[0], down_rank)
+    text_kept = plan.product_kept(captions, text_rows)
     result_arrived = settle_move(settle(result_far).astype(bf16))
     grad_normed = plan.ordered(settle(rows_near) + arrived.astype(f32))
     _, pull_attn_norm = jax.vjp(modulate, token_rows, gain_rows[0], scale_attn)
     grad_token_norm, grad_attn_gain, grad_scale_attn = pull_attn_norm(
         grad_normed.reshape(item_count, item_len, D)
     )
-    gate_up_parts = jnp.concatenate([gate_parts, up_parts], axis=-1)
-    gate_up_parts = trade_ranks(gate_up_parts.reshape(RANKS, rows, -1))
     gain_terms = gain_near + gain_far
     gain_terms = gain_terms.at[3].multiply(1.0 - cross_gate**2)
     gain_terms = [plan.place_lanes(row) for row in gain_terms]
     (
         text_moved,
+        down_parts,
+        text_kept,
         qkv_parts,
         result_arrived,
         result_near,
         grad_scale_attn,
         grad_attn_gain,
-        gate_up_parts,
         gain_terms,
     ) = fence(
         text_moved,
+        down_parts,
+        text_kept,
         qkv_parts,
         result_arrived,
         result_near,
         grad_scale_attn,
         grad_attn_gain,
-        gate_up_parts,
         gain_terms,
     )
 
     text_grad = plan.text_by_rep(plan.total(text_kept, text_moved))
-    text_grad, result_near, result_arrived, qkv_parts, gate_up_parts = fence(
-        text_grad, result_near, result_arrived, qkv_parts, gate_up_parts
+    text_grad, result_near, result_arrived, qkv_parts = fence(
+        text_grad, result_near, result_arrived, qkv_parts
     )
     text_parts = plan.reduce(text_grad)
     if plan.aligned:
@@ -1057,6 +1058,16 @@
     both = lax.all_to_all(
         jnp.concatenate([modulations, gain_blocks], axis=2), AXES, 0, 0, tiled=True
     )
+    def whole(parts, weight, sections, groups):
+        blocks = trade_ranks(parts.reshape(RANKS, weight.shape[0], -1))
+        return plan.from_ranks(blocks, sections, groups).astype(f32)
+
+    both, qkv_parts, gate_parts, up_parts, layer_out, tokens_grad = fence(
+        both, qkv_parts, gate_parts, up_parts, layer_out, tokens_grad
+    )
+    gate_up_weight_grad = whole(
+        jnp.concatenate([gate_parts, up_parts], axis=-1), gate_up_weight, 2, hi_count
+    )
     ada_weight_grad = lax.dot_general(
         activated_mine.reshape(devices, item_count, rows),
         both[:, :, : 4 * D],
@@ -1064,15 +1075,10 @@
         preferred_element_type=f32,
     )
     norm_gains_grad = jnp.sum(both[:, :, 4 * D :].astype(f32), axis=0).reshape(6, -1)
-
-    def whole(parts, weight, sections, groups):
-        blocks = trade_ranks(parts.reshape(RANKS, weight.shape[0], -1))
-        return plan.from_ranks(blocks, sections, groups).astype(f32)
-
-    gate_up_weight_grad = plan.from_ranks(gate_up_parts, 2, hi_count).astype(f32)
-    both, qkv_parts = fence(both, qkv_parts)
     qkv_weight_grad = whole(qkv_parts, qkv_weight, 3, plan.head_groups)
-    qkv_weight_grad, text_parts = fence(qkv_weight_grad, text_parts)
+    gate_up_weight_grad, qkv_weight_grad, text_parts = fence(
+        gate_up_weight_grad, qkv_weight_grad, text_parts
+    )
     text_weight_grad = whole(text_parts, text_weight, 2, plan.head_groups)
     down_weight_grad, out_weight_grad = down_parts.astype(f32), out_parts.astype(f32)
     return (

time: 859 us -> 859 us (level)
  waiting for transfers between devices: 259 us -> 293 us
  local copies, waits for them, and re-layouts: 112 us -> 91.4 us
  other arithmetic: 119 us -> 108 us
    ppermute x39, waiting for transfers between devices: 130 us -> 168 us  [swap(): return lax.ppermute(block, axis, [(at, at ^ step) for at in range(count)])]
    convert_element_type x3 -> x0, local copies, waits for them, and re-layouts: 9.78 us -> none  [local(): plan.from_ranks(gate_up_parts, 2, hi_count).astype(f32)]
    convert_element_type x0 -> x1, other arithmetic: none -> 9.64 us  [local(): layer_out = (middle + mlp_gate * result).astype(bf16).reshape(row_count, D)]
  transfers between devices with their start and end apart: 59 -> 59, of which waited for: 26 -> 31; matrix products, arithmetic and copies ran while one was open for 23% -> 20% of each run, Pallas kernels for 29% -> 29%
where the time goes in v11:
time: 859 us; the launch traced here: 850 us
  waiting for transfers between devices  293 us (34%)
  Pallas kernels  272 us (32%)
  other arithmetic  108 us (13%)
  local copies, waits for them, and re-layouts  91.4 us (11%)
  starting transfers between devices  68.8 us (8%)
  between operations  15.2 us (2%)
    ppermute x39, waiting for transfers between devices, swap(): return lax.ppermute(block, axis, [(at, at ^ step) for at in range(count)])  168 us
    pallas_call x12, Pallas kernels, product(): pl.pallas_call(kernel, grid_spec=pltpu.PrefetchScalarGridSpec(num_scalar_...  90.6 us
    pallas_call x2, Pallas kernels, attend_back(): pl.pallas_call(attend_back_kernel, grid_spec=pltpu.PrefetchScalarGridSpec...  62.2 us
    pallas_call x2, Pallas kernels, feed(): pl.pallas_call(feed_kernel, grid=(steps,), in_specs=pair_specs(rows, step...  51.9 us
    pallas_call x2, Pallas kernels, attend(): pl.pallas_call(attend_kernel, grid_spec=pltpu.PrefetchScalarGridSpec(num_...  50.7 us
    all_to_all x1, waiting for transfers between devices, local(): lax.all_to_all(jnp.concatenate([modulations, gain_blocks], axis=2), AXES,...  44.1 us
    all_to_all x1, waiting for transfers between devices, local(): lax.all_to_all(partial, AXES, 0, 0, tiled=True).astype(f32)  34 us
    all_to_all x6, waiting for transfers between devices, trade_ranks(): return lax.all_to_all(block, ('mid', 'core'), 0, 0, tiled=True)  31.6 us
  transfers between devices with their start and end apart: 59, of which 31 were waited for; matrix products, arithmetic and copies ran while one was open for 20% of the time, Pallas kernels for 29%

profile of v11, /device:TPU:8, one launch (start us, length us, event | category | flops | bytes accessed | tf_op | source)
XLA Modules:
  0.0 849.6 jit_solution(11409090236667545741)
XLA Ops:
  84.4 34.0 %all-to-all-done.2 = bf16[32,2,6144]{2,1,0:T(2,128)(2,1)S(1)} async-done(((bf16[32,2,6144]{2,1,0:T(2,128)(2,1)}), bf16[32,2,6144]{2,1,0:T(2,128)(2,1)S(1)}, u32[]{:S(2)}, u32[]{:S(2)}) %all-to-all-start.2) | async-done | bytes 786464 | tf_op jit(solution)/shard_map/all_to_all | solution.py:816
  152.3 31.5 %collective-permute-done.2.caption_ref = bf16[256,4096]{1,0:T(8,128)(2,1)} collective-permute-done((bf16[256,4096]{1,0:T(8,128)(2,1)}, bf16[256,4096]{1,0:T(8,128)(2,1)}, u32[]{:S(2)}, u32[]{:S(2)}) %collective-permute-start.2) | collective-permute-done | bytes 2097184 | tf_op jit(solution)/shard_map/ppermute | solution.py:570
  188.5 11.6 %all-gather.15.cloned.1.call-done.value_mine_ref = bf16[2048,384]{1,0:T(8,128)(2,1)} async-done(((bf16[512,384]{1,0:T(8,128)(2,1)}), bf16[2048,384]{1,0:T(8,128)(2,1)}) %all-gather.15.cloned.1.call-update) | async-done | bytes 1572880 | tf_op jit(solution)/shard_map/all_gather | solution.py:758
  200.1 23.2 %collective-permute-done.6.key_other_ref = bf16[2048,384]{1,0:T(8,128)(2,1)S(1)} collective-permute-done((bf16[2048,384]{1,0:T(8,128)(2,1)}, bf16[2048,384]{1,0:T(8,128)(2,1)S(1)}, u32[]{:S(2)}, u32[]{:S(2)}) %collective-permute-start.6) | collective-permute-done | bytes 1572896 | tf_op jit(solution)/shard_map/ppermute | solution.py:570
  241.1 19.6 %collective-permute-done.9.value_other_ref = bf16[2048,384]{1,0:T(8,128)(2,1)} collective-permute-done((bf16[2048,384]{1,0:T(8,128)(2,1)}, bf16[2048,384]{1,0:T(8,128)(2,1)}, u32[]{:S(2)}, u32[]{:S(2)}) %collective-permute-start.9) | collective-permute-done | bytes 1572896 | tf_op jit(solution)/shard_map/ppermute | solution.py:570
  264.9 25.6 %attend.2 = (bf16[1024,1536]{1,0:T(8,128)(2,1)}, bf16[512,4096]{1,0:T(8,128)(2,1)}, f32[1024,1152]{1,0:T(8,128)}, f32[512,384]{1,0:T(8,128)}, f32[512,384]{1,0:T...) custom-call(s32[4]{0:T(128)} %maximum_convert_fusion.2.kind_ref, ...), custom_call_target="tpu_custom_call" | custom-call | tf_op jit(solution)/shard_map/attend/pallas_call | solution.py:365
  311.6 25.1 %attend.3 = (bf16[1024,1536]{1,0:T(8,128)(2,1)}, bf16[512,4096]{1,0:T(8,128)(2,1)}, f32[1024,1152]{1,0:T(8,128)}, f32[512,384]{1,0:T(8,128)}, f32[512,384]{1,0:T...) custom-call(s32[4]{0:T(128)} %maximum_convert_fusion.kind_ref, ...), custom_call_target="tpu_custom_call" | custom-call | tf_op jit(solution)/shard_map/attend/pallas_call | solution.py:365
  356.0 26.0 %feed.2 = (bf16[1024,1536]{1,0:T(8,128)(2,1)}, bf16[1024,1536]{1,0:T(8,128)(2,1)}, bf16[1024,1024]{1,0:T(8,128)(2,1)}, bf16[1024,1024]{1,0:T(8,128)(2,1)}, bf16[...) custom-call(bf16[512,1536]{1,0:T(8,128)(2,1)} %copy-done.16, ...), custom_call_target="tpu_custom_call" | custom-call | tf_op jit(solution)/shard_map/feed/pallas_call | solution.py:527
  394.2 25.8 %feed.3 = (bf16[1024,1536]{1,0:T(8,128)(2,1)}, bf16[1024,1536]{1,0:T(8,128)(2,1)}, bf16[1024,1024]{1,0:T(8,128)(2,1)}, bf16[1024,1024]{1,0:T(8,128)(2,1)}, bf16[...) custom-call(bf16[512,1536]{1,0:T(8,128)(2,1)} %collective-permute-done.18.rows_ref, ...), custom_call_target="tpu_custom_call" | custom-call | tf_op jit(solution)/shard_map/feed/pallas_call | solution.py:527
  454.0 8.6 %product.17 = f32[512,1536]{1,0:T(8,128)} custom-call(s32[1]{0:T(128)} %bitcast.45.first_ref, bf16[1024,1024]{1,0:T(8,128)(2,1)} %get-tuple-element.496.refs_0_.hidden_ref, bf16[1024,1024]{1,0:T(8,128)(2,1)} %get-tuple-element.493.refs_1_.hidden_ref, bf16[1024,1536]{1,0:T(8,128)(2,1)} %get-tuple-element.400.refs_2_, ...), custom_call_target="tpu_custom_call" | custom-call | tf_op jit(solution)/shard_map/product/pallas_call | solution.py:447
  462.6 8.1 product.14
  493.2 31.2 %attend_back.2 = (bf16[1024,1536]{1,0:T(8,128)(2,1)}, bf16[1024,1152]{1,0:T(8,128)(2,1)}, bf16[512,768]{1,0:T(8,128)(2,1)}, f32[512,1536]{1,0:T(8,128)}, bf16[512,1536]{1,0:T(8,128)(2,1)}, /*index=5*/f32[4,384]{1,0:T(4,128)}) custom-call(s32[4]{0:T(128)} %maximum_convert_fusion.kind_ref, s32[4]{0:T(128)} %maximum_convert_fusion.1.len_ref, ...), custom_call_target="tpu_custom_call" | custom-call | tf_op jit(solution)/shard_map/attend_back/pallas_call | solution.py:395
  532.1 30.9 %attend_back.3 = (bf16[1024,1536]{1,0:T(8,128)(2,1)}, bf16[1024,1152]{1,0:T(8,128)(2,1)}, bf16[512,768]{1,0:T(8,128)(2,1)}, f32[512,1536]{1,0:T(8,128)}, bf16[512,1536]{1,0:T(8,128)(2,1)}, /*index=5*/f32[4,384]{1,0:T(4,128)}) custom-call(s32[4]{0:T(128)} %maximum_convert_fusion.2.kind_ref, s32[4]{0:T(128)} %maximum_convert_fusion.3.len_ref, ...), custom_call_target="tpu_custom_call" | custom-call | tf_op jit(solution)/shard_map/attend_back/pallas_call | solution.py:395
  563.1 8.4 product.18
  592.7 9.0 %product.22 = f32[768,1152]{1,0:T(8,128)} custom-call(s32[1]{0:T(128)} %constant.580.clone.1.first_ref, bf16[1024,1536]{1,0:T(8,128)(2,1)} %get-tuple-element.448.refs_0_, bf16[1024,1536]{1,0:T(8,128)(2,1)} %get-tuple-element.449.refs_1_, bf16[1024,1152]{1,0:T(8,128)(2,1)} %get-tuple-element.474.refs_2_, bf16[1024,1152]{1,0:T(8,128)(2,1)} %get-tuple-element.475.refs_3_), custom_call_target="tpu_custom_call" | custom-call | tf_op jit(solution)/shard_map/product/pallas_call | solution.py:447
  614.4 11.0 %collective-permute-done.33 = bf16[192,1536]{1,0:T(8,128)(2,1)S(1)} collective-permute-done((bf16[192,1536]{1,0:T(8,128)(2,1)}, bf16[192,1536]{1,0:T(8,128)(2,1)S(1)}, u32[]{:S(2)}, u32[]{:S(2)}) %collective-permute-start.33) | collective-permute-done | bytes 589856 | tf_op jit(solution)/shard_map/ppermute | solution.py:570
  636.4 8.2 result.2
  654.4 8.1 result.3
  662.5 7.8 product.23
  680.7 8.4 collective-permute-done.36
  689.1 26.3 %collective-permute-done.34 = bf16[2048,768]{1,0:T(8,128)(2,1)} collective-permute-done((bf16[2048,768]{1,0:T(8,128)(2,1)}, bf16[2048,768]{1,0:T(8,128)(2,1)}, u32[]{:S(2)}, u32[]{:S(2)}) %collective-permute-start.34) | collective-permute-done | bytes 3145760 | tf_op jit(solution)/shard_map/ppermute | solution.py:570
  725.3 9.6 %fusion.14 = (bf16[512,1536]{1,0:T(8,128)(2,1)}, f32[512,1536]{1,0:T(8,128)S(1)}, f32[512,1536]{1,0:T(8,128)}) fusion(f32[512,1536]{1,0:T(8,128)S(1)} %get-tuple-element.587, f32[2,1536]{1,0:T(2,128)S(1)} %copy-done.53, bf16[512,1536]{1,0:T(8,128)(2,1)} %collective-permute-done.36, f32[512,1536]{1,0:T(8,128)} %get-tuple-element.511, ...), kind=kLoop, calls=%fused_computation.34 | loop fusion | flops 18087936 | bytes 26796032 | tf_op jit(solution)/shard_map/convert_element_type | solution.py:1046
  747.8 44.1 %all-to-all-done.5 = bf16[32,2,6288]{2,1,0:T(2,128)(2,1)S(1)} async-done(((bf16[32,2,6288]{2,1,0:T(2,128)(2,1)}), bf16[32,2,6288]{2,1,0:T(2,128)(2,1)S(1)}, u32[]{:S(2)}, u32[]{:S(2)}) %all-to-all-start.5) | async-done | bytes 804896 | tf_op jit(solution)/shard_map/all_to_all | solution.py:1058
  810.3 8.3 all-to-all-done.6
  (429 shorter events, 383.8 us)
Async XLA Ops:
  7.2 43.3 %all-gather.7.cloned.1.call-start = ((), (), s32[]{:S(2)}) async-start(), calls=%async_computation.14 | async-start | bytes 1966080 | tf_op jit(solution)/shard_map/all_gather | solution.py:758
  48.5 76.4 %all-gather.9.cloned.1.call-start = ((), (), s32[]{:S(2)}) async-start(), calls=%async_computation.15 | async-start | bytes 2949120 | tf_op jit(solution)/shard_map/all_gather | solution.py:758
  68.0 51.0 %collective-permute-start.1 = (bf16[256,4096]{1,0:T(8,128)(2,1)}, bf16[256,4096]{1,0:T(8,128)(2,1)}, u32[]{:S(2)}, u32[]{:S(2)}) collective-permute-start(bf16[256,4096]{1,0:T(8,128)(2,1)} %maximum_select_fusion.2.caption_ref), channel_id=1, source_target_pairs={{0,4},{4,0},{1,5},{5,1},{2,6},{6,2},{3,7},{7,3},{8,12},{12,8},{9,1... | collective-permute-start | bytes 6291464 | tf_op jit(solution)/shard_map/ppermute | solution.py:570
  76.0 42.4 %all-to-all-start.2 = ((bf16[32,2,6144]{2,1,0:T(2,128)(2,1)}), bf16[32,2,6144]{2,1,0:T(2,128)(2,1)S(1)}, u32[]{:S(2)}, u32[]{:S(2)}) async-start(bf16[32,2,6144]{2,1,0:T(2,128)(2,1)} %reshape.777), calls=%async_computation.2 | async-start | bytes 1572864 | tf_op jit(solution)/shard_map/all_to_all | solution.py:816
  80.0 106.1 %all-gather.17.cloned.1.call-start = ((), (), s32[]{:S(2)}) async-start(), calls=%async_computation.19 | async-start | bytes 1966080 | tf_op jit(solution)/shard_map/all_gather | solution.py:758
  80.1 44.8 %collective-permute-start = (bf16[512,1536]{1,0:T(8,128)(2,1)}, bf16[512,1536]{1,0:T(8,128)(2,1)}, u32[]{:S(2)}, u32[]{:S(2)}) collective-permute-start(bf16[512,1536]{1,0:T(8,128)(2,1)} %all-gather.7.cloned.1.call-done), channel_id=1, source_target_pairs={{0,16},{16,0},{1,17},{17,1},{2,18},{18,2},{3,19},{19,3},{4,20},{20... | collective-permute-start | bytes 4718600 | tf_op jit(solution)/shard_map/ppermute | solution.py:570
  125.8 74.3 %all-gather.15.cloned.1.call-start = ((), (), s32[]{:S(2)}) async-start(), calls=%async_computation.18 | async-start | bytes 1966080 | tf_op jit(solution)/shard_map/all_gather | solution.py:758
  133.0 53.1 %collective-permute-start.3 = (bf16[1024,1152]{1,0:T(8,128)(2,1)}, bf16[1024,1152]{1,0:T(8,128)(2,1)}, u32[]{:S(2)}, u32[]{:S(2)}) collective-permute-start(bf16[1024,1152]{1,0:T(8,128)(2,1)} %all-gather.9.cloned.1.call-done), channel_id=1, source_target_pairs={{0,16},{16,0},{1,17},{17,1},{2,18},{18,2},{3,19},{19,3},{4,20},{20... | collective-permute-start | bytes 7077896 | tf_op jit(solution)/shard_map/ppermute | solution.py:570
  136.8 47.1 %collective-permute-start.2 = (bf16[256,4096]{1,0:T(8,128)(2,1)}, bf16[256,4096]{1,0:T(8,128)(2,1)}, u32[]{:S(2)}, u32[]{:S(2)}) collective-permute-start(bf16[256,4096]{1,0:T(8,128)(2,1)} %maximum_select_fusion.2.caption_ref), channel_id=1, source_target_pairs={{0,8},{8,0},{1,9},{9,1},{2,10},{10,2},{3,11},{11,3},{4,12},{12,4},... | collective-permute-start | bytes 6291464 | tf_op jit(solution)/shard_map/ppermute | solution.py:570
  139.0 102.1 %all-gather.13.cloned.1.call-start = ((), (), s32[]{:S(2)}) async-start(), calls=%async_computation.17 | async-start | bytes 1966080 | tf_op jit(solution)/shard_map/all_gather | solution.py:758
  186.1 104.3 %all-gather.11.cloned.1.call-start = ((), (), s32[]{:S(2)}) async-start(), calls=%async_computation.16 | async-start | bytes 1966080 | tf_op jit(solution)/shard_map/all_gather | solution.py:758
  225.1 301.7 %reduce-scatter.6.cloned.1.call-start = ((), (), s32[]{:S(2)}) async-start(), calls=%async_computation.20 | async-start | bytes 1966080 | tf_op jit(solution)/shard_map/reduce_scatter | solution.py:710
  238.3 52.2 %collective-permute-start.12 = (bf16[512,1536]{1,0:T(8,128)(2,1)}, bf16[512,1536]{1,0:T(8,128)(2,1)S(1)}, u32[]{:S(2)}, u32[]{:S(2)}) collective-permute-start(bf16[512,1536]{1,0:T(8,128)(2,1)} %fusion.12.result_ref), channel_id=1, source_target_pairs={{0,8},{8,0},{1,9},{9,1},{2,10},{10,2},{3,11},{11,3},{4,12},{12,4},... | collective-permute-start | bytes 4718600 | tf_op jit(solution)/shard_map/ppermute | solution.py:570
  431.5 46.9 %collective-permute-start.22 = (bf16[512,1536]{1,0:T(8,128)(2,1)}, bf16[512,1536]{1,0:T(8,128)(2,1)}, u32[]{:S(2)}, u32[]{:S(2)}) collective-permute-start(bf16[512,1536]{1,0:T(8,128)(2,1)} %add_convert_fusion.7), channel_id=1, source_target_pairs={{0,8},{8,0},{1,9},{9,1},{2,10},{10,2},{3,11},{11,3},{4,12},{12,4},... | collective-permute-start | bytes 4718600 | tf_op jit(solution)/shard_map/ppermute | solution.py:570
  433.1 45.2 %collective-permute-start.23 = (bf16[768,1024]{1,0:T(8,128)(2,1)}, bf16[768,1024]{1,0:T(8,128)(2,1)}, u32[]{:S(2)}, u32[]{:S(2)}) collective-permute-start(bf16[768,1024]{1,0:T(8,128)(2,1)} %product.12), channel_id=1, source_target_pairs={{0,16},{16,0},{1,17},{17,1},{2,18},{18,2},{3,19},{19,3},{4,20},{20... | collective-permute-start | bytes 4718600 | tf_op jit(solution)/shard_map/ppermute | solution.py:570
  482.6 88.9 %reduce-scatter.8.cloned.1.call-start = ((), (), s32[]{:S(2)}) async-start(), calls=%async_computation.21 | async-start | bytes 1966080 | tf_op jit(solution)/shard_map/reduce_scatter | solution.py:710
  531.1 149.6 %reduce-scatter.10.cloned.1.call-start = ((), (), s32[]{:S(2)}) async-start(), calls=%async_computation.22 | async-start | bytes 1966080 | tf_op jit(solution)/shard_map/reduce_scatter | solution.py:710
  531.2 40.3 %collective-permute-start.29 = (bf16[512,1536]{1,0:T(8,128)(2,1)}, bf16[512,1536]{1,0:T(8,128)(2,1)}, u32[]{:S(2)}, u32[]{:S(2)}) collective-permute-start(bf16[512,1536]{1,0:T(8,128)(2,1)} %product.14), channel_id=1, source_target_pairs={{0,16},{16,0},{1,17},{17,1},{2,18},{18,2},{3,19},{19,3},{4,20},{20... | collective-permute-start | bytes 4718600 | tf_op jit(solution)/shard_map/ppermute | solution.py:570
  571.8 42.6 %collective-permute-start.30 = (bf16[768,1152]{1,0:T(8,128)(2,1)}, bf16[768,1152]{1,0:T(8,128)(2,1)}, u32[]{:S(2)}, u32[]{:S(2)}) collective-permute-start(bf16[768,1152]{1,0:T(8,128)(2,1)} %product.18), channel_id=1, source_target_pairs={{0,16},{16,0},{1,17},{17,1},{2,18},{18,2},{3,19},{19,3},{4,20},{20... | collective-permute-start | bytes 5308424 | tf_op jit(solution)/shard_map/ppermute | solution.py:570
  579.7 45.8 %collective-permute-start.32 = (bf16[512,1536]{1,0:T(8,128)(2,1)}, bf16[512,1536]{1,0:T(8,128)(2,1)}, u32[]{:S(2)}, u32[]{:S(2)}) collective-permute-start(bf16[512,1536]{1,0:T(8,128)(2,1)} %add_convert_fusion.4), channel_id=1, source_target_pairs={{0,8},{8,0},{1,9},{9,1},{2,10},{10,2},{3,11},{11,3},{4,12},{12,4},... | collective-permute-start | bytes 4718600 | tf_op jit(solution)/shard_map/ppermute | solution.py:570
  581.4 134.1 %reduce-scatter.12.cloned.1.call-start = ((), (), s32[]{:S(2)}) async-start(), calls=%async_computation.23 | async-start | bytes 2949120 | tf_op jit(solution)/shard_map/reduce_scatter | solution.py:710
  636.4 186.7 %reduce-scatter.14.cloned.1.call-start = ((), (), s32[]{:S(2)}) async-start(), calls=%async_computation.24 | async-start | bytes 3932160 | tf_op jit(solution)/shard_map/reduce_scatter | solution.py:710
  644.6 70.8 %collective-permute-start.34 = (bf16[2048,768]{1,0:T(8,128)(2,1)}, bf16[2048,768]{1,0:T(8,128)(2,1)}, u32[]{:S(2)}, u32[]{:S(2)}) collective-permute-start(bf16[2048,768]{1,0:T(8,128)(2,1)} %product.19), channel_id=1, source_target_pairs={{0,16},{16,0},{1,17},{17,1},{2,18},{18,2},{3,19},{19,3},{4,20},{20... | collective-permute-start | bytes 9437192 | tf_op jit(solution)/shard_map/ppermute | solution.py:570
  741.2 50.6 %all-to-all-start.5 = ((bf16[32,2,6288]{2,1,0:T(2,128)(2,1)}), bf16[32,2,6288]{2,1,0:T(2,128)(2,1)S(1)}, u32[]{:S(2)}, u32[]{:S(2)}) async-start(bf16[32,2,6288]{2,1,0:T(2,128)(2,1)} %pad_maximum_fusion.3), calls=%async_computation.9 | async-start | bytes 1638400 | tf_op jit(solution)/shard_map/all_to_all | solution.py:1058
  (97 other events, 1481.4 us)
Sparse Core Ops, SparseCore 0:
  9.6 37.7 all-gather.6
  51.5 63.0 all-gather.8
  125.9 36.1 all-gather.16
  164.1 35.9 all-gather.14
  202.1 35.9 all-gather.12
  239.5 35.9 all-gather.10
  482.7 33.7 reduce-scatter.5
  531.2 34.9 reduce-scatter.7
  581.5 33.7 reduce-scatter.9
  636.5 47.7 reduce-scatter.11
  721.8 78.3 reduce-scatter.13

commit v12 on v11

--- a/solution.py
+++ b/solution.py
@@ -981,8 +981,9 @@
         out_kept, out_moved = (), ()
     text_moved = plan.product_moved(captions, text_rows)
     qkv_kept = plan.product_kept(normed_rows, qkv_rows)
-    qkv_moved, arrived, text_moved, out_kept, out_moved, qkv_kept, text_rows, hidden_rows = fence(
-        qkv_moved, arrived, text_moved, out_kept, out_moved, qkv_kept, text_rows, hidden_rows
+    result_far = result_part(hidden_rows[1], down_rank)
+    qkv_moved, arrived, text_moved, out_kept, out_moved, qkv_kept, text_rows, hidden_rows, result_far = fence(
+        qkv_moved, arrived, text_moved, out_kept, out_moved, qkv_kept, text_rows, hidden_rows, result_far
     )
 
     text_moved = plan.move(text_moved)
@@ -997,7 +998,6 @@
         out_grad = (out_grad[None] * at).reshape(D, D)
     qkv_grad, text_rows, hidden_rows, rows_near = fence(qkv_grad, text_rows, hidden_rows, rows_near)
     qkv_parts = plan.reduce(qkv_grad)
-    result_far = result_part(hidden_rows[1], down_rank)
     result_near = result_part(hidden_rows[0], down_rank)
     text_kept = plan.product_kept(captions, text_rows)
     result_arrived = settle_move(settle(result_far).astype(bf16))
@@ -1006,6 +1006,10 @@
     grad_token_norm, grad_attn_gain, grad_scale_attn = pull_attn_norm(
         grad_normed.reshape(item_count, item_len, D)
     )
+    text_kept, gate_parts, up_parts = fence(text_kept, gate_parts, up_parts)
+    gate_up_parts = jnp.concatenate([gate_parts, up_parts], axis=-1)
+    gate_up_parts = trade_ranks(gate_up_parts.reshape(RANKS, rows, -1))
+    gate_up_weight_grad = plan.from_ranks(gate_up_parts, 2, hi_count).astype(f32)
     gain_terms = gain_near + gain_far
     gain_terms = gain_terms.at[3].multiply(1.0 - cross_gate**2)
     gain_terms = [plan.place_lanes(row) for row in gain_terms]
@@ -1018,6 +1022,7 @@
         result_near,
         grad_scale_attn,
         grad_attn_gain,
+        gate_up_weight_grad,
         gain_terms,
     ) = fence(
         text_moved,
@@ -1028,6 +1033,7 @@
         result_near,
         grad_scale_attn,
         grad_attn_gain,
+        gate_up_weight_grad,
         gain_terms,
     )
 
@@ -1045,6 +1051,14 @@
     grad_mlp_gate = jnp.sum(grad_top * result, axis=1) * (1.0 - jnp.tanh(gate_mlp) ** 2)
     layer_out = (middle + mlp_gate * result).astype(bf16).reshape(row_count, D)
     tokens_grad = (grad_middle + grad_token_norm).reshape(row_count, D)
+
+    def whole(parts, weight, sections, groups):
+        blocks = trade_ranks(parts.reshape(RANKS, weight.shape[0], -1))
+        return plan.from_ranks(blocks, sections, groups).astype(f32)
+
+    qkv_blocks = trade_ranks(qkv_parts.reshape(RANKS, rows, -1))
+    qkv_blocks, grad_mlp_gate = fence(qkv_blocks, grad_mlp_gate)
+    qkv_weight_grad = plan.from_ranks(qkv_blocks, 3, plan.head_groups).astype(f32)
 
     grad_modulation = jnp.concatenate(
         [grad_scale_attn, grad_attn_gate, grad_scale_mlp, grad_mlp_gate], axis=1
@@ -1058,16 +1072,7 @@
     both = lax.all_to_all(
         jnp.concatenate([modulations, gain_blocks], axis=2), AXES, 0, 0, tiled=True
     )
-    def whole(parts, weight, sections, groups):
-        blocks = trade_ranks(parts.reshape(RANKS, weight.shape[0], -1))
-        return plan.from_ranks(blocks, sections, groups).astype(f32)
-
-    both, qkv_parts, gate_parts, up_parts, layer_out, tokens_grad = fence(
-        both, qkv_parts, gate_parts, up_parts, layer_out, tokens_grad
-    )
-    gate_up_weight_grad = whole(
-        jnp.concatenate([gate_parts, up_parts], axis=-1), gate_up_weight, 2, hi_count
-    )
+    both, layer_out, tokens_grad = fence(both, layer_out, tokens_grad)
     ada_weight_grad = lax.dot_general(
         activated_mine.reshape(devices, item_count, rows),
         both[:, :, : 4 * D],
@@ -1075,10 +1080,7 @@
         preferred_element_type=f32,
     )
     norm_gains_grad = jnp.sum(both[:, :, 4 * D :].astype(f32), axis=0).reshape(6, -1)
-    qkv_weight_grad = whole(qkv_parts, qkv_weight, 3, plan.head_groups)
-    gate_up_weight_grad, qkv_weight_grad, text_parts = fence(
-        gate_up_weight_grad, qkv_weight_grad, text_parts
-    )
+    both, text_parts = fence(both, text_parts)
     text_weight_grad = whole(text_parts, text_weight, 2, plan.head_groups)
     down_weight_grad, out_weight_grad = down_parts.astype(f32), out_parts.astype(f32)
     return (

time: 859 us -> 829 us (0.965)
  waiting for transfers between devices: 293 us -> 202 us
  blocking collectives: 0 us -> 51.2 us
  local copies, waits for them, and re-layouts: 91.4 us -> 105 us
    all_to_all x0 -> x1, blocking collectives: none -> 51.2 us  [local(): lax.all_to_all(jnp.concatenate([modulations, gain_blocks], axis=2), AXES,...]
    all_to_all x1 -> x0, waiting for transfers between devices: 44.1 us -> none  [local(): lax.all_to_all(jnp.concatenate([modulations, gain_blocks], axis=2), AXES,...]
    ppermute x39, waiting for transfers between devices: 168 us -> 139 us  [swap(): return lax.ppermute(block, axis, [(at, at ^ step) for at in range(count)])]
    all_to_all x6, waiting for transfers between devices: 31.6 us -> 10 us  [trade_ranks(): return lax.all_to_all(block, ('mid', 'core'), 0, 0, tiled=True)]
    convert_element_type x0 -> x6, local copies, waits for them, and re-layouts: none -> 14.2 us  [the longest x3 9.77 us: local(): plan.from_ranks(gate_up_parts, 2, hi_count).astype(f32)]
  transfers between devices with their start and end apart: 59 -> 58, of which waited for: 31 -> 27; matrix products, arithmetic and copies ran while one was open for 20% -> 23% of each run, Pallas kernels for 29% -> 30%
where the time goes in v12:
time: 829 us; the launch traced here: 820 us
  Pallas kernels  272 us (33%)
  waiting for transfers between devices  202 us (24%)
  other arithmetic  108 us (13%)
  local copies, waits for them, and re-layouts  105 us (13%)
  starting transfers between devices  64.9 us (8%)
  blocking collectives  51.2 us (6%)
  between operations  15.3 us (2%)
    ppermute x39, waiting for transfers between devices, swap(): return lax.ppermute(block, axis, [(at, at ^ step) for at in range(count)])  139 us
    pallas_call x12, Pallas kernels, product(): pl.pallas_call(kernel, grid_spec=pltpu.PrefetchScalarGridSpec(num_scalar_...  90.3 us
    pallas_call x2, Pallas kernels, attend_back(): pl.pallas_call(attend_back_kernel, grid_spec=pltpu.PrefetchScalarGridSpec...  62.2 us
    pallas_call x2, Pallas kernels, feed(): pl.pallas_call(feed_kernel, grid=(steps,), in_specs=pair_specs(rows, step...  51.9 us
    all_to_all x1, blocking collectives, local(): lax.all_to_all(jnp.concatenate([modulations, gain_blocks], axis=2), AXES,...  51.2 us
    pallas_call x2, Pallas kernels, attend(): pl.pallas_call(attend_kernel, grid_spec=pltpu.PrefetchScalarGridSpec(num_...  50.4 us
    all_to_all x1, waiting for transfers between devices, local(): lax.all_to_all(partial, AXES, 0, 0, tiled=True).astype(f32)  34 us
    ppermute x39, starting transfers between devices, swap(): return lax.ppermute(block, axis, [(at, at ^ step) for at in range(count)])  30.2 us
  transfers between devices with their start and end apart: 58, of which 27 were waited for; matrix products, arithmetic and copies ran while one was open for 23% of the time, Pallas kernels for 30%

profile of v12, /device:TPU:8, one launch (start us, length us, event | category | flops | bytes accessed | tf_op | source)
XLA Modules:
  0.0 819.7 jit_solution(7299451566229630275)
XLA Ops:
  84.4 34.0 %all-to-all-done.2 = bf16[32,2,6144]{2,1,0:T(2,128)(2,1)S(1)} async-done(((bf16[32,2,6144]{2,1,0:T(2,128)(2,1)}), bf16[32,2,6144]{2,1,0:T(2,128)(2,1)S(1)}, u32[]{:S(2)}, u32[]{:S(2)}) %all-to-all-start.2) | async-done | bytes 786464 | tf_op jit(solution)/shard_map/all_to_all | solution.py:816
  152.4 31.6 %collective-permute-done.2.caption_ref = bf16[256,4096]{1,0:T(8,128)(2,1)} collective-permute-done((bf16[256,4096]{1,0:T(8,128)(2,1)}, bf16[256,4096]{1,0:T(8,128)(2,1)}, u32[]{:S(2)}, u32[]{:S(2)}) %collective-permute-start.2) | collective-permute-done | bytes 2097184 | tf_op jit(solution)/shard_map/ppermute | solution.py:570
  188.7 11.4 %all-gather.15.cloned.1.call-done.value_mine_ref = bf16[2048,384]{1,0:T(8,128)(2,1)} async-done(((bf16[512,384]{1,0:T(8,128)(2,1)}), bf16[2048,384]{1,0:T(8,128)(2,1)}) %all-gather.15.cloned.1.call-update) | async-done | bytes 1572880 | tf_op jit(solution)/shard_map/all_gather | solution.py:758
  200.1 23.3 %collective-permute-done.6.key_other_ref = bf16[2048,384]{1,0:T(8,128)(2,1)S(1)} collective-permute-done((bf16[2048,384]{1,0:T(8,128)(2,1)}, bf16[2048,384]{1,0:T(8,128)(2,1)S(1)}, u32[]{:S(2)}, u32[]{:S(2)}) %collective-permute-start.6) | collective-permute-done | bytes 1572896 | tf_op jit(solution)/shard_map/ppermute | solution.py:570
  241.2 19.7 %collective-permute-done.9.value_other_ref = bf16[2048,384]{1,0:T(8,128)(2,1)} collective-permute-done((bf16[2048,384]{1,0:T(8,128)(2,1)}, bf16[2048,384]{1,0:T(8,128)(2,1)}, u32[]{:S(2)}, u32[]{:S(2)}) %collective-permute-start.9) | collective-permute-done | bytes 1572896 | tf_op jit(solution)/shard_map/ppermute | solution.py:570
  265.0 25.2 %attend.2 = (bf16[1024,1536]{1,0:T(8,128)(2,1)}, bf16[512,4096]{1,0:T(8,128)(2,1)}, f32[1024,1152]{1,0:T(8,128)}, f32[512,384]{1,0:T(8,128)}, f32[512,384]{1,0:T...) custom-call(s32[4]{0:T(128)} %maximum_convert_fusion.2.kind_ref, ...), custom_call_target="tpu_custom_call" | custom-call | tf_op jit(solution)/shard_map/attend/pallas_call | solution.py:365
  311.8 25.1 %attend.3 = (bf16[1024,1536]{1,0:T(8,128)(2,1)}, bf16[512,4096]{1,0:T(8,128)(2,1)}, f32[1024,1152]{1,0:T(8,128)}, f32[512,384]{1,0:T(8,128)}, f32[512,384]{1,0:T...) custom-call(s32[4]{0:T(128)} %maximum_convert_fusion.kind_ref, ...), custom_call_target="tpu_custom_call" | custom-call | tf_op jit(solution)/shard_map/attend/pallas_call | solution.py:365
  356.8 26.0 %feed.2 = (bf16[1024,1536]{1,0:T(8,128)(2,1)}, bf16[1024,1536]{1,0:T(8,128)(2,1)}, bf16[1024,1024]{1,0:T(8,128)(2,1)}, bf16[1024,1024]{1,0:T(8,128)(2,1)}, bf16[...) custom-call(bf16[512,1536]{1,0:T(8,128)(2,1)} %copy-done.16, ...), custom_call_target="tpu_custom_call" | custom-call | tf_op jit(solution)/shard_map/feed/pallas_call | solution.py:527
  394.9 25.8 %feed.3 = (bf16[1024,1536]{1,0:T(8,128)(2,1)}, bf16[1024,1536]{1,0:T(8,128)(2,1)}, bf16[1024,1024]{1,0:T(8,128)(2,1)}, bf16[1024,1024]{1,0:T(8,128)(2,1)}, bf16[...) custom-call(bf16[512,1536]{1,0:T(8,128)(2,1)} %collective-permute-done.18.rows_ref, ...), custom_call_target="tpu_custom_call" | custom-call | tf_op jit(solution)/shard_map/feed/pallas_call | solution.py:527
  439.3 7.8 product.13
  447.1 7.6 product.16
  454.7 8.6 %product.17 = f32[512,1536]{1,0:T(8,128)} custom-call(s32[1]{0:T(128)} %bitcast.45.first_ref, bf16[1024,1024]{1,0:T(8,128)(2,1)} %get-tuple-element.500.refs_0_.hidden_ref, bf16[1024,1024]{1,0:T(8,128)(2,1)} %get-tuple-element.478.refs_1_.hidden_ref, bf16[1024,1536]{1,0:T(8,128)(2,1)} %get-tuple-element.401.refs_2_, ...), custom_call_target="tpu_custom_call" | custom-call | tf_op jit(solution)/shard_map/product/pallas_call | solution.py:447
  463.3 8.1 product.14
  471.5 7.5 product.15
  494.5 31.3 %attend_back.2 = (bf16[1024,1536]{1,0:T(8,128)(2,1)}, bf16[1024,1152]{1,0:T(8,128)(2,1)}, bf16[512,768]{1,0:T(8,128)(2,1)}, f32[512,1536]{1,0:T(8,128)}, bf16[512,1536]{1,0:T(8,128)(2,1)}, /*index=5*/f32[4,384]{1,0:T(4,128)}) custom-call(s32[4]{0:T(128)} %maximum_convert_fusion.kind_ref, s32[4]{0:T(128)} %maximum_convert_fusion.1.len_ref, ...), custom_call_target="tpu_custom_call" | custom-call | tf_op jit(solution)/shard_map/attend_back/pallas_call | solution.py:395
  533.4 30.9 %attend_back.3 = (bf16[1024,1536]{1,0:T(8,128)(2,1)}, bf16[1024,1152]{1,0:T(8,128)(2,1)}, bf16[512,768]{1,0:T(8,128)(2,1)}, f32[512,1536]{1,0:T(8,128)}, bf16[512,1536]{1,0:T(8,128)(2,1)}, /*index=5*/f32[4,384]{1,0:T(4,128)}) custom-call(s32[4]{0:T(128)} %maximum_convert_fusion.2.kind_ref, s32[4]{0:T(128)} %maximum_convert_fusion.3.len_ref, ...), custom_call_target="tpu_custom_call" | custom-call | tf_op jit(solution)/shard_map/attend_back/pallas_call | solution.py:395
  564.3 8.4 %product.18 = bf16[768,1152]{1,0:T(8,128)(2,1)} custom-call(s32[1]{0:T(128)} %constant.578.clone.1.first_ref, bf16[1024,1536]{1,0:T(8,128)(2,1)} %get-tuple-element.449.refs_0_, bf16[1024,1536]{1,0:T(8,128)(2,1)} %get-tuple-element.450.refs_1_, bf16[1024,1152]{1,0:T(8,128)(2,1)} %get-tuple-element.475.refs_2_, bf16[1024,1152]{1,0:T(8,128)(2,1)} %get-tuple-element.476.refs_3_), custom_call_target="tpu_custom_call" | custom-call | tf_op jit(solution)/shard_map/product/pallas_call | solution.py:447
  594.0 8.4 %result.2 = (f32[512,1536]{1,0:T(8,128)}, bf16[512,1536]{1,0:T(8,128)(2,1)}) custom-call(bf16[1024,1024]{1,0:T(8,128)(2,1)} %get-tuple-element.478.refs_1_.hidden_ref, bf16[1024,1536]{1,0:T(8,128)(2,1)} %bitcast.188), custom_call_target="tpu_custom_call" | custom-call | tf_op jit(solution)/shard_map/result/pallas_call | solution.py:558
  602.4 8.7 %product.22 = f32[768,1152]{1,0:T(8,128)} custom-call(s32[1]{0:T(128)} %constant.580.clone.1.first_ref, bf16[1024,1536]{1,0:T(8,128)(2,1)} %get-tuple-element.449.refs_0_, bf16[1024,1536]{1,0:T(8,128)(2,1)} %get-tuple-element.450.refs_1_, bf16[1024,1152]{1,0:T(8,128)(2,1)} %get-tuple-element.475.refs_2_, bf16[1024,1152]{1,0:T(8,128)(2,1)} %get-tuple-element.476.refs_3_), custom_call_target="tpu_custom_call" | custom-call | tf_op jit(solution)/shard_map/product/pallas_call | solution.py:447
  642.8 7.9 product.23
  662.4 8.6 %result.3 = (f32[512,1536]{1,0:T(8,128)}, bf16[512,1536]{1,0:T(8,128)(2,1)}) custom-call(bf16[1024,1024]{1,0:T(8,128)(2,1)} %get-tuple-element.500.refs_0_.hidden_ref, bf16[1024,1536]{1,0:T(8,128)(2,1)} %bitcast.189), custom_call_target="tpu_custom_call" | custom-call | tf_op jit(solution)/shard_map/result/pallas_call | solution.py:558
  691.2 10.1 %collective-permute-done.36 = bf16[512,1536]{1,0:T(8,128)(2,1)} collective-permute-done((bf16[512,1536]{1,0:T(8,128)(2,1)}, bf16[512,1536]{1,0:T(8,128)(2,1)}, u32[]{:S(2)}, u32[]{:S(2)}) %collective-permute-start.36) | collective-permute-done | bytes 1572896 | tf_op jit(solution)/shard_map/ppermute | solution.py:570
  722.4 8.4 %fusion.14 = (bf16[512,1536]{1,0:T(8,128)(2,1)}, f32[512,1536]{1,0:T(8,128)S(1)}, f32[512,1536]{1,0:T(8,128)}) fusion(f32[512,1536]{1,0:T(8,128)S(1)} %get-tuple-element.589, f32[2,1536]{1,0:T(2,128)S(1)} %copy-done.53, bf16[512,1536]{1,0:T(8,128)(2,1)} %collective-permute-done.36, f32[512,1536]{1,0:T(8,128)} %get-tuple-element.518, ...), kind=kLoop, calls=%fused_computation.34 | loop fusion | flops 18087936 | bytes 26796032 | tf_op jit(solution)/shard_map/convert_element_type | solution.py:1052
  738.2 51.2 %all_to_all.52 = bf16[32,2,6288]{2,1,0:T(2,128)(2,1)} all-to-all(bf16[32,2,6288]{2,1,0:T(2,128)(2,1)S(1)} %pad_maximum_fusion.3), channel_id=1, replica_groups=mesh['hi'=2,'mid'=2,'core'=2,'rep'=4] {'hi','mid','core','rep'}, dimensions={0} | all-to-all | bytes 1609728 | tf_op jit(solution)/shard_map/all_to_all | solution.py:1072
  (457 shorter events, 368.6 us)
Async XLA Ops:
  7.2 43.3 %all-gather.7.cloned.1.call-start = ((), (), s32[]{:S(2)}) async-start(), calls=%async_computation.14 | async-start | bytes 1966080 | tf_op jit(solution)/shard_map/all_gather | solution.py:758
  48.5 76.4 %all-gather.9.cloned.1.call-start = ((), (), s32[]{:S(2)}) async-start(), calls=%async_computation.15 | async-start | bytes 2949120 | tf_op jit(solution)/shard_map/all_gather | solution.py:758
  68.0 51.0 %collective-permute-start.1 = (bf16[256,4096]{1,0:T(8,128)(2,1)}, bf16[256,4096]{1,0:T(8,128)(2,1)}, u32[]{:S(2)}, u32[]{:S(2)}) collective-permute-start(bf16[256,4096]{1,0:T(8,128)(2,1)} %maximum_select_fusion.2.caption_ref), channel_id=1, source_target_pairs={{0,4},{4,0},{1,5},{5,1},{2,6},{6,2},{3,7},{7,3},{8,12},{12,8},{9,1... | collective-permute-start | bytes 6291464 | tf_op jit(solution)/shard_map/ppermute | solution.py:570
  76.0 42.4 %all-to-all-start.2 = ((bf16[32,2,6144]{2,1,0:T(2,128)(2,1)}), bf16[32,2,6144]{2,1,0:T(2,128)(2,1)S(1)}, u32[]{:S(2)}, u32[]{:S(2)}) async-start(bf16[32,2,6144]{2,1,0:T(2,128)(2,1)} %reshape.777), calls=%async_computation.2 | async-start | bytes 1572864 | tf_op jit(solution)/shard_map/all_to_all | solution.py:816
  80.0 106.3 %all-gather.17.cloned.1.call-start = ((), (), s32[]{:S(2)}) async-start(), calls=%async_computation.19 | async-start | bytes 1966080 | tf_op jit(solution)/shard_map/all_gather | solution.py:758
  80.0 44.8 %collective-permute-start = (bf16[512,1536]{1,0:T(8,128)(2,1)}, bf16[512,1536]{1,0:T(8,128)(2,1)}, u32[]{:S(2)}, u32[]{:S(2)}) collective-permute-start(bf16[512,1536]{1,0:T(8,128)(2,1)} %all-gather.7.cloned.1.call-done), channel_id=1, source_target_pairs={{0,16},{16,0},{1,17},{17,1},{2,18},{18,2},{3,19},{19,3},{4,20},{20... | collective-permute-start | bytes 4718600 | tf_op jit(solution)/shard_map/ppermute | solution.py:570
  125.8 74.3 %all-gather.15.cloned.1.call-start = ((), (), s32[]{:S(2)}) async-start(), calls=%async_computation.18 | async-start | bytes 1966080 | tf_op jit(solution)/shard_map/all_gather | solution.py:758
  133.1 53.1 %collective-permute-start.3 = (bf16[1024,1152]{1,0:T(8,128)(2,1)}, bf16[1024,1152]{1,0:T(8,128)(2,1)}, u32[]{:S(2)}, u32[]{:S(2)}) collective-permute-start(bf16[1024,1152]{1,0:T(8,128)(2,1)} %all-gather.9.cloned.1.call-done), channel_id=1, source_target_pairs={{0,16},{16,0},{1,17},{17,1},{2,18},{18,2},{3,19},{19,3},{4,20},{20... | collective-permute-start | bytes 7077896 | tf_op jit(solution)/shard_map/ppermute | solution.py:570
  136.9 47.1 %collective-permute-start.2 = (bf16[256,4096]{1,0:T(8,128)(2,1)}, bf16[256,4096]{1,0:T(8,128)(2,1)}, u32[]{:S(2)}, u32[]{:S(2)}) collective-permute-start(bf16[256,4096]{1,0:T(8,128)(2,1)} %maximum_select_fusion.2.caption_ref), channel_id=1, source_target_pairs={{0,8},{8,0},{1,9},{9,1},{2,10},{10,2},{3,11},{11,3},{4,12},{12,4},... | collective-permute-start | bytes 6291464 | tf_op jit(solution)/shard_map/ppermute | solution.py:570
  139.2 102.0 %all-gather.13.cloned.1.call-start = ((), (), s32[]{:S(2)}) async-start(), calls=%async_computation.17 | async-start | bytes 1966080 | tf_op jit(solution)/shard_map/all_gather | solution.py:758
  186.3 104.0 %all-gather.11.cloned.1.call-start = ((), (), s32[]{:S(2)}) async-start(), calls=%async_computation.16 | async-start | bytes 1966080 | tf_op jit(solution)/shard_map/all_gather | solution.py:758
  225.3 302.9 %reduce-scatter.6.cloned.1.call-start = ((), (), s32[]{:S(2)}) async-start(), calls=%async_computation.20 | async-start | bytes 1966080 | tf_op jit(solution)/shard_map/reduce_scatter | solution.py:710
  238.4 51.9 %collective-permute-start.12 = (bf16[512,1536]{1,0:T(8,128)(2,1)}, bf16[512,1536]{1,0:T(8,128)(2,1)S(1)}, u32[]{:S(2)}, u32[]{:S(2)}) collective-permute-start(bf16[512,1536]{1,0:T(8,128)(2,1)} %fusion.12.result_ref), channel_id=1, source_target_pairs={{0,8},{8,0},{1,9},{9,1},{2,10},{10,2},{3,11},{11,3},{4,12},{12,4},... | collective-permute-start | bytes 4718600 | tf_op jit(solution)/shard_map/ppermute | solution.py:570
  432.1 46.9 %collective-permute-start.22 = (bf16[512,1536]{1,0:T(8,128)(2,1)}, bf16[512,1536]{1,0:T(8,128)(2,1)}, u32[]{:S(2)}, u32[]{:S(2)}) collective-permute-start(bf16[512,1536]{1,0:T(8,128)(2,1)} %add_convert_fusion.7), channel_id=1, source_target_pairs={{0,8},{8,0},{1,9},{9,1},{2,10},{10,2},{3,11},{11,3},{4,12},{12,4},... | collective-permute-start | bytes 4718600 | tf_op jit(solution)/shard_map/ppermute | solution.py:570
  433.8 45.2 %collective-permute-start.23 = (bf16[768,1024]{1,0:T(8,128)(2,1)}, bf16[768,1024]{1,0:T(8,128)(2,1)}, u32[]{:S(2)}, u32[]{:S(2)}) collective-permute-start(bf16[768,1024]{1,0:T(8,128)(2,1)} %product.12), channel_id=1, source_target_pairs={{0,16},{16,0},{1,17},{17,1},{2,18},{18,2},{3,19},{19,3},{4,20},{20... | collective-permute-start | bytes 4718600 | tf_op jit(solution)/shard_map/ppermute | solution.py:570
  483.3 89.5 %reduce-scatter.8.cloned.1.call-start = ((), (), s32[]{:S(2)}) async-start(), calls=%async_computation.21 | async-start | bytes 1966080 | tf_op jit(solution)/shard_map/reduce_scatter | solution.py:710
  532.4 158.8 %reduce-scatter.10.cloned.1.call-start = ((), (), s32[]{:S(2)}) async-start(), calls=%async_computation.22 | async-start | bytes 1966080 | tf_op jit(solution)/shard_map/reduce_scatter | solution.py:710
  573.1 50.6 %collective-permute-start.30 = (bf16[768,1152]{1,0:T(8,128)(2,1)}, bf16[768,1152]{1,0:T(8,128)(2,1)}, u32[]{:S(2)}, u32[]{:S(2)}) collective-permute-start(bf16[768,1152]{1,0:T(8,128)(2,1)} %product.18), channel_id=1, source_target_pairs={{0,16},{16,0},{1,17},{17,1},{2,18},{18,2},{3,19},{19,3},{4,20},{20... | collective-permute-start | bytes 5308424 | tf_op jit(solution)/shard_map/ppermute | solution.py:570
  581.0 45.8 %collective-permute-start.32 = (bf16[512,1536]{1,0:T(8,128)(2,1)}, bf16[512,1536]{1,0:T(8,128)(2,1)}, u32[]{:S(2)}, u32[]{:S(2)}) collective-permute-start(bf16[512,1536]{1,0:T(8,128)(2,1)} %add_convert_fusion.4), channel_id=1, source_target_pairs={{0,8},{8,0},{1,9},{9,1},{2,10},{10,2},{3,11},{11,3},{4,12},{12,4},... | collective-permute-start | bytes 4718600 | tf_op jit(solution)/shard_map/ppermute | solution.py:570
  582.7 125.9 %reduce-scatter.12.cloned.1.call-start = ((), (), s32[]{:S(2)}) async-start(), calls=%async_computation.23 | async-start | bytes 2949120 | tf_op jit(solution)/shard_map/reduce_scatter | solution.py:710
  637.7 70.8 %collective-permute-start.34 = (bf16[2048,768]{1,0:T(8,128)(2,1)}, bf16[2048,768]{1,0:T(8,128)(2,1)}, u32[]{:S(2)}, u32[]{:S(2)}) collective-permute-start(bf16[2048,768]{1,0:T(8,128)(2,1)} %product.19), channel_id=1, source_target_pairs={{0,16},{16,0},{1,17},{17,1},{2,18},{18,2},{3,19},{19,3},{4,20},{20... | collective-permute-start | bytes 9437192 | tf_op jit(solution)/shard_map/ppermute | solution.py:570
  638.9 41.9 %collective-permute-start.37 = (bf16[512,1536]{1,0:T(8,128)(2,1)}, bf16[512,1536]{1,0:T(8,128)(2,1)}, u32[]{:S(2)}, u32[]{:S(2)}) collective-permute-start(bf16[512,1536]{1,0:T(8,128)(2,1)} %get-tuple-element.504), channel_id=1, source_target_pairs={{0,4},{4,0},{1,5},{5,1},{2,6},{6,2},{3,7},{7,3},{8,12},{12,8},{9,1... | collective-permute-start | bytes 4718600 | tf_op jit(solution)/shard_map/ppermute | solution.py:570
  655.9 137.4 %reduce-scatter.14.cloned.1.call-start = ((), (), s32[]{:S(2)}) async-start(), calls=%async_computation.24 | async-start | bytes 3932160 | tf_op jit(solution)/shard_map/reduce_scatter | solution.py:710
  660.0 41.3 %collective-permute-start.36 = (bf16[512,1536]{1,0:T(8,128)(2,1)}, bf16[512,1536]{1,0:T(8,128)(2,1)}, u32[]{:S(2)}, u32[]{:S(2)}) collective-permute-start(bf16[512,1536]{1,0:T(8,128)(2,1)} %add_convert_fusion.2), channel_id=1, source_target_pairs={{0,8},{8,0},{1,9},{9,1},{2,10},{10,2},{3,11},{11,3},{4,12},{12,4},... | collective-permute-start | bytes 4718600 | tf_op jit(solution)/shard_map/ppermute | solution.py:570
  (110 other events, 1752.6 us)
Sparse Core Ops, SparseCore 0:
  9.6 37.7 all-gather.6
  51.5 63.0 all-gather.8
  125.9 36.1 all-gather.16
  164.1 35.9 all-gather.14
  202.1 35.9 all-gather.12
  239.5 35.9 all-gather.10
  483.4 33.7 reduce-scatter.5
  532.5 34.9 reduce-scatter.7
  582.8 33.7 reduce-scatter.9
  637.7 47.7 reduce-scatter.11
  715.0 78.3 reduce-scatter.13

commit v13 on v12

--- a/solution.py
+++ b/solution.py
@@ -824,7 +824,6 @@
     text_key_z = z_gather(text_key_mine)
     captions_far = swap(captions_near[0], "mid")
     qkv_rank = plan.across_hi(qkv_z)
-    down_rank = plan.natural_hi(down_rank).reshape(feed_width, D)
     token_rows = tokens.astype(f32).reshape(item_count, item_len, D)
     normed = modulate(token_rows, gain_rows[0], scale_attn)
     normed = plan.ordered(normed.astype(bf16).reshape(row_count, D))
@@ -832,8 +831,8 @@
     grad_top = out_cotangent.astype(f32).reshape(item_count, item_len, D)
     grad_result = (mlp_gate * grad_top).astype(bf16).reshape(row_count, D)
     normed_near, result_near = pair(normed), pair(grad_result)
-    text_key_z, captions_far, qkv_rank, down_rank, normed_near, result_near, tables, scalars = fence(
-        text_key_z, captions_far, qkv_rank, down_rank, normed_near, result_near, tables, scalars
+    text_key_z, captions_far, qkv_rank, normed_near, result_near, tables, scalars = fence(
+        text_key_z, captions_far, qkv_rank, normed_near, result_near, tables, scalars
     )
 
     text_value_z = z_gather(text_value_mine)
@@ -864,9 +863,10 @@
     normed_far, captions_far, kept_far, partial_far = attend(
         scalars[1], normed_far, captions_far, *attend_weights, tables
     )
+    down_rank = plan.natural_hi(down_rank).reshape(feed_width, D)
     result_far = swap(result_near[0], "mid")
-    up_z, gate_rank, result_far, normed_far, captions_far, kept_far, partial_far, attend_weights = fence(
-        up_z, gate_rank, result_far, normed_far, captions_far, kept_far, partial_far, attend_weights
+    down_rank, up_z, gate_rank, result_far, normed_far, captions_far, kept_far, partial_far, attend_weights = fence(
+        down_rank, up_z, gate_rank, result_far, normed_far, captions_far, kept_far, partial_far, attend_weights
     )
 
     across = settle(partial_far).astype(bf16)

time: 829 us -> 823 us (level)
    all_gather x6, waiting for transfers between devices: 11.4 us -> 20.2 us  [z_gather(): return lax.all_gather(block.reshape(-1, block.shape[-1]), 'rep', tiled=True)]
  transfers between devices with their start and end apart: 58 -> 58, of which waited for: 27 -> 28; matrix products, arithmetic and copies ran while one was open for 23% -> 22% of each run, Pallas kernels for 30% -> 30%
where the time goes in v13:
time: 823 us; the launch traced here: 813 us
  Pallas kernels  271 us (33%)
  waiting for transfers between devices  204 us (25%)
  other arithmetic  103 us (13%)
  local copies, waits for them, and re-layouts  102 us (12%)
  starting transfers between devices  64.4 us (8%)
  blocking collectives  51.1 us (6%)
  between operations  15.4 us (2%)
    ppermute x39, waiting for transfers between devices, swap(): return lax.ppermute(block, axis, [(at, at ^ step) for at in range(count)])  131 us
    pallas_call x12, Pallas kernels, product(): pl.pallas_call(kernel, grid_spec=pltpu.PrefetchScalarGridSpec(num_scalar_...  90 us
    pallas_call x2, Pallas kernels, attend_back(): pl.pallas_call(attend_back_kernel, grid_spec=pltpu.PrefetchScalarGridSpec...  62.5 us
    pallas_call x2, Pallas kernels, feed(): pl.pallas_call(feed_kernel, grid=(steps,), in_specs=pair_specs(rows, step...  52 us
    all_to_all x1, blocking collectives, local(): lax.all_to_all(jnp.concatenate([modulations, gain_blocks], axis=2), AXES,...  51.1 us
    pallas_call x2, Pallas kernels, attend(): pl.pallas_call(attend_kernel, grid_spec=pltpu.PrefetchScalarGridSpec(num_...  50.1 us
    all_to_all x1, waiting for transfers between devices, local(): lax.all_to_all(partial, AXES, 0, 0, tiled=True).astype(f32)  34.6 us
    ppermute x39, starting transfers between devices, swap(): return lax.ppermute(block, axis, [(at, at ^ step) for at in range(count)])  29.8 us
  transfers between devices with their start and end apart: 58, of which 28 were waited for; matrix products, arithmetic and copies ran while one was open for 22% of the time, Pallas kernels for 30%

profile of v13, /device:TPU:8, one launch (start us, length us, event | category | flops | bytes accessed | tf_op | source)
XLA Modules:
  0.0 812.8 jit_solution(14908432375672828347)
XLA Ops:
  83.1 34.6 %all-to-all-done.2 = bf16[32,2,6144]{2,1,0:T(2,128)(2,1)S(1)} async-done(((bf16[32,2,6144]{2,1,0:T(2,128)(2,1)}), bf16[32,2,6144]{2,1,0:T(2,128)(2,1)S(1)}, u32[]{:S(2)}, u32[]{:S(2)}) %all-to-all-start.2) | async-done | bytes 786464 | tf_op jit(solution)/shard_map/all_to_all | solution.py:816
  142.1 32.4 %collective-permute-done.2.caption_ref = bf16[256,4096]{1,0:T(8,128)(2,1)} collective-permute-done((bf16[256,4096]{1,0:T(8,128)(2,1)}, bf16[256,4096]{1,0:T(8,128)(2,1)}, u32[]{:S(2)}, u32[]{:S(2)}) %collective-permute-start.2) | collective-permute-done | bytes 2097184 | tf_op jit(solution)/shard_map/ppermute | solution.py:570
  182.2 17.3 %all-gather.15.cloned.1.call-done.value_mine_ref = bf16[2048,384]{1,0:T(8,128)(2,1)} async-done(((bf16[512,384]{1,0:T(8,128)(2,1)}), bf16[2048,384]{1,0:T(8,128)(2,1)}) %all-gather.15.cloned.1.call-update) | async-done | bytes 1572880 | tf_op jit(solution)/shard_map/all_gather | solution.py:758
  199.5 17.4 %collective-permute-done.6.key_other_ref = bf16[2048,384]{1,0:T(8,128)(2,1)S(1)} collective-permute-done((bf16[2048,384]{1,0:T(8,128)(2,1)}, bf16[2048,384]{1,0:T(8,128)(2,1)S(1)}, u32[]{:S(2)}, u32[]{:S(2)}) %collective-permute-start.6) | collective-permute-done | bytes 1572896 | tf_op jit(solution)/shard_map/ppermute | solution.py:570
  237.5 16.7 %collective-permute-done.9.value_other_ref = bf16[2048,384]{1,0:T(8,128)(2,1)} collective-permute-done((bf16[2048,384]{1,0:T(8,128)(2,1)}, bf16[2048,384]{1,0:T(8,128)(2,1)}, u32[]{:S(2)}, u32[]{:S(2)}) %collective-permute-start.9) | collective-permute-done | bytes 1572896 | tf_op jit(solution)/shard_map/ppermute | solution.py:570
  261.0 25.0 %attend.2 = (bf16[1024,1536]{1,0:T(8,128)(2,1)}, bf16[512,4096]{1,0:T(8,128)(2,1)}, f32[1024,1152]{1,0:T(8,128)}, f32[512,384]{1,0:T(8,128)}, f32[512,384]{1,0:T...) custom-call(s32[4]{0:T(128)} %maximum_convert_fusion.2.kind_ref, ...), custom_call_target="tpu_custom_call" | custom-call | tf_op jit(solution)/shard_map/attend/pallas_call | solution.py:365
  305.2 25.1 %attend.3 = (bf16[1024,1536]{1,0:T(8,128)(2,1)}, bf16[512,4096]{1,0:T(8,128)(2,1)}, f32[1024,1152]{1,0:T(8,128)}, f32[512,384]{1,0:T(8,128)}, f32[512,384]{1,0:T...) custom-call(s32[4]{0:T(128)} %maximum_convert_fusion.kind_ref, ...), custom_call_target="tpu_custom_call" | custom-call | tf_op jit(solution)/shard_map/attend/pallas_call | solution.py:365
  350.1 26.2 %feed.2 = (bf16[1024,1536]{1,0:T(8,128)(2,1)}, bf16[1024,1536]{1,0:T(8,128)(2,1)}, bf16[1024,1024]{1,0:T(8,128)(2,1)}, bf16[1024,1024]{1,0:T(8,128)(2,1)}, bf16[...) custom-call(bf16[512,1536]{1,0:T(8,128)(2,1)} %copy-done.17, ...), custom_call_target="tpu_custom_call" | custom-call | tf_op jit(solution)/shard_map/feed/pallas_call | solution.py:527
  388.3 25.8 %feed.3 = (bf16[1024,1536]{1,0:T(8,128)(2,1)}, bf16[1024,1536]{1,0:T(8,128)(2,1)}, bf16[1024,1024]{1,0:T(8,128)(2,1)}, bf16[1024,1024]{1,0:T(8,128)(2,1)}, bf16[...) custom-call(bf16[512,1536]{1,0:T(8,128)(2,1)} %collective-permute-done.18.rows_ref, ...), custom_call_target="tpu_custom_call" | custom-call | tf_op jit(solution)/shard_map/feed/pallas_call | solution.py:527
  432.7 7.5 product.13
  440.2 7.6 product.16
  447.7 8.6 %product.17 = f32[512,1536]{1,0:T(8,128)} custom-call(s32[1]{0:T(128)} %bitcast.45.first_ref, bf16[1024,1024]{1,0:T(8,128)(2,1)} %get-tuple-element.500.refs_0_.hidden_ref, bf16[1024,1024]{1,0:T(8,128)(2,1)} %get-tuple-element.478.refs_1_.hidden_ref, bf16[1024,1536]{1,0:T(8,128)(2,1)} %get-tuple-element.401.refs_2_, ...), custom_call_target="tpu_custom_call" | custom-call | tf_op jit(solution)/shard_map/product/pallas_call | solution.py:447
  456.4 8.1 %product.14 = bf16[512,1536]{1,0:T(8,128)(2,1)} custom-call(s32[1]{0:T(128)} %bitcast.44.first_ref, bf16[1024,1024]{1,0:T(8,128)(2,1)} %get-tuple-element.500.refs_0_.hidden_ref, bf16[1024,1024]{1,0:T(8,128)(2,1)} %get-tuple-element.478.refs_1_.hidden_ref, bf16[1024,1536]{1,0:T(8,128)(2,1)} %get-tuple-element.401.refs_2_, ...), custom_call_target="tpu_custom_call" | custom-call | tf_op jit(solution)/shard_map/product/pallas_call | solution.py:447
  464.5 7.5 product.15
  487.5 31.5 %attend_back.2 = (bf16[1024,1536]{1,0:T(8,128)(2,1)}, bf16[1024,1152]{1,0:T(8,128)(2,1)}, bf16[512,768]{1,0:T(8,128)(2,1)}, f32[512,1536]{1,0:T(8,128)}, bf16[512,1536]{1,0:T(8,128)(2,1)}, /*index=5*/f32[4,384]{1,0:T(4,128)}) custom-call(s32[4]{0:T(128)} %maximum_convert_fusion.kind_ref, s32[4]{0:T(128)} %maximum_convert_fusion.1.len_ref, ...), custom_call_target="tpu_custom_call" | custom-call | tf_op jit(solution)/shard_map/attend_back/pallas_call | solution.py:395
  526.5 30.9 %attend_back.3 = (bf16[1024,1536]{1,0:T(8,128)(2,1)}, bf16[1024,1152]{1,0:T(8,128)(2,1)}, bf16[512,768]{1,0:T(8,128)(2,1)}, f32[512,1536]{1,0:T(8,128)}, bf16[512,1536]{1,0:T(8,128)(2,1)}, /*index=5*/f32[4,384]{1,0:T(4,128)}) custom-call(s32[4]{0:T(128)} %maximum_convert_fusion.2.kind_ref, s32[4]{0:T(128)} %maximum_convert_fusion.3.len_ref, ...), custom_call_target="tpu_custom_call" | custom-call | tf_op jit(solution)/shard_map/attend_back/pallas_call | solution.py:395
  557.4 8.4 %product.18 = bf16[768,1152]{1,0:T(8,128)(2,1)} custom-call(s32[1]{0:T(128)} %constant.578.clone.1.first_ref, bf16[1024,1536]{1,0:T(8,128)(2,1)} %get-tuple-element.449.refs_0_, bf16[1024,1536]{1,0:T(8,128)(2,1)} %get-tuple-element.450.refs_1_, bf16[1024,1152]{1,0:T(8,128)(2,1)} %get-tuple-element.475.refs_2_, bf16[1024,1152]{1,0:T(8,128)(2,1)} %get-tuple-element.476.refs_3_), custom_call_target="tpu_custom_call" | custom-call | tf_op jit(solution)/shard_map/product/pallas_call | solution.py:447
  587.1 8.3 %result.2 = (f32[512,1536]{1,0:T(8,128)}, bf16[512,1536]{1,0:T(8,128)(2,1)}) custom-call(bf16[1024,1024]{1,0:T(8,128)(2,1)} %get-tuple-element.478.refs_1_.hidden_ref, bf16[1024,1536]{1,0:T(8,128)(2,1)} %bitcast.188), custom_call_target="tpu_custom_call" | custom-call | tf_op jit(solution)/shard_map/result/pallas_call | solution.py:558
  595.4 8.7 %product.22 = f32[768,1152]{1,0:T(8,128)} custom-call(s32[1]{0:T(128)} %constant.580.clone.1.first_ref, bf16[1024,1536]{1,0:T(8,128)(2,1)} %get-tuple-element.449.refs_0_, bf16[1024,1536]{1,0:T(8,128)(2,1)} %get-tuple-element.450.refs_1_, bf16[1024,1152]{1,0:T(8,128)(2,1)} %get-tuple-element.475.refs_2_, bf16[1024,1152]{1,0:T(8,128)(2,1)} %get-tuple-element.476.refs_3_), custom_call_target="tpu_custom_call" | custom-call | tf_op jit(solution)/shard_map/product/pallas_call | solution.py:447
  635.9 7.9 product.23
  655.5 8.4 %result.3 = (f32[512,1536]{1,0:T(8,128)}, bf16[512,1536]{1,0:T(8,128)(2,1)}) custom-call(bf16[1024,1024]{1,0:T(8,128)(2,1)} %get-tuple-element.500.refs_0_.hidden_ref, bf16[1024,1536]{1,0:T(8,128)(2,1)} %bitcast.189), custom_call_target="tpu_custom_call" | custom-call | tf_op jit(solution)/shard_map/result/pallas_call | solution.py:558
  684.1 10.3 %collective-permute-done.36 = bf16[512,1536]{1,0:T(8,128)(2,1)} collective-permute-done((bf16[512,1536]{1,0:T(8,128)(2,1)}, bf16[512,1536]{1,0:T(8,128)(2,1)}, u32[]{:S(2)}, u32[]{:S(2)}) %collective-permute-start.36) | collective-permute-done | bytes 1572896 | tf_op jit(solution)/shard_map/ppermute | solution.py:570
  715.5 8.4 %fusion.14 = (bf16[512,1536]{1,0:T(8,128)(2,1)}, f32[512,1536]{1,0:T(8,128)S(1)}, f32[512,1536]{1,0:T(8,128)}) fusion(f32[512,1536]{1,0:T(8,128)S(1)} %get-tuple-element.589, f32[2,1536]{1,0:T(2,128)S(1)} %copy-done.51, bf16[512,1536]{1,0:T(8,128)(2,1)} %collective-permute-done.36, f32[512,1536]{1,0:T(8,128)} %get-tuple-element.518, ...), kind=kLoop, calls=%fused_computation.34 | loop fusion | flops 18087936 | bytes 26796032 | tf_op jit(solution)/shard_map/convert_element_type | solution.py:1052
  731.3 51.1 %all_to_all.52 = bf16[32,2,6288]{2,1,0:T(2,128)(2,1)} all-to-all(bf16[32,2,6288]{2,1,0:T(2,128)(2,1)S(1)} %pad_maximum_fusion.3), channel_id=1, replica_groups=mesh['hi'=2,'mid'=2,'core'=2,'rep'=4] {'hi','mid','core','rep'}, dimensions={0} | all-to-all | bytes 1609728 | tf_op jit(solution)/shard_map/all_to_all | solution.py:1072
  (451 shorter events, 363.5 us)
Async XLA Ops:
  7.2 42.7 %all-gather.7.cloned.1.call-start = ((), (), s32[]{:S(2)}) async-start(), calls=%async_computation.14 | async-start | bytes 1966080 | tf_op jit(solution)/shard_map/all_gather | solution.py:758
  47.8 76.4 %all-gather.9.cloned.1.call-start = ((), (), s32[]{:S(2)}) async-start(), calls=%async_computation.15 | async-start | bytes 2949120 | tf_op jit(solution)/shard_map/all_gather | solution.py:758
  67.4 51.0 %collective-permute-start.1 = (bf16[256,4096]{1,0:T(8,128)(2,1)}, bf16[256,4096]{1,0:T(8,128)(2,1)}, u32[]{:S(2)}, u32[]{:S(2)}) collective-permute-start(bf16[256,4096]{1,0:T(8,128)(2,1)} %maximum_select_fusion.2.caption_ref), channel_id=1, source_target_pairs={{0,4},{4,0},{1,5},{5,1},{2,6},{6,2},{3,7},{7,3},{8,12},{12,8},{9,1... | collective-permute-start | bytes 6291464 | tf_op jit(solution)/shard_map/ppermute | solution.py:570
  75.4 42.4 %all-to-all-start.2 = ((bf16[32,2,6144]{2,1,0:T(2,128)(2,1)}), bf16[32,2,6144]{2,1,0:T(2,128)(2,1)S(1)}, u32[]{:S(2)}, u32[]{:S(2)}) async-start(bf16[32,2,6144]{2,1,0:T(2,128)(2,1)} %reshape.777), calls=%async_computation.2 | async-start | bytes 1572864 | tf_op jit(solution)/shard_map/all_to_all | solution.py:816
  79.4 100.4 %all-gather.17.cloned.1.call-start = ((), (), s32[]{:S(2)}) async-start(), calls=%async_computation.19 | async-start | bytes 1966080 | tf_op jit(solution)/shard_map/all_gather | solution.py:758
  79.4 44.8 %collective-permute-start = (bf16[512,1536]{1,0:T(8,128)(2,1)}, bf16[512,1536]{1,0:T(8,128)(2,1)}, u32[]{:S(2)}, u32[]{:S(2)}) collective-permute-start(bf16[512,1536]{1,0:T(8,128)(2,1)} %all-gather.7.cloned.1.call-done), channel_id=1, source_target_pairs={{0,16},{16,0},{1,17},{17,1},{2,18},{18,2},{3,19},{19,3},{4,20},{20... | collective-permute-start | bytes 4718600 | tf_op jit(solution)/shard_map/ppermute | solution.py:570
  125.2 74.3 %all-gather.15.cloned.1.call-start = ((), (), s32[]{:S(2)}) async-start(), calls=%async_computation.18 | async-start | bytes 1966080 | tf_op jit(solution)/shard_map/all_gather | solution.py:758
  126.6 53.2 %collective-permute-start.3 = (bf16[1024,1152]{1,0:T(8,128)(2,1)}, bf16[1024,1152]{1,0:T(8,128)(2,1)}, u32[]{:S(2)}, u32[]{:S(2)}) collective-permute-start(bf16[1024,1152]{1,0:T(8,128)(2,1)} %all-gather.9.cloned.1.call-done), channel_id=1, source_target_pairs={{0,16},{16,0},{1,17},{17,1},{2,18},{18,2},{3,19},{19,3},{4,20},{20... | collective-permute-start | bytes 7077896 | tf_op jit(solution)/shard_map/ppermute | solution.py:570
  127.3 47.1 %collective-permute-start.2 = (bf16[256,4096]{1,0:T(8,128)(2,1)}, bf16[256,4096]{1,0:T(8,128)(2,1)}, u32[]{:S(2)}, u32[]{:S(2)}) collective-permute-start(bf16[256,4096]{1,0:T(8,128)(2,1)} %maximum_select_fusion.2.caption_ref), channel_id=1, source_target_pairs={{0,8},{8,0},{1,9},{9,1},{2,10},{10,2},{3,11},{11,3},{4,12},{12,4},... | collective-permute-start | bytes 6291464 | tf_op jit(solution)/shard_map/ppermute | solution.py:570
  130.2 107.2 %all-gather.13.cloned.1.call-start = ((), (), s32[]{:S(2)}) async-start(), calls=%async_computation.17 | async-start | bytes 1966080 | tf_op jit(solution)/shard_map/all_gather | solution.py:758
  179.8 106.2 %all-gather.11.cloned.1.call-start = ((), (), s32[]{:S(2)}) async-start(), calls=%async_computation.16 | async-start | bytes 1966080 | tf_op jit(solution)/shard_map/all_gather | solution.py:758
  218.6 302.6 %reduce-scatter.6.cloned.1.call-start = ((), (), s32[]{:S(2)}) async-start(), calls=%async_computation.20 | async-start | bytes 1966080 | tf_op jit(solution)/shard_map/reduce_scatter | solution.py:710
  231.8 54.3 %collective-permute-start.12 = (bf16[512,1536]{1,0:T(8,128)(2,1)}, bf16[512,1536]{1,0:T(8,128)(2,1)}, u32[]{:S(2)}, u32[]{:S(2)}) collective-permute-start(bf16[512,1536]{1,0:T(8,128)(2,1)} %fusion.12.result_ref), channel_id=1, source_target_pairs={{0,8},{8,0},{1,9},{9,1},{2,10},{10,2},{3,11},{11,3},{4,12},{12,4},... | collective-permute-start | bytes 4718600 | tf_op jit(solution)/shard_map/ppermute | solution.py:570
  425.5 46.6 %collective-permute-start.22 = (bf16[512,1536]{1,0:T(8,128)(2,1)}, bf16[512,1536]{1,0:T(8,128)(2,1)}, u32[]{:S(2)}, u32[]{:S(2)}) collective-permute-start(bf16[512,1536]{1,0:T(8,128)(2,1)} %add_convert_fusion.7), channel_id=1, source_target_pairs={{0,8},{8,0},{1,9},{9,1},{2,10},{10,2},{3,11},{11,3},{4,12},{12,4},... | collective-permute-start | bytes 4718600 | tf_op jit(solution)/shard_map/ppermute | solution.py:570
  427.1 44.9 %collective-permute-start.23 = (bf16[768,1024]{1,0:T(8,128)(2,1)}, bf16[768,1024]{1,0:T(8,128)(2,1)}, u32[]{:S(2)}, u32[]{:S(2)}) collective-permute-start(bf16[768,1024]{1,0:T(8,128)(2,1)} %product.12), channel_id=1, source_target_pairs={{0,16},{16,0},{1,17},{17,1},{2,18},{18,2},{3,19},{19,3},{4,20},{20... | collective-permute-start | bytes 4718600 | tf_op jit(solution)/shard_map/ppermute | solution.py:570
  476.4 89.5 %reduce-scatter.8.cloned.1.call-start = ((), (), s32[]{:S(2)}) async-start(), calls=%async_computation.21 | async-start | bytes 1966080 | tf_op jit(solution)/shard_map/reduce_scatter | solution.py:710
  525.5 158.6 %reduce-scatter.10.cloned.1.call-start = ((), (), s32[]{:S(2)}) async-start(), calls=%async_computation.22 | async-start | bytes 1966080 | tf_op jit(solution)/shard_map/reduce_scatter | solution.py:710
  566.2 50.6 %collective-permute-start.30 = (bf16[768,1152]{1,0:T(8,128)(2,1)}, bf16[768,1152]{1,0:T(8,128)(2,1)}, u32[]{:S(2)}, u32[]{:S(2)}) collective-permute-start(bf16[768,1152]{1,0:T(8,128)(2,1)} %product.18), channel_id=1, source_target_pairs={{0,16},{16,0},{1,17},{17,1},{2,18},{18,2},{3,19},{19,3},{4,20},{20... | collective-permute-start | bytes 5308424 | tf_op jit(solution)/shard_map/ppermute | solution.py:570
  574.0 45.8 %collective-permute-start.32 = (bf16[512,1536]{1,0:T(8,128)(2,1)}, bf16[512,1536]{1,0:T(8,128)(2,1)}, u32[]{:S(2)}, u32[]{:S(2)}) collective-permute-start(bf16[512,1536]{1,0:T(8,128)(2,1)} %add_convert_fusion.4), channel_id=1, source_target_pairs={{0,8},{8,0},{1,9},{9,1},{2,10},{10,2},{3,11},{11,3},{4,12},{12,4},... | collective-permute-start | bytes 4718600 | tf_op jit(solution)/shard_map/ppermute | solution.py:570
  575.8 125.8 %reduce-scatter.12.cloned.1.call-start = ((), (), s32[]{:S(2)}) async-start(), calls=%async_computation.23 | async-start | bytes 2949120 | tf_op jit(solution)/shard_map/reduce_scatter | solution.py:710
  630.8 70.8 %collective-permute-start.34 = (bf16[2048,768]{1,0:T(8,128)(2,1)}, bf16[2048,768]{1,0:T(8,128)(2,1)}, u32[]{:S(2)}, u32[]{:S(2)}) collective-permute-start(bf16[2048,768]{1,0:T(8,128)(2,1)} %product.19), channel_id=1, source_target_pairs={{0,16},{16,0},{1,17},{17,1},{2,18},{18,2},{3,19},{19,3},{4,20},{20... | collective-permute-start | bytes 9437192 | tf_op jit(solution)/shard_map/ppermute | solution.py:570
  631.9 41.7 %collective-permute-start.37 = (bf16[512,1536]{1,0:T(8,128)(2,1)}, bf16[512,1536]{1,0:T(8,128)(2,1)}, u32[]{:S(2)}, u32[]{:S(2)}) collective-permute-start(bf16[512,1536]{1,0:T(8,128)(2,1)} %get-tuple-element.504), channel_id=1, source_target_pairs={{0,4},{4,0},{1,5},{5,1},{2,6},{6,2},{3,7},{7,3},{8,12},{12,8},{9,1... | collective-permute-start | bytes 4718600 | tf_op jit(solution)/shard_map/ppermute | solution.py:570
  649.0 137.3 %reduce-scatter.14.cloned.1.call-start = ((), (), s32[]{:S(2)}) async-start(), calls=%async_computation.24 | async-start | bytes 3932160 | tf_op jit(solution)/shard_map/reduce_scatter | solution.py:710
  653.0 41.3 %collective-permute-start.36 = (bf16[512,1536]{1,0:T(8,128)(2,1)}, bf16[512,1536]{1,0:T(8,128)(2,1)}, u32[]{:S(2)}, u32[]{:S(2)}) collective-permute-start(bf16[512,1536]{1,0:T(8,128)(2,1)} %add_convert_fusion.2), channel_id=1, source_target_pairs={{0,8},{8,0},{1,9},{9,1},{2,10},{10,2},{3,11},{11,3},{4,12},{12,4},... | collective-permute-start | bytes 4718600 | tf_op jit(solution)/shard_map/ppermute | solution.py:570
  (107 other events, 1744.4 us)
Sparse Core Ops, SparseCore 0:
  9.6 37.7 all-gather.6
  50.8 63.0 all-gather.8
  125.3 36.1 all-gather.16
  163.5 35.9 all-gather.14
  201.5 35.9 all-gather.12
  238.9 35.9 all-gather.10
  476.5 33.7 reduce-scatter.5
  525.6 34.9 reduce-scatter.7
  575.9 33.7 reduce-scatter.9
  630.8 47.7 reduce-scatter.11
  707.9 78.3 reduce-scatter.13
